TPU v7x, 32 devices: a whole 2x2x4 slice. The times are simulated.
32 devices in a mesh: ctx: 16 (over z, y, x), head: 2 (over core).
Axes of the slice: x: 2, y: 2, z: 4, core: 2. Of those that a mesh axis runs over, the one named last changes fastest.
Arguments:
- queries: bfloat16 [2048, 2048], P('ctx', 'head'), may hold values from -16 to 16
- key_rows: bfloat16 [2048, 2048], P('ctx', 'head'), may hold values from -16 to 16
- value_rows: bfloat16 [2048, 2048], P('ctx', 'head'), may hold values from -16 to 16
- out_weight: bfloat16 [2048, 2048], P('head'), may hold values from -0.125 to 0.125
- cotangent: bfloat16 [2048, 2048], P('ctx', 'head'), may hold values from -48 to 48
Outputs:
- output: bfloat16 [2048, 2048], P('ctx', 'head')
- grad_queries: bfloat16 [2048, 2048], P('ctx', 'head')
- grad_keys: bfloat16 [2048, 2048], P('ctx', 'head')
- grad_values: bfloat16 [2048, 2048], P('ctx', 'head')
All inputs are finite; a program needn't handle non-finite values.
Results may differ from a plain program's by a relative error of at most 0.025.
Values may be sent and summed in bfloat16 or wider, within the bound.
No kernel may reach another device: no remote copies, remote signals or barrier semaphores. Data moves between devices by JAX's collectives and lax.ppermute only.
A program may use at most 64 MiB of HBM per device.

v0:
```python
import jax
import jax.numpy as jnp
from jax import lax
from jax.sharding import PartitionSpec as P

DH = 128
LEAF = 128


def from_partner(block, axis, distance):
    count = lax.axis_size(axis)
    route = []
    for low in range(count):
        high = low | 1 << distance
        if high != low and high < count:
            route += [(low, high), (high, low)]
    return lax.ppermute(block, axis, route)


def pool_pairs(matrix):
    shaped = matrix.reshape((matrix.shape[0] // 2, 2) + matrix.shape[1:]).astype(jnp.float32)
    return ((shaped[:, 0] + shaped[:, 1]) * 0.5).astype(jnp.bfloat16)


def spread_pairs(gradient):
    halved = gradient * 0.5
    doubled = jnp.broadcast_to(halved[:, None], (halved.shape[0], 2) + halved.shape[1:])
    return doubled.reshape((halved.shape[0] * 2,) + halved.shape[1:])


def block_scores(query_heads, key_blocks):
    queried = query_heads.reshape((key_blocks.shape[0], -1) + query_heads.shape[1:])
    scored = jnp.einsum("cwhd,cbhd->cwhb", queried, key_blocks, preferred_element_type=jnp.float32)
    return scored.reshape(query_heads.shape[0], query_heads.shape[1], LEAF) * DH ** (-0.5)


def body(queries, key_rows, value_rows, out_weight, cotangent):
    token_count = queries.shape[0]
    local_heads = queries.shape[1] // DH
    head_shape = (token_count, local_heads, DH)
    query_heads = queries.reshape(head_shape)
    key_heads = key_rows.reshape(head_shape)
    value_heads = value_rows.reshape(head_shape)
    device_index = lax.axis_index("ctx")
    cross_rounds = lax.axis_size("ctx").bit_length() - 1
    local_levels = (token_count // LEAF).bit_length() - 1
    block_shape = (token_count // LEAF, LEAF, local_heads, DH)
    key_sets = [(key_heads.reshape(block_shape), value_heads.reshape(block_shape))]
    span_keys, span_values = (key_heads, value_heads)
    for round_index in range(cross_rounds):
        far_keys, far_values = from_partner((span_keys, span_values), "ctx", round_index)
        key_sets.append((far_keys[None], far_values[None]))
        if round_index + 1 < cross_rounds:
            upper_half = device_index >> round_index & 1 == 1
            span_keys = pool_pairs(
                jnp.concatenate(
                    [
                        jnp.where(upper_half, far_keys, span_keys),
                        jnp.where(upper_half, span_keys, far_keys),
                    ],
                    0,
                )
            )
            span_values = pool_pairs(
                jnp.concatenate(
                    [
                        jnp.where(upper_half, far_values, span_values),
                        jnp.where(upper_half, span_values, far_values),
                    ],
                    0,
                )
            )
    scores = [block_scores(query_heads, key_blocks) for key_blocks, value_blocks in key_sets]
    row_max = jnp.max(scores[0], -1)
    for scored in scores[1:]:
        row_max = jnp.maximum(row_max, jnp.max(scored, -1))
    weights = [jnp.exp(scored - row_max[..., None]) for scored in scores]
    row_total = jnp.zeros((token_count, local_heads), jnp.float32)
    for weight_block in weights:
        row_total = row_total + jnp.sum(weight_block, -1)
    numerator = jnp.zeros(head_shape, jnp.float32)
    for weight_block, (key_blocks, value_blocks) in zip(weights, key_sets):
        block_count = key_blocks.shape[0]
        rounded = weight_block.astype(jnp.bfloat16).reshape(block_count, -1, local_heads, LEAF)
        numerator = numerator + jnp.einsum(
            "cwhb,cbhd->cwhd", rounded, value_blocks, preferred_element_type=jnp.float32
        ).reshape(head_shape)
    attended = (numerator / row_total[..., None]).astype(jnp.bfloat16)
    partial_sums = jnp.dot(
        attended.reshape(token_count, -1), out_weight, preferred_element_type=jnp.float32
    )
    output = lax.psum_scatter(partial_sums, "head", scatter_dimension=1, tiled=True).astype(
        jnp.bfloat16
    )
    full_cotangent = lax.all_gather(cotangent, "head", axis=1, tiled=True)
    grad_attended = (
        lax.dot_general(
            full_cotangent, out_weight, (((1,), (1,)), ((), ())), preferred_element_type=jnp.float32
        )
        .astype(jnp.bfloat16)
        .reshape(head_shape)
    )
    row_delta = jnp.sum(grad_attended.astype(jnp.float32) * attended.astype(jnp.float32), -1)
    query_grad = jnp.zeros(head_shape, jnp.float32)
    key_grads = []
    value_grads = []
    for weight_block, (key_blocks, value_blocks) in zip(weights, key_sets):
        block_count = key_blocks.shape[0]
        probabilities = weight_block / row_total[..., None]
        grad_blocks = grad_attended.reshape(block_count, -1, local_heads, DH)
        query_blocks = query_heads.reshape(block_count, -1, local_heads, DH)
        value_dots = jnp.einsum(
            "cwhd,cbhd->cwhb", grad_blocks, value_blocks, preferred_element_type=jnp.float32
        ).reshape(token_count, local_heads, LEAF)
        score_grad = (
            (probabilities * (value_dots - row_delta[..., None]))
            .astype(jnp.bfloat16)
            .reshape(block_count, -1, local_heads, LEAF)
        )
        query_grad = query_grad + jnp.einsum(
            "cwhb,cbhd->cwhd", score_grad, key_blocks, preferred_element_type=jnp.float32
        ).reshape(head_shape)
        key_grads.append(
            jnp.einsum(
                "cwhb,cwhd->cbhd", score_grad, query_blocks, preferred_element_type=jnp.float32
            )
            * DH ** (-0.5)
        )
        rounded_probs = probabilities.astype(jnp.bfloat16).reshape(
            block_count, -1, local_heads, LEAF
        )
        value_grads.append(
            jnp.einsum(
                "cwhb,cwhd->cbhd", rounded_probs, grad_blocks, preferred_element_type=jnp.float32
            )
        )
    grad_queries = (query_grad * DH ** (-0.5)).astype(jnp.bfloat16).reshape(token_count, -1)
    up_keys = jnp.zeros((LEAF, local_heads, DH), jnp.float32)
    up_values = jnp.zeros((LEAF, local_heads, DH), jnp.float32)
    for round_index in reversed(range(cross_rounds)):
        pair_index = 1 + local_levels + round_index
        upper_half = device_index >> round_index & 1 == 1
        spread_keys = spread_pairs(up_keys)
        spread_values = spread_pairs(up_values)
        own_part_keys = jnp.where(upper_half, spread_keys[LEAF:], spread_keys[:LEAF])
        own_part_values = jnp.where(upper_half, spread_values[LEAF:], spread_values[:LEAF])
        send_keys = key_grads[pair_index][0] + jnp.where(
            upper_half, spread_keys[:LEAF], spread_keys[LEAF:]
        )
        send_values = value_grads[pair_index][0] + jnp.where(
            upper_half, spread_values[:LEAF], spread_values[LEAF:]
        )
        back_keys, back_values = from_partner((send_keys, send_values), "ctx", round_index)
        up_keys = own_part_keys + back_keys
        up_values = own_part_values + back_values
    grad_keys = (
        (key_grads[0].reshape(head_shape) + up_keys).astype(jnp.bfloat16).reshape(token_count, -1)
    )
    grad_values = (
        (value_grads[0].reshape(head_shape) + up_values)
        .astype(jnp.bfloat16)
        .reshape(token_count, -1)
    )
    return (output, grad_queries, grad_keys, grad_values)


def solution(mesh):
    return jax.shard_map(
        body,
        mesh=mesh,
        in_specs=(
            P("ctx", "head"),
            P("ctx", "head"),
            P("ctx", "head"),
            P("head", None),
            P("ctx", "head"),
        ),
        out_specs=(P("ctx", "head"), P("ctx", "head"), P("ctx", "head"), P("ctx", "head")),
        check_vma=False,
    )
```

profile of v0, /device:TPU:0, one launch (start us, length us, event | category | flops | bytes accessed | tf_op | source)
XLA Modules:
  0.0 186.1 jit_solution(8288524025871888588)
XLA Ops:
  7.2 1.2 copy.69
  8.6 3.0 %collective-permute-start = (bf16[128,8,128]{2,0,1:T(8,128)(2,1)S(1)}, bf16[128,8,128]{2,0,1:T(8,128)(2,1)S(1)}, u32[]{:S(2)}, u32[]{:S(2)}) collective-permute-start(bf16[128,8,128]{2,0,1:T(8,128)(2,1)S(1)} %copy.72), channel_id=1, source_target_pairs={{0,2},{2,0},{4,6},{6,4},{8,10},{10,8},{12,14},{14,12},{16,18},{18,... | collective-permute-start | bytes 786440 | tf_op jit(solution)/shard_map/ppermute | solution.py:17
  11.6 1.1 copy.85
  13.0 2.4 %all_gather.3 = bf16[128,2048]{1,0:T(8,128)(2,1)S(1)} all-gather(bf16[128,1024]{1,0:T(8,128)(2,1)} %param.9), channel_id=1, replica_groups=mesh['ctx'=16,'head'=2] {'head'}, dimensions={1}, use_global_device_ids=true | all-gather | bytes 786432 | tf_op jit(solution)/shard_map/all_gather | solution.py:95
  15.4 3.7 %convolution_convert_fusion = bf16[128,1024]{1,0:T(8,128)(2,1)S(1)} fusion(bf16[128,2048]{1,0:T(8,128)(2,1)S(1)} %all_gather.3, bf16[1024,2048]{1,0:T(8,128)(2,1)} %param.8), kind=kOutput, calls=%fused_computation.56 | convolution fusion | flops 537001984 | bytes 4980736 | tf_op jit(solution)/shard_map/dot_general | solution.py:97
  19.1 0.8 copy.106
  20.0 0.3 bitcast_reduce_fusion.4
  20.3 3.2 %collective-permute-done.4 = bf16[128,8,128]{2,0,1:T(8,128)(2,1)S(1)} collective-permute-done((bf16[128,8,128]{2,0,1:T(8,128)(2,1)S(1)}, bf16[128,8,128]{2,0,1:T(8,128)(2,1)S(1)}, u32[]{:S(2)}, u32[]{:S(2)}) %collective-permute-start.4) | collective-permute-done | bytes 262176 | tf_op jit(solution)/shard_map/ppermute | solution.py:17
  23.6 1.0 fusion.133
  24.7 1.8 collective-permute-start.1
  26.5 1.0 fusion.134
  27.6 0.3 collective-permute-start.5
  27.9 0.3 bitcast_reduce_fusion.3
  28.2 5.8 %collective-permute-done.1 = bf16[128,8,128]{2,0,1:T(8,128)(2,1)S(1)} collective-permute-done((bf16[128,8,128]{2,0,1:T(8,128)(2,1)S(1)}, bf16[128,8,128]{2,0,1:T(8,128)(2,1)S(1)}, u32[]{:S(2)}, u32[]{:S(2)}) %collective-permute-start.1) | collective-permute-done | bytes 262176 | tf_op jit(solution)/shard_map/ppermute | solution.py:17
  34.1 1.0 fusion.132
  35.1 1.9 %collective-permute-start.2 = (bf16[128,8,128]{2,0,1:T(8,128)(2,1)S(1)}, bf16[128,8,128]{2,0,1:T(8,128)(2,1)S(1)}, u32[]{:S(2)}, u32[]{:S(2)}) collective-permute-start(bf16[128,8,128]{2,0,1:T(8,128)(2,1)S(1)} %fusion.82), channel_id=1, source_target_pairs={{0,8},{8,0},{2,10},{10,2},{4,12},{12,4},{6,14},{14,6},{16,24},{24,... | collective-permute-start | bytes 786440 | tf_op jit(solution)/shard_map/ppermute | solution.py:17
  37.0 0.8 collective-permute-done.5
  38.0 0.6 copy.96
  38.9 1.6 collective-permute-start.6
  40.4 0.3 bitcast_reduce_fusion.2
  40.8 2.5 %collective-permute-done.2 = bf16[128,8,128]{2,0,1:T(8,128)(2,1)S(1)} collective-permute-done((bf16[128,8,128]{2,0,1:T(8,128)(2,1)S(1)}, bf16[128,8,128]{2,0,1:T(8,128)(2,1)S(1)}, u32[]{:S(2)}, u32[]{:S(2)}) %collective-permute-start.2) | collective-permute-done | bytes 262176 | tf_op jit(solution)/shard_map/ppermute | solution.py:17
  43.3 1.0 fusion.131
  44.4 5.5 %collective-permute-start.3 = (bf16[128,8,128]{2,0,1:T(8,128)(2,1)S(1)}, bf16[128,8,128]{2,0,1:T(8,128)(2,1)S(1)}, u32[]{:S(2)}, u32[]{:S(2)}) collective-permute-start(bf16[128,8,128]{2,0,1:T(8,128)(2,1)S(1)} %fusion.83), channel_id=1, source_target_pairs={{0,16},{16,0},{2,18},{18,2},{4,20},{20,4},{6,22},{22,6},{8,24},{24... | collective-permute-start | bytes 786440 | tf_op jit(solution)/shard_map/ppermute | solution.py:17
  50.1 0.6 copy.101
  51.0 2.5 %collective-permute-start.7 = (bf16[128,8,128]{2,0,1:T(8,128)(2,1)S(1)}, bf16[128,8,128]{2,0,1:T(8,128)(2,1)S(1)}, u32[]{:S(2)}, u32[]{:S(2)}) collective-permute-start(bf16[128,8,128]{2,0,1:T(8,128)(2,1)S(1)} %fusion.86), channel_id=1, source_target_pairs={{0,16},{16,0},{2,18},{18,2},{4,20},{20,4},{6,22},{22,6},{8,24},{24... | collective-permute-start | bytes 786440 | tf_op jit(solution)/shard_map/ppermute | solution.py:17
  53.5 0.3 bitcast_reduce_fusion.1
  53.8 11.2 %collective-permute-done.3 = bf16[128,8,128]{2,0,1:T(8,128)(2,1)S(1)} collective-permute-done((bf16[128,8,128]{2,0,1:T(8,128)(2,1)S(1)}, bf16[128,8,128]{2,0,1:T(8,128)(2,1)S(1)}, u32[]{:S(2)}, u32[]{:S(2)}) %collective-permute-start.3) | collective-permute-done | bytes 262176 | tf_op jit(solution)/shard_map/ppermute | solution.py:17
  65.0 0.3 bitcast_reduce_fusion
  65.6 0.5 fusion.49
  66.4 2.5 %collective-permute-done.7 = bf16[128,8,128]{2,0,1:T(8,128)(2,1)S(1)} collective-permute-done((bf16[128,8,128]{2,0,1:T(8,128)(2,1)S(1)}, bf16[128,8,128]{2,0,1:T(8,128)(2,1)S(1)}, u32[]{:S(2)}, u32[]{:S(2)}) %collective-permute-start.7) | collective-permute-done | bytes 262176 | tf_op jit(solution)/shard_map/ppermute | solution.py:17
  68.9 0.7 copy-done.25
  70.2 0.3 multiply_reduce_fusion
  70.6 1.7 fusion.135
  72.4 1.3 convolution_bitcast_fusion.4
  73.7 1.3 fusion.32
  75.8 0.4 fusion.34
  76.5 2.8 %collective-permute-start.12 = (f32[128,8,128]{2,0,1:T(8,128)S(1)}, f32[128,8,128]{2,0,1:T(8,128)S(1)}, u32[]{:S(2)}, u32[]{:S(2)}) collective-permute-start(f32[128,8,128]{2,0,1:T(8,128)S(1)} %convolution_bitcast_fusion.4), channel_id=1, source_target_pairs={{0,16},{16,0},{2,18},{18,2},{4,20},{20,4},{6,22},{22,6},{8,24},{24... | collective-permute-start | bytes 1572872 | tf_op jit(solution)/shard_map/ppermute | solution.py:17
  79.3 1.1 fusion.137
  80.3 1.1 fusion.136
  82.3 28.6 %collective-permute-done.8 = f32[128,8,128]{2,0,1:T(8,128)S(1)} collective-permute-done((f32[128,8,128]{2,0,1:T(8,128)S(1)}, f32[128,8,128]{2,0,1:T(8,128)S(1)}, u32[]{:S(2)}, u32[]{:S(2)}) %collective-permute-start.8) | collective-permute-done | bytes 524320 | tf_op jit(solution)/shard_map/ppermute | solution.py:17
  111.5 10.6 %collective-permute-done.12 = f32[128,8,128]{2,0,1:T(8,128)S(1)} collective-permute-done((f32[128,8,128]{2,0,1:T(8,128)S(1)}, f32[128,8,128]{2,0,1:T(8,128)S(1)}, u32[]{:S(2)}, u32[]{:S(2)}) %collective-permute-start.12) | collective-permute-done | bytes 524320 | tf_op jit(solution)/shard_map/ppermute | solution.py:17
  122.5 10.8 %collective-permute-done.9 = f32[128,8,128]{2,0,1:T(8,128)S(1)} collective-permute-done((f32[128,8,128]{2,0,1:T(8,128)S(1)}, f32[128,8,128]{2,0,1:T(8,128)S(1)}, u32[]{:S(2)}, u32[]{:S(2)}) %collective-permute-start.9) | collective-permute-done | bytes 524320 | tf_op jit(solution)/shard_map/ppermute | solution.py:17
  134.0 1.6 collective-permute-start.10
  135.6 8.8 %collective-permute-done.13 = f32[128,8,128]{2,0,1:T(8,128)S(1)} collective-permute-done((f32[128,8,128]{2,0,1:T(8,128)S(1)}, f32[128,8,128]{2,0,1:T(8,128)S(1)}, u32[]{:S(2)}, u32[]{:S(2)}) %collective-permute-start.13) | collective-permute-done | bytes 524320 | tf_op jit(solution)/shard_map/ppermute | solution.py:17
  145.0 0.3 fusion
  145.3 1.6 collective-permute-start.14
  146.8 1.0 collective-permute-done.10
  148.1 0.8 slice_select_fusion.6
  149.1 1.0 fusion.3
  150.1 1.5 collective-permute-start.11
  151.6 7.6 %collective-permute-done.14 = f32[128,8,128]{2,0,1:T(8,128)S(1)} collective-permute-done((f32[128,8,128]{2,0,1:T(8,128)S(1)}, f32[128,8,128]{2,0,1:T(8,128)S(1)}, u32[]{:S(2)}, u32[]{:S(2)}) %collective-permute-start.14) | collective-permute-done | bytes 524320 | tf_op jit(solution)/shard_map/ppermute | solution.py:17
  159.4 0.7 slice_select_fusion
  160.4 1.1 copy.142
  161.4 2.2 %fusion.1 = f32[128,8,128]{0,2,1:T(8,128)} fusion(f32[128,8,128]{0,2,1:T(8,128)} %copy.142, bf16[128,8,128]{0,2,1:T(8,128)(2,1)S(1)} %bitcast.539, f32[8,128,128]{2,1,0:T(8,128)S(1)} %get-tuple-element.62, f32[128,8]{0,1:T(8,128)S(1)} %add_add_fusion, f32[128,8]{0,1:T(8,128)S(1)} %maximum_maximum_fusion), kind=kOutput, calls=%fused_computation.11 | convolution fusion | flops 34078720 | bytes 1843200 | tf_op jit(solution)/shard_map/cwhb,cwhd->cbhd/dot_general | solution.py:133
  163.7 1.5 collective-permute-start.15
  165.1 1.4 fusion.31
  166.6 0.9 copy.144
  167.4 1.2 fusion.8
  169.1 1.8 convert_element_type.190
  171.1 1.1 add_convert_fusion.1
  172.4 0.9 copy.145
  173.2 3.9 %collective-permute-done.15 = f32[128,8,128]{0,2,1:T(8,128)} collective-permute-done((f32[128,8,128]{0,2,1:T(8,128)}, f32[128,8,128]{0,2,1:T(8,128)}, u32[]{:S(2)}, u32[]{:S(2)}) %collective-permute-start.15) | collective-permute-done | bytes 524320 | tf_op jit(solution)/shard_map/ppermute | solution.py:17
  177.1 1.4 add_convert_fusion
  178.4 0.9 copy.146
  (128 shorter events, 8.8 us)
Async XLA Ops:
  7.2 12.8 %copy-start = (bf16[128,1024]{1,0:T(8,128)(2,1)S(1)}, bf16[128,1024]{1,0:T(8,128)(2,1)}, u32[]{:S(2)}) copy-start(bf16[128,1024]{1,0:T(8,128)(2,1)} %param.5) | copy-start | bytes 786436
  7.2 161.9 %reduce-scatter.2.cloned.1.call-start = ((), (), s32[]{:S(2)}) async-start(), calls=%async_computation.1 | async-start | bytes 1572864 | tf_op jit(solution)/shard_map/reduce_scatter | solution.py:92
  8.6 11.7 %collective-permute-start = (bf16[128,8,128]{2,0,1:T(8,128)(2,1)S(1)}, bf16[128,8,128]{2,0,1:T(8,128)(2,1)S(1)}, u32[]{:S(2)}, u32[]{:S(2)}) collective-permute-start(bf16[128,8,128]{2,0,1:T(8,128)(2,1)S(1)} %copy.72), channel_id=1, source_target_pairs={{0,2},{2,0},{4,6},{6,4},{8,10},{10,8},{12,14},{14,12},{16,18},{18,... | collective-permute-start | bytes 786440 | tf_op jit(solution)/shard_map/ppermute | solution.py:17
  12.9 10.6 %collective-permute-start.4 = (bf16[128,8,128]{2,0,1:T(8,128)(2,1)S(1)}, bf16[128,8,128]{2,0,1:T(8,128)(2,1)S(1)}, u32[]{:S(2)}, u32[]{:S(2)}) collective-permute-start(bf16[128,8,128]{2,0,1:T(8,128)(2,1)S(1)} %copy.87), channel_id=1, source_target_pairs={{0,2},{2,0},{4,6},{6,4},{8,10},{10,8},{12,14},{14,12},{16,18},{18,... | collective-permute-start | bytes 786440 | tf_op jit(solution)/shard_map/ppermute | solution.py:17
  20.3 7.6 %copy-start.4 = (bf16[128,8,128]{2,0,1:T(8,128)(2,1)}, bf16[128,8,128]{2,0,1:T(8,128)(2,1)S(1)}, u32[]{:S(2)}) copy-start(bf16[128,8,128]{2,0,1:T(8,128)(2,1)S(1)} %collective-permute-done) | copy-start | bytes 786436
  23.5 4.0 %copy-start.9 = (bf16[128,8,128]{2,0,1:T(8,128)(2,1)}, bf16[128,8,128]{2,0,1:T(8,128)(2,1)S(1)}, u32[]{:S(2)}) copy-start(bf16[128,8,128]{2,0,1:T(8,128)(2,1)S(1)} %collective-permute-done.4) | copy-start | bytes 786436
  24.7 9.3 %collective-permute-start.1 = (bf16[128,8,128]{2,0,1:T(8,128)(2,1)S(1)}, bf16[128,8,128]{2,0,1:T(8,128)(2,1)S(1)}, u32[]{:S(2)}, u32[]{:S(2)}) collective-permute-start(bf16[128,8,128]{2,0,1:T(8,128)(2,1)S(1)} %fusion.81), channel_id=1, source_target_pairs={{0,4},{4,0},{2,6},{6,2},{8,12},{12,8},{10,14},{14,10},{16,20},{20,... | collective-permute-start | bytes 786440 | tf_op jit(solution)/shard_map/ppermute | solution.py:17
  27.6 10.3 %collective-permute-start.5 = (bf16[128,8,128]{2,0,1:T(8,128)(2,1)S(1)}, bf16[128,8,128]{2,0,1:T(8,128)(2,1)S(1)}, u32[]{:S(2)}, u32[]{:S(2)}) collective-permute-start(bf16[128,8,128]{2,0,1:T(8,128)(2,1)S(1)} %fusion.84), channel_id=1, source_target_pairs={{0,4},{4,0},{2,6},{6,2},{8,12},{12,8},{10,14},{14,10},{16,20},{20,... | collective-permute-start | bytes 786440 | tf_op jit(solution)/shard_map/ppermute | solution.py:17
  34.0 6.5 %copy-start.2 = (bf16[128,8,128]{2,0,1:T(8,128)(2,1)}, bf16[128,8,128]{2,0,1:T(8,128)(2,1)S(1)}, u32[]{:S(2)}) copy-start(bf16[128,8,128]{2,0,1:T(8,128)(2,1)S(1)} %collective-permute-done.1) | copy-start | bytes 786436
  35.1 8.1 %collective-permute-start.2 = (bf16[128,8,128]{2,0,1:T(8,128)(2,1)S(1)}, bf16[128,8,128]{2,0,1:T(8,128)(2,1)S(1)}, u32[]{:S(2)}, u32[]{:S(2)}) collective-permute-start(bf16[128,8,128]{2,0,1:T(8,128)(2,1)S(1)} %fusion.82), channel_id=1, source_target_pairs={{0,8},{8,0},{2,10},{10,2},{4,12},{12,4},{6,14},{14,6},{16,24},{24,... | collective-permute-start | bytes 786440 | tf_op jit(solution)/shard_map/ppermute | solution.py:17
  37.8 32.3 %copy-start.15 = (bf16[128,8,128]{2,0,1:T(8,128)(2,1)}, bf16[128,8,128]{2,0,1:T(8,128)(2,1)S(1)}, u32[]{:S(2)}) copy-start(bf16[128,8,128]{2,0,1:T(8,128)(2,1)S(1)} %collective-permute-done.5) | copy-start | bytes 786436
  38.9 11.1 %collective-permute-start.6 = (bf16[128,8,128]{2,0,1:T(8,128)(2,1)S(1)}, bf16[128,8,128]{2,0,1:T(8,128)(2,1)S(1)}, u32[]{:S(2)}, u32[]{:S(2)}) collective-permute-start(bf16[128,8,128]{2,0,1:T(8,128)(2,1)S(1)} %fusion.85), channel_id=1, source_target_pairs={{0,8},{8,0},{2,10},{10,2},{4,12},{12,4},{6,14},{14,6},{16,24},{24,... | collective-permute-start | bytes 786440 | tf_op jit(solution)/shard_map/ppermute | solution.py:17
  43.2 10.2 %copy-start.6 = (bf16[128,8,128]{2,0,1:T(8,128)(2,1)}, bf16[128,8,128]{2,0,1:T(8,128)(2,1)S(1)}, u32[]{:S(2)}) copy-start(bf16[128,8,128]{2,0,1:T(8,128)(2,1)S(1)} %collective-permute-done.2) | copy-start | bytes 786436
  44.4 20.6 %collective-permute-start.3 = (bf16[128,8,128]{2,0,1:T(8,128)(2,1)S(1)}, bf16[128,8,128]{2,0,1:T(8,128)(2,1)S(1)}, u32[]{:S(2)}, u32[]{:S(2)}) collective-permute-start(bf16[128,8,128]{2,0,1:T(8,128)(2,1)S(1)} %fusion.83), channel_id=1, source_target_pairs={{0,16},{16,0},{2,18},{18,2},{4,20},{20,4},{6,22},{22,6},{8,24},{24... | collective-permute-start | bytes 786440 | tf_op jit(solution)/shard_map/ppermute | solution.py:17
  50.0 16.1 %copy-start.17 = (bf16[128,8,128]{2,0,1:T(8,128)(2,1)}, bf16[128,8,128]{2,0,1:T(8,128)(2,1)S(1)}, u32[]{:S(2)}) copy-start(bf16[128,8,128]{2,0,1:T(8,128)(2,1)S(1)} %collective-permute-done.6) | copy-start | bytes 786436
  51.0 18.9 %copy-start.10 = (bf16[128,8,128]{2,0,1:T(8,128)(2,1)S(1)}, bf16[128,8,128]{2,0,1:T(8,128)(2,1)}, u32[]{:S(2)}) copy-start(bf16[128,8,128]{2,0,1:T(8,128)(2,1)} %copy-done.9) | copy-start | bytes 786436
  51.0 17.9 %collective-permute-start.7 = (bf16[128,8,128]{2,0,1:T(8,128)(2,1)S(1)}, bf16[128,8,128]{2,0,1:T(8,128)(2,1)S(1)}, u32[]{:S(2)}, u32[]{:S(2)}) collective-permute-start(bf16[128,8,128]{2,0,1:T(8,128)(2,1)S(1)} %fusion.86), channel_id=1, source_target_pairs={{0,16},{16,0},{2,18},{18,2},{4,20},{20,4},{6,22},{22,6},{8,24},{24... | collective-permute-start | bytes 786440 | tf_op jit(solution)/shard_map/ppermute | solution.py:17
  65.0 1.1 copy-start.23
  65.3 4.8 %copy-start.12 = (bf16[128,1024]{0,1:T(8,128)(2,1)S(1)}, bf16[128,1024]{0,1:T(8,128)(2,1)}, u32[]{:S(2)}) copy-start(bf16[128,1024]{0,1:T(8,128)(2,1)} %copy.106) | copy-start | bytes 786436
  66.1 4.5 %copy-start.1 = (bf16[1024,2048]{1,0:T(8,128)(2,1)S(1)}, bf16[1024,2048]{1,0:T(8,128)(2,1)}, u32[]{:S(2)}) copy-start(bf16[1024,2048]{1,0:T(8,128)(2,1)} %param.8) | copy-start | bytes 12582916
  68.9 0.7 copy-start.25
  72.4 2.9 %copy-start.13 = (bf16[128,1024]{0,1:T(8,128)(2,1)S(1)}, bf16[128,1024]{0,1:T(8,128)(2,1)}, u32[]{:S(2)}) copy-start(bf16[128,1024]{0,1:T(8,128)(2,1)} %copy.106) | copy-start | bytes 786436
  72.4 2.9 %copy-start.26 = (bf16[128,8,128]{2,0,1:T(8,128)(2,1)S(1)}, bf16[128,8,128]{2,0,1:T(8,128)(2,1)}, u32[]{:S(2)}) copy-start(bf16[128,8,128]{2,0,1:T(8,128)(2,1)} %copy-done.25) | copy-start | bytes 786436
  73.7 2.1 %copy-start.18 = (bf16[128,8,128]{2,0,1:T(8,128)(2,1)S(1)}, bf16[128,8,128]{2,0,1:T(8,128)(2,1)}, u32[]{:S(2)}) copy-start(bf16[128,8,128]{2,0,1:T(8,128)(2,1)} %copy-done.17) | copy-start | bytes 786436
  75.0 1.5 copy-start.22
  75.0 4.3 %copy-start.24 = (bf16[128,8,128]{2,0,1:T(8,128)(2,1)S(1)}, bf16[128,8,128]{2,0,1:T(8,128)(2,1)}, u32[]{:S(2)}) copy-start(bf16[128,8,128]{2,0,1:T(8,128)(2,1)} %copy-done.23) | copy-start | bytes 786436
  75.3 5.1 %copy-start.7 = (bf16[128,8,128]{2,0,1:T(8,128)(2,1)S(1)}, bf16[128,8,128]{2,0,1:T(8,128)(2,1)}, u32[]{:S(2)}) copy-start(bf16[128,8,128]{2,0,1:T(8,128)(2,1)} %copy-done.6) | copy-start | bytes 786436
  75.3 6.2 %copy-start.11 = (bf16[128,8,128]{2,0,1:T(8,128)(2,1)S(1)}, bf16[128,8,128]{2,0,1:T(8,128)(2,1)}, u32[]{:S(2)}) copy-start(bf16[128,8,128]{2,0,1:T(8,128)(2,1)} %copy-done.9) | copy-start | bytes 786436
  75.7 35.1 %collective-permute-start.8 = (f32[128,8,128]{2,0,1:T(8,128)S(1)}, f32[128,8,128]{2,0,1:T(8,128)S(1)}, u32[]{:S(2)}, u32[]{:S(2)}) collective-permute-start(f32[128,8,128]{2,0,1:T(8,128)S(1)} %fusion.7), channel_id=1, source_target_pairs={{0,16},{16,0},{2,18},{18,2},{4,20},{20,4},{6,22},{22,6},{8,24},{24... | collective-permute-start | bytes 1572872 | tf_op jit(solution)/shard_map/ppermute | solution.py:17
  76.2 5.7 %copy-start.5 = (bf16[128,8,128]{2,0,1:T(8,128)(2,1)S(1)}, bf16[128,8,128]{2,0,1:T(8,128)(2,1)}, u32[]{:S(2)}) copy-start(bf16[128,8,128]{2,0,1:T(8,128)(2,1)} %copy-done.4) | copy-start | bytes 786436
  76.5 45.6 %collective-permute-start.12 = (f32[128,8,128]{2,0,1:T(8,128)S(1)}, f32[128,8,128]{2,0,1:T(8,128)S(1)}, u32[]{:S(2)}, u32[]{:S(2)}) collective-permute-start(f32[128,8,128]{2,0,1:T(8,128)S(1)} %convolution_bitcast_fusion.4), channel_id=1, source_target_pairs={{0,16},{16,0},{2,18},{18,2},{4,20},{20,4},{6,22},{22,6},{8,24},{24... | collective-permute-start | bytes 1572872 | tf_op jit(solution)/shard_map/ppermute | solution.py:17
  81.7 29.6 %copy-start.16 = (bf16[128,8,128]{2,0,1:T(8,128)(2,1)S(1)}, bf16[128,8,128]{2,0,1:T(8,128)(2,1)}, u32[]{:S(2)}) copy-start(bf16[128,8,128]{2,0,1:T(8,128)(2,1)} %copy-done.15) | copy-start | bytes 786436
  111.2 22.1 %collective-permute-start.9 = (f32[128,8,128]{2,0,1:T(8,128)S(1)}, f32[128,8,128]{2,0,1:T(8,128)S(1)}, u32[]{:S(2)}, u32[]{:S(2)}) collective-permute-start(f32[128,8,128]{2,0,1:T(8,128)S(1)} %add.207), channel_id=1, source_target_pairs={{0,8},{8,0},{2,10},{10,2},{4,12},{12,4},{6,14},{14,6},{16,24},{24,... | collective-permute-start | bytes 1572872 | tf_op jit(solution)/shard_map/ppermute | solution.py:17
  111.5 22.3 %copy-start.19 = (bf16[128,8,128]{0,2,1:T(8,128)(2,1)}, bf16[128,8,128]{0,2,1:T(8,128)(2,1)S(1)}, u32[]{:S(2)}) copy-start(bf16[128,8,128]{0,2,1:T(8,128)(2,1)S(1)} %fusion.33) | copy-start | bytes 786436
  122.5 22.0 %collective-permute-start.13 = (f32[128,8,128]{2,0,1:T(8,128)S(1)}, f32[128,8,128]{2,0,1:T(8,128)S(1)}, u32[]{:S(2)}, u32[]{:S(2)}) collective-permute-start(f32[128,8,128]{2,0,1:T(8,128)S(1)} %add.214), channel_id=1, source_target_pairs={{0,8},{8,0},{2,10},{10,2},{4,12},{12,4},{6,14},{14,6},{16,24},{24,... | collective-permute-start | bytes 1572872 | tf_op jit(solution)/shard_map/ppermute | solution.py:17
  134.0 13.8 %collective-permute-start.10 = (f32[128,8,128]{2,0,1:T(8,128)S(1)}, f32[128,8,128]{2,0,1:T(8,128)S(1)}, u32[]{:S(2)}, u32[]{:S(2)}) collective-permute-start(f32[128,8,128]{2,0,1:T(8,128)S(1)} %fusion.5), channel_id=1, source_target_pairs={{0,4},{4,0},{2,6},{6,2},{8,12},{12,8},{10,14},{14,10},{16,20},{20,... | collective-permute-start | bytes 1572872 | tf_op jit(solution)/shard_map/ppermute | solution.py:17
  145.3 13.9 %collective-permute-start.14 = (f32[128,8,128]{2,0,1:T(8,128)S(1)}, f32[128,8,128]{2,0,1:T(8,128)S(1)}, u32[]{:S(2)}, u32[]{:S(2)}) collective-permute-start(f32[128,8,128]{2,0,1:T(8,128)S(1)} %fusion), channel_id=1, source_target_pairs={{0,4},{4,0},{2,6},{6,2},{8,12},{12,8},{10,14},{14,10},{16,20},{20,... | collective-permute-start | bytes 1572872 | tf_op jit(solution)/shard_map/ppermute | solution.py:17
  148.9 12.6 %copy-start.14 = (bf16[128,1024]{0,1:T(8,128)(2,1)S(1)}, bf16[128,1024]{0,1:T(8,128)(2,1)}, u32[]{:S(2)}) copy-start(bf16[128,1024]{0,1:T(8,128)(2,1)} %copy.106) | copy-start | bytes 786436
  150.1 15.1 %copy-start.3 = (bf16[128,8,128]{2,0,1:T(8,128)(2,1)S(1)}, bf16[128,8,128]{2,0,1:T(8,128)(2,1)}, u32[]{:S(2)}) copy-start(bf16[128,8,128]{2,0,1:T(8,128)(2,1)} %copy-done.2) | copy-start | bytes 786436
  150.1 15.1 %copy-start.8 = (f32[8,128,128]{2,1,0:T(8,128)S(1)}, f32[8,128,128]{2,1,0:T(8,128)}, u32[]{:S(2)}) copy-start(f32[8,128,128]{2,1,0:T(8,128)} %fusion.137) | copy-start | bytes 1572868
  150.1 20.8 %collective-permute-start.11 = (f32[128,8,128]{2,0,1:T(8,128)}, f32[128,8,128]{2,0,1:T(8,128)}, u32[]{:S(2)}, u32[]{:S(2)}) collective-permute-start(f32[128,8,128]{2,0,1:T(8,128)} %fusion.3), channel_id=1, source_target_pairs={{0,2},{2,0},{4,6},{6,4},{8,10},{10,8},{12,14},{14,12},{16,18},{18,... | collective-permute-start | bytes 1572872 | tf_op jit(solution)/shard_map/ppermute | solution.py:17
  161.4 7.2 %copy-start.21 = (f32[64,8,128]{2,0,1:T(8,128)S(1)}, f32[64,8,128]{2,0,1:T(8,128)}, u32[]{:S(2)}) copy-start(f32[64,8,128]{2,0,1:T(8,128)} %get-tuple-element.22) | copy-start | bytes 786436
  161.4 9.4 %copy-start.20 = (f32[64,8,128]{2,0,1:T(8,128)S(1)}, f32[64,8,128]{2,0,1:T(8,128)}, u32[]{:S(2)}) copy-start(f32[64,8,128]{2,0,1:T(8,128)} %get-tuple-element.28) | copy-start | bytes 786436
  163.7 13.4 %collective-permute-start.15 = (f32[128,8,128]{0,2,1:T(8,128)}, f32[128,8,128]{0,2,1:T(8,128)}, u32[]{:S(2)}, u32[]{:S(2)}) collective-permute-start(f32[128,8,128]{0,2,1:T(8,128)} %fusion.1), channel_id=1, source_target_pairs={{0,2},{2,0},{4,6},{6,4},{8,10},{10,8},{12,14},{14,12},{16,18},{18,... | collective-permute-start | bytes 1572872 | tf_op jit(solution)/shard_map/ppermute | solution.py:17
Sparse Core Ops, SparseCore 0:
  72.5 9.2 reduce-scatter.1
where the time goes:
time: 187 us; the launch traced here: 186 us
  waiting for transfers between devices  97.5 us (52%)
  starting transfers between devices  25.8 us (14%)
  matrix products  23.2 us (12%)
  local copies, waits for them, and re-layouts  15.7 us (8%)
  between operations  14.9 us (8%)
  other arithmetic  6.71 us (4%)
  blocking collectives  2.39 us (1%)
    ppermute x16, waiting for transfers between devices, from_partner(): return lax.ppermute(block, axis, route)  97.4 us
    ppermute x16, starting transfers between devices, from_partner(): return lax.ppermute(block, axis, route)  25.7 us
    unnamed x59, local copies, waits for them, and re-layouts  5.65 us
    dot_general x5, matrix products, body(): jnp.einsum('cwhb,cwhd->cbhd', rounded_probs, grad_blocks, preferred_eleme...  5.48 us
    dot_general x5, matrix products, body(): jnp.einsum('cwhb,cbhd->cwhd', score_grad, key_blocks, preferred_element_t...  4.05 us
    slice x6, local copies, waits for them, and re-layouts, pool_pairs(): return ((shaped[:, 0] + shaped[:, 1]) * 0.5).astype(jnp.bfloat16)  3.98 us
  transfers between devices with their start and end apart: 17, of which 14 were waited for; matrix products, arithmetic and copies ran while one was open for 20% of the time, Pallas kernels for 0%

commit v1 on v0

v1 whole, which is shorter than its diff:
```python
import jax
import jax.numpy as jnp
from jax import lax
from jax.experimental import pallas as pl
from jax.experimental.pallas import tpu as pltpu
from jax.sharding import PartitionSpec as P

DH = 128
PLANE = 4
SCALE = DH ** (-0.5)
BF16 = jnp.bfloat16
F32 = jnp.float32


def xor_permute(block, mask, axis="ctx"):
    count = lax.axis_size(axis)
    return lax.ppermute(block, axis, [(i, i ^ mask) for i in range(count)])


def dot(a, b, contract_a=1, contract_b=0):
    return lax.dot_general(
        a, b, (((contract_a,), (contract_b,)), ((), ())), preferred_element_type=F32
    )


def pool_matrix(rows):
    out = lax.broadcasted_iota(jnp.int32, (rows // 2, rows), 0)
    src = lax.broadcasted_iota(jnp.int32, (rows // 2, rows), 1)
    return jnp.where(src // 2 == out, 0.5, 0.0).astype(BF16)


def spread_matrix(rows, times):
    out = lax.broadcasted_iota(jnp.int32, (rows * times, rows), 0)
    src = lax.broadcasted_iota(jnp.int32, (rows * times, rows), 1)
    return jnp.where(out // times == src, 1.0 / times, 0.0).astype(BF16)


def pool(block):
    return dot(pool_matrix(block.shape[0]), block).astype(BF16)


def spread(block, times):
    return dot(spread_matrix(block.shape[0], times), block.astype(BF16))


def call(kernel, outs, *args, flops=0, name=None):
    vmem = pl.BlockSpec(memory_space=pltpu.VMEM)
    moved = sum(a.size * a.dtype.itemsize for a in args)
    return pl.pallas_call(
        kernel,
        out_shape=outs,
        in_specs=[vmem] * len(args),
        out_specs=[vmem] * len(outs),
        compiler_params=pltpu.CompilerParams(vmem_limit_bytes=32 * 1024 * 1024),
        cost_estimate=pl.CostEstimate(flops=flops, bytes_accessed=moved, transcendentals=0),
        name=name,
    )(*args)


def columns(r, width):
    place = (lax.axis_index("ctx") & (PLANE - 1)) ^ r
    return pl.ds(pl.multiple_of(place * width, width), width)


def split_kernel(q_ref, k_ref, v_ref, *outs):
    width = q_ref.shape[1] // PLANE
    rows = q_ref.shape[0]
    q_out, kv_out, top_out = outs[:PLANE], outs[PLANE : 2 * PLANE], outs[2 * PLANE :]
    for r in range(PLANE):
        here = columns(r, width)
        k, v = k_ref[:, here], v_ref[:, here]
        q_out[r][...] = q_ref[:, here]
        kv_out[r][:rows, :] = k
        kv_out[r][rows:, :] = v
        top_out[r][: rows // 4, :] = pool(pool(k))
        top_out[r][rows // 4 :, :] = pool(pool(v))


def far_kernel(*refs):
    tops, (near_out, far_out) = refs[:PLANE], refs[PLANE:]
    half = tops[0].shape[0] // 2
    rows = half * PLANE
    for part in range(2):
        whole = jnp.concatenate([top[part * half : (part + 1) * half, :] for top in tops], 0)
        near_out[part * rows : (part + 1) * rows, :] = whole
        far_out[part * rows // 2 : (part + 1) * rows // 2, :] = pool(whole)


def cotangent_kernel(own_ref, other_ref, w_ref, *outs):
    width = w_ref.shape[0] // PLANE
    half = own_ref.shape[1]
    head = lax.axis_index("head")
    own_at = pl.ds(pl.multiple_of(head * half, half), half)
    other_at = pl.ds(pl.multiple_of((1 - head) * half, half), half)
    for r in range(PLANE):
        here = columns(r, width)
        outs[r][...] = (
            dot(own_ref[...], w_ref[here, own_at], 1, 1)
            + dot(other_ref[...], w_ref[here, other_at], 1, 1)
        ).astype(BF16)


def attention_kernel(n_far, *refs):
    q_refs, kv_refs, g_refs = refs[:PLANE], refs[PLANE : 2 * PLANE], refs[2 * PLANE : 3 * PLANE]
    far_refs = refs[3 * PLANE : 3 * PLANE + n_far]
    outs = refs[3 * PLANE + n_far :]
    att_out, dq_out, dkv_out = outs[:PLANE], outs[PLANE : 2 * PLANE], outs[2 * PLANE : 3 * PLANE]
    far_out = outs[3 * PLANE :]
    rows = q_refs[0].shape[0]
    pair = 2 * rows
    width = q_refs[0].shape[1]
    for first in range(0, width, DH):
        lanes = slice(first, first + DH)
        leaf_k = [kv[:rows, lanes] for kv in kv_refs]
        leaf_v = [kv[rows:, lanes] for kv in kv_refs]
        far_k = [far[: far.shape[0] // 2, lanes] for far in far_refs]
        far_v = [far[far.shape[0] // 2 :, lanes] for far in far_refs]
        key_grads, value_grads = [], []
        for p in range(2):
            ours, theirs = (2 * p, 2 * p + 1), (2 - 2 * p, 3 - 2 * p)
            q = jnp.concatenate([q_refs[r][:, lanes] for r in ours], 0)
            g = jnp.concatenate([g_refs[r][:, lanes] for r in ours], 0)
            keys = jnp.concatenate(
                [leaf_k[r] for r in ours] + [pool(leaf_k[r]) for r in theirs] + far_k, 0
            )
            values = jnp.concatenate(
                [leaf_v[r] for r in ours] + [pool(leaf_v[r]) for r in theirs] + far_v, 0
            )
            scores = dot(keys, q, 1, 1) * SCALE
            weights = jnp.exp(scores - jnp.max(scores, 0, keepdims=True))
            total = jnp.sum(weights, 0, keepdims=True)
            inverse = 1.0 / total
            numerator = dot(values, weights.astype(BF16), 0, 0)
            attended = (numerator * inverse).astype(BF16)
            delta = jnp.sum(
                g.T.astype(F32) * attended.astype(F32), 0, keepdims=True
            )
            probabilities = weights * inverse
            value_dots = dot(values, g, 1, 1)
            score_grad = (probabilities * (value_dots - delta)).astype(BF16)
            dq = (dot(keys, score_grad, 0, 0) * SCALE).astype(BF16).T
            attended = attended.T
            for n, r in enumerate(ours):
                att_out[r][:, lanes] = attended[n * rows : (n + 1) * rows]
                dq_out[r][:, lanes] = dq[n * rows : (n + 1) * rows]
            key_grads.append(dot(score_grad, q) * SCALE)
            value_grads.append(dot(probabilities.astype(BF16), g))
        for part, grads in enumerate((key_grads, value_grads)):
            for p in range(2):
                pooled = grads[1 - p][pair : pair + rows]
                for n in range(2):
                    whole = grads[p][n * rows : (n + 1) * rows] + spread(
                        pooled[n * rows // 2 : (n + 1) * rows // 2], 2
                    )
                    dkv_out[2 * p + n][part * rows : (part + 1) * rows, lanes] = whole.astype(BF16)
            at = pair + rows
            for far in far_out:
                size = far.shape[0] // 2
                far[part * size : (part + 1) * size, lanes] = (
                    grads[0][at : at + size] + grads[1][at : at + size]
                ).astype(BF16)
                at += size


def carry_kernel(near_ref, far2_ref, far3_ref, *refs):
    extra, outs = refs[:-PLANE], refs[-PLANE:]
    rows = near_ref.shape[0] // 2
    for part in range(2):
        low = slice(part * rows // 2, (part + 1) * rows // 2)
        upper = far2_ref[low, :].astype(F32) + far3_ref[low, :].astype(F32)
        for ref in extra:
            upper = upper + ref[low, :].astype(F32)
        whole = near_ref[part * rows : (part + 1) * rows, :].astype(F32) + spread(upper, 2)
        size = rows // PLANE
        for r in range(PLANE):
            outs[r][part * size : (part + 1) * size, :] = whole[r * size : (r + 1) * size].astype(
                BF16
            )


def output_kernel(*refs):
    atts, w_ref, (own_out, other_out) = refs[:PLANE], refs[PLANE], refs[PLANE + 1 :]
    width = atts[0].shape[1]
    half = own_out.shape[1]
    head = lax.axis_index("head")
    for out, place in ((other_out, 1 - head), (own_out, head)):
        at = pl.ds(pl.multiple_of(place * half, half), half)
        total = dot(atts[0][...], w_ref[columns(0, width), at])
        for r in range(1, PLANE):
            total = total + dot(atts[r][...], w_ref[columns(r, width), at])
        out[...] = total.astype(out.dtype)


def join_kernel(*refs):
    dqs, dkvs, tops = refs[:PLANE], refs[PLANE : 2 * PLANE], refs[2 * PLANE : 3 * PLANE]
    gq_out, gk_out, gv_out = refs[3 * PLANE :]
    rows = dqs[0].shape[0]
    width = dqs[0].shape[1]
    for r in range(PLANE):
        here = columns(r, width)
        gq_out[:, here] = dqs[r][...]
        for part, out in enumerate((gk_out, gv_out)):
            top = tops[r][part * rows // 4 : (part + 1) * rows // 4, :]
            out[:, here] = (
                dkvs[r][part * rows : (part + 1) * rows, :].astype(F32) + spread(top, 4)
            ).astype(BF16)


def plane_exchange(blocks):
    return [blocks[0]] + [xor_permute(blocks[r], r) for r in range(1, PLANE)]


def pool_both(block):
    shaped = block.reshape((2, block.shape[0] // 4, 2) + block.shape[1:]).astype(F32)
    return ((shaped[:, :, 0] + shaped[:, :, 1]) * 0.5).astype(BF16).reshape(
        (block.shape[0] // 2,) + block.shape[1:]
    )


def spread_both(block):
    halved = block.astype(F32) * 0.5
    return jnp.repeat(halved, 2, axis=0)


def join_both(blocks):
    halves = [b.reshape((2, b.shape[0] // 2) + b.shape[1:]) for b in blocks]
    joined = jnp.concatenate(halves, 1)
    return joined.reshape((-1,) + joined.shape[2:])


def part_both(block, parts):
    shaped = block.reshape((2, parts, block.shape[0] // (2 * parts)) + block.shape[1:])
    return [shaped[:, n].reshape((-1,) + block.shape[1:]) for n in range(parts)]


def body(queries, key_rows, value_rows, out_weight, cotangent):
    rows, features = queries.shape
    width = features // PLANE
    top_rounds = lax.axis_size("ctx").bit_length() - 1 - 4
    shape = lambda n, w=width, t=BF16: jax.ShapeDtypeStruct((n, w), t)

    other_cotangent = xor_permute(cotangent, 1, "head")
    parts = call(
        split_kernel,
        [shape(rows)] * PLANE + [shape(2 * rows)] * PLANE + [shape(rows // 2)] * PLANE,
        queries, key_rows, value_rows, name="split",
    )
    tops = plane_exchange(parts[2 * PLANE :])
    key_values = plane_exchange(parts[PLANE : 2 * PLANE])
    query_parts = plane_exchange(parts[:PLANE])
    near, pooled = call(far_kernel, [shape(2 * rows), shape(rows)], *tops, name="pool_plane")
    fars = [xor_permute(near, PLANE), xor_permute(pooled, 2 * PLANE), xor_permute(pooled, 3 * PLANE)]
    if top_rounds > 0:
        span = pool_both(join_both([pooled, pool_both(fars[0]), fars[1], fars[2]]))
        for n in range(top_rounds):
            fars.append(xor_permute(span, 4 * PLANE << n))
            span = pool_both(join_both([span, fars[-1]]))
    grad_parts = plane_exchange(
        call(
            cotangent_kernel, [shape(rows)] * PLANE, cotangent, other_cotangent, out_weight,
            flops=4 * rows * features * features, name="grad_attended",
        )
    )
    results = call(
        lambda *refs: attention_kernel(len(fars), *refs),
        [shape(rows)] * (2 * PLANE)
        + [shape(2 * rows)] * PLANE
        + [shape(far.shape[0]) for far in fars],
        *query_parts, *key_values, *grad_parts, *fars,
        flops=12 * PLANE * rows * 5 * rows * width, name="attention",
    )
    far_grads = list(results[3 * PLANE :])
    extra = []
    if top_rounds > 0:
        up = None
        for n in reversed(range(top_rounds)):
            send = far_grads[3 + n].astype(F32)
            if up is not None:
                own_up, their_up = part_both(spread_both(up), 2)
                send = send + their_up
            back = xor_permute(send.astype(BF16), 4 * PLANE << n).astype(F32)
            up = back if up is None else back + own_up
        ups = part_both(spread_both(up), PLANE)
        extra = [ups[0].astype(BF16)]
        far_grads[0] = (far_grads[0].astype(F32) + spread_both(ups[1])).astype(BF16)
        far_grads[1] = (far_grads[1].astype(F32) + ups[2]).astype(BF16)
        far_grads[2] = (far_grads[2].astype(F32) + ups[3]).astype(BF16)
    backs = [xor_permute(far_grads[n], (n + 1) * PLANE) for n in range(3)]
    atts = plane_exchange(results[:PLANE])
    dqs = plane_exchange(results[PLANE : 2 * PLANE])
    dkvs = plane_exchange(results[2 * PLANE : 3 * PLANE])
    carried = plane_exchange(
        call(carry_kernel, [shape(rows // 2)] * PLANE, *backs, *extra, name="carry")
    )
    own_sum, other_sum = call(
        output_kernel, [shape(rows, features, F32), shape(rows, features)], *atts, out_weight,
        flops=4 * rows * features * features, name="project",
    )
    output = (own_sum + xor_permute(other_sum, 1, "head").astype(F32)).astype(BF16)
    grad_queries, grad_keys, grad_values = call(
        join_kernel, [shape(rows, features)] * 3, *dqs, *dkvs, *carried, name="join"
    )
    return (output, grad_queries, grad_keys, grad_values)


def solution(mesh):
    rows = P("ctx", "head")
    return jax.shard_map(
        body,
        mesh=mesh,
        in_specs=(rows, rows, rows, P("head", None), rows),
        out_specs=(rows, rows, rows, rows),
        check_vma=False,
    )
```

time: 187 us -> 76.3 us (0.41)
  waiting for transfers between devices: 97.5 us -> 17.1 us
  matrix products: 23.2 us -> 0 us
  starting transfers between devices: 25.8 us -> 42.5 us
  between operations: 14.9 us -> 0.72 us
  local copies, waits for them, and re-layouts: 15.7 us -> 5.99 us
  Pallas kernels: 0 us -> 8.98 us
  other arithmetic: 6.71 us -> 0.76 us
  blocking collectives: 2.39 us -> 0 us
    ppermute x16 -> x32, waiting for transfers between devices: 97.4 us -> 17.1 us  [xor_permute(): return lax.ppermute(block, axis, [(i, i ^ mask) for i in range(count)])]
    dot_general x32 -> x0, matrix products: 23.2 us -> none  [the longest x5 5.48 us: body(): jnp.einsum('cwhb,cwhd->cbhd', rounded_probs, grad_blocks, preferred_eleme...]
    ppermute x16 -> x32, starting transfers between devices: 25.7 us -> 42.5 us  [xor_permute(): return lax.ppermute(block, axis, [(i, i ^ mask) for i in range(count)])]
    pallas_call x0 -> x7, Pallas kernels: none -> 8.98 us  [call(): pl.pallas_call(kernel, out_shape=outs, in_specs=[vmem] * len(args), out_s...]
    slice x6 -> x0, local copies, waits for them, and re-layouts: 3.98 us -> none  [pool_pairs(): return ((shaped[:, 0] + shaped[:, 1]) * 0.5).astype(jnp.bfloat16)]
    convert_element_type x11 -> x1, other arithmetic: 3.75 us -> 0.76 us  [body(): (own_sum + xor_permute(other_sum, 1, 'head').astype(F32)).astype(BF16)]
    all_gather x1 -> x0, blocking collectives: 2.39 us -> none  [body(): full_cotangent = lax.all_gather(cotangent, 'head', axis=1, tiled=True)]
    convert_element_type x4 -> x0, local copies, waits for them, and re-layouts: 2.24 us -> none  [the longest x2 1.22 us: pool_pairs(): matrix.reshape((matrix.shape[0] // 2, 2) + matrix.shape[1:])]
  transfers between devices with their start and end apart: 17 -> 32, of which waited for: 14 -> 12; matrix products, arithmetic and copies ran while one was open for 20% -> 0% of each run, Pallas kernels for 0% -> 6%
where the time goes in v1:
time: 76.3 us; the launch traced here: 76 us
  starting transfers between devices  42.5 us (56%)
  waiting for transfers between devices  17.1 us (22%)
  Pallas kernels  8.98 us (12%)
  local copies, waits for them, and re-layouts  5.99 us (8%)
    ppermute x32, starting transfers between devices, xor_permute(): return lax.ppermute(block, axis, [(i, i ^ mask) for i in range(count)])  42.5 us
    ppermute x32, waiting for transfers between devices, xor_permute(): return lax.ppermute(block, axis, [(i, i ^ mask) for i in range(count)])  17.1 us
    pallas_call x7, Pallas kernels, call(): pl.pallas_call(kernel, out_shape=outs, in_specs=[vmem] * len(args), out_s...  8.98 us
    unnamed x12, local copies, waits for them, and re-layouts  5.99 us
  transfers between devices with their start and end apart: 32, of which 12 were waited for; matrix products, arithmetic and copies ran while one was open for 0% of the time, Pallas kernels for 6%

profile of v1, /device:TPU:0, one launch (start us, length us, event | category | flops | bytes accessed | tf_op | source)
XLA Modules:
  0.0 76.0 jit_solution(16122581458107420290)
XLA Ops:
  0.6 0.5 collective-permute-start.6
  1.2 0.9 %copy-done.2 = bf16[128,1024]{1,0:T(8,128)(2,1)S(1)} copy-done((bf16[128,1024]{1,0:T(8,128)(2,1)S(1)}, bf16[128,1024]{1,0:T(8,128)(2,1)}, u32[]{:S(2)}) %copy-start.2) | copy-done | bytes 262168
  2.1 0.9 %copy-done.3 = bf16[128,1024]{1,0:T(8,128)(2,1)S(1)} copy-done((bf16[128,1024]{1,0:T(8,128)(2,1)S(1)}, bf16[128,1024]{1,0:T(8,128)(2,1)}, u32[]{:S(2)}) %copy-start.3) | copy-done | bytes 262168
  3.1 0.9 %copy-done.4 = bf16[128,1024]{1,0:T(8,128)(2,1)S(1)} copy-done((bf16[128,1024]{1,0:T(8,128)(2,1)S(1)}, bf16[128,1024]{1,0:T(8,128)(2,1)}, u32[]{:S(2)}) %copy-start.4) | copy-done | bytes 262168
  4.0 0.9 %split.1 = (bf16[128,256]{1,0:T(8,128)(2,1)S(1)}, bf16[128,256]{1,0:T(8,128)(2,1)S(1)}, bf16[128,256]{1,0:T(8,128)(2,1)S(1)}, bf16[128,256]{1,0:T(8,128)(2,1)S(1...) custom-call(bf16[128,1024]{1,0:T(8,128)(2,1)S(1)} %copy-done.2, ...), custom_call_target="tpu_custom_call" | custom-call | bytes 786432 | tf_op jit(solution)/shard_map/split/pallas_call | solution.py:49
  4.9 2.5 %collective-permute-start.10 = (bf16[64,256]{1,0:T(8,128)(2,1)S(1)}, bf16[64,256]{1,0:T(8,128)(2,1)S(1)}, u32[]{:S(2)}, u32[]{:S(2)}) collective-permute-start(bf16[64,256]{1,0:T(8,128)(2,1)S(1)} %get-tuple-element.59), channel_id=1, source_target_pairs={{0,2},{2,0},{4,6},{6,4},{8,10},{10,8},{12,14},{14,12},{16,18},{18,... | collective-permute-start | bytes 98312 | tf_op jit(solution)/shard_map/ppermute | solution.py:17
  7.4 0.1 collective-permute-start
  7.5 2.0 %collective-permute-start.1 = (bf16[128,256]{1,0:T(8,128)(2,1)S(1)}, bf16[128,256]{1,0:T(8,128)(2,1)S(1)}, u32[]{:S(2)}, u32[]{:S(2)}) collective-permute-start(bf16[128,256]{1,0:T(8,128)(2,1)S(1)} %get-tuple-element.48), channel_id=1, source_target_pairs={{0,4},{2,6},{4,0},{6,2},{8,12},{10,14},{12,8},{14,10},{16,20},{18,... | collective-permute-start | bytes 196616 | tf_op jit(solution)/shard_map/ppermute | solution.py:17
  9.5 0.0 collective-permute-start.11
  9.5 3.0 %collective-permute-start.12 = (bf16[64,256]{1,0:T(8,128)(2,1)S(1)}, bf16[64,256]{1,0:T(8,128)(2,1)S(1)}, u32[]{:S(2)}, u32[]{:S(2)}) collective-permute-start(bf16[64,256]{1,0:T(8,128)(2,1)S(1)} %get-tuple-element.61), channel_id=1, source_target_pairs={{0,6},{2,4},{4,2},{6,0},{8,14},{10,12},{12,10},{14,8},{16,22},{18,... | collective-permute-start | bytes 98312 | tf_op jit(solution)/shard_map/ppermute | solution.py:17
  12.6 1.0 %collective-permute-done.11.refs_2_ = bf16[64,256]{1,0:T(8,128)(2,1)S(1)} collective-permute-done((bf16[64,256]{1,0:T(8,128)(2,1)S(1)}, bf16[64,256]{1,0:T(8,128)(2,1)S(1)}, u32[]{:S(2)}, u32[]{:S(2)}) %collective-permute-start.11) | collective-permute-done | bytes 32800 | tf_op jit(solution)/shard_map/ppermute | solution.py:17
  13.6 1.5 %collective-permute-start.2 = (bf16[128,256]{1,0:T(8,128)(2,1)S(1)}, bf16[128,256]{1,0:T(8,128)(2,1)S(1)}, u32[]{:S(2)}, u32[]{:S(2)}) collective-permute-start(bf16[128,256]{1,0:T(8,128)(2,1)S(1)} %get-tuple-element.49), channel_id=1, source_target_pairs={{0,6},{2,4},{4,2},{6,0},{8,14},{10,12},{12,10},{14,8},{16,22},{18,... | collective-permute-start | bytes 196616 | tf_op jit(solution)/shard_map/ppermute | solution.py:17
  15.0 0.0 collective-permute-done.12.refs_3_
  15.1 0.2 pool_plane.1
  15.2 3.7 %collective-permute-start.15 = (bf16[128,256]{1,0:T(8,128)(2,1)S(1)}, bf16[128,256]{1,0:T(8,128)(2,1)S(1)}, u32[]{:S(2)}, u32[]{:S(2)}) collective-permute-start(bf16[128,256]{1,0:T(8,128)(2,1)S(1)} %get-tuple-element.63), channel_id=1, source_target_pairs={{0,24},{2,26},{4,28},{6,30},{8,16},{10,18},{12,20},{14,22},{16,8},... | collective-permute-start | bytes 196616 | tf_op jit(solution)/shard_map/ppermute | solution.py:17
  18.9 1.4 %collective-permute-start.3 = (bf16[256,256]{1,0:T(8,128)(2,1)S(1)}, bf16[256,256]{1,0:T(8,128)(2,1)S(1)}, u32[]{:S(2)}, u32[]{:S(2)}) collective-permute-start(bf16[256,256]{1,0:T(8,128)(2,1)S(1)} %get-tuple-element.51), channel_id=1, source_target_pairs={{0,2},{2,0},{4,6},{6,4},{8,10},{10,8},{12,14},{14,12},{16,18},{18,... | collective-permute-start | bytes 393224 | tf_op jit(solution)/shard_map/ppermute | solution.py:17
  20.3 0.0 collective-permute-done.1.refs_2_
  20.3 1.5 %collective-permute-start.4 = (bf16[256,256]{1,0:T(8,128)(2,1)S(1)}, bf16[256,256]{1,0:T(8,128)(2,1)S(1)}, u32[]{:S(2)}, u32[]{:S(2)}) collective-permute-start(bf16[256,256]{1,0:T(8,128)(2,1)S(1)} %get-tuple-element.52), channel_id=1, source_target_pairs={{0,4},{2,6},{4,0},{6,2},{8,12},{10,14},{12,8},{14,10},{16,20},{18,... | collective-permute-start | bytes 393224 | tf_op jit(solution)/shard_map/ppermute | solution.py:17
  21.8 0.0 collective-permute-done.2.refs_3_
  21.8 0.2 collective-permute-start.14
  21.9 0.0 collective-permute-done.15.refs_14_
  21.9 2.4 %collective-permute-start.5 = (bf16[256,256]{1,0:T(8,128)(2,1)S(1)}, bf16[256,256]{1,0:T(8,128)(2,1)S(1)}, u32[]{:S(2)}, u32[]{:S(2)}) collective-permute-start(bf16[256,256]{1,0:T(8,128)(2,1)S(1)} %get-tuple-element.53), channel_id=1, source_target_pairs={{0,6},{2,4},{4,2},{6,0},{8,14},{10,12},{12,10},{14,8},{16,22},{18,... | collective-permute-start | bytes 393224 | tf_op jit(solution)/shard_map/ppermute | solution.py:17
  24.3 0.0 collective-permute-done.6.other_ref
  24.3 0.4 collective-permute-start.13
  24.7 2.2 %copy-done = bf16[1024,2048]{1,0:T(8,128)(2,1)S(1)} copy-done((bf16[1024,2048]{1,0:T(8,128)(2,1)S(1)}, bf16[1024,2048]{1,0:T(8,128)(2,1)}, u32[]{:S(2)}) %copy-start) | copy-done | bytes 4194328
  26.9 0.9 %copy-done.5 = bf16[128,1024]{1,0:T(8,128)(2,1)S(1)} copy-done((bf16[128,1024]{1,0:T(8,128)(2,1)S(1)}, bf16[128,1024]{1,0:T(8,128)(2,1)}, u32[]{:S(2)}) %copy-start.5) | copy-done | bytes 262168
  27.9 1.5 %grad_attended.1 = (bf16[128,256]{1,0:T(8,128)(2,1)S(1)}, bf16[128,256]{1,0:T(8,128)(2,1)S(1)}, bf16[128,256]{1,0:T(8,128)(2,1)S(1)}, bf16[128,256]{1,0:T(8,128)(2,1)S(1)}) custom-call(bf16[128,1024]{1,0:T(8,128)(2,1)S(1)} %copy-done.5, bf16[128,1024]{1,0:T(8,128)(2,1)S(1)} %collective-permute-done.6.other_ref, bf16[1024,2048]{1,0:T(8,128)(2,1)S(1)} %copy-done), custom_call_target="tpu_custom_call" | custom-call | flops 536870912 | bytes 4718592 | tf_op jit(solution)/shard_map/grad_attended/pallas_call | solution.py:49
  29.4 0.9 %collective-permute-start.7 = (bf16[128,256]{1,0:T(8,128)(2,1)S(1)}, bf16[128,256]{1,0:T(8,128)(2,1)S(1)}, u32[]{:S(2)}, u32[]{:S(2)}) collective-permute-start(bf16[128,256]{1,0:T(8,128)(2,1)S(1)} %get-tuple-element.55), channel_id=1, source_target_pairs={{0,2},{2,0},{4,6},{6,4},{8,10},{10,8},{12,14},{14,12},{16,18},{18,... | collective-permute-start | bytes 196616 | tf_op jit(solution)/shard_map/ppermute | solution.py:17
  30.3 1.5 %collective-permute-start.8 = (bf16[128,256]{1,0:T(8,128)(2,1)S(1)}, bf16[128,256]{1,0:T(8,128)(2,1)S(1)}, u32[]{:S(2)}, u32[]{:S(2)}) collective-permute-start(bf16[128,256]{1,0:T(8,128)(2,1)S(1)} %get-tuple-element.56), channel_id=1, source_target_pairs={{0,4},{2,6},{4,0},{6,2},{8,12},{10,14},{12,8},{14,10},{16,20},{18,... | collective-permute-start | bytes 196616 | tf_op jit(solution)/shard_map/ppermute | solution.py:17
  31.7 0.0 collective-permute-done.4.refs_6_
  31.7 1.2 %collective-permute-start.9 = (bf16[128,256]{1,0:T(8,128)(2,1)S(1)}, bf16[128,256]{1,0:T(8,128)(2,1)S(1)}, u32[]{:S(2)}, u32[]{:S(2)}) collective-permute-start(bf16[128,256]{1,0:T(8,128)(2,1)S(1)} %get-tuple-element.57), channel_id=1, source_target_pairs={{0,6},{2,4},{4,2},{6,0},{8,14},{10,12},{12,10},{14,8},{16,22},{18,... | collective-permute-start | bytes 196616 | tf_op jit(solution)/shard_map/ppermute | solution.py:17
  32.9 0.0 collective-permute-done.5.refs_7_
  32.9 0.8 %collective-permute-done.7.refs_9_ = bf16[128,256]{1,0:T(8,128)(2,1)S(1)} collective-permute-done((bf16[128,256]{1,0:T(8,128)(2,1)S(1)}, bf16[128,256]{1,0:T(8,128)(2,1)S(1)}, u32[]{:S(2)}, u32[]{:S(2)}) %collective-permute-start.7) | collective-permute-done | bytes 65568 | tf_op jit(solution)/shard_map/ppermute | solution.py:17
  33.7 0.8 %collective-permute-done.8.refs_10_ = bf16[128,256]{1,0:T(8,128)(2,1)S(1)} collective-permute-done((bf16[128,256]{1,0:T(8,128)(2,1)S(1)}, bf16[128,256]{1,0:T(8,128)(2,1)S(1)}, u32[]{:S(2)}, u32[]{:S(2)}) %collective-permute-start.8) | collective-permute-done | bytes 65568 | tf_op jit(solution)/shard_map/ppermute | solution.py:17
  34.5 2.4 %collective-permute-done.9.refs_11_ = bf16[128,256]{1,0:T(8,128)(2,1)S(1)} collective-permute-done((bf16[128,256]{1,0:T(8,128)(2,1)S(1)}, bf16[128,256]{1,0:T(8,128)(2,1)S(1)}, u32[]{:S(2)}, u32[]{:S(2)}) %collective-permute-start.9) | collective-permute-done | bytes 65568 | tf_op jit(solution)/shard_map/ppermute | solution.py:17
  36.9 4.4 %attention.1 = (bf16[128,256]{1,0:T(8,128)(2,1)S(1)}, bf16[128,256]{1,0:T(8,128)(2,1)S(1)}, bf16[128,256]{1,0:T(8,128)(2,1)S(1)}, bf16[128,256]{1,0:T(8,128)(2,1...) custom-call(bf16[128,256]{1,0:T(8,128)(2,1)S(1)} %get-tuple-element., ...), custom_call_target="tpu_custom_call" | custom-call | flops 1006632960 | bytes 1310720 | tf_op jit(solution)/shard_map/attention/pallas_call | solution.py:49
  41.3 1.3 %collective-permute-start.16 = (bf16[128,256]{1,0:T(8,128)(2,1)S(1)}, bf16[128,256]{1,0:T(8,128)(2,1)S(1)}, u32[]{:S(2)}, u32[]{:S(2)}) collective-permute-start(bf16[128,256]{1,0:T(8,128)(2,1)S(1)} %get-tuple-element.65), channel_id=1, source_target_pairs={{0,2},{2,0},{4,6},{6,4},{8,10},{10,8},{12,14},{14,12},{16,18},{18,... | collective-permute-start | bytes 196616 | tf_op jit(solution)/shard_map/ppermute | solution.py:17
  42.6 0.5 collective-permute-start.17
  43.2 1.7 %collective-permute-start.18 = (bf16[128,256]{1,0:T(8,128)(2,1)S(1)}, bf16[128,256]{1,0:T(8,128)(2,1)S(1)}, u32[]{:S(2)}, u32[]{:S(2)}) collective-permute-start(bf16[128,256]{1,0:T(8,128)(2,1)S(1)} %get-tuple-element.67), channel_id=1, source_target_pairs={{0,6},{2,4},{4,2},{6,0},{8,14},{10,12},{12,10},{14,8},{16,22},{18,... | collective-permute-start | bytes 196616 | tf_op jit(solution)/shard_map/ppermute | solution.py:17
  44.9 1.2 %collective-permute-start.20 = (bf16[128,256]{1,0:T(8,128)(2,1)S(1)}, bf16[128,256]{1,0:T(8,128)(2,1)S(1)}, u32[]{:S(2)}, u32[]{:S(2)}) collective-permute-start(bf16[128,256]{1,0:T(8,128)(2,1)S(1)} %get-tuple-element.71), channel_id=1, source_target_pairs={{0,2},{2,0},{4,6},{6,4},{8,10},{10,8},{12,14},{14,12},{16,18},{18,... | collective-permute-start | bytes 196616 | tf_op jit(solution)/shard_map/ppermute | solution.py:17
  46.1 0.8 %collective-permute-done.17.refs_2_ = bf16[128,256]{1,0:T(8,128)(2,1)S(1)} collective-permute-done((bf16[128,256]{1,0:T(8,128)(2,1)S(1)}, bf16[128,256]{1,0:T(8,128)(2,1)S(1)}, u32[]{:S(2)}, u32[]{:S(2)}) %collective-permute-start.17) | collective-permute-done | bytes 65568 | tf_op jit(solution)/shard_map/ppermute | solution.py:17
  46.9 1.4 %collective-permute-done.18.refs_3_ = bf16[128,256]{1,0:T(8,128)(2,1)S(1)} collective-permute-done((bf16[128,256]{1,0:T(8,128)(2,1)S(1)}, bf16[128,256]{1,0:T(8,128)(2,1)S(1)}, u32[]{:S(2)}, u32[]{:S(2)}) %collective-permute-start.18) | collective-permute-done | bytes 65568 | tf_op jit(solution)/shard_map/ppermute | solution.py:17
  48.3 0.7 project.1
  49.1 0.1 collective-permute-start.19
  49.1 1.7 %collective-permute-start.26 = (bf16[256,256]{1,0:T(8,128)(2,1)S(1)}, bf16[256,256]{1,0:T(8,128)(2,1)S(1)}, u32[]{:S(2)}, u32[]{:S(2)}) collective-permute-start(bf16[256,256]{1,0:T(8,128)(2,1)S(1)} %get-tuple-element.78), channel_id=1, source_target_pairs={{0,8},{2,10},{4,12},{6,14},{8,0},{10,2},{12,4},{14,6},{16,24},{18,... | collective-permute-start | bytes 393224 | tf_op jit(solution)/shard_map/ppermute | solution.py:17
  50.8 0.4 collective-permute-start.21
  51.2 2.0 %collective-permute-start.27 = (bf16[128,256]{1,0:T(8,128)(2,1)S(1)}, bf16[128,256]{1,0:T(8,128)(2,1)S(1)}, u32[]{:S(2)}, u32[]{:S(2)}) collective-permute-start(bf16[128,256]{1,0:T(8,128)(2,1)S(1)} %get-tuple-element.79), channel_id=1, source_target_pairs={{0,16},{2,18},{4,20},{6,22},{8,24},{10,26},{12,28},{14,30},{16,0},... | collective-permute-start | bytes 196616 | tf_op jit(solution)/shard_map/ppermute | solution.py:17
  53.3 1.8 %collective-permute-start.28 = (bf16[128,256]{1,0:T(8,128)(2,1)S(1)}, bf16[128,256]{1,0:T(8,128)(2,1)S(1)}, u32[]{:S(2)}, u32[]{:S(2)}) collective-permute-start(bf16[128,256]{1,0:T(8,128)(2,1)S(1)} %get-tuple-element.80), channel_id=1, source_target_pairs={{0,24},{2,26},{4,28},{6,30},{8,16},{10,18},{12,20},{14,22},{16,8},... | collective-permute-start | bytes 196616 | tf_op jit(solution)/shard_map/ppermute | solution.py:17
  55.1 0.8 %collective-permute-start.23 = (bf16[256,256]{1,0:T(8,128)(2,1)S(1)}, bf16[256,256]{1,0:T(8,128)(2,1)S(1)}, u32[]{:S(2)}, u32[]{:S(2)}) collective-permute-start(bf16[256,256]{1,0:T(8,128)(2,1)S(1)} %get-tuple-element.75), channel_id=1, source_target_pairs={{0,2},{2,0},{4,6},{6,4},{8,10},{10,8},{12,14},{14,12},{16,18},{18,... | collective-permute-start | bytes 393224 | tf_op jit(solution)/shard_map/ppermute | solution.py:17
  55.9 0.6 collective-permute-done.27.far2_ref
  56.5 1.8 %collective-permute-start.24 = (bf16[256,256]{1,0:T(8,128)(2,1)S(1)}, bf16[256,256]{1,0:T(8,128)(2,1)S(1)}, u32[]{:S(2)}, u32[]{:S(2)}) collective-permute-start(bf16[256,256]{1,0:T(8,128)(2,1)S(1)} %get-tuple-element.76), channel_id=1, source_target_pairs={{0,4},{2,6},{4,0},{6,2},{8,12},{10,14},{12,8},{14,10},{16,20},{18,... | collective-permute-start | bytes 393224 | tf_op jit(solution)/shard_map/ppermute | solution.py:17
  58.2 2.4 %collective-permute-done.28.far3_ref = bf16[128,256]{1,0:T(8,128)(2,1)S(1)} collective-permute-done((bf16[128,256]{1,0:T(8,128)(2,1)S(1)}, bf16[128,256]{1,0:T(8,128)(2,1)S(1)}, u32[]{:S(2)}, u32[]{:S(2)}) %collective-permute-start.28) | collective-permute-done | bytes 65568 | tf_op jit(solution)/shard_map/ppermute | solution.py:17
  60.6 0.9 %collective-permute-start.25 = (bf16[256,256]{1,0:T(8,128)(2,1)S(1)}, bf16[256,256]{1,0:T(8,128)(2,1)S(1)}, u32[]{:S(2)}, u32[]{:S(2)}) collective-permute-start(bf16[256,256]{1,0:T(8,128)(2,1)S(1)} %get-tuple-element.77), channel_id=1, source_target_pairs={{0,6},{2,4},{4,2},{6,0},{8,14},{10,12},{12,10},{14,8},{16,22},{18,... | collective-permute-start | bytes 393224 | tf_op jit(solution)/shard_map/ppermute | solution.py:17
  61.5 2.0 %collective-permute-start.22 = (bf16[128,256]{1,0:T(8,128)(2,1)S(1)}, bf16[128,256]{1,0:T(8,128)(2,1)S(1)}, u32[]{:S(2)}, u32[]{:S(2)}) collective-permute-start(bf16[128,256]{1,0:T(8,128)(2,1)S(1)} %get-tuple-element.73), channel_id=1, source_target_pairs={{0,6},{2,4},{4,2},{6,0},{8,14},{10,12},{12,10},{14,8},{16,22},{18,... | collective-permute-start | bytes 196616 | tf_op jit(solution)/shard_map/ppermute | solution.py:17
  63.5 0.2 carry.1
  63.7 4.2 %collective-permute-done.22.refs_3_ = bf16[128,256]{1,0:T(8,128)(2,1)S(1)} collective-permute-done((bf16[128,256]{1,0:T(8,128)(2,1)S(1)}, bf16[128,256]{1,0:T(8,128)(2,1)S(1)}, u32[]{:S(2)}, u32[]{:S(2)}) %collective-permute-start.22) | collective-permute-done | bytes 65568 | tf_op jit(solution)/shard_map/ppermute | solution.py:17
  67.9 0.6 collective-permute-start.29
  68.5 0.8 %collective-permute-start.30 = (bf16[64,256]{1,0:T(8,128)(2,1)S(1)}, bf16[64,256]{1,0:T(8,128)(2,1)S(1)}, u32[]{:S(2)}, u32[]{:S(2)}) collective-permute-start(bf16[64,256]{1,0:T(8,128)(2,1)S(1)} %get-tuple-element.83), channel_id=1, source_target_pairs={{0,4},{2,6},{4,0},{6,2},{8,12},{10,14},{12,8},{14,10},{16,20},{18,... | collective-permute-start | bytes 98312 | tf_op jit(solution)/shard_map/ppermute | solution.py:17
  69.3 2.1 %collective-permute-start.31 = (bf16[64,256]{1,0:T(8,128)(2,1)S(1)}, bf16[64,256]{1,0:T(8,128)(2,1)S(1)}, u32[]{:S(2)}, u32[]{:S(2)}) collective-permute-start(bf16[64,256]{1,0:T(8,128)(2,1)S(1)} %get-tuple-element.84), channel_id=1, source_target_pairs={{0,6},{2,4},{4,2},{6,0},{8,14},{10,12},{12,10},{14,8},{16,22},{18,... | collective-permute-start | bytes 98312 | tf_op jit(solution)/shard_map/ppermute | solution.py:17
  71.4 0.4 collective-permute-done.29.refs_9_
  71.8 0.6 collective-permute-done.30.refs_10_
  72.4 1.7 %collective-permute-done.31.refs_11_ = bf16[64,256]{1,0:T(8,128)(2,1)S(1)} collective-permute-done((bf16[64,256]{1,0:T(8,128)(2,1)S(1)}, bf16[64,256]{1,0:T(8,128)(2,1)S(1)}, u32[]{:S(2)}, u32[]{:S(2)}) %collective-permute-start.31) | collective-permute-done | bytes 32800 | tf_op jit(solution)/shard_map/ppermute | solution.py:17
  74.2 1.1 %join.1 = (bf16[128,1024]{1,0:T(8,128)(2,1)}, bf16[128,1024]{1,0:T(8,128)(2,1)}, bf16[128,1024]{1,0:T(8,128)(2,1)}) custom-call(bf16[128,256]{1,0:T(8,128)(2,1)S(1)} %get-tuple-element.70.refs_0_, bf16[128,256]{1,0:T(8,128)(2,1)S(1)} %collective-permute-done.20.refs_1_, bf16[128,256]{1,0:T(8,128)(2,1)S(1)} %collective-permute-done.21.refs_2_, ...), custom_call_target="tpu_custom_call" | custom-call | bytes 917504 | tf_op jit(solution)/shard_map/join/pallas_call | solution.py:49
  75.3 0.8 add_convert_fusion
  (20 shorter events, 0.0 us)
Async XLA Ops:
  0.6 23.7 %collective-permute-start.6 = (bf16[128,1024]{1,0:T(8,128)(2,1)}, bf16[128,1024]{1,0:T(8,128)(2,1)S(1)}, u32[]{:S(2)}, u32[]{:S(2)}) collective-permute-start(bf16[128,1024]{1,0:T(8,128)(2,1)} %own_ref.1), channel_id=1, source_target_pairs={{0,1},{1,0},{2,3},{3,2},{4,5},{5,4},{6,7},{7,6},{8,9},{9,8},{10,11... | collective-permute-start | bytes 786440 | tf_op jit(solution)/shard_map/ppermute | solution.py:17
  1.1 0.9 %copy-start.2 = (bf16[128,1024]{1,0:T(8,128)(2,1)S(1)}, bf16[128,1024]{1,0:T(8,128)(2,1)}, u32[]{:S(2)}) copy-start(bf16[128,1024]{1,0:T(8,128)(2,1)} %q_ref.1) | copy-start | bytes 786436
  2.1 0.9 %copy-start.3 = (bf16[128,1024]{1,0:T(8,128)(2,1)S(1)}, bf16[128,1024]{1,0:T(8,128)(2,1)}, u32[]{:S(2)}) copy-start(bf16[128,1024]{1,0:T(8,128)(2,1)} %k_ref.1) | copy-start | bytes 786436
  3.0 0.9 %copy-start.4 = (bf16[128,1024]{1,0:T(8,128)(2,1)S(1)}, bf16[128,1024]{1,0:T(8,128)(2,1)}, u32[]{:S(2)}) copy-start(bf16[128,1024]{1,0:T(8,128)(2,1)} %v_ref.1) | copy-start | bytes 786436
  4.9 4.6 %collective-permute-start.10 = (bf16[64,256]{1,0:T(8,128)(2,1)S(1)}, bf16[64,256]{1,0:T(8,128)(2,1)S(1)}, u32[]{:S(2)}, u32[]{:S(2)}) collective-permute-start(bf16[64,256]{1,0:T(8,128)(2,1)S(1)} %get-tuple-element.59), channel_id=1, source_target_pairs={{0,2},{2,0},{4,6},{6,4},{8,10},{10,8},{12,14},{14,12},{16,18},{18,... | collective-permute-start | bytes 98312 | tf_op jit(solution)/shard_map/ppermute | solution.py:17
  7.4 11.4 %collective-permute-start = (bf16[128,256]{1,0:T(8,128)(2,1)S(1)}, bf16[128,256]{1,0:T(8,128)(2,1)S(1)}, u32[]{:S(2)}, u32[]{:S(2)}) collective-permute-start(bf16[128,256]{1,0:T(8,128)(2,1)S(1)} %get-tuple-element.47), channel_id=1, source_target_pairs={{0,2},{2,0},{4,6},{6,4},{8,10},{10,8},{12,14},{14,12},{16,18},{18,... | collective-permute-start | bytes 196616 | tf_op jit(solution)/shard_map/ppermute | solution.py:17
  7.5 12.8 %collective-permute-start.1 = (bf16[128,256]{1,0:T(8,128)(2,1)S(1)}, bf16[128,256]{1,0:T(8,128)(2,1)S(1)}, u32[]{:S(2)}, u32[]{:S(2)}) collective-permute-start(bf16[128,256]{1,0:T(8,128)(2,1)S(1)} %get-tuple-element.48), channel_id=1, source_target_pairs={{0,4},{2,6},{4,0},{6,2},{8,12},{10,14},{12,8},{14,10},{16,20},{18,... | collective-permute-start | bytes 196616 | tf_op jit(solution)/shard_map/ppermute | solution.py:17
  9.5 4.1 %collective-permute-start.11 = (bf16[64,256]{1,0:T(8,128)(2,1)S(1)}, bf16[64,256]{1,0:T(8,128)(2,1)S(1)}, u32[]{:S(2)}, u32[]{:S(2)}) collective-permute-start(bf16[64,256]{1,0:T(8,128)(2,1)S(1)} %get-tuple-element.60), channel_id=1, source_target_pairs={{0,4},{2,6},{4,0},{6,2},{8,12},{10,14},{12,8},{14,10},{16,20},{18,... | collective-permute-start | bytes 98312 | tf_op jit(solution)/shard_map/ppermute | solution.py:17
  9.5 5.5 %collective-permute-start.12 = (bf16[64,256]{1,0:T(8,128)(2,1)S(1)}, bf16[64,256]{1,0:T(8,128)(2,1)S(1)}, u32[]{:S(2)}, u32[]{:S(2)}) collective-permute-start(bf16[64,256]{1,0:T(8,128)(2,1)S(1)} %get-tuple-element.61), channel_id=1, source_target_pairs={{0,6},{2,4},{4,2},{6,0},{8,14},{10,12},{12,10},{14,8},{16,22},{18,... | collective-permute-start | bytes 98312 | tf_op jit(solution)/shard_map/ppermute | solution.py:17
  13.6 8.2 %collective-permute-start.2 = (bf16[128,256]{1,0:T(8,128)(2,1)S(1)}, bf16[128,256]{1,0:T(8,128)(2,1)S(1)}, u32[]{:S(2)}, u32[]{:S(2)}) collective-permute-start(bf16[128,256]{1,0:T(8,128)(2,1)S(1)} %get-tuple-element.49), channel_id=1, source_target_pairs={{0,6},{2,4},{4,2},{6,0},{8,14},{10,12},{12,10},{14,8},{16,22},{18,... | collective-permute-start | bytes 196616 | tf_op jit(solution)/shard_map/ppermute | solution.py:17
  15.2 6.7 %collective-permute-start.15 = (bf16[128,256]{1,0:T(8,128)(2,1)S(1)}, bf16[128,256]{1,0:T(8,128)(2,1)S(1)}, u32[]{:S(2)}, u32[]{:S(2)}) collective-permute-start(bf16[128,256]{1,0:T(8,128)(2,1)S(1)} %get-tuple-element.63), channel_id=1, source_target_pairs={{0,24},{2,26},{4,28},{6,30},{8,16},{10,18},{12,20},{14,22},{16,8},... | collective-permute-start | bytes 196616 | tf_op jit(solution)/shard_map/ppermute | solution.py:17
  18.9 11.4 %collective-permute-start.3 = (bf16[256,256]{1,0:T(8,128)(2,1)S(1)}, bf16[256,256]{1,0:T(8,128)(2,1)S(1)}, u32[]{:S(2)}, u32[]{:S(2)}) collective-permute-start(bf16[256,256]{1,0:T(8,128)(2,1)S(1)} %get-tuple-element.51), channel_id=1, source_target_pairs={{0,2},{2,0},{4,6},{6,4},{8,10},{10,8},{12,14},{14,12},{16,18},{18,... | collective-permute-start | bytes 393224 | tf_op jit(solution)/shard_map/ppermute | solution.py:17
  20.3 11.5 %collective-permute-start.4 = (bf16[256,256]{1,0:T(8,128)(2,1)S(1)}, bf16[256,256]{1,0:T(8,128)(2,1)S(1)}, u32[]{:S(2)}, u32[]{:S(2)}) collective-permute-start(bf16[256,256]{1,0:T(8,128)(2,1)S(1)} %get-tuple-element.52), channel_id=1, source_target_pairs={{0,4},{2,6},{4,0},{6,2},{8,12},{10,14},{12,8},{14,10},{16,20},{18,... | collective-permute-start | bytes 393224 | tf_op jit(solution)/shard_map/ppermute | solution.py:17
  21.8 7.6 %collective-permute-start.14 = (bf16[128,256]{1,0:T(8,128)(2,1)S(1)}, bf16[128,256]{1,0:T(8,128)(2,1)S(1)}, u32[]{:S(2)}, u32[]{:S(2)}) collective-permute-start(bf16[128,256]{1,0:T(8,128)(2,1)S(1)} %get-tuple-element.63), channel_id=1, source_target_pairs={{0,16},{2,18},{4,20},{6,22},{8,24},{10,26},{12,28},{14,30},{16,0},... | collective-permute-start | bytes 196616 | tf_op jit(solution)/shard_map/ppermute | solution.py:17
  21.9 11.0 %collective-permute-start.5 = (bf16[256,256]{1,0:T(8,128)(2,1)S(1)}, bf16[256,256]{1,0:T(8,128)(2,1)S(1)}, u32[]{:S(2)}, u32[]{:S(2)}) collective-permute-start(bf16[256,256]{1,0:T(8,128)(2,1)S(1)} %get-tuple-element.53), channel_id=1, source_target_pairs={{0,6},{2,4},{4,2},{6,0},{8,14},{10,12},{12,10},{14,8},{16,22},{18,... | collective-permute-start | bytes 393224 | tf_op jit(solution)/shard_map/ppermute | solution.py:17
  24.3 8.6 %collective-permute-start.13 = (bf16[256,256]{1,0:T(8,128)(2,1)S(1)}, bf16[256,256]{1,0:T(8,128)(2,1)S(1)}, u32[]{:S(2)}, u32[]{:S(2)}) collective-permute-start(bf16[256,256]{1,0:T(8,128)(2,1)S(1)} %get-tuple-element.62), channel_id=1, source_target_pairs={{0,8},{2,10},{4,12},{6,14},{8,0},{10,2},{12,4},{14,6},{16,24},{18,... | collective-permute-start | bytes 393224 | tf_op jit(solution)/shard_map/ppermute | solution.py:17
  24.7 2.2 %copy-start = (bf16[1024,2048]{1,0:T(8,128)(2,1)S(1)}, bf16[1024,2048]{1,0:T(8,128)(2,1)}, u32[]{:S(2)}) copy-start(bf16[1024,2048]{1,0:T(8,128)(2,1)} %refs_4_.1) | copy-start | bytes 12582916
  26.9 0.9 %copy-start.5 = (bf16[128,1024]{1,0:T(8,128)(2,1)S(1)}, bf16[128,1024]{1,0:T(8,128)(2,1)}, u32[]{:S(2)}) copy-start(bf16[128,1024]{1,0:T(8,128)(2,1)} %own_ref.1) | copy-start | bytes 786436
  27.9 20.5 %copy-start.1 = (bf16[1024,2048]{1,0:T(8,128)(2,1)S(1)}, bf16[1024,2048]{1,0:T(8,128)(2,1)}, u32[]{:S(2)}) copy-start(bf16[1024,2048]{1,0:T(8,128)(2,1)} %refs_4_.1) | copy-start | bytes 12582916
  29.4 4.3 %collective-permute-start.7 = (bf16[128,256]{1,0:T(8,128)(2,1)S(1)}, bf16[128,256]{1,0:T(8,128)(2,1)S(1)}, u32[]{:S(2)}, u32[]{:S(2)}) collective-permute-start(bf16[128,256]{1,0:T(8,128)(2,1)S(1)} %get-tuple-element.55), channel_id=1, source_target_pairs={{0,2},{2,0},{4,6},{6,4},{8,10},{10,8},{12,14},{14,12},{16,18},{18,... | collective-permute-start | bytes 196616 | tf_op jit(solution)/shard_map/ppermute | solution.py:17
  30.3 4.3 %collective-permute-start.8 = (bf16[128,256]{1,0:T(8,128)(2,1)S(1)}, bf16[128,256]{1,0:T(8,128)(2,1)S(1)}, u32[]{:S(2)}, u32[]{:S(2)}) collective-permute-start(bf16[128,256]{1,0:T(8,128)(2,1)S(1)} %get-tuple-element.56), channel_id=1, source_target_pairs={{0,4},{2,6},{4,0},{6,2},{8,12},{10,14},{12,8},{14,10},{16,20},{18,... | collective-permute-start | bytes 196616 | tf_op jit(solution)/shard_map/ppermute | solution.py:17
  31.7 5.2 %collective-permute-start.9 = (bf16[128,256]{1,0:T(8,128)(2,1)S(1)}, bf16[128,256]{1,0:T(8,128)(2,1)S(1)}, u32[]{:S(2)}, u32[]{:S(2)}) collective-permute-start(bf16[128,256]{1,0:T(8,128)(2,1)S(1)} %get-tuple-element.57), channel_id=1, source_target_pairs={{0,6},{2,4},{4,2},{6,0},{8,14},{10,12},{12,10},{14,8},{16,22},{18,... | collective-permute-start | bytes 196616 | tf_op jit(solution)/shard_map/ppermute | solution.py:17
  41.3 4.8 %collective-permute-start.16 = (bf16[128,256]{1,0:T(8,128)(2,1)S(1)}, bf16[128,256]{1,0:T(8,128)(2,1)S(1)}, u32[]{:S(2)}, u32[]{:S(2)}) collective-permute-start(bf16[128,256]{1,0:T(8,128)(2,1)S(1)} %get-tuple-element.65), channel_id=1, source_target_pairs={{0,2},{2,0},{4,6},{6,4},{8,10},{10,8},{12,14},{14,12},{16,18},{18,... | collective-permute-start | bytes 196616 | tf_op jit(solution)/shard_map/ppermute | solution.py:17
  42.6 4.3 %collective-permute-start.17 = (bf16[128,256]{1,0:T(8,128)(2,1)S(1)}, bf16[128,256]{1,0:T(8,128)(2,1)S(1)}, u32[]{:S(2)}, u32[]{:S(2)}) collective-permute-start(bf16[128,256]{1,0:T(8,128)(2,1)S(1)} %get-tuple-element.66), channel_id=1, source_target_pairs={{0,4},{2,6},{4,0},{6,2},{8,12},{10,14},{12,8},{14,10},{16,20},{18,... | collective-permute-start | bytes 196616 | tf_op jit(solution)/shard_map/ppermute | solution.py:17
  43.2 5.2 %collective-permute-start.18 = (bf16[128,256]{1,0:T(8,128)(2,1)S(1)}, bf16[128,256]{1,0:T(8,128)(2,1)S(1)}, u32[]{:S(2)}, u32[]{:S(2)}) collective-permute-start(bf16[128,256]{1,0:T(8,128)(2,1)S(1)} %get-tuple-element.67), channel_id=1, source_target_pairs={{0,6},{2,4},{4,2},{6,0},{8,14},{10,12},{12,10},{14,8},{16,22},{18,... | collective-permute-start | bytes 196616 | tf_op jit(solution)/shard_map/ppermute | solution.py:17
  44.9 8.4 %collective-permute-start.20 = (bf16[128,256]{1,0:T(8,128)(2,1)S(1)}, bf16[128,256]{1,0:T(8,128)(2,1)S(1)}, u32[]{:S(2)}, u32[]{:S(2)}) collective-permute-start(bf16[128,256]{1,0:T(8,128)(2,1)S(1)} %get-tuple-element.71), channel_id=1, source_target_pairs={{0,2},{2,0},{4,6},{6,4},{8,10},{10,8},{12,14},{14,12},{16,18},{18,... | collective-permute-start | bytes 196616 | tf_op jit(solution)/shard_map/ppermute | solution.py:17
  49.1 26.2 %collective-permute-start.19 = (bf16[128,1024]{1,0:T(8,128)(2,1)S(1)}, bf16[128,1024]{1,0:T(8,128)(2,1)S(1)}, u32[]{:S(2)}, u32[]{:S(2)}) collective-permute-start(bf16[128,1024]{1,0:T(8,128)(2,1)S(1)} %get-tuple-element.69), channel_id=1, source_target_pairs={{0,1},{1,0},{2,3},{3,2},{4,5},{5,4},{6,7},{7,6},{8,9},{9,8},{10,11... | collective-permute-start | bytes 786440 | tf_op jit(solution)/shard_map/ppermute | solution.py:17
  49.1 12.4 %collective-permute-start.26 = (bf16[256,256]{1,0:T(8,128)(2,1)S(1)}, bf16[256,256]{1,0:T(8,128)(2,1)S(1)}, u32[]{:S(2)}, u32[]{:S(2)}) collective-permute-start(bf16[256,256]{1,0:T(8,128)(2,1)S(1)} %get-tuple-element.78), channel_id=1, source_target_pairs={{0,8},{2,10},{4,12},{6,14},{8,0},{10,2},{12,4},{14,6},{16,24},{18,... | collective-permute-start | bytes 393224 | tf_op jit(solution)/shard_map/ppermute | solution.py:17
  50.8 4.3 %collective-permute-start.21 = (bf16[128,256]{1,0:T(8,128)(2,1)S(1)}, bf16[128,256]{1,0:T(8,128)(2,1)S(1)}, u32[]{:S(2)}, u32[]{:S(2)}) collective-permute-start(bf16[128,256]{1,0:T(8,128)(2,1)S(1)} %get-tuple-element.72), channel_id=1, source_target_pairs={{0,4},{2,6},{4,0},{6,2},{8,12},{10,14},{12,8},{14,10},{16,20},{18,... | collective-permute-start | bytes 196616 | tf_op jit(solution)/shard_map/ppermute | solution.py:17
  51.2 5.2 %collective-permute-start.27 = (bf16[128,256]{1,0:T(8,128)(2,1)S(1)}, bf16[128,256]{1,0:T(8,128)(2,1)S(1)}, u32[]{:S(2)}, u32[]{:S(2)}) collective-permute-start(bf16[128,256]{1,0:T(8,128)(2,1)S(1)} %get-tuple-element.79), channel_id=1, source_target_pairs={{0,16},{2,18},{4,20},{6,22},{8,24},{10,26},{12,28},{14,30},{16,0},... | collective-permute-start | bytes 196616 | tf_op jit(solution)/shard_map/ppermute | solution.py:17
  53.3 7.3 %collective-permute-start.28 = (bf16[128,256]{1,0:T(8,128)(2,1)S(1)}, bf16[128,256]{1,0:T(8,128)(2,1)S(1)}, u32[]{:S(2)}, u32[]{:S(2)}) collective-permute-start(bf16[128,256]{1,0:T(8,128)(2,1)S(1)} %get-tuple-element.80), channel_id=1, source_target_pairs={{0,24},{2,26},{4,28},{6,30},{8,16},{10,18},{12,20},{14,22},{16,8},... | collective-permute-start | bytes 196616 | tf_op jit(solution)/shard_map/ppermute | solution.py:17
  55.1 13.4 %collective-permute-start.23 = (bf16[256,256]{1,0:T(8,128)(2,1)S(1)}, bf16[256,256]{1,0:T(8,128)(2,1)S(1)}, u32[]{:S(2)}, u32[]{:S(2)}) collective-permute-start(bf16[256,256]{1,0:T(8,128)(2,1)S(1)} %get-tuple-element.75), channel_id=1, source_target_pairs={{0,2},{2,0},{4,6},{6,4},{8,10},{10,8},{12,14},{14,12},{16,18},{18,... | collective-permute-start | bytes 393224 | tf_op jit(solution)/shard_map/ppermute | solution.py:17
  56.5 12.9 %collective-permute-start.24 = (bf16[256,256]{1,0:T(8,128)(2,1)S(1)}, bf16[256,256]{1,0:T(8,128)(2,1)S(1)}, u32[]{:S(2)}, u32[]{:S(2)}) collective-permute-start(bf16[256,256]{1,0:T(8,128)(2,1)S(1)} %get-tuple-element.76), channel_id=1, source_target_pairs={{0,4},{2,6},{4,0},{6,2},{8,12},{10,14},{12,8},{14,10},{16,20},{18,... | collective-permute-start | bytes 393224 | tf_op jit(solution)/shard_map/ppermute | solution.py:17
  60.6 10.8 %collective-permute-start.25 = (bf16[256,256]{1,0:T(8,128)(2,1)S(1)}, bf16[256,256]{1,0:T(8,128)(2,1)S(1)}, u32[]{:S(2)}, u32[]{:S(2)}) collective-permute-start(bf16[256,256]{1,0:T(8,128)(2,1)S(1)} %get-tuple-element.77), channel_id=1, source_target_pairs={{0,6},{2,4},{4,2},{6,0},{8,14},{10,12},{12,10},{14,8},{16,22},{18,... | collective-permute-start | bytes 393224 | tf_op jit(solution)/shard_map/ppermute | solution.py:17
  61.5 6.4 %collective-permute-start.22 = (bf16[128,256]{1,0:T(8,128)(2,1)S(1)}, bf16[128,256]{1,0:T(8,128)(2,1)S(1)}, u32[]{:S(2)}, u32[]{:S(2)}) collective-permute-start(bf16[128,256]{1,0:T(8,128)(2,1)S(1)} %get-tuple-element.73), channel_id=1, source_target_pairs={{0,6},{2,4},{4,2},{6,0},{8,14},{10,12},{12,10},{14,8},{16,22},{18,... | collective-permute-start | bytes 196616 | tf_op jit(solution)/shard_map/ppermute | solution.py:17
  67.9 3.9 %collective-permute-start.29 = (bf16[64,256]{1,0:T(8,128)(2,1)S(1)}, bf16[64,256]{1,0:T(8,128)(2,1)S(1)}, u32[]{:S(2)}, u32[]{:S(2)}) collective-permute-start(bf16[64,256]{1,0:T(8,128)(2,1)S(1)} %get-tuple-element.82), channel_id=1, source_target_pairs={{0,2},{2,0},{4,6},{6,4},{8,10},{10,8},{12,14},{14,12},{16,18},{18,... | collective-permute-start | bytes 98312 | tf_op jit(solution)/shard_map/ppermute | solution.py:17
  68.5 3.9 %collective-permute-start.30 = (bf16[64,256]{1,0:T(8,128)(2,1)S(1)}, bf16[64,256]{1,0:T(8,128)(2,1)S(1)}, u32[]{:S(2)}, u32[]{:S(2)}) collective-permute-start(bf16[64,256]{1,0:T(8,128)(2,1)S(1)} %get-tuple-element.83), channel_id=1, source_target_pairs={{0,4},{2,6},{4,0},{6,2},{8,12},{10,14},{12,8},{14,10},{16,20},{18,... | collective-permute-start | bytes 98312 | tf_op jit(solution)/shard_map/ppermute | solution.py:17
  69.3 4.8 %collective-permute-start.31 = (bf16[64,256]{1,0:T(8,128)(2,1)S(1)}, bf16[64,256]{1,0:T(8,128)(2,1)S(1)}, u32[]{:S(2)}, u32[]{:S(2)}) collective-permute-start(bf16[64,256]{1,0:T(8,128)(2,1)S(1)} %get-tuple-element.84), channel_id=1, source_target_pairs={{0,6},{2,4},{4,2},{6,0},{8,14},{10,12},{12,10},{14,8},{16,22},{18,... | collective-permute-start | bytes 98312 | tf_op jit(solution)/shard_map/ppermute | solution.py:17

commit v2 on v1

v2 whole, which is shorter than its diff:
```python
import jax
import jax.numpy as jnp
from jax import lax
from jax.experimental import pallas as pl
from jax.experimental.pallas import tpu as pltpu
from jax.sharding import PartitionSpec as P

DH = 128
PLANE = 4
PIECES = 2
SCALE = DH ** (-0.5)
BF16 = jnp.bfloat16
F32 = jnp.float32


def xor_permute(block, mask, axis="ctx"):
    count = lax.axis_size(axis)
    return lax.ppermute(block, axis, [(i, i ^ mask) for i in range(count)])


def dot(a, b, contract_a=1, contract_b=0):
    return lax.dot_general(
        a, b, (((contract_a,), (contract_b,)), ((), ())), preferred_element_type=F32
    )


def pool_matrix(rows):
    out = lax.broadcasted_iota(jnp.int32, (rows // 2, rows), 0)
    src = lax.broadcasted_iota(jnp.int32, (rows // 2, rows), 1)
    return jnp.where(src // 2 == out, 0.5, 0.0).astype(BF16)


def spread_matrix(rows, times):
    out = lax.broadcasted_iota(jnp.int32, (rows * times, rows), 0)
    src = lax.broadcasted_iota(jnp.int32, (rows * times, rows), 1)
    return jnp.where(out // times == src, 1.0 / times, 0.0).astype(BF16)


def pool(block):
    return dot(pool_matrix(block.shape[0]), block).astype(BF16)


def spread(block, times):
    return dot(spread_matrix(block.shape[0], times), block.astype(BF16))


def call(kernel, outs, *args, after=(), hbm=(), hbm_out=False, scratch=(), cost_us=1.0, name=None):
    vmem = pl.BlockSpec(memory_space=pltpu.VMEM)
    in_hbm = pl.BlockSpec(memory_space=pltpu.HBM)
    space = pltpu.HBM if hbm_out else pltpu.VMEM
    args = [
        pltpu.with_memory_space_constraint(a, pltpu.HBM) if n in hbm else a
        for n, a in enumerate(args)
    ]
    count = len(args)
    return pl.pallas_call(
        lambda *refs: kernel(*refs[:count], *refs[count + len(after) :]),
        out_shape=[space(out.shape, out.dtype) for out in outs],
        in_specs=[in_hbm if n in hbm else vmem for n in range(count)]
        + [pl.BlockSpec(memory_space=pl.ANY)] * len(after),
        scratch_shapes=scratch,
        out_specs=[in_hbm if hbm_out else vmem] * len(outs),
        compiler_params=pltpu.CompilerParams(vmem_limit_bytes=24 * 1024 * 1024),
        cost_estimate=pl.CostEstimate(
            flops=int(cost_us * 1e9), bytes_accessed=0, transcendentals=0
        ),
        name=name,
    )(*args, *after)


def part(n, width):
    return slice(n * width, (n + 1) * width)


def start_all(pairs, sems):
    copies = [pltpu.make_async_copy(a, b, sems.at[n]) for n, (a, b) in enumerate(pairs)]
    for copy in copies:
        copy.start()
    return copies


def columns(r, width):
    place = (lax.axis_index("ctx") & (PLANE - 1)) ^ r
    return pl.ds(pl.multiple_of(place * width, width), width)


def key_value_kernel(k_ref, v_ref, *refs):
    outs, sems = refs[:PLANE], refs[PLANE]
    rows, width = k_ref.shape[0], k_ref.shape[1] // PLANE
    pairs = []
    for r in range(PLANE):
        pairs.append((k_ref.at[:, columns(r, width)], outs[r].at[part(0, rows), :]))
        pairs.append((v_ref.at[:, columns(r, width)], outs[r].at[part(1, rows), :]))
    for copy in start_all(pairs, sems):
        copy.wait()


def cotangent_kernel(q_ref, own_ref, other_ref, w_ref, *refs):
    outs, w, own, sems, w_sems = refs[:PLANE], refs[PLANE], *refs[PLANE + 1 :]
    rows, width = q_ref.shape[0], q_ref.shape[1] // PLANE
    half = own_ref.shape[1]
    head = lax.axis_index("head")
    own_at = pl.ds(pl.multiple_of(head * half, half), half)
    other_at = pl.ds(pl.multiple_of((1 - head) * half, half), half)
    here = [columns(r, width) for r in range(PLANE)]
    w_copies = [
        pltpu.make_async_copy(w_ref.at[here[r], :], w.at[here[r], :], w_sems.at[r])
        for r in range(PLANE)
    ]
    pairs = [(own_ref, own)]
    pairs += [(q_ref.at[:, here[r]], outs[r].at[part(0, rows), :]) for r in range(PLANE)]
    copies = start_all(pairs, sems)
    w_copies[0].start()
    w_copies[1].start()
    copies[0].wait()
    for r in range(PLANE):
        w_copies[r].wait()
        if r + 2 < PLANE:
            w_copies[r + 2].start()
        outs[r][rows:, :] = (
            dot(own[...], w[here[r], own_at], 1, 1)
            + dot(other_ref[...], w[here[r], other_at], 1, 1)
        ).astype(BF16)
    for copy in copies[1:]:
        copy.wait()


def far_kernel(*refs):
    kvs, (near_out, far_out) = refs[:PLANE], refs[PLANE:]
    rows, width = kvs[0].shape[0] // 2, kvs[0].shape[1]
    wide = jnp.concatenate([kv[part(m, rows), :] for m in range(2) for kv in kvs], 1)
    near = pool(pool(wide))
    far = pool(near)
    for out, pooled in ((near_out, near), (far_out, far)):
        size = pooled.shape[0]
        for n in range(2 * PLANE):
            out[part(n, size), :] = pooled[:, part(n, width)]


def key_sets(kvs, fars, p, lanes, m):
    rows = kvs[0].shape[0] // 2
    ours, theirs = kvs[2 * p : 2 * p + 2], kvs[2 - 2 * p : 4 - 2 * p]
    return jnp.concatenate(
        [kv[part(m, rows), lanes] for kv in ours]
        + [pool(kv[part(m, rows), lanes]) for kv in theirs]
        + [far[part(m, far.shape[0] // 2), lanes] for far in fars],
        0,
    )


def attention_kernel(n_far, *refs):
    kvs, qgs, fars = refs[:PLANE], refs[PLANE : 2 * PLANE], refs[2 * PLANE : 2 * PLANE + n_far]
    outs = refs[2 * PLANE + n_far :]
    atts, grad_out, prob_out = outs[:PLANE], outs[PLANE], outs[PLANE + 1]
    far_out = outs[PLANE + 2 :]
    rows, width = qgs[0].shape[0] // 2, qgs[0].shape[1]
    start = 3 * rows
    for h in range(width // DH):
        lanes = part(h, DH)
        key_grads, value_grads = [], []
        for p in range(2):
            ours = (2 * p, 2 * p + 1)
            q = jnp.concatenate([qgs[r][:rows, lanes] for r in ours], 0)
            g = jnp.concatenate([qgs[r][rows:, lanes] for r in ours], 0)
            keys = key_sets(kvs, fars, p, lanes, 0)
            values = key_sets(kvs, fars, p, lanes, 1)
            scores = dot(keys, q, 1, 1) * SCALE
            weights = jnp.exp(scores - jnp.max(scores, 0, keepdims=True))
            inverse = 1.0 / jnp.sum(weights, 0, keepdims=True)
            numerator = dot(values, weights.astype(BF16), 0, 0)
            attended = (numerator * inverse).astype(BF16)
            delta = jnp.sum(g.T.astype(F32) * attended.astype(F32), 0, keepdims=True)
            probabilities = weights * inverse
            value_dots = dot(values, g, 1, 1)
            score_grad = (probabilities * (value_dots - delta)).astype(BF16)
            rounded = probabilities.astype(BF16)
            attended = attended.T
            for n, r in enumerate(ours):
                atts[r][:, lanes] = attended[part(n, rows)]
            grad_out[2 * h + p] = score_grad
            prob_out[2 * h + p] = rounded
            key_grads.append(dot(score_grad[start:], q) * SCALE)
            value_grads.append(dot(rounded[start:], g))
        for m, grads in enumerate((key_grads, value_grads)):
            whole, at = grads[0] + grads[1], 0
            for far in far_out:
                size = far.shape[0] // 2
                far[part(m, size), lanes] = whole[at : at + size].astype(BF16)
                at += size


def plane_kernel(n_far, *refs):
    kvs, qgs, fars = refs[:PLANE], refs[PLANE : 2 * PLANE], refs[2 * PLANE : 2 * PLANE + n_far]
    refs = refs[2 * PLANE + n_far :]
    atts, grad_ref, prob_ref = refs[:PLANE], refs[PLANE], refs[PLANE + 1]
    ads, dkvs = refs[PLANE + 2 : 2 * PLANE + 2], refs[2 * PLANE + 2 :]
    rows, width = qgs[0].shape[0] // 2, qgs[0].shape[1]
    pair = 2 * rows
    near = pair + rows
    for r in range(PLANE):
        ads[r][:rows, :] = atts[r][...]
    for h in range(width // DH):
        lanes = part(h, DH)
        key_grads, value_grads = [], []
        for p in range(2):
            ours = (2 * p, 2 * p + 1)
            q = jnp.concatenate([qgs[r][:rows, lanes] for r in ours], 0)
            g = jnp.concatenate([qgs[r][rows:, lanes] for r in ours], 0)
            keys = key_sets(kvs, fars, p, lanes, 0)
            dq = (dot(keys, grad_ref[2 * h + p], 0, 0) * SCALE).astype(BF16).T
            for n, r in enumerate(ours):
                ads[r][rows:, lanes] = dq[part(n, rows)]
            key_grads.append(dot(grad_ref[2 * h + p, :near, :], q) * SCALE)
            value_grads.append(dot(prob_ref[2 * h + p, :near, :], g))
        for m, grads in enumerate((key_grads, value_grads)):
            for p in range(2):
                pooled = grads[1 - p][pair:]
                for n in range(2):
                    dkvs[2 * p + n][part(m, rows), lanes] = grads[p][part(n, rows)] + spread(
                        pooled[part(n, rows // 2)], 2
                    )


def carry_kernel(*refs):
    dkvs, (near_ref, far2_ref, far3_ref) = refs[:PLANE], refs[PLANE : PLANE + 3]
    extra, outs = refs[PLANE + 3 : -PLANE], refs[-PLANE:]
    rows, width = near_ref.shape[0] // 2, near_ref.shape[1]
    size = rows // PLANE
    wide = lambda block, size: jnp.concatenate(
        [block[part(n, size), :].astype(F32) for n in range(2 * PLANE)], 1
    )
    upper = far2_ref[...].astype(F32) + far3_ref[...].astype(F32)
    for ref in extra:
        upper = upper + ref[...].astype(F32)
    whole = wide(near_ref, size) + spread(wide(upper, size // 2), 2)
    carried = spread(whole, 4)
    for n in range(2 * PLANE):
        m, r = divmod(n, PLANE)
        outs[r][part(m, rows), :] = (
            dkvs[r][part(m, rows), :] + carried[:, part(n, width)]
        ).astype(BF16)


def output_kernel(*refs):
    ads, w_ref, own_out, others = refs[:PLANE], refs[PLANE], refs[PLANE + 1], refs[PLANE + 2 :]
    rows, width = ads[0].shape[0] // 2, ads[0].shape[1]
    half = own_out.shape[1]
    head = lax.axis_index("head")
    total = None
    for r in range(PLANE):
        term = dot(ads[r][:rows, :], w_ref[columns(r, width), :])
        total = term if total is None else total + term

    def write(own, other):
        own_out[...] = own
        for n, out in enumerate(others):
            out[...] = other[part(n, rows // PIECES)].astype(BF16)

    @pl.when(head == 0)
    def _():
        write(total[:, :half], total[:, half:])

    @pl.when(head == 1)
    def _():
        write(total[:, half:], total[:, :half])


def join_kernel(own_ref, *refs):
    others, refs = refs[:PIECES], refs[PIECES:]
    ads, dkvs = refs[:PLANE], refs[PLANE : 2 * PLANE]
    o_out, gq_out, gk_out, gv_out, total, sems = refs[2 * PLANE :]
    rows, width = ads[0].shape[0] // 2, ads[0].shape[1]
    pairs = []
    for r in range(PLANE):
        here = columns(r, width)
        pairs.append((ads[r].at[part(1, rows), :], gq_out.at[:, here]))
        pairs.append((dkvs[r].at[part(0, rows), :], gk_out.at[:, here]))
        pairs.append((dkvs[r].at[part(1, rows), :], gv_out.at[:, here]))
    copies = start_all(pairs, sems)
    for n, other in enumerate(others):
        piece = part(n, rows // PIECES)
        total[piece, :] = (own_ref[piece, :] + other[...].astype(F32)).astype(BF16)
    last = pltpu.make_async_copy(total, o_out, sems.at[len(pairs)])
    last.start()
    for copy in copies + [last]:
        copy.wait()


def plane_exchange(blocks):
    return [blocks[0]] + [xor_permute(blocks[r], r) for r in range(1, PLANE)]


def pool_both(block):
    shaped = block.reshape((2, block.shape[0] // 4, 2) + block.shape[1:]).astype(F32)
    return ((shaped[:, :, 0] + shaped[:, :, 1]) * 0.5).astype(BF16).reshape(
        (block.shape[0] // 2,) + block.shape[1:]
    )


def spread_both(block):
    halved = block.astype(F32) * 0.5
    return jnp.repeat(halved, 2, axis=0)


def join_both(blocks):
    halves = [b.reshape((2, b.shape[0] // 2) + b.shape[1:]) for b in blocks]
    joined = jnp.concatenate(halves, 1)
    return joined.reshape((-1,) + joined.shape[2:])


def part_both(block, parts):
    shaped = block.reshape((2, parts, block.shape[0] // (2 * parts)) + block.shape[1:])
    return [shaped[:, n].reshape((-1,) + block.shape[1:]) for n in range(parts)]


def body(queries, key_rows, value_rows, out_weight, cotangent):
    rows, features = queries.shape
    width = features // PLANE
    top_rounds = lax.axis_size("ctx").bit_length() - 1 - 4
    shape = lambda *dims, t=BF16: jax.ShapeDtypeStruct(dims, t)
    dma = lambda n: pltpu.SemaphoreType.DMA((n,))
    blocks = [shape(2 * rows, width)] * PLANE

    other_cotangent = xor_permute(cotangent, 1, "head")
    key_values = call(
        key_value_kernel, blocks, key_rows, value_rows,
        hbm=(0, 1), scratch=[dma(2 * PLANE)], name="pack_keys_values",
    )
    key_values = plane_exchange(key_values)
    *query_grads, weight = call(
        cotangent_kernel, blocks + [shape(*out_weight.shape)],
        queries, cotangent, other_cotangent, out_weight,
        hbm=(0, 1, 3), scratch=[pltpu.VMEM(cotangent.shape, BF16), dma(1 + PLANE), dma(PLANE)],
        cost_us=3.0, name="grad_attended",
    )
    query_grads = plane_exchange(query_grads)
    near, pooled = call(
        far_kernel, [shape(2 * rows, width), shape(rows, width)], *key_values,
        after=(query_grads[0],), name="pool_plane",
    )
    fars = [xor_permute(near, PLANE), xor_permute(pooled, 2 * PLANE), xor_permute(pooled, 3 * PLANE)]
    if top_rounds > 0:
        span = pool_both(join_both([pooled, pool_both(fars[0]), fars[1], fars[2]]))
        for n in range(top_rounds):
            fars.append(xor_permute(span, 4 * PLANE << n))
            span = pool_both(join_both([span, fars[-1]]))
    far_rows = sum(far.shape[0] for far in fars) // 2
    kept = shape(2 * width // DH, 3 * rows + far_rows, 2 * rows)
    results = call(
        lambda *refs: attention_kernel(len(fars), *refs),
        [shape(rows, width)] * PLANE + [kept, kept] + [shape(*far.shape) for far in fars],
        *key_values, *query_grads, *fars,
        cost_us=3.7, name="attention",
    )
    kept, far_grads = results[: PLANE + 2], list(results[PLANE + 2 :])
    results = call(
        lambda *refs: plane_kernel(len(fars), *refs),
        blocks + [shape(2 * rows, width, t=F32)] * PLANE,
        *key_values, *query_grads, *fars, *kept,
        cost_us=2.3, name="plane_grads",
    )
    att_dq, dkv = results[:PLANE], results[PLANE:]
    extra = []
    if top_rounds > 0:
        up = None
        for n in reversed(range(top_rounds)):
            send = far_grads[3 + n].astype(F32)
            if up is not None:
                own_up, their_up = part_both(spread_both(up), 2)
                send = send + their_up
            back = xor_permute(send.astype(BF16), 4 * PLANE << n).astype(F32)
            up = back if up is None else back + own_up
        ups = part_both(spread_both(up), PLANE)
        extra = [ups[0].astype(BF16)]
        far_grads[0] = (far_grads[0].astype(F32) + spread_both(ups[1])).astype(BF16)
        far_grads[1] = (far_grads[1].astype(F32) + ups[2]).astype(BF16)
        far_grads[2] = (far_grads[2].astype(F32) + ups[3]).astype(BF16)
    backs = [xor_permute(far_grads[n], (n + 1) * PLANE) for n in range(3)]
    att_dq = plane_exchange(att_dq)
    dkv = call(carry_kernel, blocks, *dkv, *backs, *extra, cost_us=5.0, name="carry")
    own_sum, *other_sum = call(
        output_kernel,
        [shape(rows, features, t=F32)] + [shape(rows // PIECES, features)] * PIECES,
        *att_dq, weight, after=(dkv[0],), cost_us=0.01, name="project",
    )
    dkv = plane_exchange(dkv)
    other_sum = [xor_permute(piece, 1, "head") for piece in other_sum]
    output, grad_queries, grad_keys, grad_values = call(
        join_kernel, [shape(rows, features)] * 4, own_sum, *other_sum, *att_dq, *dkv,
        hbm_out=True, scratch=[pltpu.VMEM((rows, features), BF16), dma(3 * PLANE + 1)],
        name="join",
    )
    return (output, grad_queries, grad_keys, grad_values)


def solution(mesh):
    rows = P("ctx", "head")
    return jax.shard_map(
        body,
        mesh=mesh,
        in_specs=(rows, rows, rows, P("head", None), rows),
        out_specs=(rows, rows, rows, rows),
        check_vma=False,
    )
```

time: 76.3 us -> 49.2 us (0.64)
  starting transfers between devices: 42.5 us -> 26.5 us
  waiting for transfers between devices: 17.1 us -> 8.43 us
  local copies, waits for them, and re-layouts: 5.99 us -> 0 us
  Pallas kernels: 8.98 us -> 13.4 us
    ppermute x32 -> x21, starting transfers between devices: 42.5 us -> 26.5 us  [xor_permute(): return lax.ppermute(block, axis, [(i, i ^ mask) for i in range(count)])]
    ppermute x32 -> x21, waiting for transfers between devices: 17.1 us -> 8.43 us  [xor_permute(): return lax.ppermute(block, axis, [(i, i ^ mask) for i in range(count)])]
    unnamed x12 -> x0, local copies, waits for them, and re-layouts: 5.99 us -> none
    pallas_call x7 -> x8, Pallas kernels: 8.98 us -> 13.4 us  [call(): pl.pallas_call(lambda *refs: kernel(*refs[:count], *refs[count + len(afte...]
  transfers between devices with their start and end apart: 32 -> 21, of which waited for: 12 -> 6; matrix products, arithmetic and copies ran while one was open for 0% -> 0% of each run, Pallas kernels for 6% -> 17%
where the time goes in v2:
time: 49.2 us; the launch traced here: 49 us
  starting transfers between devices  26.5 us (54%)
  Pallas kernels  13.4 us (27%)
  waiting for transfers between devices  8.43 us (17%)
  between operations  0.71 us (1%)
    ppermute x21, starting transfers between devices, xor_permute(): return lax.ppermute(block, axis, [(i, i ^ mask) for i in range(count)])  26.5 us
    pallas_call x8, Pallas kernels, call(): pl.pallas_call(lambda *refs: kernel(*refs[:count], *refs[count + len(afte...  13.4 us
    ppermute x21, waiting for transfers between devices, xor_permute(): return lax.ppermute(block, axis, [(i, i ^ mask) for i in range(count)])  8.43 us
  transfers between devices with their start and end apart: 21, of which 6 were waited for; matrix products, arithmetic and copies ran while one was open for 0% of the time, Pallas kernels for 17%

profile of v2, /device:TPU:0, one launch (start us, length us, event | category | flops | bytes accessed | tf_op | source)
XLA Modules:
  0.0 49.0 jit_solution(10663963229451011848)
XLA Ops:
  0.6 0.5 %collective-permute-start.3 = (bf16[128,1024]{1,0:T(8,128)(2,1)}, bf16[128,1024]{1,0:T(8,128)(2,1)S(1)}, u32[]{:S(2)}, u32[]{:S(2)}) collective-permute-start(bf16[128,1024]{1,0:T(8,128)(2,1)} %refs_1_.3), channel_id=1, source_target_pairs={{0,1},{1,0},{2,3},{3,2},{4,5},{5,4},{6,7},{7,6},{8,9},{9,8},{10,11... | collective-permute-start | bytes 786440 | tf_op jit(solution)/shard_map/ppermute | solution.py:18
  1.1 1.1 %pack_keys_values.1 = (bf16[256,256]{1,0:T(8,128)(2,1)S(1)}, bf16[256,256]{1,0:T(8,128)(2,1)S(1)}, bf16[256,256]{1,0:T(8,128)(2,1)S(1)}, bf16[256,256]{1,0:T(8,128)(2,1)S(1)}) custom-call(bf16[128,1024]{1,0:T(8,128)(2,1)} %refs_0_.2, bf16[128,1024]{1,0:T(8,128)(2,1)} %refs_1_.2), custom_call_target="tpu_custom_call" | custom-call | flops 1000000000 | tf_op jit(solution)/shard_map/pack_keys_values/pallas_call | solution.py:56
  2.3 2.6 %collective-permute-start = (bf16[256,256]{1,0:T(8,128)(2,1)S(1)}, bf16[256,256]{1,0:T(8,128)(2,1)S(1)}, u32[]{:S(2)}, u32[]{:S(2)}) collective-permute-start(bf16[256,256]{1,0:T(8,128)(2,1)S(1)} %get-tuple-element.40), channel_id=1, source_target_pairs={{0,2},{2,0},{4,6},{6,4},{8,10},{10,8},{12,14},{14,12},{16,18},{18,... | collective-permute-start | bytes 393224 | tf_op jit(solution)/shard_map/ppermute | solution.py:18
  4.9 1.5 %collective-permute-start.1 = (bf16[256,256]{1,0:T(8,128)(2,1)S(1)}, bf16[256,256]{1,0:T(8,128)(2,1)S(1)}, u32[]{:S(2)}, u32[]{:S(2)}) collective-permute-start(bf16[256,256]{1,0:T(8,128)(2,1)S(1)} %get-tuple-element.41), channel_id=1, source_target_pairs={{0,4},{2,6},{4,0},{6,2},{8,12},{10,14},{12,8},{14,10},{16,20},{18,... | collective-permute-start | bytes 393224 | tf_op jit(solution)/shard_map/ppermute | solution.py:18
  6.4 0.0 collective-permute-start.2
  6.4 0.0 collective-permute-done.3.refs_2_
  6.4 4.3 %grad_attended.1 = (bf16[256,256]{1,0:T(8,128)(2,1)S(1)}, bf16[256,256]{1,0:T(8,128)(2,1)S(1)}, bf16[256,256]{1,0:T(8,128)(2,1)S(1)}, bf16[256,256]{1,0:T(8,128)(2,1)S(1)}, bf16[1024,2048]{1,0:T(8,128)(2,1)S(1)}) custom-call(bf16[128,1024]{1,0:T(8,128)(2,1)} %refs_0_.3, bf16[128,1024]{1,0:T(8,128)(2,1)} %refs_1_.3, ...), custom_call_target="tpu_custom_call" | custom-call | flops 3000000000 | tf_op jit(solution)/shard_map/grad_attended/pallas_call | solution.py:56
  10.8 2.0 %collective-permute-start.4 = (bf16[256,256]{1,0:T(8,128)(2,1)S(1)}, bf16[256,256]{1,0:T(8,128)(2,1)S(1)}, u32[]{:S(2)}, u32[]{:S(2)}) collective-permute-start(bf16[256,256]{1,0:T(8,128)(2,1)S(1)} %get-tuple-element.44), channel_id=1, source_target_pairs={{0,2},{2,0},{4,6},{6,4},{8,10},{10,8},{12,14},{14,12},{16,18},{18,... | collective-permute-start | bytes 393224 | tf_op jit(solution)/shard_map/ppermute | solution.py:18
  12.8 0.0 collective-permute-done.refs_1_
  12.8 0.5 %collective-permute-done.1.refs_2_ = bf16[256,256]{1,0:T(8,128)(2,1)S(1)} collective-permute-done((bf16[256,256]{1,0:T(8,128)(2,1)S(1)}, bf16[256,256]{1,0:T(8,128)(2,1)S(1)}, u32[]{:S(2)}, u32[]{:S(2)}) %collective-permute-start.1) | collective-permute-done | bytes 131104 | tf_op jit(solution)/shard_map/ppermute | solution.py:18
  13.3 0.0 collective-permute-done.2.refs_3_
  13.3 0.5 pool_plane.1
  13.7 3.7 %collective-permute-start.9 = (bf16[128,256]{1,0:T(8,128)(2,1)S(1)}, bf16[128,256]{1,0:T(8,128)(2,1)S(1)}, u32[]{:S(2)}, u32[]{:S(2)}) collective-permute-start(bf16[128,256]{1,0:T(8,128)(2,1)S(1)} %get-tuple-element.48), channel_id=1, source_target_pairs={{0,24},{2,26},{4,28},{6,30},{8,16},{10,18},{12,20},{14,22},{16,8},... | collective-permute-start | bytes 196616 | tf_op jit(solution)/shard_map/ppermute | solution.py:18
  17.4 1.5 %collective-permute-start.5 = (bf16[256,256]{1,0:T(8,128)(2,1)S(1)}, bf16[256,256]{1,0:T(8,128)(2,1)S(1)}, u32[]{:S(2)}, u32[]{:S(2)}) collective-permute-start(bf16[256,256]{1,0:T(8,128)(2,1)S(1)} %get-tuple-element.45), channel_id=1, source_target_pairs={{0,4},{2,6},{4,0},{6,2},{8,12},{10,14},{12,8},{14,10},{16,20},{18,... | collective-permute-start | bytes 393224 | tf_op jit(solution)/shard_map/ppermute | solution.py:18
  18.9 1.2 %collective-permute-start.6 = (bf16[256,256]{1,0:T(8,128)(2,1)S(1)}, bf16[256,256]{1,0:T(8,128)(2,1)S(1)}, u32[]{:S(2)}, u32[]{:S(2)}) collective-permute-start(bf16[256,256]{1,0:T(8,128)(2,1)S(1)} %get-tuple-element.46), channel_id=1, source_target_pairs={{0,6},{2,4},{4,2},{6,0},{8,14},{10,12},{12,10},{14,8},{16,22},{18,... | collective-permute-start | bytes 393224 | tf_op jit(solution)/shard_map/ppermute | solution.py:18
  20.1 0.0 collective-permute-start.7
  20.1 0.0 collective-permute-done.9.refs_10_
  20.1 1.3 %collective-permute-start.8 = (bf16[128,256]{1,0:T(8,128)(2,1)S(1)}, bf16[128,256]{1,0:T(8,128)(2,1)S(1)}, u32[]{:S(2)}, u32[]{:S(2)}) collective-permute-start(bf16[128,256]{1,0:T(8,128)(2,1)S(1)} %get-tuple-element.48), channel_id=1, source_target_pairs={{0,16},{2,18},{4,20},{6,22},{8,24},{10,26},{12,28},{14,30},{16,0},... | collective-permute-start | bytes 196616 | tf_op jit(solution)/shard_map/ppermute | solution.py:18
  21.4 4.1 %collective-permute-done.8.refs_9_ = bf16[128,256]{1,0:T(8,128)(2,1)S(1)} collective-permute-done((bf16[128,256]{1,0:T(8,128)(2,1)S(1)}, bf16[128,256]{1,0:T(8,128)(2,1)S(1)}, u32[]{:S(2)}, u32[]{:S(2)}) %collective-permute-start.8) | collective-permute-done | bytes 65568 | tf_op jit(solution)/shard_map/ppermute | solution.py:18
  25.4 0.0 collective-permute-done.4.refs_5_
  25.5 0.0 collective-permute-done.5.refs_6_
  25.5 0.0 collective-permute-done.6.refs_7_
  25.5 0.3 collective-permute-done.7.refs_8_
  25.8 3.8 %attention.1 = (bf16[128,256]{1,0:T(8,128)(2,1)S(1)}, bf16[128,256]{1,0:T(8,128)(2,1)S(1)}, bf16[128,256]{1,0:T(8,128)(2,1)S(1)}, bf16[128,256]{1,0:T(8,128)(2,1...) custom-call(bf16[256,256]{1,0:T(8,128)(2,1)S(1)} %get-tuple-element., ...), custom_call_target="tpu_custom_call" | custom-call | flops 3700000000 | tf_op jit(solution)/shard_map/attention/pallas_call | solution.py:56
  29.5 1.3 %collective-permute-start.14 = (bf16[128,256]{1,0:T(8,128)(2,1)S(1)}, bf16[128,256]{1,0:T(8,128)(2,1)S(1)}, u32[]{:S(2)}, u32[]{:S(2)}) collective-permute-start(bf16[128,256]{1,0:T(8,128)(2,1)S(1)} %get-tuple-element.65), channel_id=1, source_target_pairs={{0,16},{2,18},{4,20},{6,22},{8,24},{10,26},{12,28},{14,30},{16,0},... | collective-permute-start | bytes 196616 | tf_op jit(solution)/shard_map/ppermute | solution.py:18
  30.8 2.7 %collective-permute-start.15 = (bf16[128,256]{1,0:T(8,128)(2,1)S(1)}, bf16[128,256]{1,0:T(8,128)(2,1)S(1)}, u32[]{:S(2)}, u32[]{:S(2)}) collective-permute-start(bf16[128,256]{1,0:T(8,128)(2,1)S(1)} %get-tuple-element.66), channel_id=1, source_target_pairs={{0,24},{2,26},{4,28},{6,30},{8,16},{10,18},{12,20},{14,22},{16,8},... | collective-permute-start | bytes 196616 | tf_op jit(solution)/shard_map/ppermute | solution.py:18
  33.5 0.0 collective-permute-start.13
  33.5 1.5 %plane_grads.1 = (bf16[256,256]{1,0:T(8,128)(2,1)S(1)}, bf16[256,256]{1,0:T(8,128)(2,1)S(1)}, bf16[256,256]{1,0:T(8,128)(2,1)S(1)}, bf16[256,256]{1,0:T(8,128)(2...) custom-call(bf16[256,256]{1,0:T(8,128)(2,1)S(1)} %get-tuple-element., ...), custom_call_target="tpu_custom_call" | custom-call | flops 2300000000 | tf_op jit(solution)/shard_map/plane_grads/pallas_call | solution.py:56
  35.0 1.5 %collective-permute-start.10 = (bf16[256,256]{1,0:T(8,128)(2,1)S(1)}, bf16[256,256]{1,0:T(8,128)(2,1)S(1)}, u32[]{:S(2)}, u32[]{:S(2)}) collective-permute-start(bf16[256,256]{1,0:T(8,128)(2,1)S(1)} %get-tuple-element.56), channel_id=1, source_target_pairs={{0,2},{2,0},{4,6},{6,4},{8,10},{10,8},{12,14},{14,12},{16,18},{18,... | collective-permute-start | bytes 393224 | tf_op jit(solution)/shard_map/ppermute | solution.py:18
  36.5 0.8 %collective-permute-start.11 = (bf16[256,256]{1,0:T(8,128)(2,1)S(1)}, bf16[256,256]{1,0:T(8,128)(2,1)S(1)}, u32[]{:S(2)}, u32[]{:S(2)}) collective-permute-start(bf16[256,256]{1,0:T(8,128)(2,1)S(1)} %get-tuple-element.57), channel_id=1, source_target_pairs={{0,4},{2,6},{4,0},{6,2},{8,12},{10,14},{12,8},{14,10},{16,20},{18,... | collective-permute-start | bytes 393224 | tf_op jit(solution)/shard_map/ppermute | solution.py:18
  37.4 0.0 collective-permute-done.14.refs_5_
  37.4 1.2 %collective-permute-start.12 = (bf16[256,256]{1,0:T(8,128)(2,1)S(1)}, bf16[256,256]{1,0:T(8,128)(2,1)S(1)}, u32[]{:S(2)}, u32[]{:S(2)}) collective-permute-start(bf16[256,256]{1,0:T(8,128)(2,1)S(1)} %get-tuple-element.58), channel_id=1, source_target_pairs={{0,6},{2,4},{4,2},{6,0},{8,14},{10,12},{12,10},{14,8},{16,22},{18,... | collective-permute-start | bytes 393224 | tf_op jit(solution)/shard_map/ppermute | solution.py:18
  38.6 0.0 collective-permute-done.15.refs_6_
  38.6 0.0 collective-permute-done.13.refs_4_
  38.6 0.4 carry.1
  39.0 1.6 %collective-permute-start.18 = (bf16[256,256]{1,0:T(8,128)(2,1)S(1)}, bf16[256,256]{1,0:T(8,128)(2,1)S(1)}, u32[]{:S(2)}, u32[]{:S(2)}) collective-permute-start(bf16[256,256]{1,0:T(8,128)(2,1)S(1)} %get-tuple-element.71), channel_id=1, source_target_pairs={{0,2},{2,0},{4,6},{6,4},{8,10},{10,8},{12,14},{14,12},{16,18},{18,... | collective-permute-start | bytes 393224 | tf_op jit(solution)/shard_map/ppermute | solution.py:18
  40.5 0.8 %collective-permute-start.19 = (bf16[256,256]{1,0:T(8,128)(2,1)S(1)}, bf16[256,256]{1,0:T(8,128)(2,1)S(1)}, u32[]{:S(2)}, u32[]{:S(2)}) collective-permute-start(bf16[256,256]{1,0:T(8,128)(2,1)S(1)} %get-tuple-element.72), channel_id=1, source_target_pairs={{0,4},{2,6},{4,0},{6,2},{8,12},{10,14},{12,8},{14,10},{16,20},{18,... | collective-permute-start | bytes 393224 | tf_op jit(solution)/shard_map/ppermute | solution.py:18
  41.3 0.1 collective-permute-done.10.refs_1_.refs_4_
  41.4 1.8 %collective-permute-start.20 = (bf16[256,256]{1,0:T(8,128)(2,1)S(1)}, bf16[256,256]{1,0:T(8,128)(2,1)S(1)}, u32[]{:S(2)}, u32[]{:S(2)}) collective-permute-start(bf16[256,256]{1,0:T(8,128)(2,1)S(1)} %get-tuple-element.73), channel_id=1, source_target_pairs={{0,6},{2,4},{4,2},{6,0},{8,14},{10,12},{12,10},{14,8},{16,22},{18,... | collective-permute-start | bytes 393224 | tf_op jit(solution)/shard_map/ppermute | solution.py:18
  43.2 1.9 %collective-permute-done.11.refs_2_.refs_5_ = bf16[256,256]{1,0:T(8,128)(2,1)S(1)} collective-permute-done((bf16[256,256]{1,0:T(8,128)(2,1)S(1)}, bf16[256,256]{1,0:T(8,128)(2,1)S(1)}, u32[]{:S(2)}, u32[]{:S(2)}) %collective-permute-start.11) | collective-permute-done | bytes 131104 | tf_op jit(solution)/shard_map/ppermute | solution.py:18
  45.1 0.0 collective-permute-done.12.refs_3_.refs_6_
  45.1 0.7 %project.1 = (f32[128,1024]{1,0:T(8,128)S(1)}, bf16[64,1024]{1,0:T(8,128)(2,1)S(1)}, bf16[64,1024]{1,0:T(8,128)(2,1)S(1)}) custom-call(bf16[256,256]{1,0:T(8,128)(2,1)S(1)} %get-tuple-element.55.refs_0_.refs_3_, bf16[256,256]{1,0:T(8,128)(2,1)S(1)} %collective-permute-done.10.refs_1_.refs_4_, bf16[256,256]{1,0:T(8,128)(2,1)S(1)} %collective-permute-done.11.refs_2_.refs_5_, ...), custom_call_target="tpu_custom_call" | custom-call | flops 10000000 | tf_op jit(solution)/shard_map/project/pallas_call | solution.py:56
  45.9 0.1 collective-permute-start.16
  45.9 0.5 %collective-permute-start.17 = (bf16[64,1024]{1,0:T(8,128)(2,1)S(1)}, bf16[64,1024]{1,0:T(8,128)(2,1)S(1)}, u32[]{:S(2)}, u32[]{:S(2)}) collective-permute-start(bf16[64,1024]{1,0:T(8,128)(2,1)S(1)} %get-tuple-element.70), channel_id=1, source_target_pairs={{0,1},{1,0},{2,3},{3,2},{4,5},{5,4},{6,7},{7,6},{8,9},{9,8},{10,11... | collective-permute-start | bytes 393224 | tf_op jit(solution)/shard_map/ppermute | solution.py:18
  46.4 0.0 collective-permute-done.18.refs_8_
  46.4 1.5 %collective-permute-done.19.refs_9_ = bf16[256,256]{1,0:T(8,128)(2,1)S(1)} collective-permute-done((bf16[256,256]{1,0:T(8,128)(2,1)S(1)}, bf16[256,256]{1,0:T(8,128)(2,1)S(1)}, u32[]{:S(2)}, u32[]{:S(2)}) %collective-permute-start.19) | collective-permute-done | bytes 131104 | tf_op jit(solution)/shard_map/ppermute | solution.py:18
  47.9 0.0 collective-permute-done.20.refs_10_
  47.9 0.0 collective-permute-done.16.refs_1_
  47.9 0.0 collective-permute-done.17.refs_2_
  47.9 1.1 %join.1 = (bf16[128,1024]{1,0:T(8,128)(2,1)}, bf16[128,1024]{1,0:T(8,128)(2,1)}, bf16[128,1024]{1,0:T(8,128)(2,1)}, bf16[128,1024]{1,0:T(8,128)(2,1)}) custom-call(f32[128,1024]{1,0:T(8,128)S(1)} %get-tuple-element.68.refs_0_, bf16[64,1024]{1,0:T(8,128)(2,1)S(1)} %collective-permute-done.16.refs_1_, bf16[64,1024]{1,0:T(8,128)(2,1)S(1)} %collective-permute-done.17.refs_2_, ...), custom_call_target="tpu_custom_call" | custom-call | flops 1000000000 | tf_op jit(solution)/shard_map/join/pallas_call | solution.py:56
Async XLA Ops:
  0.6 5.8 %collective-permute-start.3 = (bf16[128,1024]{1,0:T(8,128)(2,1)}, bf16[128,1024]{1,0:T(8,128)(2,1)S(1)}, u32[]{:S(2)}, u32[]{:S(2)}) collective-permute-start(bf16[128,1024]{1,0:T(8,128)(2,1)} %refs_1_.3), channel_id=1, source_target_pairs={{0,1},{1,0},{2,3},{3,2},{4,5},{5,4},{6,7},{7,6},{8,9},{9,8},{10,11... | collective-permute-start | bytes 786440 | tf_op jit(solution)/shard_map/ppermute | solution.py:18
  2.3 10.5 %collective-permute-start = (bf16[256,256]{1,0:T(8,128)(2,1)S(1)}, bf16[256,256]{1,0:T(8,128)(2,1)S(1)}, u32[]{:S(2)}, u32[]{:S(2)}) collective-permute-start(bf16[256,256]{1,0:T(8,128)(2,1)S(1)} %get-tuple-element.40), channel_id=1, source_target_pairs={{0,2},{2,0},{4,6},{6,4},{8,10},{10,8},{12,14},{14,12},{16,18},{18,... | collective-permute-start | bytes 393224 | tf_op jit(solution)/shard_map/ppermute | solution.py:18
  4.9 8.4 %collective-permute-start.1 = (bf16[256,256]{1,0:T(8,128)(2,1)S(1)}, bf16[256,256]{1,0:T(8,128)(2,1)S(1)}, u32[]{:S(2)}, u32[]{:S(2)}) collective-permute-start(bf16[256,256]{1,0:T(8,128)(2,1)S(1)} %get-tuple-element.41), channel_id=1, source_target_pairs={{0,4},{2,6},{4,0},{6,2},{8,12},{10,14},{12,8},{14,10},{16,20},{18,... | collective-permute-start | bytes 393224 | tf_op jit(solution)/shard_map/ppermute | solution.py:18
  6.4 6.9 %collective-permute-start.2 = (bf16[256,256]{1,0:T(8,128)(2,1)S(1)}, bf16[256,256]{1,0:T(8,128)(2,1)S(1)}, u32[]{:S(2)}, u32[]{:S(2)}) collective-permute-start(bf16[256,256]{1,0:T(8,128)(2,1)S(1)} %get-tuple-element.42), channel_id=1, source_target_pairs={{0,6},{2,4},{4,2},{6,0},{8,14},{10,12},{12,10},{14,8},{16,22},{18,... | collective-permute-start | bytes 393224 | tf_op jit(solution)/shard_map/ppermute | solution.py:18
  10.8 14.7 %collective-permute-start.4 = (bf16[256,256]{1,0:T(8,128)(2,1)S(1)}, bf16[256,256]{1,0:T(8,128)(2,1)S(1)}, u32[]{:S(2)}, u32[]{:S(2)}) collective-permute-start(bf16[256,256]{1,0:T(8,128)(2,1)S(1)} %get-tuple-element.44), channel_id=1, source_target_pairs={{0,2},{2,0},{4,6},{6,4},{8,10},{10,8},{12,14},{14,12},{16,18},{18,... | collective-permute-start | bytes 393224 | tf_op jit(solution)/shard_map/ppermute | solution.py:18
  13.7 6.4 %collective-permute-start.9 = (bf16[128,256]{1,0:T(8,128)(2,1)S(1)}, bf16[128,256]{1,0:T(8,128)(2,1)S(1)}, u32[]{:S(2)}, u32[]{:S(2)}) collective-permute-start(bf16[128,256]{1,0:T(8,128)(2,1)S(1)} %get-tuple-element.48), channel_id=1, source_target_pairs={{0,24},{2,26},{4,28},{6,30},{8,16},{10,18},{12,20},{14,22},{16,8},... | collective-permute-start | bytes 196616 | tf_op jit(solution)/shard_map/ppermute | solution.py:18
  17.4 8.1 %collective-permute-start.5 = (bf16[256,256]{1,0:T(8,128)(2,1)S(1)}, bf16[256,256]{1,0:T(8,128)(2,1)S(1)}, u32[]{:S(2)}, u32[]{:S(2)}) collective-permute-start(bf16[256,256]{1,0:T(8,128)(2,1)S(1)} %get-tuple-element.45), channel_id=1, source_target_pairs={{0,4},{2,6},{4,0},{6,2},{8,12},{10,14},{12,8},{14,10},{16,20},{18,... | collective-permute-start | bytes 393224 | tf_op jit(solution)/shard_map/ppermute | solution.py:18
  18.9 6.5 %collective-permute-start.6 = (bf16[256,256]{1,0:T(8,128)(2,1)S(1)}, bf16[256,256]{1,0:T(8,128)(2,1)S(1)}, u32[]{:S(2)}, u32[]{:S(2)}) collective-permute-start(bf16[256,256]{1,0:T(8,128)(2,1)S(1)} %get-tuple-element.46), channel_id=1, source_target_pairs={{0,6},{2,4},{4,2},{6,0},{8,14},{10,12},{12,10},{14,8},{16,22},{18,... | collective-permute-start | bytes 393224 | tf_op jit(solution)/shard_map/ppermute | solution.py:18
  20.1 5.7 %collective-permute-start.7 = (bf16[256,256]{1,0:T(8,128)(2,1)S(1)}, bf16[256,256]{1,0:T(8,128)(2,1)S(1)}, u32[]{:S(2)}, u32[]{:S(2)}) collective-permute-start(bf16[256,256]{1,0:T(8,128)(2,1)S(1)} %get-tuple-element.47), channel_id=1, source_target_pairs={{0,8},{2,10},{4,12},{6,14},{8,0},{10,2},{12,4},{14,6},{16,24},{18,... | collective-permute-start | bytes 393224 | tf_op jit(solution)/shard_map/ppermute | solution.py:18
  20.1 5.3 %collective-permute-start.8 = (bf16[128,256]{1,0:T(8,128)(2,1)S(1)}, bf16[128,256]{1,0:T(8,128)(2,1)S(1)}, u32[]{:S(2)}, u32[]{:S(2)}) collective-permute-start(bf16[128,256]{1,0:T(8,128)(2,1)S(1)} %get-tuple-element.48), channel_id=1, source_target_pairs={{0,16},{2,18},{4,20},{6,22},{8,24},{10,26},{12,28},{14,30},{16,0},... | collective-permute-start | bytes 196616 | tf_op jit(solution)/shard_map/ppermute | solution.py:18
  29.5 7.8 %collective-permute-start.14 = (bf16[128,256]{1,0:T(8,128)(2,1)S(1)}, bf16[128,256]{1,0:T(8,128)(2,1)S(1)}, u32[]{:S(2)}, u32[]{:S(2)}) collective-permute-start(bf16[128,256]{1,0:T(8,128)(2,1)S(1)} %get-tuple-element.65), channel_id=1, source_target_pairs={{0,16},{2,18},{4,20},{6,22},{8,24},{10,26},{12,28},{14,30},{16,0},... | collective-permute-start | bytes 196616 | tf_op jit(solution)/shard_map/ppermute | solution.py:18
  30.8 7.8 %collective-permute-start.15 = (bf16[128,256]{1,0:T(8,128)(2,1)S(1)}, bf16[128,256]{1,0:T(8,128)(2,1)S(1)}, u32[]{:S(2)}, u32[]{:S(2)}) collective-permute-start(bf16[128,256]{1,0:T(8,128)(2,1)S(1)} %get-tuple-element.66), channel_id=1, source_target_pairs={{0,24},{2,26},{4,28},{6,30},{8,16},{10,18},{12,20},{14,22},{16,8},... | collective-permute-start | bytes 196616 | tf_op jit(solution)/shard_map/ppermute | solution.py:18
  33.5 5.0 %collective-permute-start.13 = (bf16[256,256]{1,0:T(8,128)(2,1)S(1)}, bf16[256,256]{1,0:T(8,128)(2,1)S(1)}, u32[]{:S(2)}, u32[]{:S(2)}) collective-permute-start(bf16[256,256]{1,0:T(8,128)(2,1)S(1)} %get-tuple-element.64), channel_id=1, source_target_pairs={{0,8},{2,10},{4,12},{6,14},{8,0},{10,2},{12,4},{14,6},{16,24},{18,... | collective-permute-start | bytes 393224 | tf_op jit(solution)/shard_map/ppermute | solution.py:18
  35.0 6.4 %collective-permute-start.10 = (bf16[256,256]{1,0:T(8,128)(2,1)S(1)}, bf16[256,256]{1,0:T(8,128)(2,1)S(1)}, u32[]{:S(2)}, u32[]{:S(2)}) collective-permute-start(bf16[256,256]{1,0:T(8,128)(2,1)S(1)} %get-tuple-element.56), channel_id=1, source_target_pairs={{0,2},{2,0},{4,6},{6,4},{8,10},{10,8},{12,14},{14,12},{16,18},{18,... | collective-permute-start | bytes 393224 | tf_op jit(solution)/shard_map/ppermute | solution.py:18
  36.5 8.6 %collective-permute-start.11 = (bf16[256,256]{1,0:T(8,128)(2,1)S(1)}, bf16[256,256]{1,0:T(8,128)(2,1)S(1)}, u32[]{:S(2)}, u32[]{:S(2)}) collective-permute-start(bf16[256,256]{1,0:T(8,128)(2,1)S(1)} %get-tuple-element.57), channel_id=1, source_target_pairs={{0,4},{2,6},{4,0},{6,2},{8,12},{10,14},{12,8},{14,10},{16,20},{18,... | collective-permute-start | bytes 393224 | tf_op jit(solution)/shard_map/ppermute | solution.py:18
  37.4 7.7 %collective-permute-start.12 = (bf16[256,256]{1,0:T(8,128)(2,1)S(1)}, bf16[256,256]{1,0:T(8,128)(2,1)S(1)}, u32[]{:S(2)}, u32[]{:S(2)}) collective-permute-start(bf16[256,256]{1,0:T(8,128)(2,1)S(1)} %get-tuple-element.58), channel_id=1, source_target_pairs={{0,6},{2,4},{4,2},{6,0},{8,14},{10,12},{12,10},{14,8},{16,22},{18,... | collective-permute-start | bytes 393224 | tf_op jit(solution)/shard_map/ppermute | solution.py:18
  39.0 7.5 %collective-permute-start.18 = (bf16[256,256]{1,0:T(8,128)(2,1)S(1)}, bf16[256,256]{1,0:T(8,128)(2,1)S(1)}, u32[]{:S(2)}, u32[]{:S(2)}) collective-permute-start(bf16[256,256]{1,0:T(8,128)(2,1)S(1)} %get-tuple-element.71), channel_id=1, source_target_pairs={{0,2},{2,0},{4,6},{6,4},{8,10},{10,8},{12,14},{14,12},{16,18},{18,... | collective-permute-start | bytes 393224 | tf_op jit(solution)/shard_map/ppermute | solution.py:18
  40.5 7.4 %collective-permute-start.19 = (bf16[256,256]{1,0:T(8,128)(2,1)S(1)}, bf16[256,256]{1,0:T(8,128)(2,1)S(1)}, u32[]{:S(2)}, u32[]{:S(2)}) collective-permute-start(bf16[256,256]{1,0:T(8,128)(2,1)S(1)} %get-tuple-element.72), channel_id=1, source_target_pairs={{0,4},{2,6},{4,0},{6,2},{8,12},{10,14},{12,8},{14,10},{16,20},{18,... | collective-permute-start | bytes 393224 | tf_op jit(solution)/shard_map/ppermute | solution.py:18
  41.4 6.5 %collective-permute-start.20 = (bf16[256,256]{1,0:T(8,128)(2,1)S(1)}, bf16[256,256]{1,0:T(8,128)(2,1)S(1)}, u32[]{:S(2)}, u32[]{:S(2)}) collective-permute-start(bf16[256,256]{1,0:T(8,128)(2,1)S(1)} %get-tuple-element.73), channel_id=1, source_target_pairs={{0,6},{2,4},{4,2},{6,0},{8,14},{10,12},{12,10},{14,8},{16,22},{18,... | collective-permute-start | bytes 393224 | tf_op jit(solution)/shard_map/ppermute | solution.py:18
  45.9 2.1 %collective-permute-start.16 = (bf16[64,1024]{1,0:T(8,128)(2,1)S(1)}, bf16[64,1024]{1,0:T(8,128)(2,1)S(1)}, u32[]{:S(2)}, u32[]{:S(2)}) collective-permute-start(bf16[64,1024]{1,0:T(8,128)(2,1)S(1)} %get-tuple-element.69), channel_id=1, source_target_pairs={{0,1},{1,0},{2,3},{3,2},{4,5},{5,4},{6,7},{7,6},{8,9},{9,8},{10,11... | collective-permute-start | bytes 393224 | tf_op jit(solution)/shard_map/ppermute | solution.py:18
  45.9 2.0 %collective-permute-start.17 = (bf16[64,1024]{1,0:T(8,128)(2,1)S(1)}, bf16[64,1024]{1,0:T(8,128)(2,1)S(1)}, u32[]{:S(2)}, u32[]{:S(2)}) collective-permute-start(bf16[64,1024]{1,0:T(8,128)(2,1)S(1)} %get-tuple-element.70), channel_id=1, source_target_pairs={{0,1},{1,0},{2,3},{3,2},{4,5},{5,4},{6,7},{7,6},{8,9},{9,8},{10,11... | collective-permute-start | bytes 393224 | tf_op jit(solution)/shard_map/ppermute | solution.py:18

commit v3 on v2

--- a/solution.py
+++ b/solution.py
@@ -9,6 +9,7 @@
 PLANE = 4
 PIECES = 2
 SCALE = DH ** (-0.5)
+SCALE2 = SCALE * 1.4426950408889634
 BF16 = jnp.bfloat16
 F32 = jnp.float32
 
@@ -96,30 +97,21 @@
 
 
 def cotangent_kernel(q_ref, own_ref, other_ref, w_ref, *refs):
-    outs, w, own, sems, w_sems = refs[:PLANE], refs[PLANE], *refs[PLANE + 1 :]
+    outs, own, sems = refs[:PLANE], *refs[PLANE:]
     rows, width = q_ref.shape[0], q_ref.shape[1] // PLANE
     half = own_ref.shape[1]
     head = lax.axis_index("head")
     own_at = pl.ds(pl.multiple_of(head * half, half), half)
     other_at = pl.ds(pl.multiple_of((1 - head) * half, half), half)
     here = [columns(r, width) for r in range(PLANE)]
-    w_copies = [
-        pltpu.make_async_copy(w_ref.at[here[r], :], w.at[here[r], :], w_sems.at[r])
-        for r in range(PLANE)
-    ]
     pairs = [(own_ref, own)]
     pairs += [(q_ref.at[:, here[r]], outs[r].at[part(0, rows), :]) for r in range(PLANE)]
     copies = start_all(pairs, sems)
-    w_copies[0].start()
-    w_copies[1].start()
     copies[0].wait()
     for r in range(PLANE):
-        w_copies[r].wait()
-        if r + 2 < PLANE:
-            w_copies[r + 2].start()
         outs[r][rows:, :] = (
-            dot(own[...], w[here[r], own_at], 1, 1)
-            + dot(other_ref[...], w[here[r], other_at], 1, 1)
+            dot(own[...], w_ref[here[r], own_at], 1, 1)
+            + dot(other_ref[...], w_ref[here[r], other_at], 1, 1)
         ).astype(BF16)
     for copy in copies[1:]:
         copy.wait()
@@ -137,52 +129,75 @@
             out[part(n, size), :] = pooled[:, part(n, width)]
 
 
-def key_sets(kvs, fars, p, lanes, m):
-    rows = kvs[0].shape[0] // 2
-    ours, theirs = kvs[2 * p : 2 * p + 2], kvs[2 - 2 * p : 4 - 2 * p]
-    return jnp.concatenate(
-        [kv[part(m, rows), lanes] for kv in ours]
-        + [pool(kv[part(m, rows), lanes]) for kv in theirs]
-        + [far[part(m, far.shape[0] // 2), lanes] for far in fars],
-        0,
-    )
-
-
-def attention_kernel(n_far, *refs):
-    kvs, qgs, fars = refs[:PLANE], refs[PLANE : 2 * PLANE], refs[2 * PLANE : 2 * PLANE + n_far]
-    outs = refs[2 * PLANE + n_far :]
-    atts, grad_out, prob_out = outs[:PLANE], outs[PLANE], outs[PLANE + 1]
-    far_out = outs[PLANE + 2 :]
+def both(blocks, p, rows, lanes):
+    return jnp.concatenate([blocks[r][rows, lanes] for r in (2 * p, 2 * p + 1)], 0)
+
+
+def near_set(kvs, p, lanes, m):
+    rows = part(m, kvs[0].shape[0] // 2)
+    other = [pool(kv[rows, lanes]) for kv in kvs[2 - 2 * p : 4 - 2 * p]]
+    return jnp.concatenate([both(kvs, p, rows, lanes)] + other, 0)
+
+
+def far_set(fars, lanes, m):
+    return jnp.concatenate([far[part(m, far.shape[0] // 2), lanes] for far in fars], 0)
+
+
+def near_kernel(*refs):
+    kvs, qgs = refs[:PLANE], refs[PLANE : 2 * PLANE]
+    weight_out, dots_out, sums_out, stats_out = refs[2 * PLANE :]
     rows, width = qgs[0].shape[0] // 2, qgs[0].shape[1]
-    start = 3 * rows
     for h in range(width // DH):
         lanes = part(h, DH)
-        key_grads, value_grads = [], []
         for p in range(2):
-            ours = (2 * p, 2 * p + 1)
-            q = jnp.concatenate([qgs[r][:rows, lanes] for r in ours], 0)
-            g = jnp.concatenate([qgs[r][rows:, lanes] for r in ours], 0)
-            keys = key_sets(kvs, fars, p, lanes, 0)
-            values = key_sets(kvs, fars, p, lanes, 1)
-            scores = dot(keys, q, 1, 1) * SCALE
-            weights = jnp.exp(scores - jnp.max(scores, 0, keepdims=True))
-            inverse = 1.0 / jnp.sum(weights, 0, keepdims=True)
-            numerator = dot(values, weights.astype(BF16), 0, 0)
+            n = 2 * h + p
+            q, g = both(qgs, p, part(0, rows), lanes), both(qgs, p, part(1, rows), lanes)
+            values = near_set(kvs, p, lanes, 1)
+            scores = dot(near_set(kvs, p, lanes, 0), q, 1, 1) * SCALE2
+            row_max = jnp.max(scores, 0, keepdims=True)
+            weights = jnp.exp2(scores - row_max)
+            weight_out[n] = weights
+            dots_out[n] = dot(values, g, 1, 1)
+            sums_out[n] = dot(values, weights.astype(BF16), 0, 0)
+            stats_out[n, 0:1, :] = row_max
+            stats_out[n, 1:2, :] = jnp.sum(weights, 0, keepdims=True)
+
+
+def far_grad_kernel(n_far, *refs):
+    qgs, fars = refs[:PLANE], refs[PLANE : PLANE + n_far]
+    sums_ref, stats_ref = refs[PLANE + n_far : PLANE + n_far + 2]
+    outs = refs[PLANE + n_far + 2 :]
+    atts, grad_out, stats_out, far_out = outs[:PLANE], outs[PLANE], outs[PLANE + 1], outs[PLANE + 2 :]
+    rows, width = qgs[0].shape[0] // 2, qgs[0].shape[1]
+    for h in range(width // DH):
+        lanes = part(h, DH)
+        keys, values = far_set(fars, lanes, 0), far_set(fars, lanes, 1)
+        grads = []
+        for p in range(2):
+            n = 2 * h + p
+            q, g = both(qgs, p, part(0, rows), lanes), both(qgs, p, part(1, rows), lanes)
+            scores = dot(keys, q, 1, 1) * SCALE2
+            near_max = stats_ref[n, 0:1, :]
+            row_max = jnp.maximum(near_max, jnp.max(scores, 0, keepdims=True))
+            weights = jnp.exp2(scores - row_max)
+            near_part = jnp.exp2(near_max - row_max)
+            inverse = 1.0 / (
+                stats_ref[n, 1:2, :] * near_part + jnp.sum(weights, 0, keepdims=True)
+            )
+            numerator = sums_ref[n] * near_part + dot(values, weights.astype(BF16), 0, 0)
             attended = (numerator * inverse).astype(BF16)
             delta = jnp.sum(g.T.astype(F32) * attended.astype(F32), 0, keepdims=True)
             probabilities = weights * inverse
-            value_dots = dot(values, g, 1, 1)
-            score_grad = (probabilities * (value_dots - delta)).astype(BF16)
-            rounded = probabilities.astype(BF16)
+            score_grad = (probabilities * (dot(values, g, 1, 1) - delta)).astype(BF16)
             attended = attended.T
-            for n, r in enumerate(ours):
-                atts[r][:, lanes] = attended[part(n, rows)]
-            grad_out[2 * h + p] = score_grad
-            prob_out[2 * h + p] = rounded
-            key_grads.append(dot(score_grad[start:], q) * SCALE)
-            value_grads.append(dot(rounded[start:], g))
-        for m, grads in enumerate((key_grads, value_grads)):
-            whole, at = grads[0] + grads[1], 0
+            for k in range(2):
+                atts[2 * p + k][:, lanes] = attended[part(k, rows)]
+            grad_out[n] = score_grad
+            stats_out[n, 0:1, :] = near_part * inverse
+            stats_out[n, 1:2, :] = delta
+            grads.append((dot(score_grad, q) * SCALE, dot(probabilities.astype(BF16), g)))
+        for m in range(2):
+            whole, at = grads[0][m] + grads[1][m], 0
             for far in far_out:
                 size = far.shape[0] // 2
                 far[part(m, size), lanes] = whole[at : at + size].astype(BF16)
@@ -191,33 +206,34 @@
 
 def plane_kernel(n_far, *refs):
     kvs, qgs, fars = refs[:PLANE], refs[PLANE : 2 * PLANE], refs[2 * PLANE : 2 * PLANE + n_far]
-    refs = refs[2 * PLANE + n_far :]
-    atts, grad_ref, prob_ref = refs[:PLANE], refs[PLANE], refs[PLANE + 1]
+    weight_ref, dots_ref = refs[2 * PLANE + n_far : 2 * PLANE + n_far + 2]
+    refs = refs[2 * PLANE + n_far + 2 :]
+    atts, grad_ref, stats_ref = refs[:PLANE], refs[PLANE], refs[PLANE + 1]
     ads, dkvs = refs[PLANE + 2 : 2 * PLANE + 2], refs[2 * PLANE + 2 :]
     rows, width = qgs[0].shape[0] // 2, qgs[0].shape[1]
     pair = 2 * rows
-    near = pair + rows
     for r in range(PLANE):
         ads[r][:rows, :] = atts[r][...]
     for h in range(width // DH):
         lanes = part(h, DH)
-        key_grads, value_grads = [], []
+        far_keys = far_set(fars, lanes, 0)
+        grads = []
         for p in range(2):
-            ours = (2 * p, 2 * p + 1)
-            q = jnp.concatenate([qgs[r][:rows, lanes] for r in ours], 0)
-            g = jnp.concatenate([qgs[r][rows:, lanes] for r in ours], 0)
-            keys = key_sets(kvs, fars, p, lanes, 0)
-            dq = (dot(keys, grad_ref[2 * h + p], 0, 0) * SCALE).astype(BF16).T
-            for n, r in enumerate(ours):
-                ads[r][rows:, lanes] = dq[part(n, rows)]
-            key_grads.append(dot(grad_ref[2 * h + p, :near, :], q) * SCALE)
-            value_grads.append(dot(prob_ref[2 * h + p, :near, :], g))
-        for m, grads in enumerate((key_grads, value_grads)):
+            n = 2 * h + p
+            q, g = both(qgs, p, part(0, rows), lanes), both(qgs, p, part(1, rows), lanes)
+            probabilities = weight_ref[n] * stats_ref[n, 0:1, :]
+            score_grad = (probabilities * (dots_ref[n] - stats_ref[n, 1:2, :])).astype(BF16)
+            dq = dot(near_set(kvs, p, lanes, 0), score_grad, 0, 0)
+            dq = ((dq + dot(far_keys, grad_ref[n], 0, 0)) * SCALE).astype(BF16).T
+            for k in range(2):
+                ads[2 * p + k][rows:, lanes] = dq[part(k, rows)]
+            grads.append((dot(score_grad, q) * SCALE, dot(probabilities.astype(BF16), g)))
+        for m in range(2):
             for p in range(2):
-                pooled = grads[1 - p][pair:]
-                for n in range(2):
-                    dkvs[2 * p + n][part(m, rows), lanes] = grads[p][part(n, rows)] + spread(
-                        pooled[part(n, rows // 2)], 2
+                pooled = grads[1 - p][m][pair:]
+                for k in range(2):
+                    dkvs[2 * p + k][part(m, rows), lanes] = grads[p][m][part(k, rows)] + spread(
+                        pooled[part(k, rows // 2)], 2
                     )
 
 
@@ -324,13 +340,12 @@
     other_cotangent = xor_permute(cotangent, 1, "head")
     key_values = call(
         key_value_kernel, blocks, key_rows, value_rows,
-        hbm=(0, 1), scratch=[dma(2 * PLANE)], name="pack_keys_values",
+        hbm=(0, 1), scratch=[dma(2 * PLANE)], cost_us=8, name="pack_keys_values",
     )
     key_values = plane_exchange(key_values)
-    *query_grads, weight = call(
-        cotangent_kernel, blocks + [shape(*out_weight.shape)],
-        queries, cotangent, other_cotangent, out_weight,
-        hbm=(0, 1, 3), scratch=[pltpu.VMEM(cotangent.shape, BF16), dma(1 + PLANE), dma(PLANE)],
+    query_grads = call(
+        cotangent_kernel, blocks, queries, cotangent, other_cotangent, out_weight,
+        hbm=(0, 1), scratch=[pltpu.VMEM(cotangent.shape, BF16), dma(1 + PLANE)],
         cost_us=3.0, name="grad_attended",
     )
     query_grads = plane_exchange(query_grads)
@@ -345,18 +360,25 @@
             fars.append(xor_permute(span, 4 * PLANE << n))
             span = pool_both(join_both([span, fars[-1]]))
     far_rows = sum(far.shape[0] for far in fars) // 2
-    kept = shape(2 * width // DH, 3 * rows + far_rows, 2 * rows)
+    cases = 2 * width // DH
+    weights, dots, sums, stats = call(
+        near_kernel,
+        [shape(cases, 3 * rows, 2 * rows, t=F32)] * 2
+        + [shape(cases, DH, 2 * rows, t=F32), shape(cases, 2, 2 * rows, t=F32)],
+        *key_values, *query_grads, cost_us=2.0, name="near_attention",
+    )
     results = call(
-        lambda *refs: attention_kernel(len(fars), *refs),
-        [shape(rows, width)] * PLANE + [kept, kept] + [shape(*far.shape) for far in fars],
-        *key_values, *query_grads, *fars,
-        cost_us=3.7, name="attention",
+        lambda *refs: far_grad_kernel(len(fars), *refs),
+        [shape(rows, width)] * PLANE
+        + [shape(cases, far_rows, 2 * rows), shape(cases, 2, 2 * rows, t=F32)]
+        + [shape(*far.shape) for far in fars],
+        *query_grads, *fars, sums, stats, cost_us=2.0, name="far_attention",
     )
     kept, far_grads = results[: PLANE + 2], list(results[PLANE + 2 :])
     results = call(
         lambda *refs: plane_kernel(len(fars), *refs),
         blocks + [shape(2 * rows, width, t=F32)] * PLANE,
-        *key_values, *query_grads, *fars, *kept,
+        *key_values, *query_grads, *fars, weights, dots, *kept,
         cost_us=2.3, name="plane_grads",
     )
     att_dq, dkv = results[:PLANE], results[PLANE:]
@@ -381,7 +403,7 @@
     own_sum, *other_sum = call(
         output_kernel,
         [shape(rows, features, t=F32)] + [shape(rows // PIECES, features)] * PIECES,
-        *att_dq, weight, after=(dkv[0],), cost_us=0.01, name="project",
+        *att_dq, out_weight, after=(dkv[0],), cost_us=0.01, name="project",
     )
     dkv = plane_exchange(dkv)
     other_sum = [xor_permute(piece, 1, "head") for piece in other_sum]

time: 49.2 us -> 46.3 us (0.941)
  starting transfers between devices: 26.5 us -> 24 us
  Pallas kernels: 13.4 us -> 11.7 us
  waiting for transfers between devices: 8.43 us -> 9.69 us
    ppermute x21, starting transfers between devices: 26.5 us -> 24 us  [xor_permute(): return lax.ppermute(block, axis, [(i, i ^ mask) for i in range(count)])]
    pallas_call x8 -> x9, Pallas kernels: 13.4 us -> 11.7 us  [call(): pl.pallas_call(lambda *refs: kernel(*refs[:count], *refs[count + len(afte...]
    ppermute x21, waiting for transfers between devices: 8.43 us -> 9.69 us  [xor_permute(): return lax.ppermute(block, axis, [(i, i ^ mask) for i in range(count)])]
  transfers between devices with their start and end apart: 21 -> 21, of which waited for: 6 -> 9; matrix products, arithmetic and copies ran while one was open for 0% -> 0% of each run, Pallas kernels for 17% -> 19%
where the time goes in v3:
time: 46.3 us; the launch traced here: 46.1 us
  starting transfers between devices  24 us (52%)
  Pallas kernels  11.7 us (25%)
  waiting for transfers between devices  9.69 us (21%)
  between operations  0.73 us (2%)
    ppermute x21, starting transfers between devices, xor_permute(): return lax.ppermute(block, axis, [(i, i ^ mask) for i in range(count)])  24 us
    pallas_call x9, Pallas kernels, call(): pl.pallas_call(lambda *refs: kernel(*refs[:count], *refs[count + len(afte...  11.7 us
    ppermute x21, waiting for transfers between devices, xor_permute(): return lax.ppermute(block, axis, [(i, i ^ mask) for i in range(count)])  9.69 us
  transfers between devices with their start and end apart: 21, of which 9 were waited for; matrix products, arithmetic and copies ran while one was open for 0% of the time, Pallas kernels for 19%

profile of v3, /device:TPU:0, one launch (start us, length us, event | category | flops | bytes accessed | tf_op | source)
XLA Modules:
  0.0 46.1 jit_solution(10674239252153999216)
XLA Ops:
  0.6 0.0 copy-start
  0.6 0.5 %collective-permute-start.3 = (bf16[128,1024]{1,0:T(8,128)(2,1)}, bf16[128,1024]{1,0:T(8,128)(2,1)S(1)}, u32[]{:S(2)}, u32[]{:S(2)}) collective-permute-start(bf16[128,1024]{1,0:T(8,128)(2,1)} %refs_1_.3), channel_id=1, source_target_pairs={{0,1},{1,0},{2,3},{3,2},{4,5},{5,4},{6,7},{7,6},{8,9},{9,8},{10,11... | collective-permute-start | bytes 786440 | tf_op jit(solution)/shard_map/ppermute | solution.py:19
  1.2 1.4 %pack_keys_values.1 = (bf16[256,256]{1,0:T(8,128)(2,1)S(1)}, bf16[256,256]{1,0:T(8,128)(2,1)S(1)}, bf16[256,256]{1,0:T(8,128)(2,1)S(1)}, bf16[256,256]{1,0:T(8,128)(2,1)S(1)}) custom-call(bf16[128,1024]{1,0:T(8,128)(2,1)} %refs_0_.2, bf16[128,1024]{1,0:T(8,128)(2,1)} %refs_1_.2), custom_call_target="tpu_custom_call" | custom-call | flops 8000000000 | tf_op jit(solution)/shard_map/pack_keys_values/pallas_call | solution.py:57
  2.6 2.5 %collective-permute-start = (bf16[256,256]{1,0:T(8,128)(2,1)S(1)}, bf16[256,256]{1,0:T(8,128)(2,1)S(1)}, u32[]{:S(2)}, u32[]{:S(2)}) collective-permute-start(bf16[256,256]{1,0:T(8,128)(2,1)S(1)} %get-tuple-element.43), channel_id=1, source_target_pairs={{0,2},{2,0},{4,6},{6,4},{8,10},{10,8},{12,14},{14,12},{16,18},{18,... | collective-permute-start | bytes 393224 | tf_op jit(solution)/shard_map/ppermute | solution.py:19
  5.0 1.5 %collective-permute-start.1 = (bf16[256,256]{1,0:T(8,128)(2,1)S(1)}, bf16[256,256]{1,0:T(8,128)(2,1)S(1)}, u32[]{:S(2)}, u32[]{:S(2)}) collective-permute-start(bf16[256,256]{1,0:T(8,128)(2,1)S(1)} %get-tuple-element.44), channel_id=1, source_target_pairs={{0,4},{2,6},{4,0},{6,2},{8,12},{10,14},{12,8},{14,10},{16,20},{18,... | collective-permute-start | bytes 393224 | tf_op jit(solution)/shard_map/ppermute | solution.py:19
  6.6 0.0 collective-permute-start.2
  6.6 0.0 collective-permute-done.3.refs_2_
  6.6 0.0 copy-done
  6.6 2.5 %grad_attended.1 = (bf16[256,256]{1,0:T(8,128)(2,1)S(1)}, bf16[256,256]{1,0:T(8,128)(2,1)S(1)}, bf16[256,256]{1,0:T(8,128)(2,1)S(1)}, bf16[256,256]{1,0:T(8,128)(2,1)S(1)}) custom-call(bf16[128,1024]{1,0:T(8,128)(2,1)} %refs_0_.3, bf16[128,1024]{1,0:T(8,128)(2,1)} %refs_1_.3, bf16[128,1024]{1,0:T(8,128)(2,1)S(1)} %collective-permute-done.3.refs_2_, ...), custom_call_target="tpu_custom_call" | custom-call | flops 3000000000 | tf_op jit(solution)/shard_map/grad_attended/pallas_call | solution.py:57
  9.1 2.0 %collective-permute-start.4 = (bf16[256,256]{1,0:T(8,128)(2,1)S(1)}, bf16[256,256]{1,0:T(8,128)(2,1)S(1)}, u32[]{:S(2)}, u32[]{:S(2)}) collective-permute-start(bf16[256,256]{1,0:T(8,128)(2,1)S(1)} %get-tuple-element.47), channel_id=1, source_target_pairs={{0,2},{2,0},{4,6},{6,4},{8,10},{10,8},{12,14},{14,12},{16,18},{18,... | collective-permute-start | bytes 393224 | tf_op jit(solution)/shard_map/ppermute | solution.py:19
  11.1 1.5 %collective-permute-start.5 = (bf16[256,256]{1,0:T(8,128)(2,1)S(1)}, bf16[256,256]{1,0:T(8,128)(2,1)S(1)}, u32[]{:S(2)}, u32[]{:S(2)}) collective-permute-start(bf16[256,256]{1,0:T(8,128)(2,1)S(1)} %get-tuple-element.48), channel_id=1, source_target_pairs={{0,4},{2,6},{4,0},{6,2},{8,12},{10,14},{12,8},{14,10},{16,20},{18,... | collective-permute-start | bytes 393224 | tf_op jit(solution)/shard_map/ppermute | solution.py:19
  12.6 0.0 collective-permute-done.refs_1_
  12.6 0.0 collective-permute-start.6
  12.6 1.0 %collective-permute-done.1.refs_2_ = bf16[256,256]{1,0:T(8,128)(2,1)S(1)} collective-permute-done((bf16[256,256]{1,0:T(8,128)(2,1)S(1)}, bf16[256,256]{1,0:T(8,128)(2,1)S(1)}, u32[]{:S(2)}, u32[]{:S(2)}) %collective-permute-start.1) | collective-permute-done | bytes 131104 | tf_op jit(solution)/shard_map/ppermute | solution.py:19
  13.7 0.1 collective-permute-done.2.refs_3_
  13.8 0.5 pool_plane.1
  14.3 3.6 %collective-permute-start.9 = (bf16[128,256]{1,0:T(8,128)(2,1)S(1)}, bf16[128,256]{1,0:T(8,128)(2,1)S(1)}, u32[]{:S(2)}, u32[]{:S(2)}) collective-permute-start(bf16[128,256]{1,0:T(8,128)(2,1)S(1)} %get-tuple-element.51), channel_id=1, source_target_pairs={{0,24},{2,26},{4,28},{6,30},{8,16},{10,18},{12,20},{14,22},{16,8},... | collective-permute-start | bytes 196616 | tf_op jit(solution)/shard_map/ppermute | solution.py:19
  17.9 0.0 collective-permute-start.8
  17.9 0.0 collective-permute-done.4.refs_5_.refs_1_
  17.9 0.8 %collective-permute-start.7 = (bf16[256,256]{1,0:T(8,128)(2,1)S(1)}, bf16[256,256]{1,0:T(8,128)(2,1)S(1)}, u32[]{:S(2)}, u32[]{:S(2)}) collective-permute-start(bf16[256,256]{1,0:T(8,128)(2,1)S(1)} %get-tuple-element.50), channel_id=1, source_target_pairs={{0,8},{2,10},{4,12},{6,14},{8,0},{10,2},{12,4},{14,6},{16,24},{18,... | collective-permute-start | bytes 393224 | tf_op jit(solution)/shard_map/ppermute | solution.py:19
  18.7 0.6 %collective-permute-done.5.refs_6_.refs_2_ = bf16[256,256]{1,0:T(8,128)(2,1)S(1)} collective-permute-done((bf16[256,256]{1,0:T(8,128)(2,1)S(1)}, bf16[256,256]{1,0:T(8,128)(2,1)S(1)}, u32[]{:S(2)}, u32[]{:S(2)}) %collective-permute-start.5) | collective-permute-done | bytes 131104 | tf_op jit(solution)/shard_map/ppermute | solution.py:19
  19.3 0.0 collective-permute-done.6.refs_7_.refs_3_
  19.3 1.8 %near_attention.1 = (f32[4,384,256]{2,1,0:T(8,128)S(1)}, f32[4,384,256]{2,1,0:T(8,128)S(1)}, f32[4,128,256]{2,1,0:T(8,128)S(1)}, f32[4,2,256]{2,1,0:T(2,128)S(1)}) custom-call(bf16[256,256]{1,0:T(8,128)(2,1)S(1)} %get-tuple-element.42.refs_0_, bf16[256,256]{1,0:T(8,128)(2,1)S(1)} %collective-permute-done.refs_1_, ...), custom_call_target="tpu_custom_call" | custom-call | flops 2000000000 | tf_op jit(solution)/shard_map/near_attention/pallas_call | solution.py:57
  21.1 0.0 collective-permute-done.9.refs_6_.refs_10_
  21.1 2.1 %collective-permute-done.8.refs_5_.refs_9_ = bf16[128,256]{1,0:T(8,128)(2,1)S(1)} collective-permute-done((bf16[128,256]{1,0:T(8,128)(2,1)S(1)}, bf16[128,256]{1,0:T(8,128)(2,1)S(1)}, u32[]{:S(2)}, u32[]{:S(2)}) %collective-permute-start.8) | collective-permute-done | bytes 65568 | tf_op jit(solution)/shard_map/ppermute | solution.py:19
  23.2 1.2 %collective-permute-done.7.refs_4_.refs_8_ = bf16[256,256]{1,0:T(8,128)(2,1)S(1)} collective-permute-done((bf16[256,256]{1,0:T(8,128)(2,1)S(1)}, bf16[256,256]{1,0:T(8,128)(2,1)S(1)}, u32[]{:S(2)}, u32[]{:S(2)}) %collective-permute-start.7) | collective-permute-done | bytes 131104 | tf_op jit(solution)/shard_map/ppermute | solution.py:19
  24.4 1.8 %far_attention.1 = (bf16[128,256]{1,0:T(8,128)(2,1)S(1)}, bf16[128,256]{1,0:T(8,128)(2,1)S(1)}, bf16[128,256]{1,0:T(8,128)(2,1)S(1)}, bf16[128,256]{1,0:T(8,128)...) custom-call(bf16[256,256]{1,0:T(8,128)(2,1)S(1)} %get-tuple-element., ...), custom_call_target="tpu_custom_call" | custom-call | flops 2000000000 | tf_op jit(solution)/shard_map/far_attention/pallas_call | solution.py:57
  26.3 1.4 %collective-permute-start.14 = (bf16[128,256]{1,0:T(8,128)(2,1)S(1)}, bf16[128,256]{1,0:T(8,128)(2,1)S(1)}, u32[]{:S(2)}, u32[]{:S(2)}) collective-permute-start(bf16[128,256]{1,0:T(8,128)(2,1)S(1)} %get-tuple-element.71), channel_id=1, source_target_pairs={{0,16},{2,18},{4,20},{6,22},{8,24},{10,26},{12,28},{14,30},{16,0},... | collective-permute-start | bytes 196616 | tf_op jit(solution)/shard_map/ppermute | solution.py:19
  27.7 2.0 %collective-permute-start.15 = (bf16[128,256]{1,0:T(8,128)(2,1)S(1)}, bf16[128,256]{1,0:T(8,128)(2,1)S(1)}, u32[]{:S(2)}, u32[]{:S(2)}) collective-permute-start(bf16[128,256]{1,0:T(8,128)(2,1)S(1)} %get-tuple-element.72), channel_id=1, source_target_pairs={{0,24},{2,26},{4,28},{6,30},{8,16},{10,18},{12,20},{14,22},{16,8},... | collective-permute-start | bytes 196616 | tf_op jit(solution)/shard_map/ppermute | solution.py:19
  29.7 0.1 collective-permute-start.13
  29.8 1.5 %plane_grads.1 = (bf16[256,256]{1,0:T(8,128)(2,1)S(1)}, bf16[256,256]{1,0:T(8,128)(2,1)S(1)}, bf16[256,256]{1,0:T(8,128)(2,1)S(1)}, bf16[256,256]{1,0:T(8,128)(2...) custom-call(bf16[256,256]{1,0:T(8,128)(2,1)S(1)} %get-tuple-element., ...), custom_call_target="tpu_custom_call" | custom-call | flops 2300000000 | tf_op jit(solution)/shard_map/plane_grads/pallas_call | solution.py:57
  31.3 1.7 %collective-permute-start.10 = (bf16[256,256]{1,0:T(8,128)(2,1)S(1)}, bf16[256,256]{1,0:T(8,128)(2,1)S(1)}, u32[]{:S(2)}, u32[]{:S(2)}) collective-permute-start(bf16[256,256]{1,0:T(8,128)(2,1)S(1)} %get-tuple-element.63), channel_id=1, source_target_pairs={{0,2},{2,0},{4,6},{6,4},{8,10},{10,8},{12,14},{14,12},{16,18},{18,... | collective-permute-start | bytes 393224 | tf_op jit(solution)/shard_map/ppermute | solution.py:19
  33.0 0.6 %collective-permute-start.11 = (bf16[256,256]{1,0:T(8,128)(2,1)S(1)}, bf16[256,256]{1,0:T(8,128)(2,1)S(1)}, u32[]{:S(2)}, u32[]{:S(2)}) collective-permute-start(bf16[256,256]{1,0:T(8,128)(2,1)S(1)} %get-tuple-element.64), channel_id=1, source_target_pairs={{0,4},{2,6},{4,0},{6,2},{8,12},{10,14},{12,8},{14,10},{16,20},{18,... | collective-permute-start | bytes 393224 | tf_op jit(solution)/shard_map/ppermute | solution.py:19
  33.6 0.0 collective-permute-done.14.refs_5_
  33.6 1.3 %collective-permute-start.12 = (bf16[256,256]{1,0:T(8,128)(2,1)S(1)}, bf16[256,256]{1,0:T(8,128)(2,1)S(1)}, u32[]{:S(2)}, u32[]{:S(2)}) collective-permute-start(bf16[256,256]{1,0:T(8,128)(2,1)S(1)} %get-tuple-element.65), channel_id=1, source_target_pairs={{0,6},{2,4},{4,2},{6,0},{8,14},{10,12},{12,10},{14,8},{16,22},{18,... | collective-permute-start | bytes 393224 | tf_op jit(solution)/shard_map/ppermute | solution.py:19
  34.9 0.0 collective-permute-done.15.refs_6_
  34.9 0.3 collective-permute-done.13.refs_4_
  35.2 0.4 carry.1
  35.6 1.7 %collective-permute-start.18 = (bf16[256,256]{1,0:T(8,128)(2,1)S(1)}, bf16[256,256]{1,0:T(8,128)(2,1)S(1)}, u32[]{:S(2)}, u32[]{:S(2)}) collective-permute-start(bf16[256,256]{1,0:T(8,128)(2,1)S(1)} %get-tuple-element.77), channel_id=1, source_target_pairs={{0,2},{2,0},{4,6},{6,4},{8,10},{10,8},{12,14},{14,12},{16,18},{18,... | collective-permute-start | bytes 393224 | tf_op jit(solution)/shard_map/ppermute | solution.py:19
  37.3 0.7 %collective-permute-start.19 = (bf16[256,256]{1,0:T(8,128)(2,1)S(1)}, bf16[256,256]{1,0:T(8,128)(2,1)S(1)}, u32[]{:S(2)}, u32[]{:S(2)}) collective-permute-start(bf16[256,256]{1,0:T(8,128)(2,1)S(1)} %get-tuple-element.78), channel_id=1, source_target_pairs={{0,4},{2,6},{4,0},{6,2},{8,12},{10,14},{12,8},{14,10},{16,20},{18,... | collective-permute-start | bytes 393224 | tf_op jit(solution)/shard_map/ppermute | solution.py:19
  38.0 0.0 collective-permute-done.10.refs_1_.refs_4_
  38.0 1.4 %collective-permute-start.20 = (bf16[256,256]{1,0:T(8,128)(2,1)S(1)}, bf16[256,256]{1,0:T(8,128)(2,1)S(1)}, u32[]{:S(2)}, u32[]{:S(2)}) collective-permute-start(bf16[256,256]{1,0:T(8,128)(2,1)S(1)} %get-tuple-element.79), channel_id=1, source_target_pairs={{0,6},{2,4},{4,2},{6,0},{8,14},{10,12},{12,10},{14,8},{16,22},{18,... | collective-permute-start | bytes 393224 | tf_op jit(solution)/shard_map/ppermute | solution.py:19
  39.4 0.0 collective-permute-done.11.refs_2_.refs_5_
  39.4 2.1 %collective-permute-done.12.refs_3_.refs_6_ = bf16[256,256]{1,0:T(8,128)(2,1)S(1)} collective-permute-done((bf16[256,256]{1,0:T(8,128)(2,1)S(1)}, bf16[256,256]{1,0:T(8,128)(2,1)S(1)}, u32[]{:S(2)}, u32[]{:S(2)}) %collective-permute-start.12) | collective-permute-done | bytes 131104 | tf_op jit(solution)/shard_map/ppermute | solution.py:19
  41.5 0.8 %project.1 = (f32[128,1024]{1,0:T(8,128)S(1)}, bf16[64,1024]{1,0:T(8,128)(2,1)S(1)}, bf16[64,1024]{1,0:T(8,128)(2,1)S(1)}) custom-call(bf16[256,256]{1,0:T(8,128)(2,1)S(1)} %get-tuple-element.62.refs_0_.refs_3_, bf16[256,256]{1,0:T(8,128)(2,1)S(1)} %collective-permute-done.10.refs_1_.refs_4_, bf16[256,256]{1,0:T(8,128)(2,1)S(1)} %collective-permute-done.11.refs_2_.refs_5_, ...), custom_call_target="tpu_custom_call" | custom-call | flops 10000000 | tf_op jit(solution)/shard_map/project/pallas_call | solution.py:57
  42.3 0.1 collective-permute-start.16
  42.3 0.5 %collective-permute-start.17 = (bf16[64,1024]{1,0:T(8,128)(2,1)S(1)}, bf16[64,1024]{1,0:T(8,128)(2,1)S(1)}, u32[]{:S(2)}, u32[]{:S(2)}) collective-permute-start(bf16[64,1024]{1,0:T(8,128)(2,1)S(1)} %get-tuple-element.76), channel_id=1, source_target_pairs={{0,1},{1,0},{2,3},{3,2},{4,5},{5,4},{6,7},{7,6},{8,9},{9,8},{10,11... | collective-permute-start | bytes 393224 | tf_op jit(solution)/shard_map/ppermute | solution.py:19
  42.8 0.5 %collective-permute-done.18.refs_8_ = bf16[256,256]{1,0:T(8,128)(2,1)S(1)} collective-permute-done((bf16[256,256]{1,0:T(8,128)(2,1)S(1)}, bf16[256,256]{1,0:T(8,128)(2,1)S(1)}, u32[]{:S(2)}, u32[]{:S(2)}) %collective-permute-start.18) | collective-permute-done | bytes 131104 | tf_op jit(solution)/shard_map/ppermute | solution.py:19
  43.4 1.7 %collective-permute-done.19.refs_9_ = bf16[256,256]{1,0:T(8,128)(2,1)S(1)} collective-permute-done((bf16[256,256]{1,0:T(8,128)(2,1)S(1)}, bf16[256,256]{1,0:T(8,128)(2,1)S(1)}, u32[]{:S(2)}, u32[]{:S(2)}) %collective-permute-start.19) | collective-permute-done | bytes 131104 | tf_op jit(solution)/shard_map/ppermute | solution.py:19
  45.0 0.0 collective-permute-done.20.refs_10_
  45.0 0.0 collective-permute-done.16.refs_1_
  45.0 0.0 collective-permute-done.17.refs_2_
  45.0 1.1 %join.1 = (bf16[128,1024]{1,0:T(8,128)(2,1)}, bf16[128,1024]{1,0:T(8,128)(2,1)}, bf16[128,1024]{1,0:T(8,128)(2,1)}, bf16[128,1024]{1,0:T(8,128)(2,1)}) custom-call(f32[128,1024]{1,0:T(8,128)S(1)} %get-tuple-element.74.refs_0_, bf16[64,1024]{1,0:T(8,128)(2,1)S(1)} %collective-permute-done.16.refs_1_, bf16[64,1024]{1,0:T(8,128)(2,1)S(1)} %collective-permute-done.17.refs_2_, ...), custom_call_target="tpu_custom_call" | custom-call | flops 1000000000 | tf_op jit(solution)/shard_map/join/pallas_call | solution.py:57
Async XLA Ops:
  0.6 5.9 %copy-start = (bf16[1024,2048]{1,0:T(8,128)(2,1)S(1)}, bf16[1024,2048]{1,0:T(8,128)(2,1)}, u32[]{:S(2)}) copy-start(bf16[1024,2048]{1,0:T(8,128)(2,1)} %refs_4_.1) | copy-start | bytes 12582916
  0.6 5.9 %collective-permute-start.3 = (bf16[128,1024]{1,0:T(8,128)(2,1)}, bf16[128,1024]{1,0:T(8,128)(2,1)S(1)}, u32[]{:S(2)}, u32[]{:S(2)}) collective-permute-start(bf16[128,1024]{1,0:T(8,128)(2,1)} %refs_1_.3), channel_id=1, source_target_pairs={{0,1},{1,0},{2,3},{3,2},{4,5},{5,4},{6,7},{7,6},{8,9},{9,8},{10,11... | collective-permute-start | bytes 786440 | tf_op jit(solution)/shard_map/ppermute | solution.py:19
  2.6 10.1 %collective-permute-start = (bf16[256,256]{1,0:T(8,128)(2,1)S(1)}, bf16[256,256]{1,0:T(8,128)(2,1)S(1)}, u32[]{:S(2)}, u32[]{:S(2)}) collective-permute-start(bf16[256,256]{1,0:T(8,128)(2,1)S(1)} %get-tuple-element.43), channel_id=1, source_target_pairs={{0,2},{2,0},{4,6},{6,4},{8,10},{10,8},{12,14},{14,12},{16,18},{18,... | collective-permute-start | bytes 393224 | tf_op jit(solution)/shard_map/ppermute | solution.py:19
  5.0 8.6 %collective-permute-start.1 = (bf16[256,256]{1,0:T(8,128)(2,1)S(1)}, bf16[256,256]{1,0:T(8,128)(2,1)S(1)}, u32[]{:S(2)}, u32[]{:S(2)}) collective-permute-start(bf16[256,256]{1,0:T(8,128)(2,1)S(1)} %get-tuple-element.44), channel_id=1, source_target_pairs={{0,4},{2,6},{4,0},{6,2},{8,12},{10,14},{12,8},{14,10},{16,20},{18,... | collective-permute-start | bytes 393224 | tf_op jit(solution)/shard_map/ppermute | solution.py:19
  6.6 7.3 %collective-permute-start.2 = (bf16[256,256]{1,0:T(8,128)(2,1)S(1)}, bf16[256,256]{1,0:T(8,128)(2,1)S(1)}, u32[]{:S(2)}, u32[]{:S(2)}) collective-permute-start(bf16[256,256]{1,0:T(8,128)(2,1)S(1)} %get-tuple-element.45), channel_id=1, source_target_pairs={{0,6},{2,4},{4,2},{6,0},{8,14},{10,12},{12,10},{14,8},{16,22},{18,... | collective-permute-start | bytes 393224 | tf_op jit(solution)/shard_map/ppermute | solution.py:19
  9.1 8.8 %collective-permute-start.4 = (bf16[256,256]{1,0:T(8,128)(2,1)S(1)}, bf16[256,256]{1,0:T(8,128)(2,1)S(1)}, u32[]{:S(2)}, u32[]{:S(2)}) collective-permute-start(bf16[256,256]{1,0:T(8,128)(2,1)S(1)} %get-tuple-element.47), channel_id=1, source_target_pairs={{0,2},{2,0},{4,6},{6,4},{8,10},{10,8},{12,14},{14,12},{16,18},{18,... | collective-permute-start | bytes 393224 | tf_op jit(solution)/shard_map/ppermute | solution.py:19
  11.1 8.2 %collective-permute-start.5 = (bf16[256,256]{1,0:T(8,128)(2,1)S(1)}, bf16[256,256]{1,0:T(8,128)(2,1)S(1)}, u32[]{:S(2)}, u32[]{:S(2)}) collective-permute-start(bf16[256,256]{1,0:T(8,128)(2,1)S(1)} %get-tuple-element.48), channel_id=1, source_target_pairs={{0,4},{2,6},{4,0},{6,2},{8,12},{10,14},{12,8},{14,10},{16,20},{18,... | collective-permute-start | bytes 393224 | tf_op jit(solution)/shard_map/ppermute | solution.py:19
  12.6 6.7 %collective-permute-start.6 = (bf16[256,256]{1,0:T(8,128)(2,1)S(1)}, bf16[256,256]{1,0:T(8,128)(2,1)S(1)}, u32[]{:S(2)}, u32[]{:S(2)}) collective-permute-start(bf16[256,256]{1,0:T(8,128)(2,1)S(1)} %get-tuple-element.49), channel_id=1, source_target_pairs={{0,6},{2,4},{4,2},{6,0},{8,14},{10,12},{12,10},{14,8},{16,22},{18,... | collective-permute-start | bytes 393224 | tf_op jit(solution)/shard_map/ppermute | solution.py:19
  14.3 6.8 %collective-permute-start.9 = (bf16[128,256]{1,0:T(8,128)(2,1)S(1)}, bf16[128,256]{1,0:T(8,128)(2,1)S(1)}, u32[]{:S(2)}, u32[]{:S(2)}) collective-permute-start(bf16[128,256]{1,0:T(8,128)(2,1)S(1)} %get-tuple-element.51), channel_id=1, source_target_pairs={{0,24},{2,26},{4,28},{6,30},{8,16},{10,18},{12,20},{14,22},{16,8},... | collective-permute-start | bytes 196616 | tf_op jit(solution)/shard_map/ppermute | solution.py:19
  17.9 5.3 %collective-permute-start.8 = (bf16[128,256]{1,0:T(8,128)(2,1)S(1)}, bf16[128,256]{1,0:T(8,128)(2,1)S(1)}, u32[]{:S(2)}, u32[]{:S(2)}) collective-permute-start(bf16[128,256]{1,0:T(8,128)(2,1)S(1)} %get-tuple-element.51), channel_id=1, source_target_pairs={{0,16},{2,18},{4,20},{6,22},{8,24},{10,26},{12,28},{14,30},{16,0},... | collective-permute-start | bytes 196616 | tf_op jit(solution)/shard_map/ppermute | solution.py:19
  17.9 6.5 %collective-permute-start.7 = (bf16[256,256]{1,0:T(8,128)(2,1)S(1)}, bf16[256,256]{1,0:T(8,128)(2,1)S(1)}, u32[]{:S(2)}, u32[]{:S(2)}) collective-permute-start(bf16[256,256]{1,0:T(8,128)(2,1)S(1)} %get-tuple-element.50), channel_id=1, source_target_pairs={{0,8},{2,10},{4,12},{6,14},{8,0},{10,2},{12,4},{14,6},{16,24},{18,... | collective-permute-start | bytes 393224 | tf_op jit(solution)/shard_map/ppermute | solution.py:19
  26.3 7.3 %collective-permute-start.14 = (bf16[128,256]{1,0:T(8,128)(2,1)S(1)}, bf16[128,256]{1,0:T(8,128)(2,1)S(1)}, u32[]{:S(2)}, u32[]{:S(2)}) collective-permute-start(bf16[128,256]{1,0:T(8,128)(2,1)S(1)} %get-tuple-element.71), channel_id=1, source_target_pairs={{0,16},{2,18},{4,20},{6,22},{8,24},{10,26},{12,28},{14,30},{16,0},... | collective-permute-start | bytes 196616 | tf_op jit(solution)/shard_map/ppermute | solution.py:19
  27.7 7.2 %collective-permute-start.15 = (bf16[128,256]{1,0:T(8,128)(2,1)S(1)}, bf16[128,256]{1,0:T(8,128)(2,1)S(1)}, u32[]{:S(2)}, u32[]{:S(2)}) collective-permute-start(bf16[128,256]{1,0:T(8,128)(2,1)S(1)} %get-tuple-element.72), channel_id=1, source_target_pairs={{0,24},{2,26},{4,28},{6,30},{8,16},{10,18},{12,20},{14,22},{16,8},... | collective-permute-start | bytes 196616 | tf_op jit(solution)/shard_map/ppermute | solution.py:19
  29.7 5.5 %collective-permute-start.13 = (bf16[256,256]{1,0:T(8,128)(2,1)S(1)}, bf16[256,256]{1,0:T(8,128)(2,1)S(1)}, u32[]{:S(2)}, u32[]{:S(2)}) collective-permute-start(bf16[256,256]{1,0:T(8,128)(2,1)S(1)} %get-tuple-element.70), channel_id=1, source_target_pairs={{0,8},{2,10},{4,12},{6,14},{8,0},{10,2},{12,4},{14,6},{16,24},{18,... | collective-permute-start | bytes 393224 | tf_op jit(solution)/shard_map/ppermute | solution.py:19
  31.3 6.7 %collective-permute-start.10 = (bf16[256,256]{1,0:T(8,128)(2,1)S(1)}, bf16[256,256]{1,0:T(8,128)(2,1)S(1)}, u32[]{:S(2)}, u32[]{:S(2)}) collective-permute-start(bf16[256,256]{1,0:T(8,128)(2,1)S(1)} %get-tuple-element.63), channel_id=1, source_target_pairs={{0,2},{2,0},{4,6},{6,4},{8,10},{10,8},{12,14},{14,12},{16,18},{18,... | collective-permute-start | bytes 393224 | tf_op jit(solution)/shard_map/ppermute | solution.py:19
  33.0 6.4 %collective-permute-start.11 = (bf16[256,256]{1,0:T(8,128)(2,1)S(1)}, bf16[256,256]{1,0:T(8,128)(2,1)S(1)}, u32[]{:S(2)}, u32[]{:S(2)}) collective-permute-start(bf16[256,256]{1,0:T(8,128)(2,1)S(1)} %get-tuple-element.64), channel_id=1, source_target_pairs={{0,4},{2,6},{4,0},{6,2},{8,12},{10,14},{12,8},{14,10},{16,20},{18,... | collective-permute-start | bytes 393224 | tf_op jit(solution)/shard_map/ppermute | solution.py:19
  33.6 7.9 %collective-permute-start.12 = (bf16[256,256]{1,0:T(8,128)(2,1)S(1)}, bf16[256,256]{1,0:T(8,128)(2,1)S(1)}, u32[]{:S(2)}, u32[]{:S(2)}) collective-permute-start(bf16[256,256]{1,0:T(8,128)(2,1)S(1)} %get-tuple-element.65), channel_id=1, source_target_pairs={{0,6},{2,4},{4,2},{6,0},{8,14},{10,12},{12,10},{14,8},{16,22},{18,... | collective-permute-start | bytes 393224 | tf_op jit(solution)/shard_map/ppermute | solution.py:19
  35.6 7.7 %collective-permute-start.18 = (bf16[256,256]{1,0:T(8,128)(2,1)S(1)}, bf16[256,256]{1,0:T(8,128)(2,1)S(1)}, u32[]{:S(2)}, u32[]{:S(2)}) collective-permute-start(bf16[256,256]{1,0:T(8,128)(2,1)S(1)} %get-tuple-element.77), channel_id=1, source_target_pairs={{0,2},{2,0},{4,6},{6,4},{8,10},{10,8},{12,14},{14,12},{16,18},{18,... | collective-permute-start | bytes 393224 | tf_op jit(solution)/shard_map/ppermute | solution.py:19
  37.3 7.7 %collective-permute-start.19 = (bf16[256,256]{1,0:T(8,128)(2,1)S(1)}, bf16[256,256]{1,0:T(8,128)(2,1)S(1)}, u32[]{:S(2)}, u32[]{:S(2)}) collective-permute-start(bf16[256,256]{1,0:T(8,128)(2,1)S(1)} %get-tuple-element.78), channel_id=1, source_target_pairs={{0,4},{2,6},{4,0},{6,2},{8,12},{10,14},{12,8},{14,10},{16,20},{18,... | collective-permute-start | bytes 393224 | tf_op jit(solution)/shard_map/ppermute | solution.py:19
  38.0 7.0 %collective-permute-start.20 = (bf16[256,256]{1,0:T(8,128)(2,1)S(1)}, bf16[256,256]{1,0:T(8,128)(2,1)S(1)}, u32[]{:S(2)}, u32[]{:S(2)}) collective-permute-start(bf16[256,256]{1,0:T(8,128)(2,1)S(1)} %get-tuple-element.79), channel_id=1, source_target_pairs={{0,6},{2,4},{4,2},{6,0},{8,14},{10,12},{12,10},{14,8},{16,22},{18,... | collective-permute-start | bytes 393224 | tf_op jit(solution)/shard_map/ppermute | solution.py:19
  42.3 2.8 %collective-permute-start.16 = (bf16[64,1024]{1,0:T(8,128)(2,1)S(1)}, bf16[64,1024]{1,0:T(8,128)(2,1)S(1)}, u32[]{:S(2)}, u32[]{:S(2)}) collective-permute-start(bf16[64,1024]{1,0:T(8,128)(2,1)S(1)} %get-tuple-element.75), channel_id=1, source_target_pairs={{0,1},{1,0},{2,3},{3,2},{4,5},{5,4},{6,7},{7,6},{8,9},{9,8},{10,11... | collective-permute-start | bytes 393224 | tf_op jit(solution)/shard_map/ppermute | solution.py:19
  42.3 2.7 %collective-permute-start.17 = (bf16[64,1024]{1,0:T(8,128)(2,1)S(1)}, bf16[64,1024]{1,0:T(8,128)(2,1)S(1)}, u32[]{:S(2)}, u32[]{:S(2)}) collective-permute-start(bf16[64,1024]{1,0:T(8,128)(2,1)S(1)} %get-tuple-element.76), channel_id=1, source_target_pairs={{0,1},{1,0},{2,3},{3,2},{4,5},{5,4},{6,7},{7,6},{8,9},{9,8},{10,11... | collective-permute-start | bytes 393224 | tf_op jit(solution)/shard_map/ppermute | solution.py:19

commit v4 on v3

--- a/solution.py
+++ b/solution.py
@@ -45,7 +45,7 @@
     return dot(spread_matrix(block.shape[0], times), block.astype(BF16))
 
 
-def call(kernel, outs, *args, after=(), hbm=(), hbm_out=False, scratch=(), cost_us=1.0, name=None):
+def call(kernel, outs, *args, after=(), aliases={}, hbm=(), hbm_out=False, scratch=(), cost_us=1.0, name=None):
     vmem = pl.BlockSpec(memory_space=pltpu.VMEM)
     in_hbm = pl.BlockSpec(memory_space=pltpu.HBM)
     space = pltpu.HBM if hbm_out else pltpu.VMEM
@@ -60,6 +60,7 @@
         in_specs=[in_hbm if n in hbm else vmem for n in range(count)]
         + [pl.BlockSpec(memory_space=pl.ANY)] * len(after),
         scratch_shapes=scratch,
+        input_output_aliases=aliases,
         out_specs=[in_hbm if hbm_out else vmem] * len(outs),
         compiler_params=pltpu.CompilerParams(vmem_limit_bytes=24 * 1024 * 1024),
         cost_estimate=pl.CostEstimate(
@@ -143,98 +144,137 @@
     return jnp.concatenate([far[part(m, far.shape[0] // 2), lanes] for far in fars], 0)
 
 
+def token_rows(qgs, m, lanes):
+    rows = part(m, qgs[0].shape[0] // 2)
+    return jnp.concatenate([qg[rows, lanes] for qg in qgs], 0)
+
+
 def near_kernel(*refs):
-    kvs, qgs = refs[:PLANE], refs[PLANE : 2 * PLANE]
-    weight_out, dots_out, sums_out, stats_out = refs[2 * PLANE :]
+    kvs, qgs, level3 = refs[:PLANE], refs[PLANE : 2 * PLANE], refs[2 * PLANE]
+    weight_out, dots_out, sums_out, stats_out, keys_out = refs[2 * PLANE + 1 :]
     rows, width = qgs[0].shape[0] // 2, qgs[0].shape[1]
-    for h in range(width // DH):
-        lanes = part(h, DH)
-        for p in range(2):
-            n = 2 * h + p
-            q, g = both(qgs, p, part(0, rows), lanes), both(qgs, p, part(1, rows), lanes)
-            values = near_set(kvs, p, lanes, 1)
-            scores = dot(near_set(kvs, p, lanes, 0), q, 1, 1) * SCALE2
-            row_max = jnp.max(scores, 0, keepdims=True)
-            weights = jnp.exp2(scores - row_max)
-            weight_out[n] = weights
-            dots_out[n] = dot(values, g, 1, 1)
-            sums_out[n] = dot(values, weights.astype(BF16), 0, 0)
-            stats_out[n, 0:1, :] = row_max
-            stats_out[n, 1:2, :] = jnp.sum(weights, 0, keepdims=True)
+    cases = [(h, p) for h in range(width // DH) for p in range(2)]
+    tokens = [part(p, 2 * rows) for h, p in cases]
+    keys, values = [
+        [
+            jnp.concatenate(
+                [near_set(kvs, p, part(h, DH), m), level3[part(m, rows), part(h, DH)]], 0
+            )
+            for h, p in cases
+        ]
+        for m in range(2)
+    ]
+    scores = [
+        dot(k, both(qgs, p, part(0, rows), part(h, DH)), 1, 1) * SCALE2
+        for k, (h, p) in zip(keys, cases)
+    ]
+    for (h, p), v, t in zip(cases, values, tokens):
+        dots_out[h, :, t] = dot(v, both(qgs, p, part(1, rows), part(h, DH)), 1, 1)
+    for n, ((h, p), t) in enumerate(zip(cases, tokens)):
+        row_max = jnp.max(scores[n], 0, keepdims=True)
+        weights = jnp.exp2(scores[n] - row_max)
+        weight_out[h, :, t] = weights
+        sums_out[h, :, t] = dot(values[n], weights.astype(BF16), 0, 0)
+        stats_out[h, 0:1, t] = row_max
+        stats_out[h, 1:2, t] = jnp.sum(weights, 0, keepdims=True)
+        keys_out[n] = keys[n]
 
 
 def far_grad_kernel(n_far, *refs):
     qgs, fars = refs[:PLANE], refs[PLANE : PLANE + n_far]
-    sums_ref, stats_ref = refs[PLANE + n_far : PLANE + n_far + 2]
-    outs = refs[PLANE + n_far + 2 :]
-    atts, grad_out, stats_out, far_out = outs[:PLANE], outs[PLANE], outs[PLANE + 1], outs[PLANE + 2 :]
+    weight_ref, dots_ref, sums_ref, stats_ref = refs[PLANE + n_far : PLANE + n_far + 4]
+    outs = refs[PLANE + n_far + 4 :]
+    ads, grad_out, stats_out, far_out = outs[:PLANE], outs[PLANE], outs[PLANE + 1], outs[PLANE + 2 :]
     rows, width = qgs[0].shape[0] // 2, qgs[0].shape[1]
-    for h in range(width // DH):
-        lanes = part(h, DH)
-        keys, values = far_set(fars, lanes, 0), far_set(fars, lanes, 1)
-        grads = []
-        for p in range(2):
-            n = 2 * h + p
-            q, g = both(qgs, p, part(0, rows), lanes), both(qgs, p, part(1, rows), lanes)
-            scores = dot(keys, q, 1, 1) * SCALE2
-            near_max = stats_ref[n, 0:1, :]
-            row_max = jnp.maximum(near_max, jnp.max(scores, 0, keepdims=True))
-            weights = jnp.exp2(scores - row_max)
-            near_part = jnp.exp2(near_max - row_max)
-            inverse = 1.0 / (
-                stats_ref[n, 1:2, :] * near_part + jnp.sum(weights, 0, keepdims=True)
+    level3 = slice(3 * rows, 4 * rows)
+    heads = range(width // DH)
+    lanes = [part(h, DH) for h in heads]
+    queries = [token_rows(qgs, 0, at) for at in lanes]
+    grads = [token_rows(qgs, 1, at) for at in lanes]
+    keys = [far_set(fars, at, 0) for at in lanes]
+    values = [far_set(fars, at, 1) for at in lanes]
+    scores = [dot(k, q, 1, 1) * SCALE2 for k, q in zip(keys, queries)]
+    dots = [dot(v, g, 1, 1) for v, g in zip(values, grads)]
+    weights, near_parts, inverses, sums = [], [], [], []
+    for h in heads:
+        near_max = stats_ref[h, 0:1, :]
+        row_max = jnp.maximum(near_max, jnp.max(scores[h], 0, keepdims=True))
+        weights.append(jnp.exp2(scores[h] - row_max))
+        near_parts.append(jnp.exp2(near_max - row_max))
+        sums.append(dot(values[h], weights[h].astype(BF16), 0, 0))
+        inverses.append(
+            1.0 / (stats_ref[h, 1:2, :] * near_parts[h] + jnp.sum(weights[h], 0, keepdims=True))
+        )
+    score_grads, probs = [], []
+    for h in heads:
+        attended = ((sums_ref[h] * near_parts[h] + sums[h]) * inverses[h]).astype(BF16)
+        delta = jnp.sum(grads[h].T.astype(F32) * attended.astype(F32), 0, keepdims=True)
+        near_scale = near_parts[h] * inverses[h]
+        near_probs = weight_ref[h, level3, :] * near_scale
+        far_probs = weights[h] * inverses[h]
+        score_grads.append(
+            jnp.concatenate(
+                [
+                    (near_probs * (dots_ref[h, level3, :] - delta)).astype(BF16),
+                    (far_probs * (dots[h] - delta)).astype(BF16),
+                ],
+                0,
             )
-            numerator = sums_ref[n] * near_part + dot(values, weights.astype(BF16), 0, 0)
-            attended = (numerator * inverse).astype(BF16)
-            delta = jnp.sum(g.T.astype(F32) * attended.astype(F32), 0, keepdims=True)
-            probabilities = weights * inverse
-            score_grad = (probabilities * (dot(values, g, 1, 1) - delta)).astype(BF16)
-            attended = attended.T
-            for k in range(2):
-                atts[2 * p + k][:, lanes] = attended[part(k, rows)]
-            grad_out[n] = score_grad
-            stats_out[n, 0:1, :] = near_part * inverse
-            stats_out[n, 1:2, :] = delta
-            grads.append((dot(score_grad, q) * SCALE, dot(probabilities.astype(BF16), g)))
-        for m in range(2):
-            whole, at = grads[0][m] + grads[1][m], 0
+        )
+        probs.append(jnp.concatenate([near_probs.astype(BF16), far_probs.astype(BF16)], 0))
+        grad_out[h] = score_grads[h][rows:]
+        stats_out[h, 0:1, :] = near_scale
+        stats_out[h, 1:2, :] = delta
+        attended = attended.T
+        for r in range(PLANE):
+            ads[r][:rows, lanes[h]] = attended[part(r, rows)]
+    for h in heads:
+        for m, whole in enumerate(
+            (dot(score_grads[h], queries[h]) * SCALE, dot(probs[h], grads[h]))
+        ):
+            at = 0
             for far in far_out:
                 size = far.shape[0] // 2
-                far[part(m, size), lanes] = whole[at : at + size].astype(BF16)
+                far[part(m, size), lanes[h]] = whole[at : at + size].astype(BF16)
                 at += size
 
 
 def plane_kernel(n_far, *refs):
-    kvs, qgs, fars = refs[:PLANE], refs[PLANE : 2 * PLANE], refs[2 * PLANE : 2 * PLANE + n_far]
-    weight_ref, dots_ref = refs[2 * PLANE + n_far : 2 * PLANE + n_far + 2]
-    refs = refs[2 * PLANE + n_far + 2 :]
-    atts, grad_ref, stats_ref = refs[:PLANE], refs[PLANE], refs[PLANE + 1]
-    ads, dkvs = refs[PLANE + 2 : 2 * PLANE + 2], refs[2 * PLANE + 2 :]
+    qgs, fars = refs[:PLANE], refs[PLANE : PLANE + n_far]
+    keys_ref, weight_ref, dots_ref, grad_ref, stats_ref = refs[PLANE + n_far : PLANE + n_far + 5]
+    refs = refs[2 * PLANE + n_far + 5 :]
+    ads, dkvs = refs[:PLANE], refs[PLANE:]
     rows, width = qgs[0].shape[0] // 2, qgs[0].shape[1]
     pair = 2 * rows
-    for r in range(PLANE):
-        ads[r][:rows, :] = atts[r][...]
+    cases = [(h, p) for h in range(width // DH) for p in range(2)]
+    score_grads, probs = [], []
+    for h, p in cases:
+        tokens = part(p, pair)
+        probabilities = weight_ref[h, :, tokens] * stats_ref[h, 0:1, tokens]
+        probs.append(probabilities.astype(BF16))
+        score_grads.append(
+            (probabilities * (dots_ref[h, :, tokens] - stats_ref[h, 1:2, tokens])).astype(BF16)
+        )
+    for n, (h, p) in enumerate(cases):
+        far_keys = far_set(fars, part(h, DH), 0)
+        dq = dot(keys_ref[n], score_grads[n], 0, 0)
+        dq = dq + dot(far_keys, grad_ref[h, :, part(p, pair)], 0, 0)
+        dq = (dq * SCALE).astype(BF16).T
+        for k in range(2):
+            ads[2 * p + k][rows:, part(h, DH)] = dq[part(k, rows)]
+    grads = []
+    for n, (h, p) in enumerate(cases):
+        q, g = [both(qgs, p, part(m, rows), part(h, DH)) for m in range(2)]
+        near = slice(0, 3 * rows)
+        grads.append((dot(score_grads[n][near], q) * SCALE, dot(probs[n][near], g)))
     for h in range(width // DH):
-        lanes = part(h, DH)
-        far_keys = far_set(fars, lanes, 0)
-        grads = []
-        for p in range(2):
-            n = 2 * h + p
-            q, g = both(qgs, p, part(0, rows), lanes), both(qgs, p, part(1, rows), lanes)
-            probabilities = weight_ref[n] * stats_ref[n, 0:1, :]
-            score_grad = (probabilities * (dots_ref[n] - stats_ref[n, 1:2, :])).astype(BF16)
-            dq = dot(near_set(kvs, p, lanes, 0), score_grad, 0, 0)
-            dq = ((dq + dot(far_keys, grad_ref[n], 0, 0)) * SCALE).astype(BF16).T
-            for k in range(2):
-                ads[2 * p + k][rows:, lanes] = dq[part(k, rows)]
-            grads.append((dot(score_grad, q) * SCALE, dot(probabilities.astype(BF16), g)))
         for m in range(2):
             for p in range(2):
-                pooled = grads[1 - p][m][pair:]
+                pooled = grads[2 * h + 1 - p][m][pair:]
                 for k in range(2):
-                    dkvs[2 * p + k][part(m, rows), lanes] = grads[p][m][part(k, rows)] + spread(
-                        pooled[part(k, rows // 2)], 2
-                    )
+                    dkvs[2 * p + k][part(m, rows), part(h, DH)] = grads[2 * h + p][m][
+                        part(k, rows)
+                    ] + spread(pooled[part(k, rows // 2)], 2)
 
 
 def carry_kernel(*refs):
@@ -289,9 +329,9 @@
     pairs = []
     for r in range(PLANE):
         here = columns(r, width)
-        pairs.append((ads[r].at[part(1, rows), :], gq_out.at[:, here]))
         pairs.append((dkvs[r].at[part(0, rows), :], gk_out.at[:, here]))
         pairs.append((dkvs[r].at[part(1, rows), :], gv_out.at[:, here]))
+        pairs.append((ads[r].at[part(1, rows), :], gq_out.at[:, here]))
     copies = start_all(pairs, sems)
     for n, other in enumerate(others):
         piece = part(n, rows // PIECES)
@@ -359,27 +399,28 @@
         for n in range(top_rounds):
             fars.append(xor_permute(span, 4 * PLANE << n))
             span = pool_both(join_both([span, fars[-1]]))
-    far_rows = sum(far.shape[0] for far in fars) // 2
-    cases = 2 * width // DH
-    weights, dots, sums, stats = call(
+    far_rows = sum(far.shape[0] for far in fars[1:]) // 2
+    heads, tokens = width // DH, PLANE * rows
+    weights, dots, sums, stats, near_keys = call(
         near_kernel,
-        [shape(cases, 3 * rows, 2 * rows, t=F32)] * 2
-        + [shape(cases, DH, 2 * rows, t=F32), shape(cases, 2, 2 * rows, t=F32)],
-        *key_values, *query_grads, cost_us=2.0, name="near_attention",
+        [shape(heads, 4 * rows, tokens, t=F32)] * 2
+        + [shape(heads, DH, tokens, t=F32), shape(heads, 2, tokens, t=F32)]
+        + [shape(2 * heads, 4 * rows, DH)],
+        *key_values, *query_grads, fars[0], cost_us=2.0, name="near_attention",
     )
     results = call(
-        lambda *refs: far_grad_kernel(len(fars), *refs),
-        [shape(rows, width)] * PLANE
-        + [shape(cases, far_rows, 2 * rows), shape(cases, 2, 2 * rows, t=F32)]
+        lambda *refs: far_grad_kernel(len(fars) - 1, *refs),
+        blocks + [shape(heads, far_rows, tokens), shape(heads, 2, tokens, t=F32)]
         + [shape(*far.shape) for far in fars],
-        *query_grads, *fars, sums, stats, cost_us=2.0, name="far_attention",
-    )
-    kept, far_grads = results[: PLANE + 2], list(results[PLANE + 2 :])
+        *query_grads, *fars[1:], weights, dots, sums, stats, cost_us=2.0, name="far_attention",
+    )
+    ads, kept, far_grads = results[:PLANE], results[PLANE : PLANE + 2], list(results[PLANE + 2 :])
+    first = PLANE + len(fars) + 4
     results = call(
-        lambda *refs: plane_kernel(len(fars), *refs),
+        lambda *refs: plane_kernel(len(fars) - 1, *refs),
         blocks + [shape(2 * rows, width, t=F32)] * PLANE,
-        *key_values, *query_grads, *fars, weights, dots, *kept,
-        cost_us=2.3, name="plane_grads",
+        *query_grads, *fars[1:], near_keys, weights, dots, *kept, *ads,
+        aliases={first + r: r for r in range(PLANE)}, cost_us=2.3, name="plane_grads",
     )
     att_dq, dkv = results[:PLANE], results[PLANE:]
     extra = []

time: 46.3 us -> 45.3 us (0.978)
  Pallas kernels: 11.7 us -> 10.2 us
  waiting for transfers between devices: 9.69 us -> 10.6 us
    pallas_call x9, Pallas kernels: 11.7 us -> 10.2 us  [call(): pl.pallas_call(lambda *refs: kernel(*refs[:count], *refs[count + len(afte...]
    ppermute x21, waiting for transfers between devices: 9.69 us -> 10.6 us  [xor_permute(): return lax.ppermute(block, axis, [(i, i ^ mask) for i in range(count)])]
  transfers between devices with their start and end apart: 21 -> 21, of which waited for: 9 -> 8; matrix products, arithmetic and copies ran while one was open for 0% -> 0% of each run, Pallas kernels for 19% -> 18%
where the time goes in v4:
time: 45.3 us; the launch traced here: 45.2 us
  starting transfers between devices  23.6 us (52%)
  waiting for transfers between devices  10.6 us (23%)
  Pallas kernels  10.2 us (23%)
  between operations  0.71 us (2%)
    ppermute x21, starting transfers between devices, xor_permute(): return lax.ppermute(block, axis, [(i, i ^ mask) for i in range(count)])  23.6 us
    ppermute x21, waiting for transfers between devices, xor_permute(): return lax.ppermute(block, axis, [(i, i ^ mask) for i in range(count)])  10.6 us
    pallas_call x9, Pallas kernels, call(): pl.pallas_call(lambda *refs: kernel(*refs[:count], *refs[count + len(afte...  10.2 us
  transfers between devices with their start and end apart: 21, of which 8 were waited for; matrix products, arithmetic and copies ran while one was open for 0% of the time, Pallas kernels for 18%

profile of v4, /device:TPU:0, one launch (start us, length us, event | category | flops | bytes accessed | tf_op | source)
XLA Modules:
  0.0 45.2 jit_solution(16983543404563381402)
XLA Ops:
  0.6 0.0 copy-start
  0.6 0.5 %collective-permute-start = (bf16[128,1024]{1,0:T(8,128)(2,1)}, bf16[128,1024]{1,0:T(8,128)(2,1)S(1)}, u32[]{:S(2)}, u32[]{:S(2)}) collective-permute-start(bf16[128,1024]{1,0:T(8,128)(2,1)} %refs_1_.2), channel_id=1, source_target_pairs={{0,1},{1,0},{2,3},{3,2},{4,5},{5,4},{6,7},{7,6},{8,9},{9,8},{10,11... | collective-permute-start | bytes 786440 | tf_op jit(solution)/shard_map/ppermute | solution.py:19
  1.2 1.4 %pack_keys_values.1 = (bf16[256,256]{1,0:T(8,128)(2,1)S(1)}, bf16[256,256]{1,0:T(8,128)(2,1)S(1)}, bf16[256,256]{1,0:T(8,128)(2,1)S(1)}, bf16[256,256]{1,0:T(8,128)(2,1)S(1)}) custom-call(bf16[128,1024]{1,0:T(8,128)(2,1)} %refs_0_.3, bf16[128,1024]{1,0:T(8,128)(2,1)} %refs_1_.3), custom_call_target="tpu_custom_call" | custom-call | flops 8000000000 | tf_op jit(solution)/shard_map/pack_keys_values/pallas_call | solution.py:57
  2.6 2.5 %collective-permute-start.4 = (bf16[256,256]{1,0:T(8,128)(2,1)S(1)}, bf16[256,256]{1,0:T(8,128)(2,1)S(1)}, u32[]{:S(2)}, u32[]{:S(2)}) collective-permute-start(bf16[256,256]{1,0:T(8,128)(2,1)S(1)} %get-tuple-element.48), channel_id=1, source_target_pairs={{0,2},{2,0},{4,6},{6,4},{8,10},{10,8},{12,14},{14,12},{16,18},{18,... | collective-permute-start | bytes 393224 | tf_op jit(solution)/shard_map/ppermute | solution.py:19
  5.0 1.5 %collective-permute-start.5 = (bf16[256,256]{1,0:T(8,128)(2,1)S(1)}, bf16[256,256]{1,0:T(8,128)(2,1)S(1)}, u32[]{:S(2)}, u32[]{:S(2)}) collective-permute-start(bf16[256,256]{1,0:T(8,128)(2,1)S(1)} %get-tuple-element.49), channel_id=1, source_target_pairs={{0,4},{2,6},{4,0},{6,2},{8,12},{10,14},{12,8},{14,10},{16,20},{18,... | collective-permute-start | bytes 393224 | tf_op jit(solution)/shard_map/ppermute | solution.py:19
  6.6 0.0 collective-permute-start.6
  6.6 0.0 collective-permute-done.refs_2_
  6.6 0.0 copy-done
  6.6 2.5 %grad_attended.1 = (bf16[256,256]{1,0:T(8,128)(2,1)S(1)}, bf16[256,256]{1,0:T(8,128)(2,1)S(1)}, bf16[256,256]{1,0:T(8,128)(2,1)S(1)}, bf16[256,256]{1,0:T(8,128)(2,1)S(1)}) custom-call(bf16[128,1024]{1,0:T(8,128)(2,1)} %refs_0_.2, bf16[128,1024]{1,0:T(8,128)(2,1)} %refs_1_.2, bf16[128,1024]{1,0:T(8,128)(2,1)S(1)} %collective-permute-done.refs_2_, ...), custom_call_target="tpu_custom_call" | custom-call | flops 3000000000 | tf_op jit(solution)/shard_map/grad_attended/pallas_call | solution.py:57
  9.1 2.0 %collective-permute-start.1 = (bf16[256,256]{1,0:T(8,128)(2,1)S(1)}, bf16[256,256]{1,0:T(8,128)(2,1)S(1)}, u32[]{:S(2)}, u32[]{:S(2)}) collective-permute-start(bf16[256,256]{1,0:T(8,128)(2,1)S(1)} %get-tuple-element.44), channel_id=1, source_target_pairs={{0,2},{2,0},{4,6},{6,4},{8,10},{10,8},{12,14},{14,12},{16,18},{18,... | collective-permute-start | bytes 393224 | tf_op jit(solution)/shard_map/ppermute | solution.py:19
  11.1 1.5 %collective-permute-start.2 = (bf16[256,256]{1,0:T(8,128)(2,1)S(1)}, bf16[256,256]{1,0:T(8,128)(2,1)S(1)}, u32[]{:S(2)}, u32[]{:S(2)}) collective-permute-start(bf16[256,256]{1,0:T(8,128)(2,1)S(1)} %get-tuple-element.45), channel_id=1, source_target_pairs={{0,4},{2,6},{4,0},{6,2},{8,12},{10,14},{12,8},{14,10},{16,20},{18,... | collective-permute-start | bytes 393224 | tf_op jit(solution)/shard_map/ppermute | solution.py:19
  12.6 0.0 collective-permute-done.4.refs_1_
  12.6 0.0 collective-permute-start.3
  12.6 1.0 %collective-permute-done.5.refs_2_ = bf16[256,256]{1,0:T(8,128)(2,1)S(1)} collective-permute-done((bf16[256,256]{1,0:T(8,128)(2,1)S(1)}, bf16[256,256]{1,0:T(8,128)(2,1)S(1)}, u32[]{:S(2)}, u32[]{:S(2)}) %collective-permute-start.5) | collective-permute-done | bytes 131104 | tf_op jit(solution)/shard_map/ppermute | solution.py:19
  13.7 0.1 collective-permute-done.6.refs_3_
  13.8 0.5 %pool_plane.1 = (bf16[256,256]{1,0:T(8,128)(2,1)S(1)}, bf16[128,256]{1,0:T(8,128)(2,1)S(1)}) custom-call(bf16[256,256]{1,0:T(8,128)(2,1)S(1)} %get-tuple-element.47.refs_0_, bf16[256,256]{1,0:T(8,128)(2,1)S(1)} %collective-permute-done.4.refs_1_, bf16[256,256]{1,0:T(8,128)(2,1)S(1)} %collective-permute-done.5.refs_2_, ...), custom_call_target="tpu_custom_call" | custom-call | flops 1000000000 | tf_op jit(solution)/shard_map/pool_plane/pallas_call | solution.py:57
  14.3 1.6 %collective-permute-start.9 = (bf16[256,256]{1,0:T(8,128)(2,1)S(1)}, bf16[256,256]{1,0:T(8,128)(2,1)S(1)}, u32[]{:S(2)}, u32[]{:S(2)}) collective-permute-start(bf16[256,256]{1,0:T(8,128)(2,1)S(1)} %get-tuple-element.52), channel_id=1, source_target_pairs={{0,8},{2,10},{4,12},{6,14},{8,0},{10,2},{12,4},{14,6},{16,24},{18,... | collective-permute-start | bytes 393224 | tf_op jit(solution)/shard_map/ppermute | solution.py:19
  15.9 2.5 %collective-permute-start.8 = (bf16[128,256]{1,0:T(8,128)(2,1)S(1)}, bf16[128,256]{1,0:T(8,128)(2,1)S(1)}, u32[]{:S(2)}, u32[]{:S(2)}) collective-permute-start(bf16[128,256]{1,0:T(8,128)(2,1)S(1)} %get-tuple-element.51), channel_id=1, source_target_pairs={{0,24},{2,26},{4,28},{6,30},{8,16},{10,18},{12,20},{14,22},{16,8},... | collective-permute-start | bytes 196616 | tf_op jit(solution)/shard_map/ppermute | solution.py:19
  18.4 0.0 collective-permute-done.1.refs_5_.refs_1_
  18.4 0.2 collective-permute-start.7
  18.6 0.7 %collective-permute-done.2.refs_6_.refs_2_ = bf16[256,256]{1,0:T(8,128)(2,1)S(1)} collective-permute-done((bf16[256,256]{1,0:T(8,128)(2,1)S(1)}, bf16[256,256]{1,0:T(8,128)(2,1)S(1)}, u32[]{:S(2)}, u32[]{:S(2)}) %collective-permute-start.2) | collective-permute-done | bytes 131104 | tf_op jit(solution)/shard_map/ppermute | solution.py:19
  19.3 0.0 collective-permute-done.3.refs_7_.refs_3_
  19.3 0.1 collective-permute-done.9.refs_8_
  19.4 1.4 %near_attention.1 = (f32[2,512,512]{2,1,0:T(8,128)S(1)}, f32[2,512,512]{2,1,0:T(8,128)S(1)}, f32[2,128,512]{2,1,0:T(8,128)S(1)}, f32[2,2,512]{2,1,0:T(2,128)S(1)}, bf16[4,512,128]{2,1,0:T(8,128)(2,1)S(1)}) custom-call(bf16[256,256]{1,0:T(8,128)(2,1)S(1)} %get-tuple-element.47.refs_0_, bf16[256,256]{1,0:T(8,128)(2,1)S(1)} %collective-permute-done.4.refs_1_, ...), custom_call_target="tpu_custom_call" | custom-call | flops 2000000000 | tf_op jit(solution)/shard_map/near_attention/pallas_call | solution.py:57
  20.8 2.4 %collective-permute-done.8.refs_5_ = bf16[128,256]{1,0:T(8,128)(2,1)S(1)} collective-permute-done((bf16[128,256]{1,0:T(8,128)(2,1)S(1)}, bf16[128,256]{1,0:T(8,128)(2,1)S(1)}, u32[]{:S(2)}, u32[]{:S(2)}) %collective-permute-start.8) | collective-permute-done | bytes 65568 | tf_op jit(solution)/shard_map/ppermute | solution.py:19
  23.1 1.4 %collective-permute-done.7.refs_4_ = bf16[128,256]{1,0:T(8,128)(2,1)S(1)} collective-permute-done((bf16[128,256]{1,0:T(8,128)(2,1)S(1)}, bf16[128,256]{1,0:T(8,128)(2,1)S(1)}, u32[]{:S(2)}, u32[]{:S(2)}) %collective-permute-start.7) | collective-permute-done | bytes 65568 | tf_op jit(solution)/shard_map/ppermute | solution.py:19
  24.6 1.1 %far_attention.1 = (bf16[256,256]{1,0:T(8,128)(2,1)S(1)}, bf16[256,256]{1,0:T(8,128)(2,1)S(1)}, bf16[256,256]{1,0:T(8,128)(2,1)S(1)}, bf16[256,256]{1,0:T(8,128)...) custom-call(bf16[256,256]{1,0:T(8,128)(2,1)S(1)} %get-tuple-element., ...), custom_call_target="tpu_custom_call" | custom-call | flops 2000000000 | tf_op jit(solution)/shard_map/far_attention/pallas_call | solution.py:57
  25.6 0.6 %collective-permute-start.14 = (bf16[128,256]{1,0:T(8,128)(2,1)S(1)}, bf16[128,256]{1,0:T(8,128)(2,1)S(1)}, u32[]{:S(2)}, u32[]{:S(2)}) collective-permute-start(bf16[128,256]{1,0:T(8,128)(2,1)S(1)} %get-tuple-element.73), channel_id=1, source_target_pairs={{0,16},{2,18},{4,20},{6,22},{8,24},{10,26},{12,28},{14,30},{16,0},... | collective-permute-start | bytes 196616 | tf_op jit(solution)/shard_map/ppermute | solution.py:19
  26.3 1.7 %collective-permute-start.15 = (bf16[128,256]{1,0:T(8,128)(2,1)S(1)}, bf16[128,256]{1,0:T(8,128)(2,1)S(1)}, u32[]{:S(2)}, u32[]{:S(2)}) collective-permute-start(bf16[128,256]{1,0:T(8,128)(2,1)S(1)} %get-tuple-element.74), channel_id=1, source_target_pairs={{0,24},{2,26},{4,28},{6,30},{8,16},{10,18},{12,20},{14,22},{16,8},... | collective-permute-start | bytes 196616 | tf_op jit(solution)/shard_map/ppermute | solution.py:19
  27.9 1.2 %collective-permute-start.13 = (bf16[256,256]{1,0:T(8,128)(2,1)S(1)}, bf16[256,256]{1,0:T(8,128)(2,1)S(1)}, u32[]{:S(2)}, u32[]{:S(2)}) collective-permute-start(bf16[256,256]{1,0:T(8,128)(2,1)S(1)} %get-tuple-element.72), channel_id=1, source_target_pairs={{0,8},{2,10},{4,12},{6,14},{8,0},{10,2},{12,4},{14,6},{16,24},{18,... | collective-permute-start | bytes 393224 | tf_op jit(solution)/shard_map/ppermute | solution.py:19
  29.2 1.2 %plane_grads.1 = (bf16[256,256]{1,0:T(8,128)(2,1)S(1)}, bf16[256,256]{1,0:T(8,128)(2,1)S(1)}, bf16[256,256]{1,0:T(8,128)(2,1)S(1)}, bf16[256,256]{1,0:T(8,128)(2...) custom-call(bf16[256,256]{1,0:T(8,128)(2,1)S(1)} %get-tuple-element., ...), custom_call_target="tpu_custom_call", output_to_operand_aliasing={{0}: (11, {}), {1}: (12, {}), {2}: (13, {}), {3}: (14, {})} | custom-call | flops 2300000000 | tf_op jit(solution)/shard_map/plane_grads/pallas_call | solution.py:57
  30.4 1.7 %collective-permute-start.10 = (bf16[256,256]{1,0:T(8,128)(2,1)S(1)}, bf16[256,256]{1,0:T(8,128)(2,1)S(1)}, u32[]{:S(2)}, u32[]{:S(2)}) collective-permute-start(bf16[256,256]{1,0:T(8,128)(2,1)S(1)} %get-tuple-element.65), channel_id=1, source_target_pairs={{0,2},{2,0},{4,6},{6,4},{8,10},{10,8},{12,14},{14,12},{16,18},{18,... | collective-permute-start | bytes 393224 | tf_op jit(solution)/shard_map/ppermute | solution.py:19
  32.1 0.6 %collective-permute-start.11 = (bf16[256,256]{1,0:T(8,128)(2,1)S(1)}, bf16[256,256]{1,0:T(8,128)(2,1)S(1)}, u32[]{:S(2)}, u32[]{:S(2)}) collective-permute-start(bf16[256,256]{1,0:T(8,128)(2,1)S(1)} %get-tuple-element.66), channel_id=1, source_target_pairs={{0,4},{2,6},{4,0},{6,2},{8,12},{10,14},{12,8},{14,10},{16,20},{18,... | collective-permute-start | bytes 393224 | tf_op jit(solution)/shard_map/ppermute | solution.py:19
  32.6 0.0 collective-permute-done.14.refs_5_
  32.6 1.3 %collective-permute-start.12 = (bf16[256,256]{1,0:T(8,128)(2,1)S(1)}, bf16[256,256]{1,0:T(8,128)(2,1)S(1)}, u32[]{:S(2)}, u32[]{:S(2)}) collective-permute-start(bf16[256,256]{1,0:T(8,128)(2,1)S(1)} %get-tuple-element.67), channel_id=1, source_target_pairs={{0,6},{2,4},{4,2},{6,0},{8,14},{10,12},{12,10},{14,8},{16,22},{18,... | collective-permute-start | bytes 393224 | tf_op jit(solution)/shard_map/ppermute | solution.py:19
  33.9 0.0 collective-permute-done.15.refs_6_
  33.9 0.0 collective-permute-done.13.refs_4_
  33.9 0.4 carry.1
  34.3 1.7 %collective-permute-start.18 = (bf16[256,256]{1,0:T(8,128)(2,1)S(1)}, bf16[256,256]{1,0:T(8,128)(2,1)S(1)}, u32[]{:S(2)}, u32[]{:S(2)}) collective-permute-start(bf16[256,256]{1,0:T(8,128)(2,1)S(1)} %get-tuple-element.79), channel_id=1, source_target_pairs={{0,2},{2,0},{4,6},{6,4},{8,10},{10,8},{12,14},{14,12},{16,18},{18,... | collective-permute-start | bytes 393224 | tf_op jit(solution)/shard_map/ppermute | solution.py:19
  36.1 0.9 %collective-permute-start.19 = (bf16[256,256]{1,0:T(8,128)(2,1)S(1)}, bf16[256,256]{1,0:T(8,128)(2,1)S(1)}, u32[]{:S(2)}, u32[]{:S(2)}) collective-permute-start(bf16[256,256]{1,0:T(8,128)(2,1)S(1)} %get-tuple-element.80), channel_id=1, source_target_pairs={{0,4},{2,6},{4,0},{6,2},{8,12},{10,14},{12,8},{14,10},{16,20},{18,... | collective-permute-start | bytes 393224 | tf_op jit(solution)/shard_map/ppermute | solution.py:19
  37.0 0.0 collective-permute-done.10.refs_1_.refs_4_
  37.0 0.9 %collective-permute-start.20 = (bf16[256,256]{1,0:T(8,128)(2,1)S(1)}, bf16[256,256]{1,0:T(8,128)(2,1)S(1)}, u32[]{:S(2)}, u32[]{:S(2)}) collective-permute-start(bf16[256,256]{1,0:T(8,128)(2,1)S(1)} %get-tuple-element.81), channel_id=1, source_target_pairs={{0,6},{2,4},{4,2},{6,0},{8,14},{10,12},{12,10},{14,8},{16,22},{18,... | collective-permute-start | bytes 393224 | tf_op jit(solution)/shard_map/ppermute | solution.py:19
  37.9 3.0 %collective-permute-done.11.refs_2_.refs_5_ = bf16[256,256]{1,0:T(8,128)(2,1)S(1)} collective-permute-done((bf16[256,256]{1,0:T(8,128)(2,1)S(1)}, bf16[256,256]{1,0:T(8,128)(2,1)S(1)}, u32[]{:S(2)}, u32[]{:S(2)}) %collective-permute-start.11) | collective-permute-done | bytes 131104 | tf_op jit(solution)/shard_map/ppermute | solution.py:19
  40.9 0.0 collective-permute-done.12.refs_3_.refs_6_
  40.9 0.7 %project.1 = (f32[128,1024]{1,0:T(8,128)S(1)}, bf16[64,1024]{1,0:T(8,128)(2,1)S(1)}, bf16[64,1024]{1,0:T(8,128)(2,1)S(1)}) custom-call(bf16[256,256]{1,0:T(8,128)(2,1)S(1)} %get-tuple-element.64.refs_0_.refs_3_, bf16[256,256]{1,0:T(8,128)(2,1)S(1)} %collective-permute-done.10.refs_1_.refs_4_, bf16[256,256]{1,0:T(8,128)(2,1)S(1)} %collective-permute-done.11.refs_2_.refs_5_, ...), custom_call_target="tpu_custom_call" | custom-call | flops 10000000 | tf_op jit(solution)/shard_map/project/pallas_call | solution.py:57
  41.7 0.1 collective-permute-start.16
  41.8 0.5 %collective-permute-start.17 = (bf16[64,1024]{1,0:T(8,128)(2,1)S(1)}, bf16[64,1024]{1,0:T(8,128)(2,1)S(1)}, u32[]{:S(2)}, u32[]{:S(2)}) collective-permute-start(bf16[64,1024]{1,0:T(8,128)(2,1)S(1)} %get-tuple-element.78), channel_id=1, source_target_pairs={{0,1},{1,0},{2,3},{3,2},{4,5},{5,4},{6,7},{7,6},{8,9},{9,8},{10,11... | collective-permute-start | bytes 393224 | tf_op jit(solution)/shard_map/ppermute | solution.py:19
  42.3 0.0 collective-permute-done.18.refs_8_
  42.3 1.8 %collective-permute-done.19.refs_9_ = bf16[256,256]{1,0:T(8,128)(2,1)S(1)} collective-permute-done((bf16[256,256]{1,0:T(8,128)(2,1)S(1)}, bf16[256,256]{1,0:T(8,128)(2,1)S(1)}, u32[]{:S(2)}, u32[]{:S(2)}) %collective-permute-start.19) | collective-permute-done | bytes 131104 | tf_op jit(solution)/shard_map/ppermute | solution.py:19
  44.1 0.0 collective-permute-done.20.refs_10_
  44.1 0.0 collective-permute-done.16.refs_1_
  44.1 0.0 collective-permute-done.17.refs_2_
  44.1 1.1 %join.1 = (bf16[128,1024]{1,0:T(8,128)(2,1)}, bf16[128,1024]{1,0:T(8,128)(2,1)}, bf16[128,1024]{1,0:T(8,128)(2,1)}, bf16[128,1024]{1,0:T(8,128)(2,1)}) custom-call(f32[128,1024]{1,0:T(8,128)S(1)} %get-tuple-element.76.refs_0_, bf16[64,1024]{1,0:T(8,128)(2,1)S(1)} %collective-permute-done.16.refs_1_, bf16[64,1024]{1,0:T(8,128)(2,1)S(1)} %collective-permute-done.17.refs_2_, ...), custom_call_target="tpu_custom_call" | custom-call | flops 1000000000 | tf_op jit(solution)/shard_map/join/pallas_call | solution.py:57
Async XLA Ops:
  0.6 5.9 %copy-start = (bf16[1024,2048]{1,0:T(8,128)(2,1)S(1)}, bf16[1024,2048]{1,0:T(8,128)(2,1)}, u32[]{:S(2)}) copy-start(bf16[1024,2048]{1,0:T(8,128)(2,1)} %refs_4_.1) | copy-start | bytes 12582916
  0.6 5.9 %collective-permute-start = (bf16[128,1024]{1,0:T(8,128)(2,1)}, bf16[128,1024]{1,0:T(8,128)(2,1)S(1)}, u32[]{:S(2)}, u32[]{:S(2)}) collective-permute-start(bf16[128,1024]{1,0:T(8,128)(2,1)} %refs_1_.2), channel_id=1, source_target_pairs={{0,1},{1,0},{2,3},{3,2},{4,5},{5,4},{6,7},{7,6},{8,9},{9,8},{10,11... | collective-permute-start | bytes 786440 | tf_op jit(solution)/shard_map/ppermute | solution.py:19
  2.6 10.1 %collective-permute-start.4 = (bf16[256,256]{1,0:T(8,128)(2,1)S(1)}, bf16[256,256]{1,0:T(8,128)(2,1)S(1)}, u32[]{:S(2)}, u32[]{:S(2)}) collective-permute-start(bf16[256,256]{1,0:T(8,128)(2,1)S(1)} %get-tuple-element.48), channel_id=1, source_target_pairs={{0,2},{2,0},{4,6},{6,4},{8,10},{10,8},{12,14},{14,12},{16,18},{18,... | collective-permute-start | bytes 393224 | tf_op jit(solution)/shard_map/ppermute | solution.py:19
  5.0 8.6 %collective-permute-start.5 = (bf16[256,256]{1,0:T(8,128)(2,1)S(1)}, bf16[256,256]{1,0:T(8,128)(2,1)S(1)}, u32[]{:S(2)}, u32[]{:S(2)}) collective-permute-start(bf16[256,256]{1,0:T(8,128)(2,1)S(1)} %get-tuple-element.49), channel_id=1, source_target_pairs={{0,4},{2,6},{4,0},{6,2},{8,12},{10,14},{12,8},{14,10},{16,20},{18,... | collective-permute-start | bytes 393224 | tf_op jit(solution)/shard_map/ppermute | solution.py:19
  6.6 7.3 %collective-permute-start.6 = (bf16[256,256]{1,0:T(8,128)(2,1)S(1)}, bf16[256,256]{1,0:T(8,128)(2,1)S(1)}, u32[]{:S(2)}, u32[]{:S(2)}) collective-permute-start(bf16[256,256]{1,0:T(8,128)(2,1)S(1)} %get-tuple-element.50), channel_id=1, source_target_pairs={{0,6},{2,4},{4,2},{6,0},{8,14},{10,12},{12,10},{14,8},{16,22},{18,... | collective-permute-start | bytes 393224 | tf_op jit(solution)/shard_map/ppermute | solution.py:19
  9.1 9.3 %collective-permute-start.1 = (bf16[256,256]{1,0:T(8,128)(2,1)S(1)}, bf16[256,256]{1,0:T(8,128)(2,1)S(1)}, u32[]{:S(2)}, u32[]{:S(2)}) collective-permute-start(bf16[256,256]{1,0:T(8,128)(2,1)S(1)} %get-tuple-element.44), channel_id=1, source_target_pairs={{0,2},{2,0},{4,6},{6,4},{8,10},{10,8},{12,14},{14,12},{16,18},{18,... | collective-permute-start | bytes 393224 | tf_op jit(solution)/shard_map/ppermute | solution.py:19
  11.1 8.2 %collective-permute-start.2 = (bf16[256,256]{1,0:T(8,128)(2,1)S(1)}, bf16[256,256]{1,0:T(8,128)(2,1)S(1)}, u32[]{:S(2)}, u32[]{:S(2)}) collective-permute-start(bf16[256,256]{1,0:T(8,128)(2,1)S(1)} %get-tuple-element.45), channel_id=1, source_target_pairs={{0,4},{2,6},{4,0},{6,2},{8,12},{10,14},{12,8},{14,10},{16,20},{18,... | collective-permute-start | bytes 393224 | tf_op jit(solution)/shard_map/ppermute | solution.py:19
  12.6 6.7 %collective-permute-start.3 = (bf16[256,256]{1,0:T(8,128)(2,1)S(1)}, bf16[256,256]{1,0:T(8,128)(2,1)S(1)}, u32[]{:S(2)}, u32[]{:S(2)}) collective-permute-start(bf16[256,256]{1,0:T(8,128)(2,1)S(1)} %get-tuple-element.46), channel_id=1, source_target_pairs={{0,6},{2,4},{4,2},{6,0},{8,14},{10,12},{12,10},{14,8},{16,22},{18,... | collective-permute-start | bytes 393224 | tf_op jit(solution)/shard_map/ppermute | solution.py:19
  14.3 5.1 %collective-permute-start.9 = (bf16[256,256]{1,0:T(8,128)(2,1)S(1)}, bf16[256,256]{1,0:T(8,128)(2,1)S(1)}, u32[]{:S(2)}, u32[]{:S(2)}) collective-permute-start(bf16[256,256]{1,0:T(8,128)(2,1)S(1)} %get-tuple-element.52), channel_id=1, source_target_pairs={{0,8},{2,10},{4,12},{6,14},{8,0},{10,2},{12,4},{14,6},{16,24},{18,... | collective-permute-start | bytes 393224 | tf_op jit(solution)/shard_map/ppermute | solution.py:19
  15.9 7.2 %collective-permute-start.8 = (bf16[128,256]{1,0:T(8,128)(2,1)S(1)}, bf16[128,256]{1,0:T(8,128)(2,1)S(1)}, u32[]{:S(2)}, u32[]{:S(2)}) collective-permute-start(bf16[128,256]{1,0:T(8,128)(2,1)S(1)} %get-tuple-element.51), channel_id=1, source_target_pairs={{0,24},{2,26},{4,28},{6,30},{8,16},{10,18},{12,20},{14,22},{16,8},... | collective-permute-start | bytes 196616 | tf_op jit(solution)/shard_map/ppermute | solution.py:19
  18.4 6.2 %collective-permute-start.7 = (bf16[128,256]{1,0:T(8,128)(2,1)S(1)}, bf16[128,256]{1,0:T(8,128)(2,1)S(1)}, u32[]{:S(2)}, u32[]{:S(2)}) collective-permute-start(bf16[128,256]{1,0:T(8,128)(2,1)S(1)} %get-tuple-element.51), channel_id=1, source_target_pairs={{0,16},{2,18},{4,20},{6,22},{8,24},{10,26},{12,28},{14,30},{16,0},... | collective-permute-start | bytes 196616 | tf_op jit(solution)/shard_map/ppermute | solution.py:19
  25.6 7.0 %collective-permute-start.14 = (bf16[128,256]{1,0:T(8,128)(2,1)S(1)}, bf16[128,256]{1,0:T(8,128)(2,1)S(1)}, u32[]{:S(2)}, u32[]{:S(2)}) collective-permute-start(bf16[128,256]{1,0:T(8,128)(2,1)S(1)} %get-tuple-element.73), channel_id=1, source_target_pairs={{0,16},{2,18},{4,20},{6,22},{8,24},{10,26},{12,28},{14,30},{16,0},... | collective-permute-start | bytes 196616 | tf_op jit(solution)/shard_map/ppermute | solution.py:19
  26.3 7.6 %collective-permute-start.15 = (bf16[128,256]{1,0:T(8,128)(2,1)S(1)}, bf16[128,256]{1,0:T(8,128)(2,1)S(1)}, u32[]{:S(2)}, u32[]{:S(2)}) collective-permute-start(bf16[128,256]{1,0:T(8,128)(2,1)S(1)} %get-tuple-element.74), channel_id=1, source_target_pairs={{0,24},{2,26},{4,28},{6,30},{8,16},{10,18},{12,20},{14,22},{16,8},... | collective-permute-start | bytes 196616 | tf_op jit(solution)/shard_map/ppermute | solution.py:19
  27.9 6.0 %collective-permute-start.13 = (bf16[256,256]{1,0:T(8,128)(2,1)S(1)}, bf16[256,256]{1,0:T(8,128)(2,1)S(1)}, u32[]{:S(2)}, u32[]{:S(2)}) collective-permute-start(bf16[256,256]{1,0:T(8,128)(2,1)S(1)} %get-tuple-element.72), channel_id=1, source_target_pairs={{0,8},{2,10},{4,12},{6,14},{8,0},{10,2},{12,4},{14,6},{16,24},{18,... | collective-permute-start | bytes 393224 | tf_op jit(solution)/shard_map/ppermute | solution.py:19
  30.4 6.6 %collective-permute-start.10 = (bf16[256,256]{1,0:T(8,128)(2,1)S(1)}, bf16[256,256]{1,0:T(8,128)(2,1)S(1)}, u32[]{:S(2)}, u32[]{:S(2)}) collective-permute-start(bf16[256,256]{1,0:T(8,128)(2,1)S(1)} %get-tuple-element.65), channel_id=1, source_target_pairs={{0,2},{2,0},{4,6},{6,4},{8,10},{10,8},{12,14},{14,12},{16,18},{18,... | collective-permute-start | bytes 393224 | tf_op jit(solution)/shard_map/ppermute | solution.py:19
  32.1 8.9 %collective-permute-start.11 = (bf16[256,256]{1,0:T(8,128)(2,1)S(1)}, bf16[256,256]{1,0:T(8,128)(2,1)S(1)}, u32[]{:S(2)}, u32[]{:S(2)}) collective-permute-start(bf16[256,256]{1,0:T(8,128)(2,1)S(1)} %get-tuple-element.66), channel_id=1, source_target_pairs={{0,4},{2,6},{4,0},{6,2},{8,12},{10,14},{12,8},{14,10},{16,20},{18,... | collective-permute-start | bytes 393224 | tf_op jit(solution)/shard_map/ppermute | solution.py:19
  32.6 8.3 %collective-permute-start.12 = (bf16[256,256]{1,0:T(8,128)(2,1)S(1)}, bf16[256,256]{1,0:T(8,128)(2,1)S(1)}, u32[]{:S(2)}, u32[]{:S(2)}) collective-permute-start(bf16[256,256]{1,0:T(8,128)(2,1)S(1)} %get-tuple-element.67), channel_id=1, source_target_pairs={{0,6},{2,4},{4,2},{6,0},{8,14},{10,12},{12,10},{14,8},{16,22},{18,... | collective-permute-start | bytes 393224 | tf_op jit(solution)/shard_map/ppermute | solution.py:19
  34.3 7.9 %collective-permute-start.18 = (bf16[256,256]{1,0:T(8,128)(2,1)S(1)}, bf16[256,256]{1,0:T(8,128)(2,1)S(1)}, u32[]{:S(2)}, u32[]{:S(2)}) collective-permute-start(bf16[256,256]{1,0:T(8,128)(2,1)S(1)} %get-tuple-element.79), channel_id=1, source_target_pairs={{0,2},{2,0},{4,6},{6,4},{8,10},{10,8},{12,14},{14,12},{16,18},{18,... | collective-permute-start | bytes 393224 | tf_op jit(solution)/shard_map/ppermute | solution.py:19
  36.1 8.0 %collective-permute-start.19 = (bf16[256,256]{1,0:T(8,128)(2,1)S(1)}, bf16[256,256]{1,0:T(8,128)(2,1)S(1)}, u32[]{:S(2)}, u32[]{:S(2)}) collective-permute-start(bf16[256,256]{1,0:T(8,128)(2,1)S(1)} %get-tuple-element.80), channel_id=1, source_target_pairs={{0,4},{2,6},{4,0},{6,2},{8,12},{10,14},{12,8},{14,10},{16,20},{18,... | collective-permute-start | bytes 393224 | tf_op jit(solution)/shard_map/ppermute | solution.py:19
  37.0 7.1 %collective-permute-start.20 = (bf16[256,256]{1,0:T(8,128)(2,1)S(1)}, bf16[256,256]{1,0:T(8,128)(2,1)S(1)}, u32[]{:S(2)}, u32[]{:S(2)}) collective-permute-start(bf16[256,256]{1,0:T(8,128)(2,1)S(1)} %get-tuple-element.81), channel_id=1, source_target_pairs={{0,6},{2,4},{4,2},{6,0},{8,14},{10,12},{12,10},{14,8},{16,22},{18,... | collective-permute-start | bytes 393224 | tf_op jit(solution)/shard_map/ppermute | solution.py:19
  41.7 2.4 %collective-permute-start.16 = (bf16[64,1024]{1,0:T(8,128)(2,1)S(1)}, bf16[64,1024]{1,0:T(8,128)(2,1)S(1)}, u32[]{:S(2)}, u32[]{:S(2)}) collective-permute-start(bf16[64,1024]{1,0:T(8,128)(2,1)S(1)} %get-tuple-element.77), channel_id=1, source_target_pairs={{0,1},{1,0},{2,3},{3,2},{4,5},{5,4},{6,7},{7,6},{8,9},{9,8},{10,11... | collective-permute-start | bytes 393224 | tf_op jit(solution)/shard_map/ppermute | solution.py:19
  41.8 2.3 %collective-permute-start.17 = (bf16[64,1024]{1,0:T(8,128)(2,1)S(1)}, bf16[64,1024]{1,0:T(8,128)(2,1)S(1)}, u32[]{:S(2)}, u32[]{:S(2)}) collective-permute-start(bf16[64,1024]{1,0:T(8,128)(2,1)S(1)} %get-tuple-element.78), channel_id=1, source_target_pairs={{0,1},{1,0},{2,3},{3,2},{4,5},{5,4},{6,7},{7,6},{8,9},{9,8},{10,11... | collective-permute-start | bytes 393224 | tf_op jit(solution)/shard_map/ppermute | solution.py:19

commit v5 on v4

--- a/solution.py
+++ b/solution.py
@@ -8,6 +8,7 @@
 DH = 128
 PLANE = 4
 PIECES = 2
+ORDER = (1, 2, 3)
 SCALE = DH ** (-0.5)
 SCALE2 = SCALE * 1.4426950408889634
 BF16 = jnp.bfloat16
@@ -118,16 +119,22 @@
         copy.wait()
 
 
+def average_matrix(rows, times):
+    out = lax.broadcasted_iota(jnp.int32, (rows // times, rows), 0)
+    src = lax.broadcasted_iota(jnp.int32, (rows // times, rows), 1)
+    return jnp.where(src // times == out, 1.0 / times, 0.0).astype(BF16)
+
+
 def far_kernel(*refs):
-    kvs, (near_out, far_out) = refs[:PLANE], refs[PLANE:]
+    kvs, outs = refs[:PLANE], refs[PLANE:]
     rows, width = kvs[0].shape[0] // 2, kvs[0].shape[1]
     wide = jnp.concatenate([kv[part(m, rows), :] for m in range(2) for kv in kvs], 1)
-    near = pool(pool(wide))
-    far = pool(near)
-    for out, pooled in ((near_out, near), (far_out, far)):
-        size = pooled.shape[0]
+    pooled = dot(
+        jnp.concatenate([average_matrix(rows, 4), average_matrix(rows, 8)], 0), wide
+    ).astype(BF16)
+    for out, first, size in zip(outs, (0, rows // 4), (rows // 4, rows // 8)):
         for n in range(2 * PLANE):
-            out[part(n, size), :] = pooled[:, part(n, width)]
+            out[part(n, size), :] = pooled[first : first + size, part(n, width)]
 
 
 def both(blocks, p, rows, lanes):
@@ -150,7 +157,7 @@
 
 
 def near_kernel(*refs):
-    kvs, qgs, level3 = refs[:PLANE], refs[PLANE : 2 * PLANE], refs[2 * PLANE]
+    kvs, qgs, first = refs[:PLANE], refs[PLANE : 2 * PLANE], refs[2 * PLANE]
     weight_out, dots_out, sums_out, stats_out, keys_out = refs[2 * PLANE + 1 :]
     rows, width = qgs[0].shape[0] // 2, qgs[0].shape[1]
     cases = [(h, p) for h in range(width // DH) for p in range(2)]
@@ -158,7 +165,7 @@
     keys, values = [
         [
             jnp.concatenate(
-                [near_set(kvs, p, part(h, DH), m), level3[part(m, rows), part(h, DH)]], 0
+                [near_set(kvs, p, part(h, DH), m), first[part(m, first.shape[0] // 2), part(h, DH)]], 0
             )
             for h, p in cases
         ]
@@ -186,7 +193,8 @@
     outs = refs[PLANE + n_far + 4 :]
     ads, grad_out, stats_out, far_out = outs[:PLANE], outs[PLANE], outs[PLANE + 1], outs[PLANE + 2 :]
     rows, width = qgs[0].shape[0] // 2, qgs[0].shape[1]
-    level3 = slice(3 * rows, 4 * rows)
+    first = slice(3 * rows, weight_ref.shape[1])
+    first_rows = weight_ref.shape[1] - 3 * rows
     heads = range(width // DH)
     lanes = [part(h, DH) for h in heads]
     queries = [token_rows(qgs, 0, at) for at in lanes]
@@ -210,19 +218,19 @@
         attended = ((sums_ref[h] * near_parts[h] + sums[h]) * inverses[h]).astype(BF16)
         delta = jnp.sum(grads[h].T.astype(F32) * attended.astype(F32), 0, keepdims=True)
         near_scale = near_parts[h] * inverses[h]
-        near_probs = weight_ref[h, level3, :] * near_scale
+        near_probs = weight_ref[h, first, :] * near_scale
         far_probs = weights[h] * inverses[h]
         score_grads.append(
             jnp.concatenate(
                 [
-                    (near_probs * (dots_ref[h, level3, :] - delta)).astype(BF16),
+                    (near_probs * (dots_ref[h, first, :] - delta)).astype(BF16),
                     (far_probs * (dots[h] - delta)).astype(BF16),
                 ],
                 0,
             )
         )
         probs.append(jnp.concatenate([near_probs.astype(BF16), far_probs.astype(BF16)], 0))
-        grad_out[h] = score_grads[h][rows:]
+        grad_out[h] = score_grads[h][first_rows:]
         stats_out[h, 0:1, :] = near_scale
         stats_out[h, 1:2, :] = delta
         attended = attended.T
@@ -267,29 +275,29 @@
         q, g = [both(qgs, p, part(m, rows), part(h, DH)) for m in range(2)]
         near = slice(0, 3 * rows)
         grads.append((dot(score_grads[n][near], q) * SCALE, dot(probs[n][near], g)))
-    for h in range(width // DH):
-        for m in range(2):
-            for p in range(2):
-                pooled = grads[2 * h + 1 - p][m][pair:]
-                for k in range(2):
-                    dkvs[2 * p + k][part(m, rows), part(h, DH)] = grads[2 * h + p][m][
-                        part(k, rows)
-                    ] + spread(pooled[part(k, rows // 2)], 2)
+    places = [
+        (h, m, p, k) for h in range(width // DH) for m in range(2) for p in range(2) for k in range(2)
+    ]
+    pooled = [
+        grads[2 * h + 1 - p][m][pair + k * rows // 2 : pair + (k + 1) * rows // 2]
+        for h, m, p, k in places
+    ]
+    carried = spread(jnp.concatenate(pooled, 1), 2)
+    for n, (h, m, p, k) in enumerate(places):
+        dkvs[2 * p + k][part(m, rows), part(h, DH)] = (
+            grads[2 * h + p][m][part(k, rows)] + carried[:, part(n, DH)]
+        )
 
 
 def carry_kernel(*refs):
-    dkvs, (near_ref, far2_ref, far3_ref) = refs[:PLANE], refs[PLANE : PLANE + 3]
-    extra, outs = refs[PLANE + 3 : -PLANE], refs[-PLANE:]
-    rows, width = near_ref.shape[0] // 2, near_ref.shape[1]
-    size = rows // PLANE
-    wide = lambda block, size: jnp.concatenate(
-        [block[part(n, size), :].astype(F32) for n in range(2 * PLANE)], 1
-    )
-    upper = far2_ref[...].astype(F32) + far3_ref[...].astype(F32)
-    for ref in extra:
-        upper = upper + ref[...].astype(F32)
-    whole = wide(near_ref, size) + spread(wide(upper, size // 2), 2)
-    carried = spread(whole, 4)
+    dkvs, far_refs, outs = refs[:PLANE], refs[PLANE:-PLANE], refs[-PLANE:]
+    rows, width = dkvs[0].shape[0] // 2, dkvs[0].shape[1]
+    wide, matrix = [], []
+    for far in far_refs:
+        size = far.shape[0] // (2 * PLANE)
+        wide.append(jnp.concatenate([far[part(n, size), :] for n in range(2 * PLANE)], 1))
+        matrix.append(spread_matrix(size, rows // size))
+    carried = dot(jnp.concatenate(matrix, 1), jnp.concatenate(wide, 0))
     for n in range(2 * PLANE):
         m, r = divmod(n, PLANE)
         outs[r][part(m, rows), :] = (
@@ -393,19 +401,21 @@
         far_kernel, [shape(2 * rows, width), shape(rows, width)], *key_values,
         after=(query_grads[0],), name="pool_plane",
     )
-    fars = [xor_permute(near, PLANE), xor_permute(pooled, 2 * PLANE), xor_permute(pooled, 3 * PLANE)]
+    fars = [xor_permute(near if n == 1 else pooled, n * PLANE) for n in ORDER]
     if top_rounds > 0:
-        span = pool_both(join_both([pooled, pool_both(fars[0]), fars[1], fars[2]]))
+        got = dict(zip(ORDER, fars))
+        span = pool_both(join_both([pooled, pool_both(got[1]), got[2], got[3]]))
         for n in range(top_rounds):
             fars.append(xor_permute(span, 4 * PLANE << n))
             span = pool_both(join_both([span, fars[-1]]))
     far_rows = sum(far.shape[0] for far in fars[1:]) // 2
     heads, tokens = width // DH, PLANE * rows
+    near_rows = 3 * rows + fars[0].shape[0] // 2
     weights, dots, sums, stats, near_keys = call(
         near_kernel,
-        [shape(heads, 4 * rows, tokens, t=F32)] * 2
+        [shape(heads, near_rows, tokens, t=F32)] * 2
         + [shape(heads, DH, tokens, t=F32), shape(heads, 2, tokens, t=F32)]
-        + [shape(2 * heads, 4 * rows, DH)],
+        + [shape(2 * heads, near_rows, DH)],
         *key_values, *query_grads, fars[0], cost_us=2.0, name="near_attention",
     )
     results = call(
@@ -435,10 +445,10 @@
             up = back if up is None else back + own_up
         ups = part_both(spread_both(up), PLANE)
         extra = [ups[0].astype(BF16)]
-        far_grads[0] = (far_grads[0].astype(F32) + spread_both(ups[1])).astype(BF16)
-        far_grads[1] = (far_grads[1].astype(F32) + ups[2]).astype(BF16)
-        far_grads[2] = (far_grads[2].astype(F32) + ups[3]).astype(BF16)
-    backs = [xor_permute(far_grads[n], (n + 1) * PLANE) for n in range(3)]
+        ups[1] = spread_both(ups[1])
+        for at, n in enumerate(ORDER):
+            far_grads[at] = (far_grads[at].astype(F32) + ups[n]).astype(BF16)
+    backs = [xor_permute(far_grads[at], n * PLANE) for at, n in enumerate(ORDER)]
     att_dq = plane_exchange(att_dq)
     dkv = call(carry_kernel, blocks, *dkv, *backs, *extra, cost_us=5.0, name="carry")
     own_sum, *other_sum = call(

time: 45.3 us -> 45.1 us (level)
  starting transfers between devices: 23.6 us -> 24.6 us
  waiting for transfers between devices: 10.6 us -> 9.68 us
    ppermute x21, starting transfers between devices: 23.6 us -> 24.6 us  [xor_permute(): return lax.ppermute(block, axis, [(i, i ^ mask) for i in range(count)])]
    ppermute x21, waiting for transfers between devices: 10.6 us -> 9.68 us  [xor_permute(): return lax.ppermute(block, axis, [(i, i ^ mask) for i in range(count)])]
  transfers between devices with their start and end apart: 21 -> 21, of which waited for: 8 -> 8; matrix products, arithmetic and copies ran while one was open for 0% -> 0% of each run, Pallas kernels for 18% -> 17%
where the time goes in v5:
time: 45.1 us; the launch traced here: 44.9 us
  starting transfers between devices  24.6 us (55%)
  Pallas kernels  9.9 us (22%)
  waiting for transfers between devices  9.68 us (21%)
  between operations  0.72 us (2%)
    ppermute x21, starting transfers between devices, xor_permute(): return lax.ppermute(block, axis, [(i, i ^ mask) for i in range(count)])  24.6 us
    pallas_call x9, Pallas kernels, call(): pl.pallas_call(lambda *refs: kernel(*refs[:count], *refs[count + len(afte...  9.9 us
    ppermute x21, waiting for transfers between devices, xor_permute(): return lax.ppermute(block, axis, [(i, i ^ mask) for i in range(count)])  9.68 us
  transfers between devices with their start and end apart: 21, of which 8 were waited for; matrix products, arithmetic and copies ran while one was open for 0% of the time, Pallas kernels for 17%

profile of v5, /device:TPU:0, one launch (start us, length us, event | category | flops | bytes accessed | tf_op | source)
XLA Modules:
  0.0 44.9 jit_solution(4948389522203757938)
XLA Ops:
  0.6 0.0 copy-start
  0.6 0.5 %collective-permute-start = (bf16[128,1024]{1,0:T(8,128)(2,1)}, bf16[128,1024]{1,0:T(8,128)(2,1)S(1)}, u32[]{:S(2)}, u32[]{:S(2)}) collective-permute-start(bf16[128,1024]{1,0:T(8,128)(2,1)} %refs_1_.2), channel_id=1, source_target_pairs={{0,1},{1,0},{2,3},{3,2},{4,5},{5,4},{6,7},{7,6},{8,9},{9,8},{10,11... | collective-permute-start | bytes 786440 | tf_op jit(solution)/shard_map/ppermute | solution.py:20
  1.2 1.4 %pack_keys_values.1 = (bf16[256,256]{1,0:T(8,128)(2,1)S(1)}, bf16[256,256]{1,0:T(8,128)(2,1)S(1)}, bf16[256,256]{1,0:T(8,128)(2,1)S(1)}, bf16[256,256]{1,0:T(8,128)(2,1)S(1)}) custom-call(bf16[128,1024]{1,0:T(8,128)(2,1)} %refs_0_.3, bf16[128,1024]{1,0:T(8,128)(2,1)} %refs_1_.3), custom_call_target="tpu_custom_call" | custom-call | flops 8000000000 | tf_op jit(solution)/shard_map/pack_keys_values/pallas_call | solution.py:58
  2.6 2.5 %collective-permute-start.4 = (bf16[256,256]{1,0:T(8,128)(2,1)S(1)}, bf16[256,256]{1,0:T(8,128)(2,1)S(1)}, u32[]{:S(2)}, u32[]{:S(2)}) collective-permute-start(bf16[256,256]{1,0:T(8,128)(2,1)S(1)} %get-tuple-element.48), channel_id=1, source_target_pairs={{0,2},{2,0},{4,6},{6,4},{8,10},{10,8},{12,14},{14,12},{16,18},{18,... | collective-permute-start | bytes 393224 | tf_op jit(solution)/shard_map/ppermute | solution.py:20
  5.0 1.5 %collective-permute-start.5 = (bf16[256,256]{1,0:T(8,128)(2,1)S(1)}, bf16[256,256]{1,0:T(8,128)(2,1)S(1)}, u32[]{:S(2)}, u32[]{:S(2)}) collective-permute-start(bf16[256,256]{1,0:T(8,128)(2,1)S(1)} %get-tuple-element.49), channel_id=1, source_target_pairs={{0,4},{2,6},{4,0},{6,2},{8,12},{10,14},{12,8},{14,10},{16,20},{18,... | collective-permute-start | bytes 393224 | tf_op jit(solution)/shard_map/ppermute | solution.py:20
  6.6 0.0 collective-permute-start.6
  6.6 0.0 collective-permute-done.refs_2_
  6.6 0.0 copy-done
  6.6 2.5 %grad_attended.1 = (bf16[256,256]{1,0:T(8,128)(2,1)S(1)}, bf16[256,256]{1,0:T(8,128)(2,1)S(1)}, bf16[256,256]{1,0:T(8,128)(2,1)S(1)}, bf16[256,256]{1,0:T(8,128)(2,1)S(1)}) custom-call(bf16[128,1024]{1,0:T(8,128)(2,1)} %refs_0_.2, bf16[128,1024]{1,0:T(8,128)(2,1)} %refs_1_.2, bf16[128,1024]{1,0:T(8,128)(2,1)S(1)} %collective-permute-done.refs_2_, ...), custom_call_target="tpu_custom_call" | custom-call | flops 3000000000 | tf_op jit(solution)/shard_map/grad_attended/pallas_call | solution.py:58
  9.1 2.0 %collective-permute-start.1 = (bf16[256,256]{1,0:T(8,128)(2,1)S(1)}, bf16[256,256]{1,0:T(8,128)(2,1)S(1)}, u32[]{:S(2)}, u32[]{:S(2)}) collective-permute-start(bf16[256,256]{1,0:T(8,128)(2,1)S(1)} %get-tuple-element.44), channel_id=1, source_target_pairs={{0,2},{2,0},{4,6},{6,4},{8,10},{10,8},{12,14},{14,12},{16,18},{18,... | collective-permute-start | bytes 393224 | tf_op jit(solution)/shard_map/ppermute | solution.py:20
  11.1 1.5 %collective-permute-start.2 = (bf16[256,256]{1,0:T(8,128)(2,1)S(1)}, bf16[256,256]{1,0:T(8,128)(2,1)S(1)}, u32[]{:S(2)}, u32[]{:S(2)}) collective-permute-start(bf16[256,256]{1,0:T(8,128)(2,1)S(1)} %get-tuple-element.45), channel_id=1, source_target_pairs={{0,4},{2,6},{4,0},{6,2},{8,12},{10,14},{12,8},{14,10},{16,20},{18,... | collective-permute-start | bytes 393224 | tf_op jit(solution)/shard_map/ppermute | solution.py:20
  12.6 0.0 collective-permute-done.4.refs_1_
  12.6 0.0 collective-permute-start.3
  12.6 1.0 %collective-permute-done.5.refs_2_ = bf16[256,256]{1,0:T(8,128)(2,1)S(1)} collective-permute-done((bf16[256,256]{1,0:T(8,128)(2,1)S(1)}, bf16[256,256]{1,0:T(8,128)(2,1)S(1)}, u32[]{:S(2)}, u32[]{:S(2)}) %collective-permute-start.5) | collective-permute-done | bytes 131104 | tf_op jit(solution)/shard_map/ppermute | solution.py:20
  13.7 0.1 collective-permute-done.6.refs_3_
  13.8 0.2 pool_plane.1
  14.0 1.6 %collective-permute-start.9 = (bf16[256,256]{1,0:T(8,128)(2,1)S(1)}, bf16[256,256]{1,0:T(8,128)(2,1)S(1)}, u32[]{:S(2)}, u32[]{:S(2)}) collective-permute-start(bf16[256,256]{1,0:T(8,128)(2,1)S(1)} %get-tuple-element.52), channel_id=1, source_target_pairs={{0,8},{2,10},{4,12},{6,14},{8,0},{10,2},{12,4},{14,6},{16,24},{18,... | collective-permute-start | bytes 393224 | tf_op jit(solution)/shard_map/ppermute | solution.py:20
  15.7 2.5 %collective-permute-start.8 = (bf16[128,256]{1,0:T(8,128)(2,1)S(1)}, bf16[128,256]{1,0:T(8,128)(2,1)S(1)}, u32[]{:S(2)}, u32[]{:S(2)}) collective-permute-start(bf16[128,256]{1,0:T(8,128)(2,1)S(1)} %get-tuple-element.51), channel_id=1, source_target_pairs={{0,24},{2,26},{4,28},{6,30},{8,16},{10,18},{12,20},{14,22},{16,8},... | collective-permute-start | bytes 196616 | tf_op jit(solution)/shard_map/ppermute | solution.py:20
  18.1 0.0 collective-permute-done.1.refs_5_.refs_1_
  18.2 0.4 collective-permute-start.7
  18.6 0.7 %collective-permute-done.2.refs_6_.refs_2_ = bf16[256,256]{1,0:T(8,128)(2,1)S(1)} collective-permute-done((bf16[256,256]{1,0:T(8,128)(2,1)S(1)}, bf16[256,256]{1,0:T(8,128)(2,1)S(1)}, u32[]{:S(2)}, u32[]{:S(2)}) %collective-permute-start.2) | collective-permute-done | bytes 131104 | tf_op jit(solution)/shard_map/ppermute | solution.py:20
  19.3 0.0 collective-permute-done.3.refs_7_.refs_3_
  19.3 0.0 collective-permute-done.9.refs_8_
  19.3 1.4 %near_attention.1 = (f32[2,512,512]{2,1,0:T(8,128)S(1)}, f32[2,512,512]{2,1,0:T(8,128)S(1)}, f32[2,128,512]{2,1,0:T(8,128)S(1)}, f32[2,2,512]{2,1,0:T(2,128)S(1)}, bf16[4,512,128]{2,1,0:T(8,128)(2,1)S(1)}) custom-call(bf16[256,256]{1,0:T(8,128)(2,1)S(1)} %get-tuple-element.47.refs_0_, bf16[256,256]{1,0:T(8,128)(2,1)S(1)} %collective-permute-done.4.refs_1_, ...), custom_call_target="tpu_custom_call" | custom-call | flops 2000000000 | tf_op jit(solution)/shard_map/near_attention/pallas_call | solution.py:58
  20.7 2.2 %collective-permute-done.8.refs_5_ = bf16[128,256]{1,0:T(8,128)(2,1)S(1)} collective-permute-done((bf16[128,256]{1,0:T(8,128)(2,1)S(1)}, bf16[128,256]{1,0:T(8,128)(2,1)S(1)}, u32[]{:S(2)}, u32[]{:S(2)}) %collective-permute-start.8) | collective-permute-done | bytes 65568 | tf_op jit(solution)/shard_map/ppermute | solution.py:20
  22.9 1.4 %collective-permute-done.7.refs_4_ = bf16[128,256]{1,0:T(8,128)(2,1)S(1)} collective-permute-done((bf16[128,256]{1,0:T(8,128)(2,1)S(1)}, bf16[128,256]{1,0:T(8,128)(2,1)S(1)}, u32[]{:S(2)}, u32[]{:S(2)}) %collective-permute-start.7) | collective-permute-done | bytes 65568 | tf_op jit(solution)/shard_map/ppermute | solution.py:20
  24.3 1.1 %far_attention.1 = (bf16[256,256]{1,0:T(8,128)(2,1)S(1)}, bf16[256,256]{1,0:T(8,128)(2,1)S(1)}, bf16[256,256]{1,0:T(8,128)(2,1)S(1)}, bf16[256,256]{1,0:T(8,128)...) custom-call(bf16[256,256]{1,0:T(8,128)(2,1)S(1)} %get-tuple-element., ...), custom_call_target="tpu_custom_call" | custom-call | flops 2000000000 | tf_op jit(solution)/shard_map/far_attention/pallas_call | solution.py:58
  25.4 0.7 %collective-permute-start.14 = (bf16[128,256]{1,0:T(8,128)(2,1)S(1)}, bf16[128,256]{1,0:T(8,128)(2,1)S(1)}, u32[]{:S(2)}, u32[]{:S(2)}) collective-permute-start(bf16[128,256]{1,0:T(8,128)(2,1)S(1)} %get-tuple-element.73), channel_id=1, source_target_pairs={{0,16},{2,18},{4,20},{6,22},{8,24},{10,26},{12,28},{14,30},{16,0},... | collective-permute-start | bytes 196616 | tf_op jit(solution)/shard_map/ppermute | solution.py:20
  26.1 1.7 %collective-permute-start.15 = (bf16[128,256]{1,0:T(8,128)(2,1)S(1)}, bf16[128,256]{1,0:T(8,128)(2,1)S(1)}, u32[]{:S(2)}, u32[]{:S(2)}) collective-permute-start(bf16[128,256]{1,0:T(8,128)(2,1)S(1)} %get-tuple-element.74), channel_id=1, source_target_pairs={{0,24},{2,26},{4,28},{6,30},{8,16},{10,18},{12,20},{14,22},{16,8},... | collective-permute-start | bytes 196616 | tf_op jit(solution)/shard_map/ppermute | solution.py:20
  27.8 1.2 %collective-permute-start.13 = (bf16[256,256]{1,0:T(8,128)(2,1)S(1)}, bf16[256,256]{1,0:T(8,128)(2,1)S(1)}, u32[]{:S(2)}, u32[]{:S(2)}) collective-permute-start(bf16[256,256]{1,0:T(8,128)(2,1)S(1)} %get-tuple-element.72), channel_id=1, source_target_pairs={{0,8},{2,10},{4,12},{6,14},{8,0},{10,2},{12,4},{14,6},{16,24},{18,... | collective-permute-start | bytes 393224 | tf_op jit(solution)/shard_map/ppermute | solution.py:20
  29.0 1.1 %plane_grads.1 = (bf16[256,256]{1,0:T(8,128)(2,1)S(1)}, bf16[256,256]{1,0:T(8,128)(2,1)S(1)}, bf16[256,256]{1,0:T(8,128)(2,1)S(1)}, bf16[256,256]{1,0:T(8,128)(2...) custom-call(bf16[256,256]{1,0:T(8,128)(2,1)S(1)} %get-tuple-element., ...), custom_call_target="tpu_custom_call", output_to_operand_aliasing={{0}: (11, {}), {1}: (12, {}), {2}: (13, {}), {3}: (14, {})} | custom-call | flops 2300000000 | tf_op jit(solution)/shard_map/plane_grads/pallas_call | solution.py:58
  30.1 1.7 %collective-permute-start.10 = (bf16[256,256]{1,0:T(8,128)(2,1)S(1)}, bf16[256,256]{1,0:T(8,128)(2,1)S(1)}, u32[]{:S(2)}, u32[]{:S(2)}) collective-permute-start(bf16[256,256]{1,0:T(8,128)(2,1)S(1)} %get-tuple-element.65), channel_id=1, source_target_pairs={{0,2},{2,0},{4,6},{6,4},{8,10},{10,8},{12,14},{14,12},{16,18},{18,... | collective-permute-start | bytes 393224 | tf_op jit(solution)/shard_map/ppermute | solution.py:20
  31.8 0.6 %collective-permute-start.11 = (bf16[256,256]{1,0:T(8,128)(2,1)S(1)}, bf16[256,256]{1,0:T(8,128)(2,1)S(1)}, u32[]{:S(2)}, u32[]{:S(2)}) collective-permute-start(bf16[256,256]{1,0:T(8,128)(2,1)S(1)} %get-tuple-element.66), channel_id=1, source_target_pairs={{0,4},{2,6},{4,0},{6,2},{8,12},{10,14},{12,8},{14,10},{16,20},{18,... | collective-permute-start | bytes 393224 | tf_op jit(solution)/shard_map/ppermute | solution.py:20
  32.4 0.0 collective-permute-done.14.refs_5_
  32.4 2.0 %collective-permute-start.12 = (bf16[256,256]{1,0:T(8,128)(2,1)S(1)}, bf16[256,256]{1,0:T(8,128)(2,1)S(1)}, u32[]{:S(2)}, u32[]{:S(2)}) collective-permute-start(bf16[256,256]{1,0:T(8,128)(2,1)S(1)} %get-tuple-element.67), channel_id=1, source_target_pairs={{0,6},{2,4},{4,2},{6,0},{8,14},{10,12},{12,10},{14,8},{16,22},{18,... | collective-permute-start | bytes 393224 | tf_op jit(solution)/shard_map/ppermute | solution.py:20
  34.4 0.0 collective-permute-done.15.refs_6_
  34.4 0.0 collective-permute-done.13.refs_4_
  34.4 0.3 carry.1
  34.8 1.0 %collective-permute-start.18 = (bf16[256,256]{1,0:T(8,128)(2,1)S(1)}, bf16[256,256]{1,0:T(8,128)(2,1)S(1)}, u32[]{:S(2)}, u32[]{:S(2)}) collective-permute-start(bf16[256,256]{1,0:T(8,128)(2,1)S(1)} %get-tuple-element.79), channel_id=1, source_target_pairs={{0,2},{2,0},{4,6},{6,4},{8,10},{10,8},{12,14},{14,12},{16,18},{18,... | collective-permute-start | bytes 393224 | tf_op jit(solution)/shard_map/ppermute | solution.py:20
  35.7 1.0 %collective-permute-start.19 = (bf16[256,256]{1,0:T(8,128)(2,1)S(1)}, bf16[256,256]{1,0:T(8,128)(2,1)S(1)}, u32[]{:S(2)}, u32[]{:S(2)}) collective-permute-start(bf16[256,256]{1,0:T(8,128)(2,1)S(1)} %get-tuple-element.80), channel_id=1, source_target_pairs={{0,4},{2,6},{4,0},{6,2},{8,12},{10,14},{12,8},{14,10},{16,20},{18,... | collective-permute-start | bytes 393224 | tf_op jit(solution)/shard_map/ppermute | solution.py:20
  36.8 0.0 collective-permute-done.10.refs_1_.refs_4_
  36.8 1.6 %collective-permute-start.20 = (bf16[256,256]{1,0:T(8,128)(2,1)S(1)}, bf16[256,256]{1,0:T(8,128)(2,1)S(1)}, u32[]{:S(2)}, u32[]{:S(2)}) collective-permute-start(bf16[256,256]{1,0:T(8,128)(2,1)S(1)} %get-tuple-element.81), channel_id=1, source_target_pairs={{0,6},{2,4},{4,2},{6,0},{8,14},{10,12},{12,10},{14,8},{16,22},{18,... | collective-permute-start | bytes 393224 | tf_op jit(solution)/shard_map/ppermute | solution.py:20
  38.3 0.0 collective-permute-done.11.refs_2_.refs_5_
  38.3 1.5 %collective-permute-done.12.refs_3_.refs_6_ = bf16[256,256]{1,0:T(8,128)(2,1)S(1)} collective-permute-done((bf16[256,256]{1,0:T(8,128)(2,1)S(1)}, bf16[256,256]{1,0:T(8,128)(2,1)S(1)}, u32[]{:S(2)}, u32[]{:S(2)}) %collective-permute-start.12) | collective-permute-done | bytes 131104 | tf_op jit(solution)/shard_map/ppermute | solution.py:20
  39.9 0.7 %project.1 = (f32[128,1024]{1,0:T(8,128)S(1)}, bf16[64,1024]{1,0:T(8,128)(2,1)S(1)}, bf16[64,1024]{1,0:T(8,128)(2,1)S(1)}) custom-call(bf16[256,256]{1,0:T(8,128)(2,1)S(1)} %get-tuple-element.64.refs_0_.refs_3_, bf16[256,256]{1,0:T(8,128)(2,1)S(1)} %collective-permute-done.10.refs_1_.refs_4_, bf16[256,256]{1,0:T(8,128)(2,1)S(1)} %collective-permute-done.11.refs_2_.refs_5_, ...), custom_call_target="tpu_custom_call" | custom-call | flops 10000000 | tf_op jit(solution)/shard_map/project/pallas_call | solution.py:58
  40.6 0.1 collective-permute-start.16
  40.7 0.5 %collective-permute-start.17 = (bf16[64,1024]{1,0:T(8,128)(2,1)S(1)}, bf16[64,1024]{1,0:T(8,128)(2,1)S(1)}, u32[]{:S(2)}, u32[]{:S(2)}) collective-permute-start(bf16[64,1024]{1,0:T(8,128)(2,1)S(1)} %get-tuple-element.78), channel_id=1, source_target_pairs={{0,1},{1,0},{2,3},{3,2},{4,5},{5,4},{6,7},{7,6},{8,9},{9,8},{10,11... | collective-permute-start | bytes 393224 | tf_op jit(solution)/shard_map/ppermute | solution.py:20
  41.2 0.1 collective-permute-done.18.refs_8_
  41.3 2.5 %collective-permute-done.19.refs_9_ = bf16[256,256]{1,0:T(8,128)(2,1)S(1)} collective-permute-done((bf16[256,256]{1,0:T(8,128)(2,1)S(1)}, bf16[256,256]{1,0:T(8,128)(2,1)S(1)}, u32[]{:S(2)}, u32[]{:S(2)}) %collective-permute-start.19) | collective-permute-done | bytes 131104 | tf_op jit(solution)/shard_map/ppermute | solution.py:20
  43.8 0.0 collective-permute-done.20.refs_10_
  43.8 0.0 collective-permute-done.16.refs_1_
  43.8 0.0 collective-permute-done.17.refs_2_
  43.8 1.1 %join.1 = (bf16[128,1024]{1,0:T(8,128)(2,1)}, bf16[128,1024]{1,0:T(8,128)(2,1)}, bf16[128,1024]{1,0:T(8,128)(2,1)}, bf16[128,1024]{1,0:T(8,128)(2,1)}) custom-call(f32[128,1024]{1,0:T(8,128)S(1)} %get-tuple-element.76.refs_0_, bf16[64,1024]{1,0:T(8,128)(2,1)S(1)} %collective-permute-done.16.refs_1_, bf16[64,1024]{1,0:T(8,128)(2,1)S(1)} %collective-permute-done.17.refs_2_, ...), custom_call_target="tpu_custom_call" | custom-call | flops 1000000000 | tf_op jit(solution)/shard_map/join/pallas_call | solution.py:58
Async XLA Ops:
  0.6 5.9 %copy-start = (bf16[1024,2048]{1,0:T(8,128)(2,1)S(1)}, bf16[1024,2048]{1,0:T(8,128)(2,1)}, u32[]{:S(2)}) copy-start(bf16[1024,2048]{1,0:T(8,128)(2,1)} %refs_4_.1) | copy-start | bytes 12582916
  0.6 5.9 %collective-permute-start = (bf16[128,1024]{1,0:T(8,128)(2,1)}, bf16[128,1024]{1,0:T(8,128)(2,1)S(1)}, u32[]{:S(2)}, u32[]{:S(2)}) collective-permute-start(bf16[128,1024]{1,0:T(8,128)(2,1)} %refs_1_.2), channel_id=1, source_target_pairs={{0,1},{1,0},{2,3},{3,2},{4,5},{5,4},{6,7},{7,6},{8,9},{9,8},{10,11... | collective-permute-start | bytes 786440 | tf_op jit(solution)/shard_map/ppermute | solution.py:20
  2.6 10.1 %collective-permute-start.4 = (bf16[256,256]{1,0:T(8,128)(2,1)S(1)}, bf16[256,256]{1,0:T(8,128)(2,1)S(1)}, u32[]{:S(2)}, u32[]{:S(2)}) collective-permute-start(bf16[256,256]{1,0:T(8,128)(2,1)S(1)} %get-tuple-element.48), channel_id=1, source_target_pairs={{0,2},{2,0},{4,6},{6,4},{8,10},{10,8},{12,14},{14,12},{16,18},{18,... | collective-permute-start | bytes 393224 | tf_op jit(solution)/shard_map/ppermute | solution.py:20
  5.0 8.6 %collective-permute-start.5 = (bf16[256,256]{1,0:T(8,128)(2,1)S(1)}, bf16[256,256]{1,0:T(8,128)(2,1)S(1)}, u32[]{:S(2)}, u32[]{:S(2)}) collective-permute-start(bf16[256,256]{1,0:T(8,128)(2,1)S(1)} %get-tuple-element.49), channel_id=1, source_target_pairs={{0,4},{2,6},{4,0},{6,2},{8,12},{10,14},{12,8},{14,10},{16,20},{18,... | collective-permute-start | bytes 393224 | tf_op jit(solution)/shard_map/ppermute | solution.py:20
  6.6 7.3 %collective-permute-start.6 = (bf16[256,256]{1,0:T(8,128)(2,1)S(1)}, bf16[256,256]{1,0:T(8,128)(2,1)S(1)}, u32[]{:S(2)}, u32[]{:S(2)}) collective-permute-start(bf16[256,256]{1,0:T(8,128)(2,1)S(1)} %get-tuple-element.50), channel_id=1, source_target_pairs={{0,6},{2,4},{4,2},{6,0},{8,14},{10,12},{12,10},{14,8},{16,22},{18,... | collective-permute-start | bytes 393224 | tf_op jit(solution)/shard_map/ppermute | solution.py:20
  9.1 9.1 %collective-permute-start.1 = (bf16[256,256]{1,0:T(8,128)(2,1)S(1)}, bf16[256,256]{1,0:T(8,128)(2,1)S(1)}, u32[]{:S(2)}, u32[]{:S(2)}) collective-permute-start(bf16[256,256]{1,0:T(8,128)(2,1)S(1)} %get-tuple-element.44), channel_id=1, source_target_pairs={{0,2},{2,0},{4,6},{6,4},{8,10},{10,8},{12,14},{14,12},{16,18},{18,... | collective-permute-start | bytes 393224 | tf_op jit(solution)/shard_map/ppermute | solution.py:20
  11.1 8.2 %collective-permute-start.2 = (bf16[256,256]{1,0:T(8,128)(2,1)S(1)}, bf16[256,256]{1,0:T(8,128)(2,1)S(1)}, u32[]{:S(2)}, u32[]{:S(2)}) collective-permute-start(bf16[256,256]{1,0:T(8,128)(2,1)S(1)} %get-tuple-element.45), channel_id=1, source_target_pairs={{0,4},{2,6},{4,0},{6,2},{8,12},{10,14},{12,8},{14,10},{16,20},{18,... | collective-permute-start | bytes 393224 | tf_op jit(solution)/shard_map/ppermute | solution.py:20
  12.6 6.7 %collective-permute-start.3 = (bf16[256,256]{1,0:T(8,128)(2,1)S(1)}, bf16[256,256]{1,0:T(8,128)(2,1)S(1)}, u32[]{:S(2)}, u32[]{:S(2)}) collective-permute-start(bf16[256,256]{1,0:T(8,128)(2,1)S(1)} %get-tuple-element.46), channel_id=1, source_target_pairs={{0,6},{2,4},{4,2},{6,0},{8,14},{10,12},{12,10},{14,8},{16,22},{18,... | collective-permute-start | bytes 393224 | tf_op jit(solution)/shard_map/ppermute | solution.py:20
  14.0 5.3 %collective-permute-start.9 = (bf16[256,256]{1,0:T(8,128)(2,1)S(1)}, bf16[256,256]{1,0:T(8,128)(2,1)S(1)}, u32[]{:S(2)}, u32[]{:S(2)}) collective-permute-start(bf16[256,256]{1,0:T(8,128)(2,1)S(1)} %get-tuple-element.52), channel_id=1, source_target_pairs={{0,8},{2,10},{4,12},{6,14},{8,0},{10,2},{12,4},{14,6},{16,24},{18,... | collective-permute-start | bytes 393224 | tf_op jit(solution)/shard_map/ppermute | solution.py:20
  15.7 7.2 %collective-permute-start.8 = (bf16[128,256]{1,0:T(8,128)(2,1)S(1)}, bf16[128,256]{1,0:T(8,128)(2,1)S(1)}, u32[]{:S(2)}, u32[]{:S(2)}) collective-permute-start(bf16[128,256]{1,0:T(8,128)(2,1)S(1)} %get-tuple-element.51), channel_id=1, source_target_pairs={{0,24},{2,26},{4,28},{6,30},{8,16},{10,18},{12,20},{14,22},{16,8},... | collective-permute-start | bytes 196616 | tf_op jit(solution)/shard_map/ppermute | solution.py:20
  18.2 6.2 %collective-permute-start.7 = (bf16[128,256]{1,0:T(8,128)(2,1)S(1)}, bf16[128,256]{1,0:T(8,128)(2,1)S(1)}, u32[]{:S(2)}, u32[]{:S(2)}) collective-permute-start(bf16[128,256]{1,0:T(8,128)(2,1)S(1)} %get-tuple-element.51), channel_id=1, source_target_pairs={{0,16},{2,18},{4,20},{6,22},{8,24},{10,26},{12,28},{14,30},{16,0},... | collective-permute-start | bytes 196616 | tf_op jit(solution)/shard_map/ppermute | solution.py:20
  25.4 7.0 %collective-permute-start.14 = (bf16[128,256]{1,0:T(8,128)(2,1)S(1)}, bf16[128,256]{1,0:T(8,128)(2,1)S(1)}, u32[]{:S(2)}, u32[]{:S(2)}) collective-permute-start(bf16[128,256]{1,0:T(8,128)(2,1)S(1)} %get-tuple-element.73), channel_id=1, source_target_pairs={{0,16},{2,18},{4,20},{6,22},{8,24},{10,26},{12,28},{14,30},{16,0},... | collective-permute-start | bytes 196616 | tf_op jit(solution)/shard_map/ppermute | solution.py:20
  26.1 8.3 %collective-permute-start.15 = (bf16[128,256]{1,0:T(8,128)(2,1)S(1)}, bf16[128,256]{1,0:T(8,128)(2,1)S(1)}, u32[]{:S(2)}, u32[]{:S(2)}) collective-permute-start(bf16[128,256]{1,0:T(8,128)(2,1)S(1)} %get-tuple-element.74), channel_id=1, source_target_pairs={{0,24},{2,26},{4,28},{6,30},{8,16},{10,18},{12,20},{14,22},{16,8},... | collective-permute-start | bytes 196616 | tf_op jit(solution)/shard_map/ppermute | solution.py:20
  27.8 6.7 %collective-permute-start.13 = (bf16[256,256]{1,0:T(8,128)(2,1)S(1)}, bf16[256,256]{1,0:T(8,128)(2,1)S(1)}, u32[]{:S(2)}, u32[]{:S(2)}) collective-permute-start(bf16[256,256]{1,0:T(8,128)(2,1)S(1)} %get-tuple-element.72), channel_id=1, source_target_pairs={{0,8},{2,10},{4,12},{6,14},{8,0},{10,2},{12,4},{14,6},{16,24},{18,... | collective-permute-start | bytes 393224 | tf_op jit(solution)/shard_map/ppermute | solution.py:20
  30.1 6.6 %collective-permute-start.10 = (bf16[256,256]{1,0:T(8,128)(2,1)S(1)}, bf16[256,256]{1,0:T(8,128)(2,1)S(1)}, u32[]{:S(2)}, u32[]{:S(2)}) collective-permute-start(bf16[256,256]{1,0:T(8,128)(2,1)S(1)} %get-tuple-element.65), channel_id=1, source_target_pairs={{0,2},{2,0},{4,6},{6,4},{8,10},{10,8},{12,14},{14,12},{16,18},{18,... | collective-permute-start | bytes 393224 | tf_op jit(solution)/shard_map/ppermute | solution.py:20
  31.8 6.5 %collective-permute-start.11 = (bf16[256,256]{1,0:T(8,128)(2,1)S(1)}, bf16[256,256]{1,0:T(8,128)(2,1)S(1)}, u32[]{:S(2)}, u32[]{:S(2)}) collective-permute-start(bf16[256,256]{1,0:T(8,128)(2,1)S(1)} %get-tuple-element.66), channel_id=1, source_target_pairs={{0,4},{2,6},{4,0},{6,2},{8,12},{10,14},{12,8},{14,10},{16,20},{18,... | collective-permute-start | bytes 393224 | tf_op jit(solution)/shard_map/ppermute | solution.py:20
  32.4 7.5 %collective-permute-start.12 = (bf16[256,256]{1,0:T(8,128)(2,1)S(1)}, bf16[256,256]{1,0:T(8,128)(2,1)S(1)}, u32[]{:S(2)}, u32[]{:S(2)}) collective-permute-start(bf16[256,256]{1,0:T(8,128)(2,1)S(1)} %get-tuple-element.67), channel_id=1, source_target_pairs={{0,6},{2,4},{4,2},{6,0},{8,14},{10,12},{12,10},{14,8},{16,22},{18,... | collective-permute-start | bytes 393224 | tf_op jit(solution)/shard_map/ppermute | solution.py:20
  34.8 6.5 %collective-permute-start.18 = (bf16[256,256]{1,0:T(8,128)(2,1)S(1)}, bf16[256,256]{1,0:T(8,128)(2,1)S(1)}, u32[]{:S(2)}, u32[]{:S(2)}) collective-permute-start(bf16[256,256]{1,0:T(8,128)(2,1)S(1)} %get-tuple-element.79), channel_id=1, source_target_pairs={{0,2},{2,0},{4,6},{6,4},{8,10},{10,8},{12,14},{14,12},{16,18},{18,... | collective-permute-start | bytes 393224 | tf_op jit(solution)/shard_map/ppermute | solution.py:20
  35.7 8.1 %collective-permute-start.19 = (bf16[256,256]{1,0:T(8,128)(2,1)S(1)}, bf16[256,256]{1,0:T(8,128)(2,1)S(1)}, u32[]{:S(2)}, u32[]{:S(2)}) collective-permute-start(bf16[256,256]{1,0:T(8,128)(2,1)S(1)} %get-tuple-element.80), channel_id=1, source_target_pairs={{0,4},{2,6},{4,0},{6,2},{8,12},{10,14},{12,8},{14,10},{16,20},{18,... | collective-permute-start | bytes 393224 | tf_op jit(solution)/shard_map/ppermute | solution.py:20
  36.8 7.1 %collective-permute-start.20 = (bf16[256,256]{1,0:T(8,128)(2,1)S(1)}, bf16[256,256]{1,0:T(8,128)(2,1)S(1)}, u32[]{:S(2)}, u32[]{:S(2)}) collective-permute-start(bf16[256,256]{1,0:T(8,128)(2,1)S(1)} %get-tuple-element.81), channel_id=1, source_target_pairs={{0,6},{2,4},{4,2},{6,0},{8,14},{10,12},{12,10},{14,8},{16,22},{18,... | collective-permute-start | bytes 393224 | tf_op jit(solution)/shard_map/ppermute | solution.py:20
  40.6 3.2 %collective-permute-start.16 = (bf16[64,1024]{1,0:T(8,128)(2,1)S(1)}, bf16[64,1024]{1,0:T(8,128)(2,1)S(1)}, u32[]{:S(2)}, u32[]{:S(2)}) collective-permute-start(bf16[64,1024]{1,0:T(8,128)(2,1)S(1)} %get-tuple-element.77), channel_id=1, source_target_pairs={{0,1},{1,0},{2,3},{3,2},{4,5},{5,4},{6,7},{7,6},{8,9},{9,8},{10,11... | collective-permute-start | bytes 393224 | tf_op jit(solution)/shard_map/ppermute | solution.py:20
  40.7 3.1 %collective-permute-start.17 = (bf16[64,1024]{1,0:T(8,128)(2,1)S(1)}, bf16[64,1024]{1,0:T(8,128)(2,1)S(1)}, u32[]{:S(2)}, u32[]{:S(2)}) collective-permute-start(bf16[64,1024]{1,0:T(8,128)(2,1)S(1)} %get-tuple-element.78), channel_id=1, source_target_pairs={{0,1},{1,0},{2,3},{3,2},{4,5},{5,4},{6,7},{7,6},{8,9},{9,8},{10,11... | collective-permute-start | bytes 393224 | tf_op jit(solution)/shard_map/ppermute | solution.py:20

commit v6 on v5

--- a/solution.py
+++ b/solution.py
@@ -8,6 +8,7 @@
 DH = 128
 PLANE = 4
 PIECES = 2
+FARTHEST = (3, 1, 2, 0)
 ORDER = (1, 2, 3)
 SCALE = DH ** (-0.5)
 SCALE2 = SCALE * 1.4426950408889634
@@ -46,7 +47,7 @@
     return dot(spread_matrix(block.shape[0], times), block.astype(BF16))
 
 
-def call(kernel, outs, *args, after=(), aliases={}, hbm=(), hbm_out=False, scratch=(), cost_us=1.0, name=None):
+def call(kernel, outs, *args, planes=(), after=(), aliases={}, hbm=(), hbm_out=False, scratch=(), cost_us=1.0, name=None):
     vmem = pl.BlockSpec(memory_space=pltpu.VMEM)
     in_hbm = pl.BlockSpec(memory_space=pltpu.HBM)
     space = pltpu.HBM if hbm_out else pltpu.VMEM
@@ -55,20 +56,28 @@
         for n, a in enumerate(args)
     ]
     count = len(args)
+    order = list(range(count))
+    for first in planes:
+        order[first : first + PLANE] = [first + r for r in FARTHEST]
+    places = [order.index(n) for n in range(count)]
+
+    def run(*refs):
+        kernel(*[refs[at] for at in places], *refs[count + len(after) :])
+
     return pl.pallas_call(
-        lambda *refs: kernel(*refs[:count], *refs[count + len(after) :]),
+        run,
         out_shape=[space(out.shape, out.dtype) for out in outs],
-        in_specs=[in_hbm if n in hbm else vmem for n in range(count)]
+        in_specs=[in_hbm if n in hbm else vmem for n in order]
         + [pl.BlockSpec(memory_space=pl.ANY)] * len(after),
         scratch_shapes=scratch,
-        input_output_aliases=aliases,
+        input_output_aliases={places[n]: out for n, out in aliases.items()},
         out_specs=[in_hbm if hbm_out else vmem] * len(outs),
         compiler_params=pltpu.CompilerParams(vmem_limit_bytes=24 * 1024 * 1024),
         cost_estimate=pl.CostEstimate(
             flops=int(cost_us * 1e9), bytes_accessed=0, transcendentals=0
         ),
         name=name,
-    )(*args, *after)
+    )(*[args[n] for n in order], *after)
 
 
 def part(n, width):
@@ -98,25 +107,19 @@
         copy.wait()
 
 
-def cotangent_kernel(q_ref, own_ref, other_ref, w_ref, *refs):
-    outs, own, sems = refs[:PLANE], *refs[PLANE:]
+def cotangent_kernel(q_ref, own_ref, other_ref, w_ref, *outs):
     rows, width = q_ref.shape[0], q_ref.shape[1] // PLANE
     half = own_ref.shape[1]
     head = lax.axis_index("head")
     own_at = pl.ds(pl.multiple_of(head * half, half), half)
     other_at = pl.ds(pl.multiple_of((1 - head) * half, half), half)
-    here = [columns(r, width) for r in range(PLANE)]
-    pairs = [(own_ref, own)]
-    pairs += [(q_ref.at[:, here[r]], outs[r].at[part(0, rows), :]) for r in range(PLANE)]
-    copies = start_all(pairs, sems)
-    copies[0].wait()
     for r in range(PLANE):
+        here = columns(r, width)
+        outs[r][:rows, :] = q_ref[:, here]
         outs[r][rows:, :] = (
-            dot(own[...], w_ref[here[r], own_at], 1, 1)
-            + dot(other_ref[...], w_ref[here[r], other_at], 1, 1)
+            dot(own_ref[...], w_ref[here, own_at], 1, 1)
+            + dot(other_ref[...], w_ref[here, other_at], 1, 1)
         ).astype(BF16)
-    for copy in copies[1:]:
-        copy.wait()
 
 
 def average_matrix(rows, times):
@@ -132,7 +135,7 @@
     pooled = dot(
         jnp.concatenate([average_matrix(rows, 4), average_matrix(rows, 8)], 0), wide
     ).astype(BF16)
-    for out, first, size in zip(outs, (0, rows // 4), (rows // 4, rows // 8)):
+    for out, first, size in zip(outs, (0, rows // 4, rows // 4), (rows // 4, rows // 8, rows // 8)):
         for n in range(2 * PLANE):
             out[part(n, size), :] = pooled[first : first + size, part(n, width)]
 
@@ -393,15 +396,14 @@
     key_values = plane_exchange(key_values)
     query_grads = call(
         cotangent_kernel, blocks, queries, cotangent, other_cotangent, out_weight,
-        hbm=(0, 1), scratch=[pltpu.VMEM(cotangent.shape, BF16), dma(1 + PLANE)],
         cost_us=3.0, name="grad_attended",
     )
     query_grads = plane_exchange(query_grads)
-    near, pooled = call(
-        far_kernel, [shape(2 * rows, width), shape(rows, width)], *key_values,
-        after=(query_grads[0],), name="pool_plane",
-    )
-    fars = [xor_permute(near if n == 1 else pooled, n * PLANE) for n in ORDER]
+    near, pooled, pooled3 = call(
+        far_kernel, [shape(2 * rows, width)] + [shape(rows, width)] * 2, *key_values, planes=(0,),
+        after=(query_grads[0],), cost_us=1.0, name="pool_plane",
+    )
+    fars = [xor_permute({1: near, 2: pooled, 3: pooled3}[n], n * PLANE) for n in ORDER]
     if top_rounds > 0:
         got = dict(zip(ORDER, fars))
         span = pool_both(join_both([pooled, pool_both(got[1]), got[2], got[3]]))
@@ -416,13 +418,13 @@
         [shape(heads, near_rows, tokens, t=F32)] * 2
         + [shape(heads, DH, tokens, t=F32), shape(heads, 2, tokens, t=F32)]
         + [shape(2 * heads, near_rows, DH)],
-        *key_values, *query_grads, fars[0], cost_us=2.0, name="near_attention",
+        *key_values, *query_grads, fars[0], planes=(0, PLANE), cost_us=2.0, name="near_attention",
     )
     results = call(
         lambda *refs: far_grad_kernel(len(fars) - 1, *refs),
         blocks + [shape(heads, far_rows, tokens), shape(heads, 2, tokens, t=F32)]
         + [shape(*far.shape) for far in fars],
-        *query_grads, *fars[1:], weights, dots, sums, stats, cost_us=2.0, name="far_attention",
+        *query_grads, *fars[1:], weights, dots, sums, stats, planes=(0,), cost_us=2.0, name="far_attention",
     )
     ads, kept, far_grads = results[:PLANE], results[PLANE : PLANE + 2], list(results[PLANE + 2 :])
     first = PLANE + len(fars) + 4
@@ -454,14 +456,14 @@
     own_sum, *other_sum = call(
         output_kernel,
         [shape(rows, features, t=F32)] + [shape(rows // PIECES, features)] * PIECES,
-        *att_dq, out_weight, after=(dkv[0],), cost_us=0.01, name="project",
+        *att_dq, out_weight, planes=(0,), after=(dkv[0],), cost_us=0.01, name="project",
     )
     dkv = plane_exchange(dkv)
     other_sum = [xor_permute(piece, 1, "head") for piece in other_sum]
     output, grad_queries, grad_keys, grad_values = call(
-        join_kernel, [shape(rows, features)] * 4, own_sum, *other_sum, *att_dq, *dkv,
+        join_kernel, [shape(rows, features)] * 4, own_sum, *other_sum, *att_dq, *dkv, planes=(1 + PIECES, 1 + PIECES + PLANE),
         hbm_out=True, scratch=[pltpu.VMEM((rows, features), BF16), dma(3 * PLANE + 1)],
-        name="join",
+        cost_us=1.0, name="join",
     )
     return (output, grad_queries, grad_keys, grad_values)
 

time: 45.1 us -> 44.3 us (0.982)
  starting transfers between devices: 24.6 us -> 27.2 us
  waiting for transfers between devices: 9.68 us -> 7.29 us
  Pallas kernels: 9.9 us -> 8.91 us
    ppermute x21, starting transfers between devices: 24.6 us -> 27.2 us  [xor_permute(): return lax.ppermute(block, axis, [(i, i ^ mask) for i in range(count)])]
    ppermute x21, waiting for transfers between devices: 9.68 us -> 7.29 us  [xor_permute(): return lax.ppermute(block, axis, [(i, i ^ mask) for i in range(count)])]
    pallas_call x9, Pallas kernels: 9.9 us -> 8.91 us  [call(): pl.pallas_call(run, out_shape=[space(out.shape, out.dtype) for out in out...]
  transfers between devices with their start and end apart: 21 -> 21, of which waited for: 8 -> 8; matrix products, arithmetic and copies ran while one was open for 0% -> 0% of each run, Pallas kernels for 17% -> 15%
where the time goes in v6:
time: 44.3 us; the launch traced here: 44.1 us
  starting transfers between devices  27.2 us (61%)
  Pallas kernels  8.91 us (20%)
  waiting for transfers between devices  7.29 us (16%)
  between operations  0.75 us (2%)
    ppermute x21, starting transfers between devices, xor_permute(): return lax.ppermute(block, axis, [(i, i ^ mask) for i in range(count)])  27.2 us
    pallas_call x9, Pallas kernels, call(): pl.pallas_call(run, out_shape=[space(out.shape, out.dtype) for out in out...  8.91 us
    ppermute x21, waiting for transfers between devices, xor_permute(): return lax.ppermute(block, axis, [(i, i ^ mask) for i in range(count)])  7.29 us
  transfers between devices with their start and end apart: 21, of which 8 were waited for; matrix products, arithmetic and copies ran while one was open for 0% of the time, Pallas kernels for 15%

profile of v6, /device:TPU:0, one launch (start us, length us, event | category | flops | bytes accessed | tf_op | source)
XLA Modules:
  0.0 44.1 jit_solution(10572447415211700893)
XLA Ops:
  0.6 0.0 copy-start.2
  0.6 0.0 copy-start
  0.7 0.0 copy-start.1
  0.7 0.5 %collective-permute-start = (bf16[128,1024]{1,0:T(8,128)(2,1)}, bf16[128,1024]{1,0:T(8,128)(2,1)S(1)}, u32[]{:S(2)}, u32[]{:S(2)}) collective-permute-start(bf16[128,1024]{1,0:T(8,128)(2,1)} %refs_1_.2), channel_id=1, source_target_pairs={{0,1},{1,0},{2,3},{3,2},{4,5},{5,4},{6,7},{7,6},{8,9},{9,8},{10,11... | collective-permute-start | bytes 786440 | tf_op jit(solution)/shard_map/ppermute | solution.py:21
  1.2 1.4 %pack_keys_values.1 = (bf16[256,256]{1,0:T(8,128)(2,1)S(1)}, bf16[256,256]{1,0:T(8,128)(2,1)S(1)}, bf16[256,256]{1,0:T(8,128)(2,1)S(1)}, bf16[256,256]{1,0:T(8,128)(2,1)S(1)}) custom-call(bf16[128,1024]{1,0:T(8,128)(2,1)} %refs_0_.3, bf16[128,1024]{1,0:T(8,128)(2,1)} %refs_1_.3), custom_call_target="tpu_custom_call" | custom-call | flops 8000000000 | tf_op jit(solution)/shard_map/pack_keys_values/pallas_call | solution.py:67
  2.6 3.4 %collective-permute-start.4 = (bf16[256,256]{1,0:T(8,128)(2,1)S(1)}, bf16[256,256]{1,0:T(8,128)(2,1)S(1)}, u32[]{:S(2)}, u32[]{:S(2)}) collective-permute-start(bf16[256,256]{1,0:T(8,128)(2,1)S(1)} %get-tuple-element.48), channel_id=1, source_target_pairs={{0,6},{2,4},{4,2},{6,0},{8,14},{10,12},{12,10},{14,8},{16,22},{18,... | collective-permute-start | bytes 393224 | tf_op jit(solution)/shard_map/ppermute | solution.py:21
  6.0 0.5 %collective-permute-start.5 = (bf16[256,256]{1,0:T(8,128)(2,1)S(1)}, bf16[256,256]{1,0:T(8,128)(2,1)S(1)}, u32[]{:S(2)}, u32[]{:S(2)}) collective-permute-start(bf16[256,256]{1,0:T(8,128)(2,1)S(1)} %get-tuple-element.49), channel_id=1, source_target_pairs={{0,2},{2,0},{4,6},{6,4},{8,10},{10,8},{12,14},{14,12},{16,18},{18,... | collective-permute-start | bytes 393224 | tf_op jit(solution)/shard_map/ppermute | solution.py:21
  6.5 0.1 collective-permute-start.6
  6.6 0.0 collective-permute-done.refs_2_
  6.7 0.0 copy-done.2
  6.7 0.0 copy-done
  6.7 0.0 copy-done.1
  6.7 1.5 %grad_attended.1 = (bf16[256,256]{1,0:T(8,128)(2,1)S(1)}, bf16[256,256]{1,0:T(8,128)(2,1)S(1)}, bf16[256,256]{1,0:T(8,128)(2,1)S(1)}, bf16[256,256]{1,0:T(8,128)(2,1)S(1)}) custom-call(bf16[128,1024]{1,0:T(8,128)(2,1)S(1)} %copy-done.1, bf16[128,1024]{1,0:T(8,128)(2,1)S(1)} %copy-done.2, bf16[128,1024]{1,0:T(8,128)(2,1)S(1)} %collective-permute-done.refs_2_, ...), custom_call_target="tpu_custom_call" | custom-call | flops 3000000000 | tf_op jit(solution)/shard_map/grad_attended/pallas_call | solution.py:67
  8.2 2.0 %collective-permute-start.1 = (bf16[256,256]{1,0:T(8,128)(2,1)S(1)}, bf16[256,256]{1,0:T(8,128)(2,1)S(1)}, u32[]{:S(2)}, u32[]{:S(2)}) collective-permute-start(bf16[256,256]{1,0:T(8,128)(2,1)S(1)} %get-tuple-element.45), channel_id=1, source_target_pairs={{0,2},{2,0},{4,6},{6,4},{8,10},{10,8},{12,14},{14,12},{16,18},{18,... | collective-permute-start | bytes 393224 | tf_op jit(solution)/shard_map/ppermute | solution.py:21
  10.1 1.5 %collective-permute-start.2 = (bf16[256,256]{1,0:T(8,128)(2,1)S(1)}, bf16[256,256]{1,0:T(8,128)(2,1)S(1)}, u32[]{:S(2)}, u32[]{:S(2)}) collective-permute-start(bf16[256,256]{1,0:T(8,128)(2,1)S(1)} %get-tuple-element.46), channel_id=1, source_target_pairs={{0,4},{2,6},{4,0},{6,2},{8,12},{10,14},{12,8},{14,10},{16,20},{18,... | collective-permute-start | bytes 393224 | tf_op jit(solution)/shard_map/ppermute | solution.py:21
  11.7 0.0 collective-permute-done.4.refs_0_
  11.7 1.7 %collective-permute-start.3 = (bf16[256,256]{1,0:T(8,128)(2,1)S(1)}, bf16[256,256]{1,0:T(8,128)(2,1)S(1)}, u32[]{:S(2)}, u32[]{:S(2)}) collective-permute-start(bf16[256,256]{1,0:T(8,128)(2,1)S(1)} %get-tuple-element.47), channel_id=1, source_target_pairs={{0,6},{2,4},{4,2},{6,0},{8,14},{10,12},{12,10},{14,8},{16,22},{18,... | collective-permute-start | bytes 393224 | tf_op jit(solution)/shard_map/ppermute | solution.py:21
  13.3 0.4 collective-permute-done.5.refs_1_
  13.7 0.0 collective-permute-done.6.refs_2_
  13.7 0.2 pool_plane.1
  14.0 1.6 %collective-permute-start.9 = (bf16[256,256]{1,0:T(8,128)(2,1)S(1)}, bf16[256,256]{1,0:T(8,128)(2,1)S(1)}, u32[]{:S(2)}, u32[]{:S(2)}) collective-permute-start(bf16[256,256]{1,0:T(8,128)(2,1)S(1)} %get-tuple-element.54), channel_id=1, source_target_pairs={{0,8},{2,10},{4,12},{6,14},{8,0},{10,2},{12,4},{14,6},{16,24},{18,... | collective-permute-start | bytes 393224 | tf_op jit(solution)/shard_map/ppermute | solution.py:21
  15.6 2.6 %collective-permute-start.7 = (bf16[128,256]{1,0:T(8,128)(2,1)S(1)}, bf16[128,256]{1,0:T(8,128)(2,1)S(1)}, u32[]{:S(2)}, u32[]{:S(2)}) collective-permute-start(bf16[128,256]{1,0:T(8,128)(2,1)S(1)} %get-tuple-element.52), channel_id=1, source_target_pairs={{0,16},{2,18},{4,20},{6,22},{8,24},{10,26},{12,28},{14,30},{16,0},... | collective-permute-start | bytes 196616 | tf_op jit(solution)/shard_map/ppermute | solution.py:21
  18.2 0.0 collective-permute-done.1.refs_5_.refs_1_
  18.2 2.0 %collective-permute-start.8 = (bf16[128,256]{1,0:T(8,128)(2,1)S(1)}, bf16[128,256]{1,0:T(8,128)(2,1)S(1)}, u32[]{:S(2)}, u32[]{:S(2)}) collective-permute-start(bf16[128,256]{1,0:T(8,128)(2,1)S(1)} %get-tuple-element.53), channel_id=1, source_target_pairs={{0,24},{2,26},{4,28},{6,30},{8,16},{10,18},{12,20},{14,22},{16,8},... | collective-permute-start | bytes 196616 | tf_op jit(solution)/shard_map/ppermute | solution.py:21
  20.1 0.0 collective-permute-done.2.refs_6_.refs_2_
  20.1 0.0 collective-permute-done.3.refs_4_.refs_0_.refs_3_
  20.2 0.0 collective-permute-done.9.refs_8_
  20.2 1.4 %near_attention.1 = (f32[2,512,512]{2,1,0:T(8,128)S(1)}, f32[2,512,512]{2,1,0:T(8,128)S(1)}, f32[2,128,512]{2,1,0:T(8,128)S(1)}, f32[2,2,512]{2,1,0:T(2,128)S(1)}, bf16[4,512,128]{2,1,0:T(8,128)(2,1)S(1)}) custom-call(bf16[256,256]{1,0:T(8,128)(2,1)S(1)} %collective-permute-done.4.refs_0_, bf16[256,256]{1,0:T(8,128)(2,1)S(1)} %collective-permute-done.5.refs_1_, ...), custom_call_target="tpu_custom_call" | custom-call | flops 2000000000 | tf_op jit(solution)/shard_map/near_attention/pallas_call | solution.py:67
  21.6 0.4 collective-permute-done.7.refs_4_
  22.0 2.3 %collective-permute-done.8.refs_5_ = bf16[128,256]{1,0:T(8,128)(2,1)S(1)} collective-permute-done((bf16[128,256]{1,0:T(8,128)(2,1)S(1)}, bf16[128,256]{1,0:T(8,128)(2,1)S(1)}, u32[]{:S(2)}, u32[]{:S(2)}) %collective-permute-start.8) | collective-permute-done | bytes 65568 | tf_op jit(solution)/shard_map/ppermute | solution.py:21
  24.3 1.1 %far_attention.1 = (bf16[256,256]{1,0:T(8,128)(2,1)S(1)}, bf16[256,256]{1,0:T(8,128)(2,1)S(1)}, bf16[256,256]{1,0:T(8,128)(2,1)S(1)}, bf16[256,256]{1,0:T(8,128)...) custom-call(bf16[256,256]{1,0:T(8,128)(2,1)S(1)} %collective-permute, ...), custom_call_target="tpu_custom_call" | custom-call | flops 2000000000 | tf_op jit(solution)/shard_map/far_attention/pallas_call | solution.py:67
  25.4 1.9 %collective-permute-start.14 = (bf16[128,256]{1,0:T(8,128)(2,1)S(1)}, bf16[128,256]{1,0:T(8,128)(2,1)S(1)}, u32[]{:S(2)}, u32[]{:S(2)}) collective-permute-start(bf16[128,256]{1,0:T(8,128)(2,1)S(1)} %get-tuple-element.75), channel_id=1, source_target_pairs={{0,16},{2,18},{4,20},{6,22},{8,24},{10,26},{12,28},{14,30},{16,0},... | collective-permute-start | bytes 196616 | tf_op jit(solution)/shard_map/ppermute | solution.py:21
  27.2 1.5 %collective-permute-start.15 = (bf16[128,256]{1,0:T(8,128)(2,1)S(1)}, bf16[128,256]{1,0:T(8,128)(2,1)S(1)}, u32[]{:S(2)}, u32[]{:S(2)}) collective-permute-start(bf16[128,256]{1,0:T(8,128)(2,1)S(1)} %get-tuple-element.76), channel_id=1, source_target_pairs={{0,24},{2,26},{4,28},{6,30},{8,16},{10,18},{12,20},{14,22},{16,8},... | collective-permute-start | bytes 196616 | tf_op jit(solution)/shard_map/ppermute | solution.py:21
  28.8 0.2 collective-permute-start.13
  28.9 1.1 %plane_grads.1 = (bf16[256,256]{1,0:T(8,128)(2,1)S(1)}, bf16[256,256]{1,0:T(8,128)(2,1)S(1)}, bf16[256,256]{1,0:T(8,128)(2,1)S(1)}, bf16[256,256]{1,0:T(8,128)(2...) custom-call(bf16[256,256]{1,0:T(8,128)(2,1)S(1)} %get-tuple-element., ...), custom_call_target="tpu_custom_call", output_to_operand_aliasing={{0}: (11, {}), {1}: (12, {}), {2}: (13, {}), {3}: (14, {})} | custom-call | flops 2300000000 | tf_op jit(solution)/shard_map/plane_grads/pallas_call | solution.py:67
  30.1 2.3 %collective-permute-start.10 = (bf16[256,256]{1,0:T(8,128)(2,1)S(1)}, bf16[256,256]{1,0:T(8,128)(2,1)S(1)}, u32[]{:S(2)}, u32[]{:S(2)}) collective-permute-start(bf16[256,256]{1,0:T(8,128)(2,1)S(1)} %get-tuple-element.66), channel_id=1, source_target_pairs={{0,6},{2,4},{4,2},{6,0},{8,14},{10,12},{12,10},{14,8},{16,22},{18,... | collective-permute-start | bytes 393224 | tf_op jit(solution)/shard_map/ppermute | solution.py:21
  32.4 0.5 %collective-permute-start.11 = (bf16[256,256]{1,0:T(8,128)(2,1)S(1)}, bf16[256,256]{1,0:T(8,128)(2,1)S(1)}, u32[]{:S(2)}, u32[]{:S(2)}) collective-permute-start(bf16[256,256]{1,0:T(8,128)(2,1)S(1)} %get-tuple-element.67), channel_id=1, source_target_pairs={{0,2},{2,0},{4,6},{6,4},{8,10},{10,8},{12,14},{14,12},{16,18},{18,... | collective-permute-start | bytes 393224 | tf_op jit(solution)/shard_map/ppermute | solution.py:21
  32.9 0.0 collective-permute-done.14.refs_5_
  32.9 0.7 %collective-permute-start.12 = (bf16[256,256]{1,0:T(8,128)(2,1)S(1)}, bf16[256,256]{1,0:T(8,128)(2,1)S(1)}, u32[]{:S(2)}, u32[]{:S(2)}) collective-permute-start(bf16[256,256]{1,0:T(8,128)(2,1)S(1)} %get-tuple-element.68), channel_id=1, source_target_pairs={{0,4},{2,6},{4,0},{6,2},{8,12},{10,14},{12,8},{14,10},{16,20},{18,... | collective-permute-start | bytes 393224 | tf_op jit(solution)/shard_map/ppermute | solution.py:21
  33.6 0.0 collective-permute-done.15.refs_6_
  33.6 0.8 %collective-permute-done.13.refs_4_ = bf16[256,256]{1,0:T(8,128)(2,1)S(1)} collective-permute-done((bf16[256,256]{1,0:T(8,128)(2,1)S(1)}, bf16[256,256]{1,0:T(8,128)(2,1)S(1)}, u32[]{:S(2)}, u32[]{:S(2)}) %collective-permute-start.13) | collective-permute-done | bytes 131104 | tf_op jit(solution)/shard_map/ppermute | solution.py:21
  34.4 0.3 carry.1
  34.8 2.4 %collective-permute-start.18 = (bf16[256,256]{1,0:T(8,128)(2,1)S(1)}, bf16[256,256]{1,0:T(8,128)(2,1)S(1)}, u32[]{:S(2)}, u32[]{:S(2)}) collective-permute-start(bf16[256,256]{1,0:T(8,128)(2,1)S(1)} %get-tuple-element.81), channel_id=1, source_target_pairs={{0,6},{2,4},{4,2},{6,0},{8,14},{10,12},{12,10},{14,8},{16,22},{18,... | collective-permute-start | bytes 393224 | tf_op jit(solution)/shard_map/ppermute | solution.py:21
  37.1 0.5 %collective-permute-start.19 = (bf16[256,256]{1,0:T(8,128)(2,1)S(1)}, bf16[256,256]{1,0:T(8,128)(2,1)S(1)}, u32[]{:S(2)}, u32[]{:S(2)}) collective-permute-start(bf16[256,256]{1,0:T(8,128)(2,1)S(1)} %get-tuple-element.82), channel_id=1, source_target_pairs={{0,2},{2,0},{4,6},{6,4},{8,10},{10,8},{12,14},{14,12},{16,18},{18,... | collective-permute-start | bytes 393224 | tf_op jit(solution)/shard_map/ppermute | solution.py:21
  37.7 0.0 collective-permute-done.10.refs_0_.refs_3_
  37.7 0.7 %collective-permute-start.20 = (bf16[256,256]{1,0:T(8,128)(2,1)S(1)}, bf16[256,256]{1,0:T(8,128)(2,1)S(1)}, u32[]{:S(2)}, u32[]{:S(2)}) collective-permute-start(bf16[256,256]{1,0:T(8,128)(2,1)S(1)} %get-tuple-element.83), channel_id=1, source_target_pairs={{0,4},{2,6},{4,0},{6,2},{8,12},{10,14},{12,8},{14,10},{16,20},{18,... | collective-permute-start | bytes 393224 | tf_op jit(solution)/shard_map/ppermute | solution.py:21
  38.4 1.2 %collective-permute-done.11.refs_1_.refs_4_ = bf16[256,256]{1,0:T(8,128)(2,1)S(1)} collective-permute-done((bf16[256,256]{1,0:T(8,128)(2,1)S(1)}, bf16[256,256]{1,0:T(8,128)(2,1)S(1)}, u32[]{:S(2)}, u32[]{:S(2)}) %collective-permute-start.11) | collective-permute-done | bytes 131104 | tf_op jit(solution)/shard_map/ppermute | solution.py:21
  39.6 0.7 %collective-permute-done.12.refs_2_.refs_5_ = bf16[256,256]{1,0:T(8,128)(2,1)S(1)} collective-permute-done((bf16[256,256]{1,0:T(8,128)(2,1)S(1)}, bf16[256,256]{1,0:T(8,128)(2,1)S(1)}, u32[]{:S(2)}, u32[]{:S(2)}) %collective-permute-start.12) | collective-permute-done | bytes 131104 | tf_op jit(solution)/shard_map/ppermute | solution.py:21
  40.4 0.7 %project.1 = (f32[128,1024]{1,0:T(8,128)S(1)}, bf16[64,1024]{1,0:T(8,128)(2,1)S(1)}, bf16[64,1024]{1,0:T(8,128)(2,1)S(1)}) custom-call(bf16[256,256]{1,0:T(8,128)(2,1)S(1)} %collective-permute-done.10.refs_0_.refs_3_, bf16[256,256]{1,0:T(8,128)(2,1)S(1)} %collective-permute-done.11.refs_1_.refs_4_, ...), custom_call_target="tpu_custom_call" | custom-call | flops 10000000 | tf_op jit(solution)/shard_map/project/pallas_call | solution.py:67
  41.1 0.1 collective-permute-start.16
  41.2 0.5 %collective-permute-start.17 = (bf16[64,1024]{1,0:T(8,128)(2,1)S(1)}, bf16[64,1024]{1,0:T(8,128)(2,1)S(1)}, u32[]{:S(2)}, u32[]{:S(2)}) collective-permute-start(bf16[64,1024]{1,0:T(8,128)(2,1)S(1)} %get-tuple-element.80), channel_id=1, source_target_pairs={{0,1},{1,0},{2,3},{3,2},{4,5},{5,4},{6,7},{7,6},{8,9},{9,8},{10,11... | collective-permute-start | bytes 393224 | tf_op jit(solution)/shard_map/ppermute | solution.py:21
  41.7 0.0 collective-permute-done.18.refs_7_
  41.7 1.2 %collective-permute-done.19.refs_8_ = bf16[256,256]{1,0:T(8,128)(2,1)S(1)} collective-permute-done((bf16[256,256]{1,0:T(8,128)(2,1)S(1)}, bf16[256,256]{1,0:T(8,128)(2,1)S(1)}, u32[]{:S(2)}, u32[]{:S(2)}) %collective-permute-start.19) | collective-permute-done | bytes 131104 | tf_op jit(solution)/shard_map/ppermute | solution.py:21
  42.9 0.1 collective-permute-done.20.refs_9_
  43.0 0.0 collective-permute-done.16.refs_1_
  43.0 0.0 collective-permute-done.17.refs_2_
  43.0 1.1 %join.1 = (bf16[128,1024]{1,0:T(8,128)(2,1)}, bf16[128,1024]{1,0:T(8,128)(2,1)}, bf16[128,1024]{1,0:T(8,128)(2,1)}, bf16[128,1024]{1,0:T(8,128)(2,1)}) custom-call(f32[128,1024]{1,0:T(8,128)S(1)} %get-tuple-element.78.refs_0_, bf16[64,1024]{1,0:T(8,128)(2,1)S(1)} %collective-permute-done.16.refs_1_, bf16[64,1024]{1,0:T(8,128)(2,1)S(1)} %collective-permute-done.17.refs_2_, ...), custom_call_target="tpu_custom_call" | custom-call | flops 1000000000 | tf_op jit(solution)/shard_map/join/pallas_call | solution.py:67
Async XLA Ops:
  0.6 6.0 %copy-start.2 = (bf16[128,1024]{1,0:T(8,128)(2,1)S(1)}, bf16[128,1024]{1,0:T(8,128)(2,1)}, u32[]{:S(2)}) copy-start(bf16[128,1024]{1,0:T(8,128)(2,1)} %refs_1_.2) | copy-start | bytes 786436
  0.6 6.0 %copy-start = (bf16[1024,2048]{1,0:T(8,128)(2,1)S(1)}, bf16[1024,2048]{1,0:T(8,128)(2,1)}, u32[]{:S(2)}) copy-start(bf16[1024,2048]{1,0:T(8,128)(2,1)} %refs_4_.1) | copy-start | bytes 12582916
  0.7 6.0 %copy-start.1 = (bf16[128,1024]{1,0:T(8,128)(2,1)S(1)}, bf16[128,1024]{1,0:T(8,128)(2,1)}, u32[]{:S(2)}) copy-start(bf16[128,1024]{1,0:T(8,128)(2,1)} %refs_0_.2) | copy-start | bytes 786436
  0.7 6.0 %collective-permute-start = (bf16[128,1024]{1,0:T(8,128)(2,1)}, bf16[128,1024]{1,0:T(8,128)(2,1)S(1)}, u32[]{:S(2)}, u32[]{:S(2)}) collective-permute-start(bf16[128,1024]{1,0:T(8,128)(2,1)} %refs_1_.2), channel_id=1, source_target_pairs={{0,1},{1,0},{2,3},{3,2},{4,5},{5,4},{6,7},{7,6},{8,9},{9,8},{10,11... | collective-permute-start | bytes 786440 | tf_op jit(solution)/shard_map/ppermute | solution.py:21
  2.6 9.1 %collective-permute-start.4 = (bf16[256,256]{1,0:T(8,128)(2,1)S(1)}, bf16[256,256]{1,0:T(8,128)(2,1)S(1)}, u32[]{:S(2)}, u32[]{:S(2)}) collective-permute-start(bf16[256,256]{1,0:T(8,128)(2,1)S(1)} %get-tuple-element.48), channel_id=1, source_target_pairs={{0,6},{2,4},{4,2},{6,0},{8,14},{10,12},{12,10},{14,8},{16,22},{18,... | collective-permute-start | bytes 393224 | tf_op jit(solution)/shard_map/ppermute | solution.py:21
  6.0 7.7 %collective-permute-start.5 = (bf16[256,256]{1,0:T(8,128)(2,1)S(1)}, bf16[256,256]{1,0:T(8,128)(2,1)S(1)}, u32[]{:S(2)}, u32[]{:S(2)}) collective-permute-start(bf16[256,256]{1,0:T(8,128)(2,1)S(1)} %get-tuple-element.49), channel_id=1, source_target_pairs={{0,2},{2,0},{4,6},{6,4},{8,10},{10,8},{12,14},{14,12},{16,18},{18,... | collective-permute-start | bytes 393224 | tf_op jit(solution)/shard_map/ppermute | solution.py:21
  6.5 7.2 %collective-permute-start.6 = (bf16[256,256]{1,0:T(8,128)(2,1)S(1)}, bf16[256,256]{1,0:T(8,128)(2,1)S(1)}, u32[]{:S(2)}, u32[]{:S(2)}) collective-permute-start(bf16[256,256]{1,0:T(8,128)(2,1)S(1)} %get-tuple-element.50), channel_id=1, source_target_pairs={{0,4},{2,6},{4,0},{6,2},{8,12},{10,14},{12,8},{14,10},{16,20},{18,... | collective-permute-start | bytes 393224 | tf_op jit(solution)/shard_map/ppermute | solution.py:21
  8.2 10.0 %collective-permute-start.1 = (bf16[256,256]{1,0:T(8,128)(2,1)S(1)}, bf16[256,256]{1,0:T(8,128)(2,1)S(1)}, u32[]{:S(2)}, u32[]{:S(2)}) collective-permute-start(bf16[256,256]{1,0:T(8,128)(2,1)S(1)} %get-tuple-element.45), channel_id=1, source_target_pairs={{0,2},{2,0},{4,6},{6,4},{8,10},{10,8},{12,14},{14,12},{16,18},{18,... | collective-permute-start | bytes 393224 | tf_op jit(solution)/shard_map/ppermute | solution.py:21
  10.1 10.0 %collective-permute-start.2 = (bf16[256,256]{1,0:T(8,128)(2,1)S(1)}, bf16[256,256]{1,0:T(8,128)(2,1)S(1)}, u32[]{:S(2)}, u32[]{:S(2)}) collective-permute-start(bf16[256,256]{1,0:T(8,128)(2,1)S(1)} %get-tuple-element.46), channel_id=1, source_target_pairs={{0,4},{2,6},{4,0},{6,2},{8,12},{10,14},{12,8},{14,10},{16,20},{18,... | collective-permute-start | bytes 393224 | tf_op jit(solution)/shard_map/ppermute | solution.py:21
  11.7 8.5 %collective-permute-start.3 = (bf16[256,256]{1,0:T(8,128)(2,1)S(1)}, bf16[256,256]{1,0:T(8,128)(2,1)S(1)}, u32[]{:S(2)}, u32[]{:S(2)}) collective-permute-start(bf16[256,256]{1,0:T(8,128)(2,1)S(1)} %get-tuple-element.47), channel_id=1, source_target_pairs={{0,6},{2,4},{4,2},{6,0},{8,14},{10,12},{12,10},{14,8},{16,22},{18,... | collective-permute-start | bytes 393224 | tf_op jit(solution)/shard_map/ppermute | solution.py:21
  14.0 6.2 %collective-permute-start.9 = (bf16[256,256]{1,0:T(8,128)(2,1)S(1)}, bf16[256,256]{1,0:T(8,128)(2,1)S(1)}, u32[]{:S(2)}, u32[]{:S(2)}) collective-permute-start(bf16[256,256]{1,0:T(8,128)(2,1)S(1)} %get-tuple-element.54), channel_id=1, source_target_pairs={{0,8},{2,10},{4,12},{6,14},{8,0},{10,2},{12,4},{14,6},{16,24},{18,... | collective-permute-start | bytes 393224 | tf_op jit(solution)/shard_map/ppermute | solution.py:21
  15.6 6.4 %collective-permute-start.7 = (bf16[128,256]{1,0:T(8,128)(2,1)S(1)}, bf16[128,256]{1,0:T(8,128)(2,1)S(1)}, u32[]{:S(2)}, u32[]{:S(2)}) collective-permute-start(bf16[128,256]{1,0:T(8,128)(2,1)S(1)} %get-tuple-element.52), channel_id=1, source_target_pairs={{0,16},{2,18},{4,20},{6,22},{8,24},{10,26},{12,28},{14,30},{16,0},... | collective-permute-start | bytes 196616 | tf_op jit(solution)/shard_map/ppermute | solution.py:21
  18.2 6.1 %collective-permute-start.8 = (bf16[128,256]{1,0:T(8,128)(2,1)S(1)}, bf16[128,256]{1,0:T(8,128)(2,1)S(1)}, u32[]{:S(2)}, u32[]{:S(2)}) collective-permute-start(bf16[128,256]{1,0:T(8,128)(2,1)S(1)} %get-tuple-element.53), channel_id=1, source_target_pairs={{0,24},{2,26},{4,28},{6,30},{8,16},{10,18},{12,20},{14,22},{16,8},... | collective-permute-start | bytes 196616 | tf_op jit(solution)/shard_map/ppermute | solution.py:21
  25.4 7.6 %collective-permute-start.14 = (bf16[128,256]{1,0:T(8,128)(2,1)S(1)}, bf16[128,256]{1,0:T(8,128)(2,1)S(1)}, u32[]{:S(2)}, u32[]{:S(2)}) collective-permute-start(bf16[128,256]{1,0:T(8,128)(2,1)S(1)} %get-tuple-element.75), channel_id=1, source_target_pairs={{0,16},{2,18},{4,20},{6,22},{8,24},{10,26},{12,28},{14,30},{16,0},... | collective-permute-start | bytes 196616 | tf_op jit(solution)/shard_map/ppermute | solution.py:21
  27.2 6.4 %collective-permute-start.15 = (bf16[128,256]{1,0:T(8,128)(2,1)S(1)}, bf16[128,256]{1,0:T(8,128)(2,1)S(1)}, u32[]{:S(2)}, u32[]{:S(2)}) collective-permute-start(bf16[128,256]{1,0:T(8,128)(2,1)S(1)} %get-tuple-element.76), channel_id=1, source_target_pairs={{0,24},{2,26},{4,28},{6,30},{8,16},{10,18},{12,20},{14,22},{16,8},... | collective-permute-start | bytes 196616 | tf_op jit(solution)/shard_map/ppermute | solution.py:21
  28.8 5.7 %collective-permute-start.13 = (bf16[256,256]{1,0:T(8,128)(2,1)S(1)}, bf16[256,256]{1,0:T(8,128)(2,1)S(1)}, u32[]{:S(2)}, u32[]{:S(2)}) collective-permute-start(bf16[256,256]{1,0:T(8,128)(2,1)S(1)} %get-tuple-element.74), channel_id=1, source_target_pairs={{0,8},{2,10},{4,12},{6,14},{8,0},{10,2},{12,4},{14,6},{16,24},{18,... | collective-permute-start | bytes 393224 | tf_op jit(solution)/shard_map/ppermute | solution.py:21
  30.1 7.6 %collective-permute-start.10 = (bf16[256,256]{1,0:T(8,128)(2,1)S(1)}, bf16[256,256]{1,0:T(8,128)(2,1)S(1)}, u32[]{:S(2)}, u32[]{:S(2)}) collective-permute-start(bf16[256,256]{1,0:T(8,128)(2,1)S(1)} %get-tuple-element.66), channel_id=1, source_target_pairs={{0,6},{2,4},{4,2},{6,0},{8,14},{10,12},{12,10},{14,8},{16,22},{18,... | collective-permute-start | bytes 393224 | tf_op jit(solution)/shard_map/ppermute | solution.py:21
  32.4 7.2 %collective-permute-start.11 = (bf16[256,256]{1,0:T(8,128)(2,1)S(1)}, bf16[256,256]{1,0:T(8,128)(2,1)S(1)}, u32[]{:S(2)}, u32[]{:S(2)}) collective-permute-start(bf16[256,256]{1,0:T(8,128)(2,1)S(1)} %get-tuple-element.67), channel_id=1, source_target_pairs={{0,2},{2,0},{4,6},{6,4},{8,10},{10,8},{12,14},{14,12},{16,18},{18,... | collective-permute-start | bytes 393224 | tf_op jit(solution)/shard_map/ppermute | solution.py:21
  32.9 7.4 %collective-permute-start.12 = (bf16[256,256]{1,0:T(8,128)(2,1)S(1)}, bf16[256,256]{1,0:T(8,128)(2,1)S(1)}, u32[]{:S(2)}, u32[]{:S(2)}) collective-permute-start(bf16[256,256]{1,0:T(8,128)(2,1)S(1)} %get-tuple-element.68), channel_id=1, source_target_pairs={{0,4},{2,6},{4,0},{6,2},{8,12},{10,14},{12,8},{14,10},{16,20},{18,... | collective-permute-start | bytes 393224 | tf_op jit(solution)/shard_map/ppermute | solution.py:21
  34.8 6.9 %collective-permute-start.18 = (bf16[256,256]{1,0:T(8,128)(2,1)S(1)}, bf16[256,256]{1,0:T(8,128)(2,1)S(1)}, u32[]{:S(2)}, u32[]{:S(2)}) collective-permute-start(bf16[256,256]{1,0:T(8,128)(2,1)S(1)} %get-tuple-element.81), channel_id=1, source_target_pairs={{0,6},{2,4},{4,2},{6,0},{8,14},{10,12},{12,10},{14,8},{16,22},{18,... | collective-permute-start | bytes 393224 | tf_op jit(solution)/shard_map/ppermute | solution.py:21
  37.1 5.8 %collective-permute-start.19 = (bf16[256,256]{1,0:T(8,128)(2,1)S(1)}, bf16[256,256]{1,0:T(8,128)(2,1)S(1)}, u32[]{:S(2)}, u32[]{:S(2)}) collective-permute-start(bf16[256,256]{1,0:T(8,128)(2,1)S(1)} %get-tuple-element.82), channel_id=1, source_target_pairs={{0,2},{2,0},{4,6},{6,4},{8,10},{10,8},{12,14},{14,12},{16,18},{18,... | collective-permute-start | bytes 393224 | tf_op jit(solution)/shard_map/ppermute | solution.py:21
  37.7 5.4 %collective-permute-start.20 = (bf16[256,256]{1,0:T(8,128)(2,1)S(1)}, bf16[256,256]{1,0:T(8,128)(2,1)S(1)}, u32[]{:S(2)}, u32[]{:S(2)}) collective-permute-start(bf16[256,256]{1,0:T(8,128)(2,1)S(1)} %get-tuple-element.83), channel_id=1, source_target_pairs={{0,4},{2,6},{4,0},{6,2},{8,12},{10,14},{12,8},{14,10},{16,20},{18,... | collective-permute-start | bytes 393224 | tf_op jit(solution)/shard_map/ppermute | solution.py:21
  41.1 1.9 %collective-permute-start.16 = (bf16[64,1024]{1,0:T(8,128)(2,1)S(1)}, bf16[64,1024]{1,0:T(8,128)(2,1)S(1)}, u32[]{:S(2)}, u32[]{:S(2)}) collective-permute-start(bf16[64,1024]{1,0:T(8,128)(2,1)S(1)} %get-tuple-element.79), channel_id=1, source_target_pairs={{0,1},{1,0},{2,3},{3,2},{4,5},{5,4},{6,7},{7,6},{8,9},{9,8},{10,11... | collective-permute-start | bytes 393224 | tf_op jit(solution)/shard_map/ppermute | solution.py:21
  41.2 1.8 %collective-permute-start.17 = (bf16[64,1024]{1,0:T(8,128)(2,1)S(1)}, bf16[64,1024]{1,0:T(8,128)(2,1)S(1)}, u32[]{:S(2)}, u32[]{:S(2)}) collective-permute-start(bf16[64,1024]{1,0:T(8,128)(2,1)S(1)} %get-tuple-element.80), channel_id=1, source_target_pairs={{0,1},{1,0},{2,3},{3,2},{4,5},{5,4},{6,7},{7,6},{8,9},{9,8},{10,11... | collective-permute-start | bytes 393224 | tf_op jit(solution)/shard_map/ppermute | solution.py:21

commit v7 on v6

--- a/solution.py
+++ b/solution.py
@@ -8,7 +8,10 @@
 DH = 128
 PLANE = 4
 PIECES = 2
-FARTHEST = (3, 1, 2, 0)
+OKV = (3, 1, 2, 0)
+OQG = (2, 1, 3, 0)
+OAD = (3, 1, 2, 0)
+ODKV = (2, 3, 1, 0)
 ORDER = (1, 2, 3)
 SCALE = DH ** (-0.5)
 SCALE2 = SCALE * 1.4426950408889634
@@ -58,7 +61,7 @@
     count = len(args)
     order = list(range(count))
     for first in planes:
-        order[first : first + PLANE] = [first + r for r in FARTHEST]
+        order[first[0] : first[0] + PLANE] = [first[0] + r for r in first[1]]
     places = [order.index(n) for n in range(count)]
 
     def run(*refs):
@@ -400,7 +403,7 @@
     )
     query_grads = plane_exchange(query_grads)
     near, pooled, pooled3 = call(
-        far_kernel, [shape(2 * rows, width)] + [shape(rows, width)] * 2, *key_values, planes=(0,),
+        far_kernel, [shape(2 * rows, width)] + [shape(rows, width)] * 2, *key_values, planes=((0, OKV),),
         after=(query_grads[0],), cost_us=1.0, name="pool_plane",
     )
     fars = [xor_permute({1: near, 2: pooled, 3: pooled3}[n], n * PLANE) for n in ORDER]
@@ -418,13 +421,13 @@
         [shape(heads, near_rows, tokens, t=F32)] * 2
         + [shape(heads, DH, tokens, t=F32), shape(heads, 2, tokens, t=F32)]
         + [shape(2 * heads, near_rows, DH)],
-        *key_values, *query_grads, fars[0], planes=(0, PLANE), cost_us=2.0, name="near_attention",
+        *key_values, *query_grads, fars[0], planes=((0, OKV), (PLANE, OQG)), cost_us=2.0, name="near_attention",
     )
     results = call(
         lambda *refs: far_grad_kernel(len(fars) - 1, *refs),
         blocks + [shape(heads, far_rows, tokens), shape(heads, 2, tokens, t=F32)]
         + [shape(*far.shape) for far in fars],
-        *query_grads, *fars[1:], weights, dots, sums, stats, planes=(0,), cost_us=2.0, name="far_attention",
+        *query_grads, *fars[1:], weights, dots, sums, stats, planes=((0, OQG),), cost_us=2.0, name="far_attention",
     )
     ads, kept, far_grads = results[:PLANE], results[PLANE : PLANE + 2], list(results[PLANE + 2 :])
     first = PLANE + len(fars) + 4
@@ -456,12 +459,12 @@
     own_sum, *other_sum = call(
         output_kernel,
         [shape(rows, features, t=F32)] + [shape(rows // PIECES, features)] * PIECES,
-        *att_dq, out_weight, planes=(0,), after=(dkv[0],), cost_us=0.01, name="project",
+        *att_dq, out_weight, planes=((0, OAD),), after=(dkv[0],), cost_us=0.01, name="project",
     )
     dkv = plane_exchange(dkv)
     other_sum = [xor_permute(piece, 1, "head") for piece in other_sum]
     output, grad_queries, grad_keys, grad_values = call(
-        join_kernel, [shape(rows, features)] * 4, own_sum, *other_sum, *att_dq, *dkv, planes=(1 + PIECES, 1 + PIECES + PLANE),
+        join_kernel, [shape(rows, features)] * 4, own_sum, *other_sum, *att_dq, *dkv, planes=((1 + PIECES, OAD), (1 + PIECES + PLANE, ODKV)),
         hbm_out=True, scratch=[pltpu.VMEM((rows, features), BF16), dma(3 * PLANE + 1)],
         cost_us=1.0, name="join",
     )

time: 44.3 us -> 44.2 us (level)
  no operation moved by 1% of the time
where the time goes in v7:
time: 44.2 us; the launch traced here: 44.1 us
  starting transfers between devices  27.1 us (61%)
  Pallas kernels  8.91 us (20%)
  waiting for transfers between devices  7.29 us (16%)
  between operations  0.75 us (2%)
    ppermute x21, starting transfers between devices, xor_permute(): return lax.ppermute(block, axis, [(i, i ^ mask) for i in range(count)])  27.1 us
    pallas_call x9, Pallas kernels, call(): pl.pallas_call(run, out_shape=[space(out.shape, out.dtype) for out in out...  8.91 us
    ppermute x21, waiting for transfers between devices, xor_permute(): return lax.ppermute(block, axis, [(i, i ^ mask) for i in range(count)])  7.29 us
  transfers between devices with their start and end apart: 21, of which 8 were waited for; matrix products, arithmetic and copies ran while one was open for 0% of the time, Pallas kernels for 15%

profile of v7, /device:TPU:0, one launch (start us, length us, event | category | flops | bytes accessed | tf_op | source)
XLA Modules:
  0.0 44.1 jit_solution(15109546448462085771)
XLA Ops:
  0.6 0.0 copy-start.2
  0.6 0.0 copy-start
  0.7 0.0 copy-start.1
  0.7 0.5 %collective-permute-start = (bf16[128,1024]{1,0:T(8,128)(2,1)}, bf16[128,1024]{1,0:T(8,128)(2,1)S(1)}, u32[]{:S(2)}, u32[]{:S(2)}) collective-permute-start(bf16[128,1024]{1,0:T(8,128)(2,1)} %refs_1_.2), channel_id=1, source_target_pairs={{0,1},{1,0},{2,3},{3,2},{4,5},{5,4},{6,7},{7,6},{8,9},{9,8},{10,11... | collective-permute-start | bytes 786440 | tf_op jit(solution)/shard_map/ppermute | solution.py:24
  1.2 1.4 %pack_keys_values.1 = (bf16[256,256]{1,0:T(8,128)(2,1)S(1)}, bf16[256,256]{1,0:T(8,128)(2,1)S(1)}, bf16[256,256]{1,0:T(8,128)(2,1)S(1)}, bf16[256,256]{1,0:T(8,128)(2,1)S(1)}) custom-call(bf16[128,1024]{1,0:T(8,128)(2,1)} %refs_0_.3, bf16[128,1024]{1,0:T(8,128)(2,1)} %refs_1_.3), custom_call_target="tpu_custom_call" | custom-call | flops 8000000000 | tf_op jit(solution)/shard_map/pack_keys_values/pallas_call | solution.py:70
  2.6 3.4 %collective-permute-start.4 = (bf16[256,256]{1,0:T(8,128)(2,1)S(1)}, bf16[256,256]{1,0:T(8,128)(2,1)S(1)}, u32[]{:S(2)}, u32[]{:S(2)}) collective-permute-start(bf16[256,256]{1,0:T(8,128)(2,1)S(1)} %get-tuple-element.48), channel_id=1, source_target_pairs={{0,6},{2,4},{4,2},{6,0},{8,14},{10,12},{12,10},{14,8},{16,22},{18,... | collective-permute-start | bytes 393224 | tf_op jit(solution)/shard_map/ppermute | solution.py:24
  6.0 0.5 %collective-permute-start.5 = (bf16[256,256]{1,0:T(8,128)(2,1)S(1)}, bf16[256,256]{1,0:T(8,128)(2,1)S(1)}, u32[]{:S(2)}, u32[]{:S(2)}) collective-permute-start(bf16[256,256]{1,0:T(8,128)(2,1)S(1)} %get-tuple-element.49), channel_id=1, source_target_pairs={{0,2},{2,0},{4,6},{6,4},{8,10},{10,8},{12,14},{14,12},{16,18},{18,... | collective-permute-start | bytes 393224 | tf_op jit(solution)/shard_map/ppermute | solution.py:24
  6.5 0.1 collective-permute-start.6
  6.6 0.0 collective-permute-done.refs_2_
  6.7 0.0 copy-done.2
  6.7 0.0 copy-done
  6.7 0.0 copy-done.1
  6.7 1.5 %grad_attended.1 = (bf16[256,256]{1,0:T(8,128)(2,1)S(1)}, bf16[256,256]{1,0:T(8,128)(2,1)S(1)}, bf16[256,256]{1,0:T(8,128)(2,1)S(1)}, bf16[256,256]{1,0:T(8,128)(2,1)S(1)}) custom-call(bf16[128,1024]{1,0:T(8,128)(2,1)S(1)} %copy-done.1, bf16[128,1024]{1,0:T(8,128)(2,1)S(1)} %copy-done.2, bf16[128,1024]{1,0:T(8,128)(2,1)S(1)} %collective-permute-done.refs_2_, ...), custom_call_target="tpu_custom_call" | custom-call | flops 3000000000 | tf_op jit(solution)/shard_map/grad_attended/pallas_call | solution.py:70
  8.2 2.0 %collective-permute-start.1 = (bf16[256,256]{1,0:T(8,128)(2,1)S(1)}, bf16[256,256]{1,0:T(8,128)(2,1)S(1)}, u32[]{:S(2)}, u32[]{:S(2)}) collective-permute-start(bf16[256,256]{1,0:T(8,128)(2,1)S(1)} %get-tuple-element.45), channel_id=1, source_target_pairs={{0,2},{2,0},{4,6},{6,4},{8,10},{10,8},{12,14},{14,12},{16,18},{18,... | collective-permute-start | bytes 393224 | tf_op jit(solution)/shard_map/ppermute | solution.py:24
  10.1 1.5 %collective-permute-start.2 = (bf16[256,256]{1,0:T(8,128)(2,1)S(1)}, bf16[256,256]{1,0:T(8,128)(2,1)S(1)}, u32[]{:S(2)}, u32[]{:S(2)}) collective-permute-start(bf16[256,256]{1,0:T(8,128)(2,1)S(1)} %get-tuple-element.46), channel_id=1, source_target_pairs={{0,4},{2,6},{4,0},{6,2},{8,12},{10,14},{12,8},{14,10},{16,20},{18,... | collective-permute-start | bytes 393224 | tf_op jit(solution)/shard_map/ppermute | solution.py:24
  11.7 0.0 collective-permute-done.4.refs_0_
  11.7 1.7 %collective-permute-start.3 = (bf16[256,256]{1,0:T(8,128)(2,1)S(1)}, bf16[256,256]{1,0:T(8,128)(2,1)S(1)}, u32[]{:S(2)}, u32[]{:S(2)}) collective-permute-start(bf16[256,256]{1,0:T(8,128)(2,1)S(1)} %get-tuple-element.47), channel_id=1, source_target_pairs={{0,6},{2,4},{4,2},{6,0},{8,14},{10,12},{12,10},{14,8},{16,22},{18,... | collective-permute-start | bytes 393224 | tf_op jit(solution)/shard_map/ppermute | solution.py:24
  13.3 0.4 collective-permute-done.5.refs_1_
  13.7 0.0 collective-permute-done.6.refs_2_
  13.7 0.2 pool_plane.1
  14.0 1.6 %collective-permute-start.9 = (bf16[256,256]{1,0:T(8,128)(2,1)S(1)}, bf16[256,256]{1,0:T(8,128)(2,1)S(1)}, u32[]{:S(2)}, u32[]{:S(2)}) collective-permute-start(bf16[256,256]{1,0:T(8,128)(2,1)S(1)} %get-tuple-element.54), channel_id=1, source_target_pairs={{0,8},{2,10},{4,12},{6,14},{8,0},{10,2},{12,4},{14,6},{16,24},{18,... | collective-permute-start | bytes 393224 | tf_op jit(solution)/shard_map/ppermute | solution.py:24
  15.6 2.6 %collective-permute-start.7 = (bf16[128,256]{1,0:T(8,128)(2,1)S(1)}, bf16[128,256]{1,0:T(8,128)(2,1)S(1)}, u32[]{:S(2)}, u32[]{:S(2)}) collective-permute-start(bf16[128,256]{1,0:T(8,128)(2,1)S(1)} %get-tuple-element.52), channel_id=1, source_target_pairs={{0,16},{2,18},{4,20},{6,22},{8,24},{10,26},{12,28},{14,30},{16,0},... | collective-permute-start | bytes 196616 | tf_op jit(solution)/shard_map/ppermute | solution.py:24
  18.2 0.0 collective-permute-done.1.refs_5_.refs_1_
  18.2 2.0 %collective-permute-start.8 = (bf16[128,256]{1,0:T(8,128)(2,1)S(1)}, bf16[128,256]{1,0:T(8,128)(2,1)S(1)}, u32[]{:S(2)}, u32[]{:S(2)}) collective-permute-start(bf16[128,256]{1,0:T(8,128)(2,1)S(1)} %get-tuple-element.53), channel_id=1, source_target_pairs={{0,24},{2,26},{4,28},{6,30},{8,16},{10,18},{12,20},{14,22},{16,8},... | collective-permute-start | bytes 196616 | tf_op jit(solution)/shard_map/ppermute | solution.py:24
  20.1 0.0 collective-permute-done.2.refs_4_.refs_0_.refs_2_
  20.1 0.0 collective-permute-done.3.refs_6_.refs_2_.refs_3_
  20.2 0.0 collective-permute-done.9.refs_8_
  20.2 1.4 %near_attention.1 = (f32[2,512,512]{2,1,0:T(8,128)S(1)}, f32[2,512,512]{2,1,0:T(8,128)S(1)}, f32[2,128,512]{2,1,0:T(8,128)S(1)}, f32[2,2,512]{2,1,0:T(2,128)S(1)}, bf16[4,512,128]{2,1,0:T(8,128)(2,1)S(1)}) custom-call(bf16[256,256]{1,0:T(8,128)(2,1)S(1)} %collective-permute-done.4.refs_0_, bf16[256,256]{1,0:T(8,128)(2,1)S(1)} %collective-permute-done.5.refs_1_, ...), custom_call_target="tpu_custom_call" | custom-call | flops 2000000000 | tf_op jit(solution)/shard_map/near_attention/pallas_call | solution.py:70
  21.6 0.4 collective-permute-done.7.refs_4_
  22.0 2.3 %collective-permute-done.8.refs_5_ = bf16[128,256]{1,0:T(8,128)(2,1)S(1)} collective-permute-done((bf16[128,256]{1,0:T(8,128)(2,1)S(1)}, bf16[128,256]{1,0:T(8,128)(2,1)S(1)}, u32[]{:S(2)}, u32[]{:S(2)}) %collective-permute-start.8) | collective-permute-done | bytes 65568 | tf_op jit(solution)/shard_map/ppermute | solution.py:24
  24.3 1.1 %far_attention.1 = (bf16[256,256]{1,0:T(8,128)(2,1)S(1)}, bf16[256,256]{1,0:T(8,128)(2,1)S(1)}, bf16[256,256]{1,0:T(8,128)(2,1)S(1)}, bf16[256,256]{1,0:T(8,128)...) custom-call(bf16[256,256]{1,0:T(8,128)(2,1)S(1)} %collective-permute, ...), custom_call_target="tpu_custom_call" | custom-call | flops 2000000000 | tf_op jit(solution)/shard_map/far_attention/pallas_call | solution.py:70
  25.4 1.9 %collective-permute-start.14 = (bf16[128,256]{1,0:T(8,128)(2,1)S(1)}, bf16[128,256]{1,0:T(8,128)(2,1)S(1)}, u32[]{:S(2)}, u32[]{:S(2)}) collective-permute-start(bf16[128,256]{1,0:T(8,128)(2,1)S(1)} %get-tuple-element.75), channel_id=1, source_target_pairs={{0,16},{2,18},{4,20},{6,22},{8,24},{10,26},{12,28},{14,30},{16,0},... | collective-permute-start | bytes 196616 | tf_op jit(solution)/shard_map/ppermute | solution.py:24
  27.3 1.5 %collective-permute-start.15 = (bf16[128,256]{1,0:T(8,128)(2,1)S(1)}, bf16[128,256]{1,0:T(8,128)(2,1)S(1)}, u32[]{:S(2)}, u32[]{:S(2)}) collective-permute-start(bf16[128,256]{1,0:T(8,128)(2,1)S(1)} %get-tuple-element.76), channel_id=1, source_target_pairs={{0,24},{2,26},{4,28},{6,30},{8,16},{10,18},{12,20},{14,22},{16,8},... | collective-permute-start | bytes 196616 | tf_op jit(solution)/shard_map/ppermute | solution.py:24
  28.8 0.2 collective-permute-start.13
  28.9 1.1 %plane_grads.1 = (bf16[256,256]{1,0:T(8,128)(2,1)S(1)}, bf16[256,256]{1,0:T(8,128)(2,1)S(1)}, bf16[256,256]{1,0:T(8,128)(2,1)S(1)}, bf16[256,256]{1,0:T(8,128)(2...) custom-call(bf16[256,256]{1,0:T(8,128)(2,1)S(1)} %get-tuple-element., ...), custom_call_target="tpu_custom_call", output_to_operand_aliasing={{0}: (11, {}), {1}: (12, {}), {2}: (13, {}), {3}: (14, {})} | custom-call | flops 2300000000 | tf_op jit(solution)/shard_map/plane_grads/pallas_call | solution.py:70
  30.1 2.3 %collective-permute-start.10 = (bf16[256,256]{1,0:T(8,128)(2,1)S(1)}, bf16[256,256]{1,0:T(8,128)(2,1)S(1)}, u32[]{:S(2)}, u32[]{:S(2)}) collective-permute-start(bf16[256,256]{1,0:T(8,128)(2,1)S(1)} %get-tuple-element.66), channel_id=1, source_target_pairs={{0,6},{2,4},{4,2},{6,0},{8,14},{10,12},{12,10},{14,8},{16,22},{18,... | collective-permute-start | bytes 393224 | tf_op jit(solution)/shard_map/ppermute | solution.py:24
  32.4 0.5 %collective-permute-start.11 = (bf16[256,256]{1,0:T(8,128)(2,1)S(1)}, bf16[256,256]{1,0:T(8,128)(2,1)S(1)}, u32[]{:S(2)}, u32[]{:S(2)}) collective-permute-start(bf16[256,256]{1,0:T(8,128)(2,1)S(1)} %get-tuple-element.67), channel_id=1, source_target_pairs={{0,2},{2,0},{4,6},{6,4},{8,10},{10,8},{12,14},{14,12},{16,18},{18,... | collective-permute-start | bytes 393224 | tf_op jit(solution)/shard_map/ppermute | solution.py:24
  32.9 0.0 collective-permute-done.14.refs_5_
  32.9 0.7 %collective-permute-start.12 = (bf16[256,256]{1,0:T(8,128)(2,1)S(1)}, bf16[256,256]{1,0:T(8,128)(2,1)S(1)}, u32[]{:S(2)}, u32[]{:S(2)}) collective-permute-start(bf16[256,256]{1,0:T(8,128)(2,1)S(1)} %get-tuple-element.68), channel_id=1, source_target_pairs={{0,4},{2,6},{4,0},{6,2},{8,12},{10,14},{12,8},{14,10},{16,20},{18,... | collective-permute-start | bytes 393224 | tf_op jit(solution)/shard_map/ppermute | solution.py:24
  33.6 0.0 collective-permute-done.15.refs_6_
  33.6 0.8 %collective-permute-done.13.refs_4_ = bf16[256,256]{1,0:T(8,128)(2,1)S(1)} collective-permute-done((bf16[256,256]{1,0:T(8,128)(2,1)S(1)}, bf16[256,256]{1,0:T(8,128)(2,1)S(1)}, u32[]{:S(2)}, u32[]{:S(2)}) %collective-permute-start.13) | collective-permute-done | bytes 131104 | tf_op jit(solution)/shard_map/ppermute | solution.py:24
  34.4 0.3 carry.1
  34.8 1.4 %collective-permute-start.18 = (bf16[256,256]{1,0:T(8,128)(2,1)S(1)}, bf16[256,256]{1,0:T(8,128)(2,1)S(1)}, u32[]{:S(2)}, u32[]{:S(2)}) collective-permute-start(bf16[256,256]{1,0:T(8,128)(2,1)S(1)} %get-tuple-element.81), channel_id=1, source_target_pairs={{0,4},{2,6},{4,0},{6,2},{8,12},{10,14},{12,8},{14,10},{16,20},{18,... | collective-permute-start | bytes 393224 | tf_op jit(solution)/shard_map/ppermute | solution.py:24
  36.2 1.6 %collective-permute-start.19 = (bf16[256,256]{1,0:T(8,128)(2,1)S(1)}, bf16[256,256]{1,0:T(8,128)(2,1)S(1)}, u32[]{:S(2)}, u32[]{:S(2)}) collective-permute-start(bf16[256,256]{1,0:T(8,128)(2,1)S(1)} %get-tuple-element.82), channel_id=1, source_target_pairs={{0,6},{2,4},{4,2},{6,0},{8,14},{10,12},{12,10},{14,8},{16,22},{18,... | collective-permute-start | bytes 393224 | tf_op jit(solution)/shard_map/ppermute | solution.py:24
  37.8 0.0 collective-permute-done.10.refs_0_.refs_3_
  37.8 0.5 %collective-permute-start.20 = (bf16[256,256]{1,0:T(8,128)(2,1)S(1)}, bf16[256,256]{1,0:T(8,128)(2,1)S(1)}, u32[]{:S(2)}, u32[]{:S(2)}) collective-permute-start(bf16[256,256]{1,0:T(8,128)(2,1)S(1)} %get-tuple-element.83), channel_id=1, source_target_pairs={{0,2},{2,0},{4,6},{6,4},{8,10},{10,8},{12,14},{14,12},{16,18},{18,... | collective-permute-start | bytes 393224 | tf_op jit(solution)/shard_map/ppermute | solution.py:24
  38.3 1.3 %collective-permute-done.11.refs_1_.refs_4_ = bf16[256,256]{1,0:T(8,128)(2,1)S(1)} collective-permute-done((bf16[256,256]{1,0:T(8,128)(2,1)S(1)}, bf16[256,256]{1,0:T(8,128)(2,1)S(1)}, u32[]{:S(2)}, u32[]{:S(2)}) %collective-permute-start.11) | collective-permute-done | bytes 131104 | tf_op jit(solution)/shard_map/ppermute | solution.py:24
  39.6 0.5 %collective-permute-done.12.refs_2_.refs_5_ = bf16[256,256]{1,0:T(8,128)(2,1)S(1)} collective-permute-done((bf16[256,256]{1,0:T(8,128)(2,1)S(1)}, bf16[256,256]{1,0:T(8,128)(2,1)S(1)}, u32[]{:S(2)}, u32[]{:S(2)}) %collective-permute-start.12) | collective-permute-done | bytes 131104 | tf_op jit(solution)/shard_map/ppermute | solution.py:24
  40.1 0.8 %project.1 = (f32[128,1024]{1,0:T(8,128)S(1)}, bf16[64,1024]{1,0:T(8,128)(2,1)S(1)}, bf16[64,1024]{1,0:T(8,128)(2,1)S(1)}) custom-call(bf16[256,256]{1,0:T(8,128)(2,1)S(1)} %collective-permute-done.10.refs_0_.refs_3_, bf16[256,256]{1,0:T(8,128)(2,1)S(1)} %collective-permute-done.11.refs_1_.refs_4_, ...), custom_call_target="tpu_custom_call" | custom-call | flops 10000000 | tf_op jit(solution)/shard_map/project/pallas_call | solution.py:70
  40.9 0.1 collective-permute-start.16
  41.0 0.5 %collective-permute-start.17 = (bf16[64,1024]{1,0:T(8,128)(2,1)S(1)}, bf16[64,1024]{1,0:T(8,128)(2,1)S(1)}, u32[]{:S(2)}, u32[]{:S(2)}) collective-permute-start(bf16[64,1024]{1,0:T(8,128)(2,1)S(1)} %get-tuple-element.80), channel_id=1, source_target_pairs={{0,1},{1,0},{2,3},{3,2},{4,5},{5,4},{6,7},{7,6},{8,9},{9,8},{10,11... | collective-permute-start | bytes 393224 | tf_op jit(solution)/shard_map/ppermute | solution.py:24
  41.5 1.5 %collective-permute-done.18.refs_7_ = bf16[256,256]{1,0:T(8,128)(2,1)S(1)} collective-permute-done((bf16[256,256]{1,0:T(8,128)(2,1)S(1)}, bf16[256,256]{1,0:T(8,128)(2,1)S(1)}, u32[]{:S(2)}, u32[]{:S(2)}) %collective-permute-start.18) | collective-permute-done | bytes 131104 | tf_op jit(solution)/shard_map/ppermute | solution.py:24
  42.9 0.0 collective-permute-done.19.refs_8_
  42.9 0.1 collective-permute-done.20.refs_9_
  43.0 0.0 collective-permute-done.16.refs_1_
  43.0 0.0 collective-permute-done.17.refs_2_
  43.0 1.1 %join.1 = (bf16[128,1024]{1,0:T(8,128)(2,1)}, bf16[128,1024]{1,0:T(8,128)(2,1)}, bf16[128,1024]{1,0:T(8,128)(2,1)}, bf16[128,1024]{1,0:T(8,128)(2,1)}) custom-call(f32[128,1024]{1,0:T(8,128)S(1)} %get-tuple-element.78.refs_0_, bf16[64,1024]{1,0:T(8,128)(2,1)S(1)} %collective-permute-done.16.refs_1_, bf16[64,1024]{1,0:T(8,128)(2,1)S(1)} %collective-permute-done.17.refs_2_, ...), custom_call_target="tpu_custom_call" | custom-call | flops 1000000000 | tf_op jit(solution)/shard_map/join/pallas_call | solution.py:70
Async XLA Ops:
  0.6 6.0 %copy-start.2 = (bf16[128,1024]{1,0:T(8,128)(2,1)S(1)}, bf16[128,1024]{1,0:T(8,128)(2,1)}, u32[]{:S(2)}) copy-start(bf16[128,1024]{1,0:T(8,128)(2,1)} %refs_1_.2) | copy-start | bytes 786436
  0.6 6.0 %copy-start = (bf16[1024,2048]{1,0:T(8,128)(2,1)S(1)}, bf16[1024,2048]{1,0:T(8,128)(2,1)}, u32[]{:S(2)}) copy-start(bf16[1024,2048]{1,0:T(8,128)(2,1)} %refs_4_.1) | copy-start | bytes 12582916
  0.7 6.0 %copy-start.1 = (bf16[128,1024]{1,0:T(8,128)(2,1)S(1)}, bf16[128,1024]{1,0:T(8,128)(2,1)}, u32[]{:S(2)}) copy-start(bf16[128,1024]{1,0:T(8,128)(2,1)} %refs_0_.2) | copy-start | bytes 786436
  0.7 6.0 %collective-permute-start = (bf16[128,1024]{1,0:T(8,128)(2,1)}, bf16[128,1024]{1,0:T(8,128)(2,1)S(1)}, u32[]{:S(2)}, u32[]{:S(2)}) collective-permute-start(bf16[128,1024]{1,0:T(8,128)(2,1)} %refs_1_.2), channel_id=1, source_target_pairs={{0,1},{1,0},{2,3},{3,2},{4,5},{5,4},{6,7},{7,6},{8,9},{9,8},{10,11... | collective-permute-start | bytes 786440 | tf_op jit(solution)/shard_map/ppermute | solution.py:24
  2.6 9.1 %collective-permute-start.4 = (bf16[256,256]{1,0:T(8,128)(2,1)S(1)}, bf16[256,256]{1,0:T(8,128)(2,1)S(1)}, u32[]{:S(2)}, u32[]{:S(2)}) collective-permute-start(bf16[256,256]{1,0:T(8,128)(2,1)S(1)} %get-tuple-element.48), channel_id=1, source_target_pairs={{0,6},{2,4},{4,2},{6,0},{8,14},{10,12},{12,10},{14,8},{16,22},{18,... | collective-permute-start | bytes 393224 | tf_op jit(solution)/shard_map/ppermute | solution.py:24
  6.0 7.7 %collective-permute-start.5 = (bf16[256,256]{1,0:T(8,128)(2,1)S(1)}, bf16[256,256]{1,0:T(8,128)(2,1)S(1)}, u32[]{:S(2)}, u32[]{:S(2)}) collective-permute-start(bf16[256,256]{1,0:T(8,128)(2,1)S(1)} %get-tuple-element.49), channel_id=1, source_target_pairs={{0,2},{2,0},{4,6},{6,4},{8,10},{10,8},{12,14},{14,12},{16,18},{18,... | collective-permute-start | bytes 393224 | tf_op jit(solution)/shard_map/ppermute | solution.py:24
  6.5 7.2 %collective-permute-start.6 = (bf16[256,256]{1,0:T(8,128)(2,1)S(1)}, bf16[256,256]{1,0:T(8,128)(2,1)S(1)}, u32[]{:S(2)}, u32[]{:S(2)}) collective-permute-start(bf16[256,256]{1,0:T(8,128)(2,1)S(1)} %get-tuple-element.50), channel_id=1, source_target_pairs={{0,4},{2,6},{4,0},{6,2},{8,12},{10,14},{12,8},{14,10},{16,20},{18,... | collective-permute-start | bytes 393224 | tf_op jit(solution)/shard_map/ppermute | solution.py:24
  8.2 10.0 %collective-permute-start.1 = (bf16[256,256]{1,0:T(8,128)(2,1)S(1)}, bf16[256,256]{1,0:T(8,128)(2,1)S(1)}, u32[]{:S(2)}, u32[]{:S(2)}) collective-permute-start(bf16[256,256]{1,0:T(8,128)(2,1)S(1)} %get-tuple-element.45), channel_id=1, source_target_pairs={{0,2},{2,0},{4,6},{6,4},{8,10},{10,8},{12,14},{14,12},{16,18},{18,... | collective-permute-start | bytes 393224 | tf_op jit(solution)/shard_map/ppermute | solution.py:24
  10.1 10.0 %collective-permute-start.2 = (bf16[256,256]{1,0:T(8,128)(2,1)S(1)}, bf16[256,256]{1,0:T(8,128)(2,1)S(1)}, u32[]{:S(2)}, u32[]{:S(2)}) collective-permute-start(bf16[256,256]{1,0:T(8,128)(2,1)S(1)} %get-tuple-element.46), channel_id=1, source_target_pairs={{0,4},{2,6},{4,0},{6,2},{8,12},{10,14},{12,8},{14,10},{16,20},{18,... | collective-permute-start | bytes 393224 | tf_op jit(solution)/shard_map/ppermute | solution.py:24
  11.7 8.5 %collective-permute-start.3 = (bf16[256,256]{1,0:T(8,128)(2,1)S(1)}, bf16[256,256]{1,0:T(8,128)(2,1)S(1)}, u32[]{:S(2)}, u32[]{:S(2)}) collective-permute-start(bf16[256,256]{1,0:T(8,128)(2,1)S(1)} %get-tuple-element.47), channel_id=1, source_target_pairs={{0,6},{2,4},{4,2},{6,0},{8,14},{10,12},{12,10},{14,8},{16,22},{18,... | collective-permute-start | bytes 393224 | tf_op jit(solution)/shard_map/ppermute | solution.py:24
  14.0 6.2 %collective-permute-start.9 = (bf16[256,256]{1,0:T(8,128)(2,1)S(1)}, bf16[256,256]{1,0:T(8,128)(2,1)S(1)}, u32[]{:S(2)}, u32[]{:S(2)}) collective-permute-start(bf16[256,256]{1,0:T(8,128)(2,1)S(1)} %get-tuple-element.54), channel_id=1, source_target_pairs={{0,8},{2,10},{4,12},{6,14},{8,0},{10,2},{12,4},{14,6},{16,24},{18,... | collective-permute-start | bytes 393224 | tf_op jit(solution)/shard_map/ppermute | solution.py:24
  15.6 6.4 %collective-permute-start.7 = (bf16[128,256]{1,0:T(8,128)(2,1)S(1)}, bf16[128,256]{1,0:T(8,128)(2,1)S(1)}, u32[]{:S(2)}, u32[]{:S(2)}) collective-permute-start(bf16[128,256]{1,0:T(8,128)(2,1)S(1)} %get-tuple-element.52), channel_id=1, source_target_pairs={{0,16},{2,18},{4,20},{6,22},{8,24},{10,26},{12,28},{14,30},{16,0},... | collective-permute-start | bytes 196616 | tf_op jit(solution)/shard_map/ppermute | solution.py:24
  18.2 6.1 %collective-permute-start.8 = (bf16[128,256]{1,0:T(8,128)(2,1)S(1)}, bf16[128,256]{1,0:T(8,128)(2,1)S(1)}, u32[]{:S(2)}, u32[]{:S(2)}) collective-permute-start(bf16[128,256]{1,0:T(8,128)(2,1)S(1)} %get-tuple-element.53), channel_id=1, source_target_pairs={{0,24},{2,26},{4,28},{6,30},{8,16},{10,18},{12,20},{14,22},{16,8},... | collective-permute-start | bytes 196616 | tf_op jit(solution)/shard_map/ppermute | solution.py:24
  25.4 7.6 %collective-permute-start.14 = (bf16[128,256]{1,0:T(8,128)(2,1)S(1)}, bf16[128,256]{1,0:T(8,128)(2,1)S(1)}, u32[]{:S(2)}, u32[]{:S(2)}) collective-permute-start(bf16[128,256]{1,0:T(8,128)(2,1)S(1)} %get-tuple-element.75), channel_id=1, source_target_pairs={{0,16},{2,18},{4,20},{6,22},{8,24},{10,26},{12,28},{14,30},{16,0},... | collective-permute-start | bytes 196616 | tf_op jit(solution)/shard_map/ppermute | solution.py:24
  27.3 6.4 %collective-permute-start.15 = (bf16[128,256]{1,0:T(8,128)(2,1)S(1)}, bf16[128,256]{1,0:T(8,128)(2,1)S(1)}, u32[]{:S(2)}, u32[]{:S(2)}) collective-permute-start(bf16[128,256]{1,0:T(8,128)(2,1)S(1)} %get-tuple-element.76), channel_id=1, source_target_pairs={{0,24},{2,26},{4,28},{6,30},{8,16},{10,18},{12,20},{14,22},{16,8},... | collective-permute-start | bytes 196616 | tf_op jit(solution)/shard_map/ppermute | solution.py:24
  28.8 5.7 %collective-permute-start.13 = (bf16[256,256]{1,0:T(8,128)(2,1)S(1)}, bf16[256,256]{1,0:T(8,128)(2,1)S(1)}, u32[]{:S(2)}, u32[]{:S(2)}) collective-permute-start(bf16[256,256]{1,0:T(8,128)(2,1)S(1)} %get-tuple-element.74), channel_id=1, source_target_pairs={{0,8},{2,10},{4,12},{6,14},{8,0},{10,2},{12,4},{14,6},{16,24},{18,... | collective-permute-start | bytes 393224 | tf_op jit(solution)/shard_map/ppermute | solution.py:24
  30.1 7.7 %collective-permute-start.10 = (bf16[256,256]{1,0:T(8,128)(2,1)S(1)}, bf16[256,256]{1,0:T(8,128)(2,1)S(1)}, u32[]{:S(2)}, u32[]{:S(2)}) collective-permute-start(bf16[256,256]{1,0:T(8,128)(2,1)S(1)} %get-tuple-element.66), channel_id=1, source_target_pairs={{0,6},{2,4},{4,2},{6,0},{8,14},{10,12},{12,10},{14,8},{16,22},{18,... | collective-permute-start | bytes 393224 | tf_op jit(solution)/shard_map/ppermute | solution.py:24
  32.4 7.2 %collective-permute-start.11 = (bf16[256,256]{1,0:T(8,128)(2,1)S(1)}, bf16[256,256]{1,0:T(8,128)(2,1)S(1)}, u32[]{:S(2)}, u32[]{:S(2)}) collective-permute-start(bf16[256,256]{1,0:T(8,128)(2,1)S(1)} %get-tuple-element.67), channel_id=1, source_target_pairs={{0,2},{2,0},{4,6},{6,4},{8,10},{10,8},{12,14},{14,12},{16,18},{18,... | collective-permute-start | bytes 393224 | tf_op jit(solution)/shard_map/ppermute | solution.py:24
  32.9 7.2 %collective-permute-start.12 = (bf16[256,256]{1,0:T(8,128)(2,1)S(1)}, bf16[256,256]{1,0:T(8,128)(2,1)S(1)}, u32[]{:S(2)}, u32[]{:S(2)}) collective-permute-start(bf16[256,256]{1,0:T(8,128)(2,1)S(1)} %get-tuple-element.68), channel_id=1, source_target_pairs={{0,4},{2,6},{4,0},{6,2},{8,12},{10,14},{12,8},{14,10},{16,20},{18,... | collective-permute-start | bytes 393224 | tf_op jit(solution)/shard_map/ppermute | solution.py:24
  34.8 8.2 %collective-permute-start.18 = (bf16[256,256]{1,0:T(8,128)(2,1)S(1)}, bf16[256,256]{1,0:T(8,128)(2,1)S(1)}, u32[]{:S(2)}, u32[]{:S(2)}) collective-permute-start(bf16[256,256]{1,0:T(8,128)(2,1)S(1)} %get-tuple-element.81), channel_id=1, source_target_pairs={{0,4},{2,6},{4,0},{6,2},{8,12},{10,14},{12,8},{14,10},{16,20},{18,... | collective-permute-start | bytes 393224 | tf_op jit(solution)/shard_map/ppermute | solution.py:24
  36.2 6.7 %collective-permute-start.19 = (bf16[256,256]{1,0:T(8,128)(2,1)S(1)}, bf16[256,256]{1,0:T(8,128)(2,1)S(1)}, u32[]{:S(2)}, u32[]{:S(2)}) collective-permute-start(bf16[256,256]{1,0:T(8,128)(2,1)S(1)} %get-tuple-element.82), channel_id=1, source_target_pairs={{0,6},{2,4},{4,2},{6,0},{8,14},{10,12},{12,10},{14,8},{16,22},{18,... | collective-permute-start | bytes 393224 | tf_op jit(solution)/shard_map/ppermute | solution.py:24
  37.8 5.2 %collective-permute-start.20 = (bf16[256,256]{1,0:T(8,128)(2,1)S(1)}, bf16[256,256]{1,0:T(8,128)(2,1)S(1)}, u32[]{:S(2)}, u32[]{:S(2)}) collective-permute-start(bf16[256,256]{1,0:T(8,128)(2,1)S(1)} %get-tuple-element.83), channel_id=1, source_target_pairs={{0,2},{2,0},{4,6},{6,4},{8,10},{10,8},{12,14},{14,12},{16,18},{18,... | collective-permute-start | bytes 393224 | tf_op jit(solution)/shard_map/ppermute | solution.py:24
  40.9 2.1 %collective-permute-start.16 = (bf16[64,1024]{1,0:T(8,128)(2,1)S(1)}, bf16[64,1024]{1,0:T(8,128)(2,1)S(1)}, u32[]{:S(2)}, u32[]{:S(2)}) collective-permute-start(bf16[64,1024]{1,0:T(8,128)(2,1)S(1)} %get-tuple-element.79), channel_id=1, source_target_pairs={{0,1},{1,0},{2,3},{3,2},{4,5},{5,4},{6,7},{7,6},{8,9},{9,8},{10,11... | collective-permute-start | bytes 393224 | tf_op jit(solution)/shard_map/ppermute | solution.py:24
  41.0 2.0 %collective-permute-start.17 = (bf16[64,1024]{1,0:T(8,128)(2,1)S(1)}, bf16[64,1024]{1,0:T(8,128)(2,1)S(1)}, u32[]{:S(2)}, u32[]{:S(2)}) collective-permute-start(bf16[64,1024]{1,0:T(8,128)(2,1)S(1)} %get-tuple-element.80), channel_id=1, source_target_pairs={{0,1},{1,0},{2,3},{3,2},{4,5},{5,4},{6,7},{7,6},{8,9},{9,8},{10,11... | collective-permute-start | bytes 393224 | tf_op jit(solution)/shard_map/ppermute | solution.py:24

commit v8 on v7

--- a/solution.py
+++ b/solution.py
@@ -100,17 +100,23 @@
 
 
 def key_value_kernel(k_ref, v_ref, *refs):
-    outs, sems = refs[:PLANE], refs[PLANE]
+    outs, sems = refs[:-1], refs[-1]
     rows, width = k_ref.shape[0], k_ref.shape[1] // PLANE
     pairs = []
-    for r in range(PLANE):
-        pairs.append((k_ref.at[:, columns(r, width)], outs[r].at[part(0, rows), :]))
-        pairs.append((v_ref.at[:, columns(r, width)], outs[r].at[part(1, rows), :]))
+    for r, out in enumerate(outs, 1):
+        pairs.append((k_ref.at[:, columns(r, width)], out.at[part(0, rows), :]))
+        pairs.append((v_ref.at[:, columns(r, width)], out.at[part(1, rows), :]))
     for copy in start_all(pairs, sems):
         copy.wait()
 
 
-def cotangent_kernel(q_ref, own_ref, other_ref, w_ref, *outs):
+def cotangent_kernel(q_ref, own_ref, other_ref, w_ref, k_ref, v_ref, *refs):
+    outs, kv_out, sems = refs[:PLANE], refs[PLANE], refs[PLANE + 1]
+    mine = columns(0, w_ref.shape[0] // PLANE)
+    copies = start_all(
+        [(ref.at[:, mine], kv_out.at[part(m, q_ref.shape[0]), :]) for m, ref in enumerate((k_ref, v_ref))],
+        sems,
+    )
     rows, width = q_ref.shape[0], q_ref.shape[1] // PLANE
     half = own_ref.shape[1]
     head = lax.axis_index("head")
@@ -123,6 +129,8 @@
             dot(own_ref[...], w_ref[here, own_at], 1, 1)
             + dot(other_ref[...], w_ref[here, other_at], 1, 1)
         ).astype(BF16)
+    for copy in copies:
+        copy.wait()
 
 
 def average_matrix(rows, times):
@@ -164,7 +172,7 @@
 
 def near_kernel(*refs):
     kvs, qgs, first = refs[:PLANE], refs[PLANE : 2 * PLANE], refs[2 * PLANE]
-    weight_out, dots_out, sums_out, stats_out, keys_out = refs[2 * PLANE + 1 :]
+    weight_out, dots_out, sums_out, stats_out, keys_out, turned_out = refs[2 * PLANE + 1 :]
     rows, width = qgs[0].shape[0] // 2, qgs[0].shape[1]
     cases = [(h, p) for h in range(width // DH) for p in range(2)]
     tokens = [part(p, 2 * rows) for h, p in cases]
@@ -191,12 +199,13 @@
         stats_out[h, 0:1, t] = row_max
         stats_out[h, 1:2, t] = jnp.sum(weights, 0, keepdims=True)
         keys_out[n] = keys[n]
+        turned_out[h, :, t] = both(qgs, p, part(1, rows), part(h, DH)).T
 
 
 def far_grad_kernel(n_far, *refs):
     qgs, fars = refs[:PLANE], refs[PLANE : PLANE + n_far]
-    weight_ref, dots_ref, sums_ref, stats_ref = refs[PLANE + n_far : PLANE + n_far + 4]
-    outs = refs[PLANE + n_far + 4 :]
+    weight_ref, dots_ref, sums_ref, stats_ref, turned_ref = refs[PLANE + n_far : PLANE + n_far + 5]
+    outs = refs[PLANE + n_far + 5 :]
     ads, grad_out, stats_out, far_out = outs[:PLANE], outs[PLANE], outs[PLANE + 1], outs[PLANE + 2 :]
     rows, width = qgs[0].shape[0] // 2, qgs[0].shape[1]
     first = slice(3 * rows, weight_ref.shape[1])
@@ -222,7 +231,7 @@
     score_grads, probs = [], []
     for h in heads:
         attended = ((sums_ref[h] * near_parts[h] + sums[h]) * inverses[h]).astype(BF16)
-        delta = jnp.sum(grads[h].T.astype(F32) * attended.astype(F32), 0, keepdims=True)
+        delta = jnp.sum(turned_ref[h].astype(F32) * attended.astype(F32), 0, keepdims=True)
         near_scale = near_parts[h] * inverses[h]
         near_probs = weight_ref[h, first, :] * near_scale
         far_probs = weights[h] * inverses[h]
@@ -393,14 +402,14 @@
 
     other_cotangent = xor_permute(cotangent, 1, "head")
     key_values = call(
-        key_value_kernel, blocks, key_rows, value_rows,
-        hbm=(0, 1), scratch=[dma(2 * PLANE)], cost_us=8, name="pack_keys_values",
-    )
-    key_values = plane_exchange(key_values)
-    query_grads = call(
-        cotangent_kernel, blocks, queries, cotangent, other_cotangent, out_weight,
-        cost_us=3.0, name="grad_attended",
-    )
+        key_value_kernel, blocks[1:], key_rows, value_rows,
+        hbm=(0, 1), scratch=[dma(2 * PLANE - 2)], cost_us=8, name="pack_keys_values",
+    )
+    *query_grads, own_keys_values = call(
+        cotangent_kernel, blocks + blocks[:1], queries, cotangent, other_cotangent, out_weight,
+        key_rows, value_rows, hbm=(4, 5), scratch=[dma(2)], cost_us=3.0, name="grad_attended",
+    )
+    key_values = plane_exchange([own_keys_values, *key_values])
     query_grads = plane_exchange(query_grads)
     near, pooled, pooled3 = call(
         far_kernel, [shape(2 * rows, width)] + [shape(rows, width)] * 2, *key_values, planes=((0, OKV),),
@@ -416,18 +425,18 @@
     far_rows = sum(far.shape[0] for far in fars[1:]) // 2
     heads, tokens = width // DH, PLANE * rows
     near_rows = 3 * rows + fars[0].shape[0] // 2
-    weights, dots, sums, stats, near_keys = call(
+    weights, dots, sums, stats, near_keys, turned = call(
         near_kernel,
         [shape(heads, near_rows, tokens, t=F32)] * 2
         + [shape(heads, DH, tokens, t=F32), shape(heads, 2, tokens, t=F32)]
-        + [shape(2 * heads, near_rows, DH)],
+        + [shape(2 * heads, near_rows, DH), shape(heads, DH, tokens)],
         *key_values, *query_grads, fars[0], planes=((0, OKV), (PLANE, OQG)), cost_us=2.0, name="near_attention",
     )
     results = call(
         lambda *refs: far_grad_kernel(len(fars) - 1, *refs),
         blocks + [shape(heads, far_rows, tokens), shape(heads, 2, tokens, t=F32)]
         + [shape(*far.shape) for far in fars],
-        *query_grads, *fars[1:], weights, dots, sums, stats, planes=((0, OQG),), cost_us=2.0, name="far_attention",
+        *query_grads, *fars[1:], weights, dots, sums, stats, turned, planes=((0, OQG),), cost_us=2.0, name="far_attention",
     )
     ads, kept, far_grads = results[:PLANE], results[PLANE : PLANE + 2], list(results[PLANE + 2 :])
     first = PLANE + len(fars) + 4
@@ -455,7 +464,7 @@
             far_grads[at] = (far_grads[at].astype(F32) + ups[n]).astype(BF16)
     backs = [xor_permute(far_grads[at], n * PLANE) for at, n in enumerate(ORDER)]
     att_dq = plane_exchange(att_dq)
-    dkv = call(carry_kernel, blocks, *dkv, *backs, *extra, cost_us=5.0, name="carry")
+    dkv = call(carry_kernel, blocks, *dkv, *backs[1:], backs[0], *extra, cost_us=5.0, name="carry")
     own_sum, *other_sum = call(
         output_kernel,
         [shape(rows, features, t=F32)] + [shape(rows // PIECES, features)] * PIECES,

time: 44.2 us -> 44.2 us (level)
  starting transfers between devices: 27.1 us -> 26.4 us
  Pallas kernels: 8.91 us -> 9.53 us
    ppermute x21, starting transfers between devices: 27.1 us -> 26.4 us  [xor_permute(): return lax.ppermute(block, axis, [(i, i ^ mask) for i in range(count)])]
    pallas_call x9, Pallas kernels: 8.91 us -> 9.53 us  [call(): pl.pallas_call(run, out_shape=[space(out.shape, out.dtype) for out in out...]
  transfers between devices with their start and end apart: 21 -> 21, of which waited for: 8 -> 8; matrix products, arithmetic and copies ran while one was open for 0% -> 0% of each run, Pallas kernels for 15% -> 17%
where the time goes in v8:
time: 44.2 us; the launch traced here: 44 us
  starting transfers between devices  26.4 us (60%)
  Pallas kernels  9.53 us (22%)
  waiting for transfers between devices  7.28 us (16%)
  between operations  0.75 us (2%)
    ppermute x21, starting transfers between devices, xor_permute(): return lax.ppermute(block, axis, [(i, i ^ mask) for i in range(count)])  26.4 us
    pallas_call x9, Pallas kernels, call(): pl.pallas_call(run, out_shape=[space(out.shape, out.dtype) for out in out...  9.53 us
    ppermute x21, waiting for transfers between devices, xor_permute(): return lax.ppermute(block, axis, [(i, i ^ mask) for i in range(count)])  7.28 us
  transfers between devices with their start and end apart: 21, of which 8 were waited for; matrix products, arithmetic and copies ran while one was open for 0% of the time, Pallas kernels for 17%

profile of v8, /device:TPU:0, one launch (start us, length us, event | category | flops | bytes accessed | tf_op | source)
XLA Modules:
  0.0 44.0 jit_solution(9716957353187895381)
XLA Ops:
  0.6 0.0 copy-start.2
  0.6 0.0 copy-start
  0.7 0.0 copy-start.1
  0.7 0.5 %collective-permute-start = (bf16[128,1024]{1,0:T(8,128)(2,1)}, bf16[128,1024]{1,0:T(8,128)(2,1)S(1)}, u32[]{:S(2)}, u32[]{:S(2)}) collective-permute-start(bf16[128,1024]{1,0:T(8,128)(2,1)} %refs_1_.2), channel_id=1, source_target_pairs={{0,1},{1,0},{2,3},{3,2},{4,5},{5,4},{6,7},{7,6},{8,9},{9,8},{10,11... | collective-permute-start | bytes 786440 | tf_op jit(solution)/shard_map/ppermute | solution.py:24
  1.2 1.3 %pack_keys_values.1 = (bf16[256,256]{1,0:T(8,128)(2,1)S(1)}, bf16[256,256]{1,0:T(8,128)(2,1)S(1)}, bf16[256,256]{1,0:T(8,128)(2,1)S(1)}) custom-call(bf16[128,1024]{1,0:T(8,128)(2,1)} %refs_0_.3, bf16[128,1024]{1,0:T(8,128)(2,1)} %refs_1_.3), custom_call_target="tpu_custom_call" | custom-call | flops 8000000000 | tf_op jit(solution)/shard_map/pack_keys_values/pallas_call | solution.py:70
  2.5 3.4 %collective-permute-start.4 = (bf16[256,256]{1,0:T(8,128)(2,1)S(1)}, bf16[256,256]{1,0:T(8,128)(2,1)S(1)}, u32[]{:S(2)}, u32[]{:S(2)}) collective-permute-start(bf16[256,256]{1,0:T(8,128)(2,1)S(1)} %get-tuple-element.49), channel_id=1, source_target_pairs={{0,6},{2,4},{4,2},{6,0},{8,14},{10,12},{12,10},{14,8},{16,22},{18,... | collective-permute-start | bytes 393224 | tf_op jit(solution)/shard_map/ppermute | solution.py:24
  5.9 0.5 %collective-permute-start.5 = (bf16[256,256]{1,0:T(8,128)(2,1)S(1)}, bf16[256,256]{1,0:T(8,128)(2,1)S(1)}, u32[]{:S(2)}, u32[]{:S(2)}) collective-permute-start(bf16[256,256]{1,0:T(8,128)(2,1)S(1)} %get-tuple-element.50), channel_id=1, source_target_pairs={{0,2},{2,0},{4,6},{6,4},{8,10},{10,8},{12,14},{14,12},{16,18},{18,... | collective-permute-start | bytes 393224 | tf_op jit(solution)/shard_map/ppermute | solution.py:24
  6.5 0.1 collective-permute-start.6
  6.6 0.0 collective-permute-done.refs_2_
  6.6 0.0 copy-done.2
  6.6 0.0 copy-done
  6.6 0.0 copy-done.1
  6.6 2.2 %grad_attended.1 = (bf16[256,256]{1,0:T(8,128)(2,1)S(1)}, bf16[256,256]{1,0:T(8,128)(2,1)S(1)}, bf16[256,256]{1,0:T(8,128)(2,1)S(1)}, bf16[256,256]{1,0:T(8,128)(2,1)S(1)}, bf16[256,256]{1,0:T(8,128)(2,1)S(1)}) custom-call(bf16[128,1024]{1,0:T(8,128)(2,1)S(1)} %copy-done.1, bf16[128,1024]{1,0:T(8,128)(2,1)S(1)} %copy-done.2, ...), custom_call_target="tpu_custom_call" | custom-call | flops 3000000000 | tf_op jit(solution)/shard_map/grad_attended/pallas_call | solution.py:70
  8.8 2.0 %collective-permute-start.1 = (bf16[256,256]{1,0:T(8,128)(2,1)S(1)}, bf16[256,256]{1,0:T(8,128)(2,1)S(1)}, u32[]{:S(2)}, u32[]{:S(2)}) collective-permute-start(bf16[256,256]{1,0:T(8,128)(2,1)S(1)} %get-tuple-element.46), channel_id=1, source_target_pairs={{0,2},{2,0},{4,6},{6,4},{8,10},{10,8},{12,14},{14,12},{16,18},{18,... | collective-permute-start | bytes 393224 | tf_op jit(solution)/shard_map/ppermute | solution.py:24
  10.7 1.5 %collective-permute-start.2 = (bf16[256,256]{1,0:T(8,128)(2,1)S(1)}, bf16[256,256]{1,0:T(8,128)(2,1)S(1)}, u32[]{:S(2)}, u32[]{:S(2)}) collective-permute-start(bf16[256,256]{1,0:T(8,128)(2,1)S(1)} %get-tuple-element.47), channel_id=1, source_target_pairs={{0,4},{2,6},{4,0},{6,2},{8,12},{10,14},{12,8},{14,10},{16,20},{18,... | collective-permute-start | bytes 393224 | tf_op jit(solution)/shard_map/ppermute | solution.py:24
  12.3 0.0 collective-permute-done.4.refs_0_
  12.3 1.0 %collective-permute-start.3 = (bf16[256,256]{1,0:T(8,128)(2,1)S(1)}, bf16[256,256]{1,0:T(8,128)(2,1)S(1)}, u32[]{:S(2)}, u32[]{:S(2)}) collective-permute-start(bf16[256,256]{1,0:T(8,128)(2,1)S(1)} %get-tuple-element.48), channel_id=1, source_target_pairs={{0,6},{2,4},{4,2},{6,0},{8,14},{10,12},{12,10},{14,8},{16,22},{18,... | collective-permute-start | bytes 393224 | tf_op jit(solution)/shard_map/ppermute | solution.py:24
  13.2 0.4 collective-permute-done.5.refs_1_
  13.7 0.0 collective-permute-done.6.refs_2_
  13.7 0.2 pool_plane.1
  13.9 1.6 %collective-permute-start.9 = (bf16[256,256]{1,0:T(8,128)(2,1)S(1)}, bf16[256,256]{1,0:T(8,128)(2,1)S(1)}, u32[]{:S(2)}, u32[]{:S(2)}) collective-permute-start(bf16[256,256]{1,0:T(8,128)(2,1)S(1)} %get-tuple-element.55), channel_id=1, source_target_pairs={{0,8},{2,10},{4,12},{6,14},{8,0},{10,2},{12,4},{14,6},{16,24},{18,... | collective-permute-start | bytes 393224 | tf_op jit(solution)/shard_map/ppermute | solution.py:24
  15.5 2.6 %collective-permute-start.7 = (bf16[128,256]{1,0:T(8,128)(2,1)S(1)}, bf16[128,256]{1,0:T(8,128)(2,1)S(1)}, u32[]{:S(2)}, u32[]{:S(2)}) collective-permute-start(bf16[128,256]{1,0:T(8,128)(2,1)S(1)} %get-tuple-element.53), channel_id=1, source_target_pairs={{0,16},{2,18},{4,20},{6,22},{8,24},{10,26},{12,28},{14,30},{16,0},... | collective-permute-start | bytes 196616 | tf_op jit(solution)/shard_map/ppermute | solution.py:24
  18.1 0.0 collective-permute-done.1.refs_5_.refs_1_
  18.1 1.9 %collective-permute-start.8 = (bf16[128,256]{1,0:T(8,128)(2,1)S(1)}, bf16[128,256]{1,0:T(8,128)(2,1)S(1)}, u32[]{:S(2)}, u32[]{:S(2)}) collective-permute-start(bf16[128,256]{1,0:T(8,128)(2,1)S(1)} %get-tuple-element.54), channel_id=1, source_target_pairs={{0,24},{2,26},{4,28},{6,30},{8,16},{10,18},{12,20},{14,22},{16,8},... | collective-permute-start | bytes 196616 | tf_op jit(solution)/shard_map/ppermute | solution.py:24
  20.1 0.0 collective-permute-done.2.refs_4_.refs_0_.refs_2_
  20.1 0.0 collective-permute-done.3.refs_6_.refs_2_.refs_3_
  20.1 0.0 collective-permute-done.9.refs_8_
  20.1 1.4 %near_attention.1 = (f32[2,512,512]{2,1,0:T(8,128)S(1)}, f32[2,512,512]{2,1,0:T(8,128)S(1)}, f32[2,128,512]{2,1,0:T(8,128)S(1)}, f32[2,2,512]{2,1,0:T(2,128)S(1)...) custom-call(bf16[256,256]{1,0:T(8,128)(2,1)S(1)} %collective-permute-done.4.refs_0_, ...), custom_call_target="tpu_custom_call" | custom-call | flops 2000000000 | tf_op jit(solution)/shard_map/near_attention/pallas_call | solution.py:70
  21.5 0.4 collective-permute-done.7.refs_4_
  21.9 2.4 %collective-permute-done.8.refs_5_ = bf16[128,256]{1,0:T(8,128)(2,1)S(1)} collective-permute-done((bf16[128,256]{1,0:T(8,128)(2,1)S(1)}, bf16[128,256]{1,0:T(8,128)(2,1)S(1)}, u32[]{:S(2)}, u32[]{:S(2)}) %collective-permute-start.8) | collective-permute-done | bytes 65568 | tf_op jit(solution)/shard_map/ppermute | solution.py:24
  24.2 1.1 %far_attention.1 = (bf16[256,256]{1,0:T(8,128)(2,1)S(1)}, bf16[256,256]{1,0:T(8,128)(2,1)S(1)}, bf16[256,256]{1,0:T(8,128)(2,1)S(1)}, bf16[256,256]{1,0:T(8,128)...) custom-call(bf16[256,256]{1,0:T(8,128)(2,1)S(1)} %collective-permute, ...), custom_call_target="tpu_custom_call" | custom-call | flops 2000000000 | tf_op jit(solution)/shard_map/far_attention/pallas_call | solution.py:70
  25.3 1.9 %collective-permute-start.13 = (bf16[128,256]{1,0:T(8,128)(2,1)S(1)}, bf16[128,256]{1,0:T(8,128)(2,1)S(1)}, u32[]{:S(2)}, u32[]{:S(2)}) collective-permute-start(bf16[128,256]{1,0:T(8,128)(2,1)S(1)} %get-tuple-element.76), channel_id=1, source_target_pairs={{0,16},{2,18},{4,20},{6,22},{8,24},{10,26},{12,28},{14,30},{16,0},... | collective-permute-start | bytes 196616 | tf_op jit(solution)/shard_map/ppermute | solution.py:24
  27.2 1.5 %collective-permute-start.14 = (bf16[128,256]{1,0:T(8,128)(2,1)S(1)}, bf16[128,256]{1,0:T(8,128)(2,1)S(1)}, u32[]{:S(2)}, u32[]{:S(2)}) collective-permute-start(bf16[128,256]{1,0:T(8,128)(2,1)S(1)} %get-tuple-element.77), channel_id=1, source_target_pairs={{0,24},{2,26},{4,28},{6,30},{8,16},{10,18},{12,20},{14,22},{16,8},... | collective-permute-start | bytes 196616 | tf_op jit(solution)/shard_map/ppermute | solution.py:24
  28.7 0.2 collective-permute-start.15
  28.9 1.1 %plane_grads.1 = (bf16[256,256]{1,0:T(8,128)(2,1)S(1)}, bf16[256,256]{1,0:T(8,128)(2,1)S(1)}, bf16[256,256]{1,0:T(8,128)(2,1)S(1)}, bf16[256,256]{1,0:T(8,128)(2...) custom-call(bf16[256,256]{1,0:T(8,128)(2,1)S(1)} %get-tuple-element., ...), custom_call_target="tpu_custom_call", output_to_operand_aliasing={{0}: (11, {}), {1}: (12, {}), {2}: (13, {}), {3}: (14, {})} | custom-call | flops 2300000000 | tf_op jit(solution)/shard_map/plane_grads/pallas_call | solution.py:70
  30.0 2.3 %collective-permute-start.10 = (bf16[256,256]{1,0:T(8,128)(2,1)S(1)}, bf16[256,256]{1,0:T(8,128)(2,1)S(1)}, u32[]{:S(2)}, u32[]{:S(2)}) collective-permute-start(bf16[256,256]{1,0:T(8,128)(2,1)S(1)} %get-tuple-element.68), channel_id=1, source_target_pairs={{0,6},{2,4},{4,2},{6,0},{8,14},{10,12},{12,10},{14,8},{16,22},{18,... | collective-permute-start | bytes 393224 | tf_op jit(solution)/shard_map/ppermute | solution.py:24
  32.3 0.5 %collective-permute-start.11 = (bf16[256,256]{1,0:T(8,128)(2,1)S(1)}, bf16[256,256]{1,0:T(8,128)(2,1)S(1)}, u32[]{:S(2)}, u32[]{:S(2)}) collective-permute-start(bf16[256,256]{1,0:T(8,128)(2,1)S(1)} %get-tuple-element.69), channel_id=1, source_target_pairs={{0,2},{2,0},{4,6},{6,4},{8,10},{10,8},{12,14},{14,12},{16,18},{18,... | collective-permute-start | bytes 393224 | tf_op jit(solution)/shard_map/ppermute | solution.py:24
  32.9 0.0 collective-permute-done.13.refs_4_
  32.9 0.7 %collective-permute-start.12 = (bf16[256,256]{1,0:T(8,128)(2,1)S(1)}, bf16[256,256]{1,0:T(8,128)(2,1)S(1)}, u32[]{:S(2)}, u32[]{:S(2)}) collective-permute-start(bf16[256,256]{1,0:T(8,128)(2,1)S(1)} %get-tuple-element.70), channel_id=1, source_target_pairs={{0,4},{2,6},{4,0},{6,2},{8,12},{10,14},{12,8},{14,10},{16,20},{18,... | collective-permute-start | bytes 393224 | tf_op jit(solution)/shard_map/ppermute | solution.py:24
  33.6 0.0 collective-permute-done.14.refs_5_
  33.6 0.8 %collective-permute-done.15.refs_6_ = bf16[256,256]{1,0:T(8,128)(2,1)S(1)} collective-permute-done((bf16[256,256]{1,0:T(8,128)(2,1)S(1)}, bf16[256,256]{1,0:T(8,128)(2,1)S(1)}, u32[]{:S(2)}, u32[]{:S(2)}) %collective-permute-start.15) | collective-permute-done | bytes 131104 | tf_op jit(solution)/shard_map/ppermute | solution.py:24
  34.4 0.3 carry.1
  34.7 1.4 %collective-permute-start.18 = (bf16[256,256]{1,0:T(8,128)(2,1)S(1)}, bf16[256,256]{1,0:T(8,128)(2,1)S(1)}, u32[]{:S(2)}, u32[]{:S(2)}) collective-permute-start(bf16[256,256]{1,0:T(8,128)(2,1)S(1)} %get-tuple-element.83), channel_id=1, source_target_pairs={{0,4},{2,6},{4,0},{6,2},{8,12},{10,14},{12,8},{14,10},{16,20},{18,... | collective-permute-start | bytes 393224 | tf_op jit(solution)/shard_map/ppermute | solution.py:24
  36.1 1.6 %collective-permute-start.19 = (bf16[256,256]{1,0:T(8,128)(2,1)S(1)}, bf16[256,256]{1,0:T(8,128)(2,1)S(1)}, u32[]{:S(2)}, u32[]{:S(2)}) collective-permute-start(bf16[256,256]{1,0:T(8,128)(2,1)S(1)} %get-tuple-element.84), channel_id=1, source_target_pairs={{0,6},{2,4},{4,2},{6,0},{8,14},{10,12},{12,10},{14,8},{16,22},{18,... | collective-permute-start | bytes 393224 | tf_op jit(solution)/shard_map/ppermute | solution.py:24
  37.7 0.0 collective-permute-done.10.refs_0_.refs_3_
  37.7 0.5 %collective-permute-start.20 = (bf16[256,256]{1,0:T(8,128)(2,1)S(1)}, bf16[256,256]{1,0:T(8,128)(2,1)S(1)}, u32[]{:S(2)}, u32[]{:S(2)}) collective-permute-start(bf16[256,256]{1,0:T(8,128)(2,1)S(1)} %get-tuple-element.85), channel_id=1, source_target_pairs={{0,2},{2,0},{4,6},{6,4},{8,10},{10,8},{12,14},{14,12},{16,18},{18,... | collective-permute-start | bytes 393224 | tf_op jit(solution)/shard_map/ppermute | solution.py:24
  38.3 1.2 %collective-permute-done.11.refs_1_.refs_4_ = bf16[256,256]{1,0:T(8,128)(2,1)S(1)} collective-permute-done((bf16[256,256]{1,0:T(8,128)(2,1)S(1)}, bf16[256,256]{1,0:T(8,128)(2,1)S(1)}, u32[]{:S(2)}, u32[]{:S(2)}) %collective-permute-start.11) | collective-permute-done | bytes 131104 | tf_op jit(solution)/shard_map/ppermute | solution.py:24
  39.5 0.5 %collective-permute-done.12.refs_2_.refs_5_ = bf16[256,256]{1,0:T(8,128)(2,1)S(1)} collective-permute-done((bf16[256,256]{1,0:T(8,128)(2,1)S(1)}, bf16[256,256]{1,0:T(8,128)(2,1)S(1)}, u32[]{:S(2)}, u32[]{:S(2)}) %collective-permute-start.12) | collective-permute-done | bytes 131104 | tf_op jit(solution)/shard_map/ppermute | solution.py:24
  40.1 0.8 %project.1 = (f32[128,1024]{1,0:T(8,128)S(1)}, bf16[64,1024]{1,0:T(8,128)(2,1)S(1)}, bf16[64,1024]{1,0:T(8,128)(2,1)S(1)}) custom-call(bf16[256,256]{1,0:T(8,128)(2,1)S(1)} %collective-permute-done.10.refs_0_.refs_3_, bf16[256,256]{1,0:T(8,128)(2,1)S(1)} %collective-permute-done.11.refs_1_.refs_4_, ...), custom_call_target="tpu_custom_call" | custom-call | flops 10000000 | tf_op jit(solution)/shard_map/project/pallas_call | solution.py:70
  40.8 0.1 collective-permute-start.16
  40.9 0.5 %collective-permute-start.17 = (bf16[64,1024]{1,0:T(8,128)(2,1)S(1)}, bf16[64,1024]{1,0:T(8,128)(2,1)S(1)}, u32[]{:S(2)}, u32[]{:S(2)}) collective-permute-start(bf16[64,1024]{1,0:T(8,128)(2,1)S(1)} %get-tuple-element.82), channel_id=1, source_target_pairs={{0,1},{1,0},{2,3},{3,2},{4,5},{5,4},{6,7},{7,6},{8,9},{9,8},{10,11... | collective-permute-start | bytes 393224 | tf_op jit(solution)/shard_map/ppermute | solution.py:24
  41.4 1.5 %collective-permute-done.18.refs_7_ = bf16[256,256]{1,0:T(8,128)(2,1)S(1)} collective-permute-done((bf16[256,256]{1,0:T(8,128)(2,1)S(1)}, bf16[256,256]{1,0:T(8,128)(2,1)S(1)}, u32[]{:S(2)}, u32[]{:S(2)}) %collective-permute-start.18) | collective-permute-done | bytes 131104 | tf_op jit(solution)/shard_map/ppermute | solution.py:24
  42.9 0.0 collective-permute-done.19.refs_8_
  42.9 0.1 collective-permute-done.20.refs_9_
  42.9 0.0 collective-permute-done.16.refs_1_
  42.9 0.0 collective-permute-done.17.refs_2_
  42.9 1.1 %join.1 = (bf16[128,1024]{1,0:T(8,128)(2,1)}, bf16[128,1024]{1,0:T(8,128)(2,1)}, bf16[128,1024]{1,0:T(8,128)(2,1)}, bf16[128,1024]{1,0:T(8,128)(2,1)}) custom-call(f32[128,1024]{1,0:T(8,128)S(1)} %get-tuple-element.80.refs_0_, bf16[64,1024]{1,0:T(8,128)(2,1)S(1)} %collective-permute-done.16.refs_1_, bf16[64,1024]{1,0:T(8,128)(2,1)S(1)} %collective-permute-done.17.refs_2_, ...), custom_call_target="tpu_custom_call" | custom-call | flops 1000000000 | tf_op jit(solution)/shard_map/join/pallas_call | solution.py:70
Async XLA Ops:
  0.6 5.9 %copy-start.2 = (bf16[128,1024]{1,0:T(8,128)(2,1)S(1)}, bf16[128,1024]{1,0:T(8,128)(2,1)}, u32[]{:S(2)}) copy-start(bf16[128,1024]{1,0:T(8,128)(2,1)} %refs_1_.2) | copy-start | bytes 786436
  0.6 5.9 %copy-start = (bf16[1024,2048]{1,0:T(8,128)(2,1)S(1)}, bf16[1024,2048]{1,0:T(8,128)(2,1)}, u32[]{:S(2)}) copy-start(bf16[1024,2048]{1,0:T(8,128)(2,1)} %refs_4_.3) | copy-start | bytes 12582916
  0.7 5.9 %copy-start.1 = (bf16[128,1024]{1,0:T(8,128)(2,1)S(1)}, bf16[128,1024]{1,0:T(8,128)(2,1)}, u32[]{:S(2)}) copy-start(bf16[128,1024]{1,0:T(8,128)(2,1)} %refs_0_.2) | copy-start | bytes 786436
  0.7 5.9 %collective-permute-start = (bf16[128,1024]{1,0:T(8,128)(2,1)}, bf16[128,1024]{1,0:T(8,128)(2,1)S(1)}, u32[]{:S(2)}, u32[]{:S(2)}) collective-permute-start(bf16[128,1024]{1,0:T(8,128)(2,1)} %refs_1_.2), channel_id=1, source_target_pairs={{0,1},{1,0},{2,3},{3,2},{4,5},{5,4},{6,7},{7,6},{8,9},{9,8},{10,11... | collective-permute-start | bytes 786440 | tf_op jit(solution)/shard_map/ppermute | solution.py:24
  2.5 9.8 %collective-permute-start.4 = (bf16[256,256]{1,0:T(8,128)(2,1)S(1)}, bf16[256,256]{1,0:T(8,128)(2,1)S(1)}, u32[]{:S(2)}, u32[]{:S(2)}) collective-permute-start(bf16[256,256]{1,0:T(8,128)(2,1)S(1)} %get-tuple-element.49), channel_id=1, source_target_pairs={{0,6},{2,4},{4,2},{6,0},{8,14},{10,12},{12,10},{14,8},{16,22},{18,... | collective-permute-start | bytes 393224 | tf_op jit(solution)/shard_map/ppermute | solution.py:24
  5.9 7.7 %collective-permute-start.5 = (bf16[256,256]{1,0:T(8,128)(2,1)S(1)}, bf16[256,256]{1,0:T(8,128)(2,1)S(1)}, u32[]{:S(2)}, u32[]{:S(2)}) collective-permute-start(bf16[256,256]{1,0:T(8,128)(2,1)S(1)} %get-tuple-element.50), channel_id=1, source_target_pairs={{0,2},{2,0},{4,6},{6,4},{8,10},{10,8},{12,14},{14,12},{16,18},{18,... | collective-permute-start | bytes 393224 | tf_op jit(solution)/shard_map/ppermute | solution.py:24
  6.5 7.2 %collective-permute-start.6 = (bf16[256,256]{1,0:T(8,128)(2,1)S(1)}, bf16[256,256]{1,0:T(8,128)(2,1)S(1)}, u32[]{:S(2)}, u32[]{:S(2)}) collective-permute-start(bf16[256,256]{1,0:T(8,128)(2,1)S(1)} %get-tuple-element.51), channel_id=1, source_target_pairs={{0,4},{2,6},{4,0},{6,2},{8,12},{10,14},{12,8},{14,10},{16,20},{18,... | collective-permute-start | bytes 393224 | tf_op jit(solution)/shard_map/ppermute | solution.py:24
  8.8 9.3 %collective-permute-start.1 = (bf16[256,256]{1,0:T(8,128)(2,1)S(1)}, bf16[256,256]{1,0:T(8,128)(2,1)S(1)}, u32[]{:S(2)}, u32[]{:S(2)}) collective-permute-start(bf16[256,256]{1,0:T(8,128)(2,1)S(1)} %get-tuple-element.46), channel_id=1, source_target_pairs={{0,2},{2,0},{4,6},{6,4},{8,10},{10,8},{12,14},{14,12},{16,18},{18,... | collective-permute-start | bytes 393224 | tf_op jit(solution)/shard_map/ppermute | solution.py:24
  10.7 9.3 %collective-permute-start.2 = (bf16[256,256]{1,0:T(8,128)(2,1)S(1)}, bf16[256,256]{1,0:T(8,128)(2,1)S(1)}, u32[]{:S(2)}, u32[]{:S(2)}) collective-permute-start(bf16[256,256]{1,0:T(8,128)(2,1)S(1)} %get-tuple-element.47), channel_id=1, source_target_pairs={{0,4},{2,6},{4,0},{6,2},{8,12},{10,14},{12,8},{14,10},{16,20},{18,... | collective-permute-start | bytes 393224 | tf_op jit(solution)/shard_map/ppermute | solution.py:24
  12.3 7.8 %collective-permute-start.3 = (bf16[256,256]{1,0:T(8,128)(2,1)S(1)}, bf16[256,256]{1,0:T(8,128)(2,1)S(1)}, u32[]{:S(2)}, u32[]{:S(2)}) collective-permute-start(bf16[256,256]{1,0:T(8,128)(2,1)S(1)} %get-tuple-element.48), channel_id=1, source_target_pairs={{0,6},{2,4},{4,2},{6,0},{8,14},{10,12},{12,10},{14,8},{16,22},{18,... | collective-permute-start | bytes 393224 | tf_op jit(solution)/shard_map/ppermute | solution.py:24
  13.9 6.2 %collective-permute-start.9 = (bf16[256,256]{1,0:T(8,128)(2,1)S(1)}, bf16[256,256]{1,0:T(8,128)(2,1)S(1)}, u32[]{:S(2)}, u32[]{:S(2)}) collective-permute-start(bf16[256,256]{1,0:T(8,128)(2,1)S(1)} %get-tuple-element.55), channel_id=1, source_target_pairs={{0,8},{2,10},{4,12},{6,14},{8,0},{10,2},{12,4},{14,6},{16,24},{18,... | collective-permute-start | bytes 393224 | tf_op jit(solution)/shard_map/ppermute | solution.py:24
  15.5 6.4 %collective-permute-start.7 = (bf16[128,256]{1,0:T(8,128)(2,1)S(1)}, bf16[128,256]{1,0:T(8,128)(2,1)S(1)}, u32[]{:S(2)}, u32[]{:S(2)}) collective-permute-start(bf16[128,256]{1,0:T(8,128)(2,1)S(1)} %get-tuple-element.53), channel_id=1, source_target_pairs={{0,16},{2,18},{4,20},{6,22},{8,24},{10,26},{12,28},{14,30},{16,0},... | collective-permute-start | bytes 196616 | tf_op jit(solution)/shard_map/ppermute | solution.py:24
  18.1 6.1 %collective-permute-start.8 = (bf16[128,256]{1,0:T(8,128)(2,1)S(1)}, bf16[128,256]{1,0:T(8,128)(2,1)S(1)}, u32[]{:S(2)}, u32[]{:S(2)}) collective-permute-start(bf16[128,256]{1,0:T(8,128)(2,1)S(1)} %get-tuple-element.54), channel_id=1, source_target_pairs={{0,24},{2,26},{4,28},{6,30},{8,16},{10,18},{12,20},{14,22},{16,8},... | collective-permute-start | bytes 196616 | tf_op jit(solution)/shard_map/ppermute | solution.py:24
  25.3 7.6 %collective-permute-start.13 = (bf16[128,256]{1,0:T(8,128)(2,1)S(1)}, bf16[128,256]{1,0:T(8,128)(2,1)S(1)}, u32[]{:S(2)}, u32[]{:S(2)}) collective-permute-start(bf16[128,256]{1,0:T(8,128)(2,1)S(1)} %get-tuple-element.76), channel_id=1, source_target_pairs={{0,16},{2,18},{4,20},{6,22},{8,24},{10,26},{12,28},{14,30},{16,0},... | collective-permute-start | bytes 196616 | tf_op jit(solution)/shard_map/ppermute | solution.py:24
  27.2 6.4 %collective-permute-start.14 = (bf16[128,256]{1,0:T(8,128)(2,1)S(1)}, bf16[128,256]{1,0:T(8,128)(2,1)S(1)}, u32[]{:S(2)}, u32[]{:S(2)}) collective-permute-start(bf16[128,256]{1,0:T(8,128)(2,1)S(1)} %get-tuple-element.77), channel_id=1, source_target_pairs={{0,24},{2,26},{4,28},{6,30},{8,16},{10,18},{12,20},{14,22},{16,8},... | collective-permute-start | bytes 196616 | tf_op jit(solution)/shard_map/ppermute | solution.py:24
  28.7 5.7 %collective-permute-start.15 = (bf16[256,256]{1,0:T(8,128)(2,1)S(1)}, bf16[256,256]{1,0:T(8,128)(2,1)S(1)}, u32[]{:S(2)}, u32[]{:S(2)}) collective-permute-start(bf16[256,256]{1,0:T(8,128)(2,1)S(1)} %get-tuple-element.78), channel_id=1, source_target_pairs={{0,8},{2,10},{4,12},{6,14},{8,0},{10,2},{12,4},{14,6},{16,24},{18,... | collective-permute-start | bytes 393224 | tf_op jit(solution)/shard_map/ppermute | solution.py:24
  30.0 7.7 %collective-permute-start.10 = (bf16[256,256]{1,0:T(8,128)(2,1)S(1)}, bf16[256,256]{1,0:T(8,128)(2,1)S(1)}, u32[]{:S(2)}, u32[]{:S(2)}) collective-permute-start(bf16[256,256]{1,0:T(8,128)(2,1)S(1)} %get-tuple-element.68), channel_id=1, source_target_pairs={{0,6},{2,4},{4,2},{6,0},{8,14},{10,12},{12,10},{14,8},{16,22},{18,... | collective-permute-start | bytes 393224 | tf_op jit(solution)/shard_map/ppermute | solution.py:24
  32.3 7.2 %collective-permute-start.11 = (bf16[256,256]{1,0:T(8,128)(2,1)S(1)}, bf16[256,256]{1,0:T(8,128)(2,1)S(1)}, u32[]{:S(2)}, u32[]{:S(2)}) collective-permute-start(bf16[256,256]{1,0:T(8,128)(2,1)S(1)} %get-tuple-element.69), channel_id=1, source_target_pairs={{0,2},{2,0},{4,6},{6,4},{8,10},{10,8},{12,14},{14,12},{16,18},{18,... | collective-permute-start | bytes 393224 | tf_op jit(solution)/shard_map/ppermute | solution.py:24
  32.9 7.2 %collective-permute-start.12 = (bf16[256,256]{1,0:T(8,128)(2,1)S(1)}, bf16[256,256]{1,0:T(8,128)(2,1)S(1)}, u32[]{:S(2)}, u32[]{:S(2)}) collective-permute-start(bf16[256,256]{1,0:T(8,128)(2,1)S(1)} %get-tuple-element.70), channel_id=1, source_target_pairs={{0,4},{2,6},{4,0},{6,2},{8,12},{10,14},{12,8},{14,10},{16,20},{18,... | collective-permute-start | bytes 393224 | tf_op jit(solution)/shard_map/ppermute | solution.py:24
  34.7 8.1 %collective-permute-start.18 = (bf16[256,256]{1,0:T(8,128)(2,1)S(1)}, bf16[256,256]{1,0:T(8,128)(2,1)S(1)}, u32[]{:S(2)}, u32[]{:S(2)}) collective-permute-start(bf16[256,256]{1,0:T(8,128)(2,1)S(1)} %get-tuple-element.83), channel_id=1, source_target_pairs={{0,4},{2,6},{4,0},{6,2},{8,12},{10,14},{12,8},{14,10},{16,20},{18,... | collective-permute-start | bytes 393224 | tf_op jit(solution)/shard_map/ppermute | solution.py:24
  36.1 6.7 %collective-permute-start.19 = (bf16[256,256]{1,0:T(8,128)(2,1)S(1)}, bf16[256,256]{1,0:T(8,128)(2,1)S(1)}, u32[]{:S(2)}, u32[]{:S(2)}) collective-permute-start(bf16[256,256]{1,0:T(8,128)(2,1)S(1)} %get-tuple-element.84), channel_id=1, source_target_pairs={{0,6},{2,4},{4,2},{6,0},{8,14},{10,12},{12,10},{14,8},{16,22},{18,... | collective-permute-start | bytes 393224 | tf_op jit(solution)/shard_map/ppermute | solution.py:24
  37.7 5.2 %collective-permute-start.20 = (bf16[256,256]{1,0:T(8,128)(2,1)S(1)}, bf16[256,256]{1,0:T(8,128)(2,1)S(1)}, u32[]{:S(2)}, u32[]{:S(2)}) collective-permute-start(bf16[256,256]{1,0:T(8,128)(2,1)S(1)} %get-tuple-element.85), channel_id=1, source_target_pairs={{0,2},{2,0},{4,6},{6,4},{8,10},{10,8},{12,14},{14,12},{16,18},{18,... | collective-permute-start | bytes 393224 | tf_op jit(solution)/shard_map/ppermute | solution.py:24
  40.8 2.1 %collective-permute-start.16 = (bf16[64,1024]{1,0:T(8,128)(2,1)S(1)}, bf16[64,1024]{1,0:T(8,128)(2,1)S(1)}, u32[]{:S(2)}, u32[]{:S(2)}) collective-permute-start(bf16[64,1024]{1,0:T(8,128)(2,1)S(1)} %get-tuple-element.81), channel_id=1, source_target_pairs={{0,1},{1,0},{2,3},{3,2},{4,5},{5,4},{6,7},{7,6},{8,9},{9,8},{10,11... | collective-permute-start | bytes 393224 | tf_op jit(solution)/shard_map/ppermute | solution.py:24
  40.9 2.0 %collective-permute-start.17 = (bf16[64,1024]{1,0:T(8,128)(2,1)S(1)}, bf16[64,1024]{1,0:T(8,128)(2,1)S(1)}, u32[]{:S(2)}, u32[]{:S(2)}) collective-permute-start(bf16[64,1024]{1,0:T(8,128)(2,1)S(1)} %get-tuple-element.82), channel_id=1, source_target_pairs={{0,1},{1,0},{2,3},{3,2},{4,5},{5,4},{6,7},{7,6},{8,9},{9,8},{10,11... | collective-permute-start | bytes 393224 | tf_op jit(solution)/shard_map/ppermute | solution.py:24

commit v9 on v8

--- a/solution.py
+++ b/solution.py
@@ -53,7 +53,7 @@
 def call(kernel, outs, *args, planes=(), after=(), aliases={}, hbm=(), hbm_out=False, scratch=(), cost_us=1.0, name=None):
     vmem = pl.BlockSpec(memory_space=pltpu.VMEM)
     in_hbm = pl.BlockSpec(memory_space=pltpu.HBM)
-    space = pltpu.HBM if hbm_out else pltpu.VMEM
+    out_hbm = range(len(outs)) if hbm_out is True else hbm_out or ()
     args = [
         pltpu.with_memory_space_constraint(a, pltpu.HBM) if n in hbm else a
         for n, a in enumerate(args)
@@ -69,12 +69,15 @@
 
     return pl.pallas_call(
         run,
-        out_shape=[space(out.shape, out.dtype) for out in outs],
+        out_shape=[
+            (pltpu.HBM if n in out_hbm else pltpu.VMEM)(out.shape, out.dtype)
+            for n, out in enumerate(outs)
+        ],
         in_specs=[in_hbm if n in hbm else vmem for n in order]
         + [pl.BlockSpec(memory_space=pl.ANY)] * len(after),
         scratch_shapes=scratch,
         input_output_aliases={places[n]: out for n, out in aliases.items()},
-        out_specs=[in_hbm if hbm_out else vmem] * len(outs),
+        out_specs=[in_hbm if n in out_hbm else vmem for n in range(len(outs))],
         compiler_params=pltpu.CompilerParams(vmem_limit_bytes=24 * 1024 * 1024),
         cost_estimate=pl.CostEstimate(
             flops=int(cost_us * 1e9), bytes_accessed=0, transcendentals=0
@@ -321,10 +324,15 @@
 
 
 def output_kernel(*refs):
-    ads, w_ref, own_out, others = refs[:PLANE], refs[PLANE], refs[PLANE + 1], refs[PLANE + 2 :]
+    ads, w_ref, gq_out, own_out = refs[:PLANE], *refs[PLANE : PLANE + 3]
+    others, sems = refs[PLANE + 3 : -1], refs[-1]
     rows, width = ads[0].shape[0] // 2, ads[0].shape[1]
     half = own_out.shape[1]
     head = lax.axis_index("head")
+    copies = start_all(
+        [(ads[r].at[part(1, rows), :], gq_out.at[:, columns(r, width)]) for r in range(PLANE)],
+        sems,
+    )
     total = None
     for r in range(PLANE):
         term = dot(ads[r][:rows, :], w_ref[columns(r, width), :])
@@ -343,18 +351,20 @@
     def _():
         write(total[:, half:], total[:, :half])
 
+    for copy in copies:
+        copy.wait()
+
 
 def join_kernel(own_ref, *refs):
     others, refs = refs[:PIECES], refs[PIECES:]
-    ads, dkvs = refs[:PLANE], refs[PLANE : 2 * PLANE]
-    o_out, gq_out, gk_out, gv_out, total, sems = refs[2 * PLANE :]
-    rows, width = ads[0].shape[0] // 2, ads[0].shape[1]
+    dkvs = refs[:PLANE]
+    o_out, gk_out, gv_out, total, sems = refs[PLANE:]
+    rows, width = dkvs[0].shape[0] // 2, dkvs[0].shape[1]
     pairs = []
     for r in range(PLANE):
         here = columns(r, width)
         pairs.append((dkvs[r].at[part(0, rows), :], gk_out.at[:, here]))
         pairs.append((dkvs[r].at[part(1, rows), :], gv_out.at[:, here]))
-        pairs.append((ads[r].at[part(1, rows), :], gq_out.at[:, here]))
     copies = start_all(pairs, sems)
     for n, other in enumerate(others):
         piece = part(n, rows // PIECES)
@@ -465,16 +475,19 @@
     backs = [xor_permute(far_grads[at], n * PLANE) for at, n in enumerate(ORDER)]
     att_dq = plane_exchange(att_dq)
     dkv = call(carry_kernel, blocks, *dkv, *backs[1:], backs[0], *extra, cost_us=5.0, name="carry")
-    own_sum, *other_sum = call(
+    grad_queries, own_sum, *other_sum = call(
         output_kernel,
-        [shape(rows, features, t=F32)] + [shape(rows // PIECES, features)] * PIECES,
-        *att_dq, out_weight, planes=((0, OAD),), after=(dkv[0],), cost_us=0.01, name="project",
+        [shape(rows, features), shape(rows, features, t=F32)]
+        + [shape(rows // PIECES, features)] * PIECES,
+        *att_dq, out_weight, planes=((0, OAD),), after=(dkv[0],),
+        hbm_out=(0,), scratch=[dma(PLANE)], cost_us=0.01, name="project",
     )
     dkv = plane_exchange(dkv)
     other_sum = [xor_permute(piece, 1, "head") for piece in other_sum]
-    output, grad_queries, grad_keys, grad_values = call(
-        join_kernel, [shape(rows, features)] * 4, own_sum, *other_sum, *att_dq, *dkv, planes=((1 + PIECES, OAD), (1 + PIECES + PLANE, ODKV)),
-        hbm_out=True, scratch=[pltpu.VMEM((rows, features), BF16), dma(3 * PLANE + 1)],
+    output, grad_keys, grad_values = call(
+        join_kernel, [shape(rows, features)] * 3, own_sum, *other_sum, *dkv,
+        planes=((1 + PIECES, ODKV),),
+        hbm_out=True, scratch=[pltpu.VMEM((rows, features), BF16), dma(2 * PLANE + 1)],
         cost_us=1.0, name="join",
     )
     return (output, grad_queries, grad_keys, grad_values)

time: 44.2 us -> 44.1 us (level)
  waiting for transfers between devices: 7.28 us -> 6.76 us
    ppermute x21, waiting for transfers between devices: 7.28 us -> 6.76 us  [xor_permute(): return lax.ppermute(block, axis, [(i, i ^ mask) for i in range(count)])]
  transfers between devices with their start and end apart: 21 -> 21, of which waited for: 8 -> 8; matrix products, arithmetic and copies ran while one was open for 0% -> 0% of each run, Pallas kernels for 17% -> 18%
where the time goes in v9:
time: 44.1 us; the launch traced here: 43.9 us
  starting transfers between devices  26.4 us (60%)
  Pallas kernels  9.97 us (23%)
  waiting for transfers between devices  6.76 us (15%)
  between operations  0.75 us (2%)
    ppermute x21, starting transfers between devices, xor_permute(): return lax.ppermute(block, axis, [(i, i ^ mask) for i in range(count)])  26.4 us
    pallas_call x9, Pallas kernels, call(): pl.pallas_call(run, out_shape=[(pltpu.HBM if n in out_hbm else pltpu.VMEM...  9.97 us
    ppermute x21, waiting for transfers between devices, xor_permute(): return lax.ppermute(block, axis, [(i, i ^ mask) for i in range(count)])  6.76 us
  transfers between devices with their start and end apart: 21, of which 8 were waited for; matrix products, arithmetic and copies ran while one was open for 0% of the time, Pallas kernels for 18%

profile of v9, /device:TPU:0, one launch (start us, length us, event | category | flops | bytes accessed | tf_op | source)
XLA Modules:
  0.0 43.9 jit_solution(12065561067890747808)
XLA Ops:
  0.6 0.0 copy-start.2
  0.6 0.0 copy-start
  0.7 0.0 copy-start.1
  0.7 0.5 %collective-permute-start = (bf16[128,1024]{1,0:T(8,128)(2,1)}, bf16[128,1024]{1,0:T(8,128)(2,1)S(1)}, u32[]{:S(2)}, u32[]{:S(2)}) collective-permute-start(bf16[128,1024]{1,0:T(8,128)(2,1)} %refs_1_.2), channel_id=1, source_target_pairs={{0,1},{1,0},{2,3},{3,2},{4,5},{5,4},{6,7},{7,6},{8,9},{9,8},{10,11... | collective-permute-start | bytes 786440 | tf_op jit(solution)/shard_map/ppermute | solution.py:24
  1.2 1.3 %pack_keys_values.1 = (bf16[256,256]{1,0:T(8,128)(2,1)S(1)}, bf16[256,256]{1,0:T(8,128)(2,1)S(1)}, bf16[256,256]{1,0:T(8,128)(2,1)S(1)}) custom-call(bf16[128,1024]{1,0:T(8,128)(2,1)} %refs_0_.3, bf16[128,1024]{1,0:T(8,128)(2,1)} %refs_1_.3), custom_call_target="tpu_custom_call" | custom-call | flops 8000000000 | tf_op jit(solution)/shard_map/pack_keys_values/pallas_call | solution.py:70
  2.5 3.4 %collective-permute-start.4 = (bf16[256,256]{1,0:T(8,128)(2,1)S(1)}, bf16[256,256]{1,0:T(8,128)(2,1)S(1)}, u32[]{:S(2)}, u32[]{:S(2)}) collective-permute-start(bf16[256,256]{1,0:T(8,128)(2,1)S(1)} %get-tuple-element.53), channel_id=1, source_target_pairs={{0,6},{2,4},{4,2},{6,0},{8,14},{10,12},{12,10},{14,8},{16,22},{18,... | collective-permute-start | bytes 393224 | tf_op jit(solution)/shard_map/ppermute | solution.py:24
  5.9 0.5 %collective-permute-start.5 = (bf16[256,256]{1,0:T(8,128)(2,1)S(1)}, bf16[256,256]{1,0:T(8,128)(2,1)S(1)}, u32[]{:S(2)}, u32[]{:S(2)}) collective-permute-start(bf16[256,256]{1,0:T(8,128)(2,1)S(1)} %get-tuple-element.54), channel_id=1, source_target_pairs={{0,2},{2,0},{4,6},{6,4},{8,10},{10,8},{12,14},{14,12},{16,18},{18,... | collective-permute-start | bytes 393224 | tf_op jit(solution)/shard_map/ppermute | solution.py:24
  6.5 0.1 collective-permute-start.6
  6.6 0.0 collective-permute-done.refs_2_
  6.6 0.0 copy-done.2
  6.6 0.0 copy-done
  6.6 0.0 copy-done.1
  6.6 2.2 %grad_attended.1 = (bf16[256,256]{1,0:T(8,128)(2,1)S(1)}, bf16[256,256]{1,0:T(8,128)(2,1)S(1)}, bf16[256,256]{1,0:T(8,128)(2,1)S(1)}, bf16[256,256]{1,0:T(8,128)(2,1)S(1)}, bf16[256,256]{1,0:T(8,128)(2,1)S(1)}) custom-call(bf16[128,1024]{1,0:T(8,128)(2,1)S(1)} %copy-done.1, bf16[128,1024]{1,0:T(8,128)(2,1)S(1)} %copy-done.2, ...), custom_call_target="tpu_custom_call" | custom-call | flops 3000000000 | tf_op jit(solution)/shard_map/grad_attended/pallas_call | solution.py:70
  8.8 2.0 %collective-permute-start.1 = (bf16[256,256]{1,0:T(8,128)(2,1)S(1)}, bf16[256,256]{1,0:T(8,128)(2,1)S(1)}, u32[]{:S(2)}, u32[]{:S(2)}) collective-permute-start(bf16[256,256]{1,0:T(8,128)(2,1)S(1)} %get-tuple-element.50), channel_id=1, source_target_pairs={{0,2},{2,0},{4,6},{6,4},{8,10},{10,8},{12,14},{14,12},{16,18},{18,... | collective-permute-start | bytes 393224 | tf_op jit(solution)/shard_map/ppermute | solution.py:24
  10.7 1.5 %collective-permute-start.2 = (bf16[256,256]{1,0:T(8,128)(2,1)S(1)}, bf16[256,256]{1,0:T(8,128)(2,1)S(1)}, u32[]{:S(2)}, u32[]{:S(2)}) collective-permute-start(bf16[256,256]{1,0:T(8,128)(2,1)S(1)} %get-tuple-element.51), channel_id=1, source_target_pairs={{0,4},{2,6},{4,0},{6,2},{8,12},{10,14},{12,8},{14,10},{16,20},{18,... | collective-permute-start | bytes 393224 | tf_op jit(solution)/shard_map/ppermute | solution.py:24
  12.3 0.0 collective-permute-done.4.refs_0_
  12.3 1.0 %collective-permute-start.3 = (bf16[256,256]{1,0:T(8,128)(2,1)S(1)}, bf16[256,256]{1,0:T(8,128)(2,1)S(1)}, u32[]{:S(2)}, u32[]{:S(2)}) collective-permute-start(bf16[256,256]{1,0:T(8,128)(2,1)S(1)} %get-tuple-element.52), channel_id=1, source_target_pairs={{0,6},{2,4},{4,2},{6,0},{8,14},{10,12},{12,10},{14,8},{16,22},{18,... | collective-permute-start | bytes 393224 | tf_op jit(solution)/shard_map/ppermute | solution.py:24
  13.2 0.4 collective-permute-done.5.refs_1_
  13.7 0.0 collective-permute-done.6.refs_2_
  13.7 0.2 pool_plane.1
  13.9 1.6 %collective-permute-start.9 = (bf16[256,256]{1,0:T(8,128)(2,1)S(1)}, bf16[256,256]{1,0:T(8,128)(2,1)S(1)}, u32[]{:S(2)}, u32[]{:S(2)}) collective-permute-start(bf16[256,256]{1,0:T(8,128)(2,1)S(1)} %get-tuple-element.59), channel_id=1, source_target_pairs={{0,8},{2,10},{4,12},{6,14},{8,0},{10,2},{12,4},{14,6},{16,24},{18,... | collective-permute-start | bytes 393224 | tf_op jit(solution)/shard_map/ppermute | solution.py:24
  15.5 2.6 %collective-permute-start.7 = (bf16[128,256]{1,0:T(8,128)(2,1)S(1)}, bf16[128,256]{1,0:T(8,128)(2,1)S(1)}, u32[]{:S(2)}, u32[]{:S(2)}) collective-permute-start(bf16[128,256]{1,0:T(8,128)(2,1)S(1)} %get-tuple-element.57), channel_id=1, source_target_pairs={{0,16},{2,18},{4,20},{6,22},{8,24},{10,26},{12,28},{14,30},{16,0},... | collective-permute-start | bytes 196616 | tf_op jit(solution)/shard_map/ppermute | solution.py:24
  18.1 0.0 collective-permute-done.1.refs_5_.refs_1_
  18.1 1.9 %collective-permute-start.8 = (bf16[128,256]{1,0:T(8,128)(2,1)S(1)}, bf16[128,256]{1,0:T(8,128)(2,1)S(1)}, u32[]{:S(2)}, u32[]{:S(2)}) collective-permute-start(bf16[128,256]{1,0:T(8,128)(2,1)S(1)} %get-tuple-element.58), channel_id=1, source_target_pairs={{0,24},{2,26},{4,28},{6,30},{8,16},{10,18},{12,20},{14,22},{16,8},... | collective-permute-start | bytes 196616 | tf_op jit(solution)/shard_map/ppermute | solution.py:24
  20.1 0.0 collective-permute-done.2.refs_4_.refs_0_.refs_2_
  20.1 0.0 collective-permute-done.3.refs_6_.refs_2_.refs_3_
  20.1 0.0 collective-permute-done.9.refs_8_
  20.1 1.4 %near_attention.1 = (f32[2,512,512]{2,1,0:T(8,128)S(1)}, f32[2,512,512]{2,1,0:T(8,128)S(1)}, f32[2,128,512]{2,1,0:T(8,128)S(1)}, f32[2,2,512]{2,1,0:T(2,128)S(1)...) custom-call(bf16[256,256]{1,0:T(8,128)(2,1)S(1)} %collective-permute-done.4.refs_0_, ...), custom_call_target="tpu_custom_call" | custom-call | flops 2000000000 | tf_op jit(solution)/shard_map/near_attention/pallas_call | solution.py:70
  21.5 0.4 collective-permute-done.7.refs_4_
  21.9 2.4 %collective-permute-done.8.refs_5_ = bf16[128,256]{1,0:T(8,128)(2,1)S(1)} collective-permute-done((bf16[128,256]{1,0:T(8,128)(2,1)S(1)}, bf16[128,256]{1,0:T(8,128)(2,1)S(1)}, u32[]{:S(2)}, u32[]{:S(2)}) %collective-permute-start.8) | collective-permute-done | bytes 65568 | tf_op jit(solution)/shard_map/ppermute | solution.py:24
  24.2 1.1 %far_attention.1 = (bf16[256,256]{1,0:T(8,128)(2,1)S(1)}, bf16[256,256]{1,0:T(8,128)(2,1)S(1)}, bf16[256,256]{1,0:T(8,128)(2,1)S(1)}, bf16[256,256]{1,0:T(8,128)...) custom-call(bf16[256,256]{1,0:T(8,128)(2,1)S(1)} %collective-permute, ...), custom_call_target="tpu_custom_call" | custom-call | flops 2000000000 | tf_op jit(solution)/shard_map/far_attention/pallas_call | solution.py:70
  25.3 1.9 %collective-permute-start.13 = (bf16[128,256]{1,0:T(8,128)(2,1)S(1)}, bf16[128,256]{1,0:T(8,128)(2,1)S(1)}, u32[]{:S(2)}, u32[]{:S(2)}) collective-permute-start(bf16[128,256]{1,0:T(8,128)(2,1)S(1)} %get-tuple-element.80), channel_id=1, source_target_pairs={{0,16},{2,18},{4,20},{6,22},{8,24},{10,26},{12,28},{14,30},{16,0},... | collective-permute-start | bytes 196616 | tf_op jit(solution)/shard_map/ppermute | solution.py:24
  27.2 1.5 %collective-permute-start.14 = (bf16[128,256]{1,0:T(8,128)(2,1)S(1)}, bf16[128,256]{1,0:T(8,128)(2,1)S(1)}, u32[]{:S(2)}, u32[]{:S(2)}) collective-permute-start(bf16[128,256]{1,0:T(8,128)(2,1)S(1)} %get-tuple-element.81), channel_id=1, source_target_pairs={{0,24},{2,26},{4,28},{6,30},{8,16},{10,18},{12,20},{14,22},{16,8},... | collective-permute-start | bytes 196616 | tf_op jit(solution)/shard_map/ppermute | solution.py:24
  28.7 0.2 collective-permute-start.15
  28.9 1.1 %plane_grads.1 = (bf16[256,256]{1,0:T(8,128)(2,1)S(1)}, bf16[256,256]{1,0:T(8,128)(2,1)S(1)}, bf16[256,256]{1,0:T(8,128)(2,1)S(1)}, bf16[256,256]{1,0:T(8,128)(2...) custom-call(bf16[256,256]{1,0:T(8,128)(2,1)S(1)} %get-tuple-element., ...), custom_call_target="tpu_custom_call", output_to_operand_aliasing={{0}: (11, {}), {1}: (12, {}), {2}: (13, {}), {3}: (14, {})} | custom-call | flops 2300000000 | tf_op jit(solution)/shard_map/plane_grads/pallas_call | solution.py:70
  30.0 2.3 %collective-permute-start.10 = (bf16[256,256]{1,0:T(8,128)(2,1)S(1)}, bf16[256,256]{1,0:T(8,128)(2,1)S(1)}, u32[]{:S(2)}, u32[]{:S(2)}) collective-permute-start(bf16[256,256]{1,0:T(8,128)(2,1)S(1)} %get-tuple-element.72), channel_id=1, source_target_pairs={{0,6},{2,4},{4,2},{6,0},{8,14},{10,12},{12,10},{14,8},{16,22},{18,... | collective-permute-start | bytes 393224 | tf_op jit(solution)/shard_map/ppermute | solution.py:24
  32.3 0.5 %collective-permute-start.11 = (bf16[256,256]{1,0:T(8,128)(2,1)S(1)}, bf16[256,256]{1,0:T(8,128)(2,1)S(1)}, u32[]{:S(2)}, u32[]{:S(2)}) collective-permute-start(bf16[256,256]{1,0:T(8,128)(2,1)S(1)} %get-tuple-element.73), channel_id=1, source_target_pairs={{0,2},{2,0},{4,6},{6,4},{8,10},{10,8},{12,14},{14,12},{16,18},{18,... | collective-permute-start | bytes 393224 | tf_op jit(solution)/shard_map/ppermute | solution.py:24
  32.9 0.0 collective-permute-done.13.refs_4_
  32.9 0.7 %collective-permute-start.12 = (bf16[256,256]{1,0:T(8,128)(2,1)S(1)}, bf16[256,256]{1,0:T(8,128)(2,1)S(1)}, u32[]{:S(2)}, u32[]{:S(2)}) collective-permute-start(bf16[256,256]{1,0:T(8,128)(2,1)S(1)} %get-tuple-element.74), channel_id=1, source_target_pairs={{0,4},{2,6},{4,0},{6,2},{8,12},{10,14},{12,8},{14,10},{16,20},{18,... | collective-permute-start | bytes 393224 | tf_op jit(solution)/shard_map/ppermute | solution.py:24
  33.6 0.0 collective-permute-done.14.refs_5_
  33.6 0.8 %collective-permute-done.15.refs_6_ = bf16[256,256]{1,0:T(8,128)(2,1)S(1)} collective-permute-done((bf16[256,256]{1,0:T(8,128)(2,1)S(1)}, bf16[256,256]{1,0:T(8,128)(2,1)S(1)}, u32[]{:S(2)}, u32[]{:S(2)}) %collective-permute-start.15) | collective-permute-done | bytes 131104 | tf_op jit(solution)/shard_map/ppermute | solution.py:24
  34.4 0.3 carry.1
  34.7 1.4 %collective-permute-start.18 = (bf16[256,256]{1,0:T(8,128)(2,1)S(1)}, bf16[256,256]{1,0:T(8,128)(2,1)S(1)}, u32[]{:S(2)}, u32[]{:S(2)}) collective-permute-start(bf16[256,256]{1,0:T(8,128)(2,1)S(1)} %get-tuple-element.87), channel_id=1, source_target_pairs={{0,4},{2,6},{4,0},{6,2},{8,12},{10,14},{12,8},{14,10},{16,20},{18,... | collective-permute-start | bytes 393224 | tf_op jit(solution)/shard_map/ppermute | solution.py:24
  36.1 1.6 %collective-permute-start.19 = (bf16[256,256]{1,0:T(8,128)(2,1)S(1)}, bf16[256,256]{1,0:T(8,128)(2,1)S(1)}, u32[]{:S(2)}, u32[]{:S(2)}) collective-permute-start(bf16[256,256]{1,0:T(8,128)(2,1)S(1)} %get-tuple-element.88), channel_id=1, source_target_pairs={{0,6},{2,4},{4,2},{6,0},{8,14},{10,12},{12,10},{14,8},{16,22},{18,... | collective-permute-start | bytes 393224 | tf_op jit(solution)/shard_map/ppermute | solution.py:24
  37.7 0.0 collective-permute-done.10.refs_0_
  37.7 0.5 %collective-permute-start.20 = (bf16[256,256]{1,0:T(8,128)(2,1)S(1)}, bf16[256,256]{1,0:T(8,128)(2,1)S(1)}, u32[]{:S(2)}, u32[]{:S(2)}) collective-permute-start(bf16[256,256]{1,0:T(8,128)(2,1)S(1)} %get-tuple-element.89), channel_id=1, source_target_pairs={{0,2},{2,0},{4,6},{6,4},{8,10},{10,8},{12,14},{14,12},{16,18},{18,... | collective-permute-start | bytes 393224 | tf_op jit(solution)/shard_map/ppermute | solution.py:24
  38.3 1.2 %collective-permute-done.11.refs_1_ = bf16[256,256]{1,0:T(8,128)(2,1)S(1)} collective-permute-done((bf16[256,256]{1,0:T(8,128)(2,1)S(1)}, bf16[256,256]{1,0:T(8,128)(2,1)S(1)}, u32[]{:S(2)}, u32[]{:S(2)}) %collective-permute-start.11) | collective-permute-done | bytes 131104 | tf_op jit(solution)/shard_map/ppermute | solution.py:24
  39.5 0.5 %collective-permute-done.12.refs_2_ = bf16[256,256]{1,0:T(8,128)(2,1)S(1)} collective-permute-done((bf16[256,256]{1,0:T(8,128)(2,1)S(1)}, bf16[256,256]{1,0:T(8,128)(2,1)S(1)}, u32[]{:S(2)}, u32[]{:S(2)}) %collective-permute-start.12) | collective-permute-done | bytes 131104 | tf_op jit(solution)/shard_map/ppermute | solution.py:24
  40.1 1.3 %project.1 = (bf16[128,1024]{1,0:T(8,128)(2,1)}, f32[128,1024]{1,0:T(8,128)S(1)}, bf16[64,1024]{1,0:T(8,128)(2,1)S(1)}, bf16[64,1024]{1,0:T(8,128)(2,1)S(1)}) custom-call(bf16[256,256]{1,0:T(8,128)(2,1)S(1)} %collective-permute-done.10.refs_0_, bf16[256,256]{1,0:T(8,128)(2,1)S(1)} %collective-permute-done.11.refs_1_, ...), custom_call_target="tpu_custom_call" | custom-call | flops 10000000 | tf_op jit(solution)/shard_map/project/pallas_call | solution.py:70
  41.4 0.1 collective-permute-start.16
  41.4 0.5 %collective-permute-start.17 = (bf16[64,1024]{1,0:T(8,128)(2,1)S(1)}, bf16[64,1024]{1,0:T(8,128)(2,1)S(1)}, u32[]{:S(2)}, u32[]{:S(2)}) collective-permute-start(bf16[64,1024]{1,0:T(8,128)(2,1)S(1)} %get-tuple-element.86), channel_id=1, source_target_pairs={{0,1},{1,0},{2,3},{3,2},{4,5},{5,4},{6,7},{7,6},{8,9},{9,8},{10,11... | collective-permute-start | bytes 393224 | tf_op jit(solution)/shard_map/ppermute | solution.py:24
  41.9 0.9 %collective-permute-done.18.refs_3_ = bf16[256,256]{1,0:T(8,128)(2,1)S(1)} collective-permute-done((bf16[256,256]{1,0:T(8,128)(2,1)S(1)}, bf16[256,256]{1,0:T(8,128)(2,1)S(1)}, u32[]{:S(2)}, u32[]{:S(2)}) %collective-permute-start.18) | collective-permute-done | bytes 131104 | tf_op jit(solution)/shard_map/ppermute | solution.py:24
  42.9 0.0 collective-permute-done.19.refs_4_
  42.9 0.1 collective-permute-done.20.refs_5_
  42.9 0.0 collective-permute-done.16.refs_1_
  42.9 0.0 collective-permute-done.17.refs_2_
  43.0 1.0 %join.1 = (bf16[128,1024]{1,0:T(8,128)(2,1)}, bf16[128,1024]{1,0:T(8,128)(2,1)}, bf16[128,1024]{1,0:T(8,128)(2,1)}) custom-call(f32[128,1024]{1,0:T(8,128)S(1)} %get-tuple-element.84.refs_0_, bf16[64,1024]{1,0:T(8,128)(2,1)S(1)} %collective-permute-done.16.refs_1_, bf16[64,1024]{1,0:T(8,128)(2,1)S(1)} %collective-permute-done.17.refs_2_, ...), custom_call_target="tpu_custom_call" | custom-call | flops 1000000000 | tf_op jit(solution)/shard_map/join/pallas_call | solution.py:70
Async XLA Ops:
  0.6 5.9 %copy-start.2 = (bf16[128,1024]{1,0:T(8,128)(2,1)S(1)}, bf16[128,1024]{1,0:T(8,128)(2,1)}, u32[]{:S(2)}) copy-start(bf16[128,1024]{1,0:T(8,128)(2,1)} %refs_1_.2) | copy-start | bytes 786436
  0.6 5.9 %copy-start = (bf16[1024,2048]{1,0:T(8,128)(2,1)S(1)}, bf16[1024,2048]{1,0:T(8,128)(2,1)}, u32[]{:S(2)}) copy-start(bf16[1024,2048]{1,0:T(8,128)(2,1)} %refs_4_.3) | copy-start | bytes 12582916
  0.7 5.9 %copy-start.1 = (bf16[128,1024]{1,0:T(8,128)(2,1)S(1)}, bf16[128,1024]{1,0:T(8,128)(2,1)}, u32[]{:S(2)}) copy-start(bf16[128,1024]{1,0:T(8,128)(2,1)} %refs_0_.2) | copy-start | bytes 786436
  0.7 5.9 %collective-permute-start = (bf16[128,1024]{1,0:T(8,128)(2,1)}, bf16[128,1024]{1,0:T(8,128)(2,1)S(1)}, u32[]{:S(2)}, u32[]{:S(2)}) collective-permute-start(bf16[128,1024]{1,0:T(8,128)(2,1)} %refs_1_.2), channel_id=1, source_target_pairs={{0,1},{1,0},{2,3},{3,2},{4,5},{5,4},{6,7},{7,6},{8,9},{9,8},{10,11... | collective-permute-start | bytes 786440 | tf_op jit(solution)/shard_map/ppermute | solution.py:24
  2.5 9.8 %collective-permute-start.4 = (bf16[256,256]{1,0:T(8,128)(2,1)S(1)}, bf16[256,256]{1,0:T(8,128)(2,1)S(1)}, u32[]{:S(2)}, u32[]{:S(2)}) collective-permute-start(bf16[256,256]{1,0:T(8,128)(2,1)S(1)} %get-tuple-element.53), channel_id=1, source_target_pairs={{0,6},{2,4},{4,2},{6,0},{8,14},{10,12},{12,10},{14,8},{16,22},{18,... | collective-permute-start | bytes 393224 | tf_op jit(solution)/shard_map/ppermute | solution.py:24
  5.9 7.7 %collective-permute-start.5 = (bf16[256,256]{1,0:T(8,128)(2,1)S(1)}, bf16[256,256]{1,0:T(8,128)(2,1)S(1)}, u32[]{:S(2)}, u32[]{:S(2)}) collective-permute-start(bf16[256,256]{1,0:T(8,128)(2,1)S(1)} %get-tuple-element.54), channel_id=1, source_target_pairs={{0,2},{2,0},{4,6},{6,4},{8,10},{10,8},{12,14},{14,12},{16,18},{18,... | collective-permute-start | bytes 393224 | tf_op jit(solution)/shard_map/ppermute | solution.py:24
  6.5 7.2 %collective-permute-start.6 = (bf16[256,256]{1,0:T(8,128)(2,1)S(1)}, bf16[256,256]{1,0:T(8,128)(2,1)S(1)}, u32[]{:S(2)}, u32[]{:S(2)}) collective-permute-start(bf16[256,256]{1,0:T(8,128)(2,1)S(1)} %get-tuple-element.55), channel_id=1, source_target_pairs={{0,4},{2,6},{4,0},{6,2},{8,12},{10,14},{12,8},{14,10},{16,20},{18,... | collective-permute-start | bytes 393224 | tf_op jit(solution)/shard_map/ppermute | solution.py:24
  8.8 9.3 %collective-permute-start.1 = (bf16[256,256]{1,0:T(8,128)(2,1)S(1)}, bf16[256,256]{1,0:T(8,128)(2,1)S(1)}, u32[]{:S(2)}, u32[]{:S(2)}) collective-permute-start(bf16[256,256]{1,0:T(8,128)(2,1)S(1)} %get-tuple-element.50), channel_id=1, source_target_pairs={{0,2},{2,0},{4,6},{6,4},{8,10},{10,8},{12,14},{14,12},{16,18},{18,... | collective-permute-start | bytes 393224 | tf_op jit(solution)/shard_map/ppermute | solution.py:24
  10.7 9.3 %collective-permute-start.2 = (bf16[256,256]{1,0:T(8,128)(2,1)S(1)}, bf16[256,256]{1,0:T(8,128)(2,1)S(1)}, u32[]{:S(2)}, u32[]{:S(2)}) collective-permute-start(bf16[256,256]{1,0:T(8,128)(2,1)S(1)} %get-tuple-element.51), channel_id=1, source_target_pairs={{0,4},{2,6},{4,0},{6,2},{8,12},{10,14},{12,8},{14,10},{16,20},{18,... | collective-permute-start | bytes 393224 | tf_op jit(solution)/shard_map/ppermute | solution.py:24
  12.3 7.8 %collective-permute-start.3 = (bf16[256,256]{1,0:T(8,128)(2,1)S(1)}, bf16[256,256]{1,0:T(8,128)(2,1)S(1)}, u32[]{:S(2)}, u32[]{:S(2)}) collective-permute-start(bf16[256,256]{1,0:T(8,128)(2,1)S(1)} %get-tuple-element.52), channel_id=1, source_target_pairs={{0,6},{2,4},{4,2},{6,0},{8,14},{10,12},{12,10},{14,8},{16,22},{18,... | collective-permute-start | bytes 393224 | tf_op jit(solution)/shard_map/ppermute | solution.py:24
  13.9 6.2 %collective-permute-start.9 = (bf16[256,256]{1,0:T(8,128)(2,1)S(1)}, bf16[256,256]{1,0:T(8,128)(2,1)S(1)}, u32[]{:S(2)}, u32[]{:S(2)}) collective-permute-start(bf16[256,256]{1,0:T(8,128)(2,1)S(1)} %get-tuple-element.59), channel_id=1, source_target_pairs={{0,8},{2,10},{4,12},{6,14},{8,0},{10,2},{12,4},{14,6},{16,24},{18,... | collective-permute-start | bytes 393224 | tf_op jit(solution)/shard_map/ppermute | solution.py:24
  15.5 6.4 %collective-permute-start.7 = (bf16[128,256]{1,0:T(8,128)(2,1)S(1)}, bf16[128,256]{1,0:T(8,128)(2,1)S(1)}, u32[]{:S(2)}, u32[]{:S(2)}) collective-permute-start(bf16[128,256]{1,0:T(8,128)(2,1)S(1)} %get-tuple-element.57), channel_id=1, source_target_pairs={{0,16},{2,18},{4,20},{6,22},{8,24},{10,26},{12,28},{14,30},{16,0},... | collective-permute-start | bytes 196616 | tf_op jit(solution)/shard_map/ppermute | solution.py:24
  18.1 6.1 %collective-permute-start.8 = (bf16[128,256]{1,0:T(8,128)(2,1)S(1)}, bf16[128,256]{1,0:T(8,128)(2,1)S(1)}, u32[]{:S(2)}, u32[]{:S(2)}) collective-permute-start(bf16[128,256]{1,0:T(8,128)(2,1)S(1)} %get-tuple-element.58), channel_id=1, source_target_pairs={{0,24},{2,26},{4,28},{6,30},{8,16},{10,18},{12,20},{14,22},{16,8},... | collective-permute-start | bytes 196616 | tf_op jit(solution)/shard_map/ppermute | solution.py:24
  25.3 7.6 %collective-permute-start.13 = (bf16[128,256]{1,0:T(8,128)(2,1)S(1)}, bf16[128,256]{1,0:T(8,128)(2,1)S(1)}, u32[]{:S(2)}, u32[]{:S(2)}) collective-permute-start(bf16[128,256]{1,0:T(8,128)(2,1)S(1)} %get-tuple-element.80), channel_id=1, source_target_pairs={{0,16},{2,18},{4,20},{6,22},{8,24},{10,26},{12,28},{14,30},{16,0},... | collective-permute-start | bytes 196616 | tf_op jit(solution)/shard_map/ppermute | solution.py:24
  27.2 6.4 %collective-permute-start.14 = (bf16[128,256]{1,0:T(8,128)(2,1)S(1)}, bf16[128,256]{1,0:T(8,128)(2,1)S(1)}, u32[]{:S(2)}, u32[]{:S(2)}) collective-permute-start(bf16[128,256]{1,0:T(8,128)(2,1)S(1)} %get-tuple-element.81), channel_id=1, source_target_pairs={{0,24},{2,26},{4,28},{6,30},{8,16},{10,18},{12,20},{14,22},{16,8},... | collective-permute-start | bytes 196616 | tf_op jit(solution)/shard_map/ppermute | solution.py:24
  28.7 5.7 %collective-permute-start.15 = (bf16[256,256]{1,0:T(8,128)(2,1)S(1)}, bf16[256,256]{1,0:T(8,128)(2,1)S(1)}, u32[]{:S(2)}, u32[]{:S(2)}) collective-permute-start(bf16[256,256]{1,0:T(8,128)(2,1)S(1)} %get-tuple-element.82), channel_id=1, source_target_pairs={{0,8},{2,10},{4,12},{6,14},{8,0},{10,2},{12,4},{14,6},{16,24},{18,... | collective-permute-start | bytes 393224 | tf_op jit(solution)/shard_map/ppermute | solution.py:24
  30.0 7.7 %collective-permute-start.10 = (bf16[256,256]{1,0:T(8,128)(2,1)S(1)}, bf16[256,256]{1,0:T(8,128)(2,1)S(1)}, u32[]{:S(2)}, u32[]{:S(2)}) collective-permute-start(bf16[256,256]{1,0:T(8,128)(2,1)S(1)} %get-tuple-element.72), channel_id=1, source_target_pairs={{0,6},{2,4},{4,2},{6,0},{8,14},{10,12},{12,10},{14,8},{16,22},{18,... | collective-permute-start | bytes 393224 | tf_op jit(solution)/shard_map/ppermute | solution.py:24
  32.3 7.2 %collective-permute-start.11 = (bf16[256,256]{1,0:T(8,128)(2,1)S(1)}, bf16[256,256]{1,0:T(8,128)(2,1)S(1)}, u32[]{:S(2)}, u32[]{:S(2)}) collective-permute-start(bf16[256,256]{1,0:T(8,128)(2,1)S(1)} %get-tuple-element.73), channel_id=1, source_target_pairs={{0,2},{2,0},{4,6},{6,4},{8,10},{10,8},{12,14},{14,12},{16,18},{18,... | collective-permute-start | bytes 393224 | tf_op jit(solution)/shard_map/ppermute | solution.py:24
  32.9 7.2 %collective-permute-start.12 = (bf16[256,256]{1,0:T(8,128)(2,1)S(1)}, bf16[256,256]{1,0:T(8,128)(2,1)S(1)}, u32[]{:S(2)}, u32[]{:S(2)}) collective-permute-start(bf16[256,256]{1,0:T(8,128)(2,1)S(1)} %get-tuple-element.74), channel_id=1, source_target_pairs={{0,4},{2,6},{4,0},{6,2},{8,12},{10,14},{12,8},{14,10},{16,20},{18,... | collective-permute-start | bytes 393224 | tf_op jit(solution)/shard_map/ppermute | solution.py:24
  34.7 8.1 %collective-permute-start.18 = (bf16[256,256]{1,0:T(8,128)(2,1)S(1)}, bf16[256,256]{1,0:T(8,128)(2,1)S(1)}, u32[]{:S(2)}, u32[]{:S(2)}) collective-permute-start(bf16[256,256]{1,0:T(8,128)(2,1)S(1)} %get-tuple-element.87), channel_id=1, source_target_pairs={{0,4},{2,6},{4,0},{6,2},{8,12},{10,14},{12,8},{14,10},{16,20},{18,... | collective-permute-start | bytes 393224 | tf_op jit(solution)/shard_map/ppermute | solution.py:24
  36.1 6.7 %collective-permute-start.19 = (bf16[256,256]{1,0:T(8,128)(2,1)S(1)}, bf16[256,256]{1,0:T(8,128)(2,1)S(1)}, u32[]{:S(2)}, u32[]{:S(2)}) collective-permute-start(bf16[256,256]{1,0:T(8,128)(2,1)S(1)} %get-tuple-element.88), channel_id=1, source_target_pairs={{0,6},{2,4},{4,2},{6,0},{8,14},{10,12},{12,10},{14,8},{16,22},{18,... | collective-permute-start | bytes 393224 | tf_op jit(solution)/shard_map/ppermute | solution.py:24
  37.7 5.2 %collective-permute-start.20 = (bf16[256,256]{1,0:T(8,128)(2,1)S(1)}, bf16[256,256]{1,0:T(8,128)(2,1)S(1)}, u32[]{:S(2)}, u32[]{:S(2)}) collective-permute-start(bf16[256,256]{1,0:T(8,128)(2,1)S(1)} %get-tuple-element.89), channel_id=1, source_target_pairs={{0,2},{2,0},{4,6},{6,4},{8,10},{10,8},{12,14},{14,12},{16,18},{18,... | collective-permute-start | bytes 393224 | tf_op jit(solution)/shard_map/ppermute | solution.py:24
  41.4 1.6 %collective-permute-start.16 = (bf16[64,1024]{1,0:T(8,128)(2,1)S(1)}, bf16[64,1024]{1,0:T(8,128)(2,1)S(1)}, u32[]{:S(2)}, u32[]{:S(2)}) collective-permute-start(bf16[64,1024]{1,0:T(8,128)(2,1)S(1)} %get-tuple-element.85), channel_id=1, source_target_pairs={{0,1},{1,0},{2,3},{3,2},{4,5},{5,4},{6,7},{7,6},{8,9},{9,8},{10,11... | collective-permute-start | bytes 393224 | tf_op jit(solution)/shard_map/ppermute | solution.py:24
  41.4 1.5 %collective-permute-start.17 = (bf16[64,1024]{1,0:T(8,128)(2,1)S(1)}, bf16[64,1024]{1,0:T(8,128)(2,1)S(1)}, u32[]{:S(2)}, u32[]{:S(2)}) collective-permute-start(bf16[64,1024]{1,0:T(8,128)(2,1)S(1)} %get-tuple-element.86), channel_id=1, source_target_pairs={{0,1},{1,0},{2,3},{3,2},{4,5},{5,4},{6,7},{7,6},{8,9},{9,8},{10,11... | collective-permute-start | bytes 393224 | tf_op jit(solution)/shard_map/ppermute | solution.py:24

commit v10 on v9

--- a/solution.py
+++ b/solution.py
@@ -324,15 +324,16 @@
 
 
 def output_kernel(*refs):
-    ads, w_ref, gq_out, own_out = refs[:PLANE], *refs[PLANE : PLANE + 3]
-    others, sems = refs[PLANE + 3 : -1], refs[-1]
+    ads, w_ref, dkv_ref = refs[:PLANE], *refs[PLANE : PLANE + 2]
+    gq_out, gk_out, gv_out, own_out = refs[PLANE + 2 : PLANE + 6]
+    others, sems = refs[PLANE + 6 : -1], refs[-1]
     rows, width = ads[0].shape[0] // 2, ads[0].shape[1]
     half = own_out.shape[1]
     head = lax.axis_index("head")
-    copies = start_all(
-        [(ads[r].at[part(1, rows), :], gq_out.at[:, columns(r, width)]) for r in range(PLANE)],
-        sems,
-    )
+    pairs = [(ads[r].at[part(1, rows), :], gq_out.at[:, columns(r, width)]) for r in range(PLANE)]
+    for m, out in enumerate((gk_out, gv_out)):
+        pairs.append((dkv_ref.at[part(m, rows), :], out.at[:, columns(0, width)]))
+    copies = start_all(pairs, sems)
     total = None
     for r in range(PLANE):
         term = dot(ads[r][:rows, :], w_ref[columns(r, width), :])
@@ -357,14 +358,14 @@
 
 def join_kernel(own_ref, *refs):
     others, refs = refs[:PIECES], refs[PIECES:]
-    dkvs = refs[:PLANE]
-    o_out, gk_out, gv_out, total, sems = refs[PLANE:]
+    dkvs = refs[: PLANE - 1]
+    o_out, gk_out, gv_out, total, sems = refs[PLANE + 1 :]
     rows, width = dkvs[0].shape[0] // 2, dkvs[0].shape[1]
     pairs = []
-    for r in range(PLANE):
+    for r, dkv in zip(ODKV, dkvs):
         here = columns(r, width)
-        pairs.append((dkvs[r].at[part(0, rows), :], gk_out.at[:, here]))
-        pairs.append((dkvs[r].at[part(1, rows), :], gv_out.at[:, here]))
+        pairs.append((dkv.at[part(0, rows), :], gk_out.at[:, here]))
+        pairs.append((dkv.at[part(1, rows), :], gv_out.at[:, here]))
     copies = start_all(pairs, sems)
     for n, other in enumerate(others):
         piece = part(n, rows // PIECES)
@@ -475,19 +476,21 @@
     backs = [xor_permute(far_grads[at], n * PLANE) for at, n in enumerate(ORDER)]
     att_dq = plane_exchange(att_dq)
     dkv = call(carry_kernel, blocks, *dkv, *backs[1:], backs[0], *extra, cost_us=5.0, name="carry")
-    grad_queries, own_sum, *other_sum = call(
+    grad_queries, grad_keys, grad_values, own_sum, *other_sum = call(
         output_kernel,
-        [shape(rows, features), shape(rows, features, t=F32)]
+        [shape(rows, features)] * 3 + [shape(rows, features, t=F32)]
         + [shape(rows // PIECES, features)] * PIECES,
-        *att_dq, out_weight, planes=((0, OAD),), after=(dkv[0],),
-        hbm_out=(0,), scratch=[dma(PLANE)], cost_us=0.01, name="project",
+        *att_dq, out_weight, dkv[0], planes=((0, OAD),),
+        hbm_out=(0, 1, 2), scratch=[dma(PLANE + 2)], cost_us=0.01, name="project",
     )
     dkv = plane_exchange(dkv)
     other_sum = [xor_permute(piece, 1, "head") for piece in other_sum]
     output, grad_keys, grad_values = call(
-        join_kernel, [shape(rows, features)] * 3, own_sum, *other_sum, *dkv,
-        planes=((1 + PIECES, ODKV),),
-        hbm_out=True, scratch=[pltpu.VMEM((rows, features), BF16), dma(2 * PLANE + 1)],
+        join_kernel, [shape(rows, features)] * 3, own_sum, *other_sum,
+        *[dkv[r] for r in ODKV[:-1]], grad_keys, grad_values,
+        hbm=(PIECES + PLANE, PIECES + PLANE + 1),
+        aliases={PIECES + PLANE: 1, PIECES + PLANE + 1: 2},
+        hbm_out=True, scratch=[pltpu.VMEM((rows, features), BF16), dma(2 * PLANE - 1)],
         cost_us=1.0, name="join",
     )
     return (output, grad_queries, grad_keys, grad_values)

time: 44.1 us -> 44.1 us (level)
  transfers between devices with their start and end apart: 21 -> 21, of which waited for: 8 -> 9; matrix products, arithmetic and copies ran while one was open for 0% -> 0% of each run, Pallas kernels for 18% -> 18%
where the time goes in v10:
time: 44.1 us; the launch traced here: 43.9 us
  starting transfers between devices  26.4 us (60%)
  Pallas kernels  9.93 us (23%)
  waiting for transfers between devices  6.76 us (15%)
  between operations  0.75 us (2%)
    ppermute x21, starting transfers between devices, xor_permute(): return lax.ppermute(block, axis, [(i, i ^ mask) for i in range(count)])  26.4 us
    pallas_call x9, Pallas kernels, call(): pl.pallas_call(run, out_shape=[(pltpu.HBM if n in out_hbm else pltpu.VMEM...  9.93 us
    ppermute x21, waiting for transfers between devices, xor_permute(): return lax.ppermute(block, axis, [(i, i ^ mask) for i in range(count)])  6.76 us
  transfers between devices with their start and end apart: 21, of which 9 were waited for; matrix products, arithmetic and copies ran while one was open for 0% of the time, Pallas kernels for 18%

profile of v10, /device:TPU:0, one launch (start us, length us, event | category | flops | bytes accessed | tf_op | source)
XLA Modules:
  0.0 43.9 jit_solution(17133448519331760741)
XLA Ops:
  0.6 0.0 copy-start.2
  0.6 0.0 copy-start
  0.7 0.0 copy-start.1
  0.7 0.5 %collective-permute-start = (bf16[128,1024]{1,0:T(8,128)(2,1)}, bf16[128,1024]{1,0:T(8,128)(2,1)S(1)}, u32[]{:S(2)}, u32[]{:S(2)}) collective-permute-start(bf16[128,1024]{1,0:T(8,128)(2,1)} %refs_1_.2), channel_id=1, source_target_pairs={{0,1},{1,0},{2,3},{3,2},{4,5},{5,4},{6,7},{7,6},{8,9},{9,8},{10,11... | collective-permute-start | bytes 786440 | tf_op jit(solution)/shard_map/ppermute | solution.py:24
  1.2 1.3 %pack_keys_values.1 = (bf16[256,256]{1,0:T(8,128)(2,1)S(1)}, bf16[256,256]{1,0:T(8,128)(2,1)S(1)}, bf16[256,256]{1,0:T(8,128)(2,1)S(1)}) custom-call(bf16[128,1024]{1,0:T(8,128)(2,1)} %refs_0_.3, bf16[128,1024]{1,0:T(8,128)(2,1)} %refs_1_.3), custom_call_target="tpu_custom_call" | custom-call | flops 8000000000 | tf_op jit(solution)/shard_map/pack_keys_values/pallas_call | solution.py:70
  2.5 3.4 %collective-permute-start.4 = (bf16[256,256]{1,0:T(8,128)(2,1)S(1)}, bf16[256,256]{1,0:T(8,128)(2,1)S(1)}, u32[]{:S(2)}, u32[]{:S(2)}) collective-permute-start(bf16[256,256]{1,0:T(8,128)(2,1)S(1)} %get-tuple-element.55), channel_id=1, source_target_pairs={{0,6},{2,4},{4,2},{6,0},{8,14},{10,12},{12,10},{14,8},{16,22},{18,... | collective-permute-start | bytes 393224 | tf_op jit(solution)/shard_map/ppermute | solution.py:24
  5.9 0.5 %collective-permute-start.5 = (bf16[256,256]{1,0:T(8,128)(2,1)S(1)}, bf16[256,256]{1,0:T(8,128)(2,1)S(1)}, u32[]{:S(2)}, u32[]{:S(2)}) collective-permute-start(bf16[256,256]{1,0:T(8,128)(2,1)S(1)} %get-tuple-element.56), channel_id=1, source_target_pairs={{0,2},{2,0},{4,6},{6,4},{8,10},{10,8},{12,14},{14,12},{16,18},{18,... | collective-permute-start | bytes 393224 | tf_op jit(solution)/shard_map/ppermute | solution.py:24
  6.5 0.1 collective-permute-start.6
  6.6 0.0 collective-permute-done.refs_2_
  6.6 0.0 copy-done.2
  6.6 0.0 copy-done
  6.6 0.0 copy-done.1
  6.6 2.2 %grad_attended.1 = (bf16[256,256]{1,0:T(8,128)(2,1)S(1)}, bf16[256,256]{1,0:T(8,128)(2,1)S(1)}, bf16[256,256]{1,0:T(8,128)(2,1)S(1)}, bf16[256,256]{1,0:T(8,128)(2,1)S(1)}, bf16[256,256]{1,0:T(8,128)(2,1)S(1)}) custom-call(bf16[128,1024]{1,0:T(8,128)(2,1)S(1)} %copy-done.1, bf16[128,1024]{1,0:T(8,128)(2,1)S(1)} %copy-done.2, ...), custom_call_target="tpu_custom_call" | custom-call | flops 3000000000 | tf_op jit(solution)/shard_map/grad_attended/pallas_call | solution.py:70
  8.8 2.0 %collective-permute-start.1 = (bf16[256,256]{1,0:T(8,128)(2,1)S(1)}, bf16[256,256]{1,0:T(8,128)(2,1)S(1)}, u32[]{:S(2)}, u32[]{:S(2)}) collective-permute-start(bf16[256,256]{1,0:T(8,128)(2,1)S(1)} %get-tuple-element.52), channel_id=1, source_target_pairs={{0,2},{2,0},{4,6},{6,4},{8,10},{10,8},{12,14},{14,12},{16,18},{18,... | collective-permute-start | bytes 393224 | tf_op jit(solution)/shard_map/ppermute | solution.py:24
  10.7 1.5 %collective-permute-start.2 = (bf16[256,256]{1,0:T(8,128)(2,1)S(1)}, bf16[256,256]{1,0:T(8,128)(2,1)S(1)}, u32[]{:S(2)}, u32[]{:S(2)}) collective-permute-start(bf16[256,256]{1,0:T(8,128)(2,1)S(1)} %get-tuple-element.53), channel_id=1, source_target_pairs={{0,4},{2,6},{4,0},{6,2},{8,12},{10,14},{12,8},{14,10},{16,20},{18,... | collective-permute-start | bytes 393224 | tf_op jit(solution)/shard_map/ppermute | solution.py:24
  12.3 0.0 collective-permute-done.4.refs_0_
  12.3 1.0 %collective-permute-start.3 = (bf16[256,256]{1,0:T(8,128)(2,1)S(1)}, bf16[256,256]{1,0:T(8,128)(2,1)S(1)}, u32[]{:S(2)}, u32[]{:S(2)}) collective-permute-start(bf16[256,256]{1,0:T(8,128)(2,1)S(1)} %get-tuple-element.54), channel_id=1, source_target_pairs={{0,6},{2,4},{4,2},{6,0},{8,14},{10,12},{12,10},{14,8},{16,22},{18,... | collective-permute-start | bytes 393224 | tf_op jit(solution)/shard_map/ppermute | solution.py:24
  13.2 0.4 collective-permute-done.5.refs_1_
  13.7 0.0 collective-permute-done.6.refs_2_
  13.7 0.2 pool_plane.1
  13.9 1.6 %collective-permute-start.9 = (bf16[256,256]{1,0:T(8,128)(2,1)S(1)}, bf16[256,256]{1,0:T(8,128)(2,1)S(1)}, u32[]{:S(2)}, u32[]{:S(2)}) collective-permute-start(bf16[256,256]{1,0:T(8,128)(2,1)S(1)} %get-tuple-element.61), channel_id=1, source_target_pairs={{0,8},{2,10},{4,12},{6,14},{8,0},{10,2},{12,4},{14,6},{16,24},{18,... | collective-permute-start | bytes 393224 | tf_op jit(solution)/shard_map/ppermute | solution.py:24
  15.5 2.6 %collective-permute-start.7 = (bf16[128,256]{1,0:T(8,128)(2,1)S(1)}, bf16[128,256]{1,0:T(8,128)(2,1)S(1)}, u32[]{:S(2)}, u32[]{:S(2)}) collective-permute-start(bf16[128,256]{1,0:T(8,128)(2,1)S(1)} %get-tuple-element.59), channel_id=1, source_target_pairs={{0,16},{2,18},{4,20},{6,22},{8,24},{10,26},{12,28},{14,30},{16,0},... | collective-permute-start | bytes 196616 | tf_op jit(solution)/shard_map/ppermute | solution.py:24
  18.1 0.0 collective-permute-done.1.refs_5_.refs_1_
  18.1 1.9 %collective-permute-start.8 = (bf16[128,256]{1,0:T(8,128)(2,1)S(1)}, bf16[128,256]{1,0:T(8,128)(2,1)S(1)}, u32[]{:S(2)}, u32[]{:S(2)}) collective-permute-start(bf16[128,256]{1,0:T(8,128)(2,1)S(1)} %get-tuple-element.60), channel_id=1, source_target_pairs={{0,24},{2,26},{4,28},{6,30},{8,16},{10,18},{12,20},{14,22},{16,8},... | collective-permute-start | bytes 196616 | tf_op jit(solution)/shard_map/ppermute | solution.py:24
  20.1 0.0 collective-permute-done.2.refs_4_.refs_0_.refs_2_
  20.1 0.0 collective-permute-done.3.refs_6_.refs_2_.refs_3_
  20.1 0.0 collective-permute-done.9.refs_8_
  20.1 1.4 %near_attention.1 = (f32[2,512,512]{2,1,0:T(8,128)S(1)}, f32[2,512,512]{2,1,0:T(8,128)S(1)}, f32[2,128,512]{2,1,0:T(8,128)S(1)}, f32[2,2,512]{2,1,0:T(2,128)S(1)...) custom-call(bf16[256,256]{1,0:T(8,128)(2,1)S(1)} %collective-permute-done.4.refs_0_, ...), custom_call_target="tpu_custom_call" | custom-call | flops 2000000000 | tf_op jit(solution)/shard_map/near_attention/pallas_call | solution.py:70
  21.5 0.4 collective-permute-done.7.refs_4_
  21.9 2.4 %collective-permute-done.8.refs_5_ = bf16[128,256]{1,0:T(8,128)(2,1)S(1)} collective-permute-done((bf16[128,256]{1,0:T(8,128)(2,1)S(1)}, bf16[128,256]{1,0:T(8,128)(2,1)S(1)}, u32[]{:S(2)}, u32[]{:S(2)}) %collective-permute-start.8) | collective-permute-done | bytes 65568 | tf_op jit(solution)/shard_map/ppermute | solution.py:24
  24.2 1.1 %far_attention.1 = (bf16[256,256]{1,0:T(8,128)(2,1)S(1)}, bf16[256,256]{1,0:T(8,128)(2,1)S(1)}, bf16[256,256]{1,0:T(8,128)(2,1)S(1)}, bf16[256,256]{1,0:T(8,128)...) custom-call(bf16[256,256]{1,0:T(8,128)(2,1)S(1)} %collective-permute, ...), custom_call_target="tpu_custom_call" | custom-call | flops 2000000000 | tf_op jit(solution)/shard_map/far_attention/pallas_call | solution.py:70
  25.3 1.9 %collective-permute-start.13 = (bf16[128,256]{1,0:T(8,128)(2,1)S(1)}, bf16[128,256]{1,0:T(8,128)(2,1)S(1)}, u32[]{:S(2)}, u32[]{:S(2)}) collective-permute-start(bf16[128,256]{1,0:T(8,128)(2,1)S(1)} %get-tuple-element.82), channel_id=1, source_target_pairs={{0,16},{2,18},{4,20},{6,22},{8,24},{10,26},{12,28},{14,30},{16,0},... | collective-permute-start | bytes 196616 | tf_op jit(solution)/shard_map/ppermute | solution.py:24
  27.2 1.5 %collective-permute-start.14 = (bf16[128,256]{1,0:T(8,128)(2,1)S(1)}, bf16[128,256]{1,0:T(8,128)(2,1)S(1)}, u32[]{:S(2)}, u32[]{:S(2)}) collective-permute-start(bf16[128,256]{1,0:T(8,128)(2,1)S(1)} %get-tuple-element.83), channel_id=1, source_target_pairs={{0,24},{2,26},{4,28},{6,30},{8,16},{10,18},{12,20},{14,22},{16,8},... | collective-permute-start | bytes 196616 | tf_op jit(solution)/shard_map/ppermute | solution.py:24
  28.7 0.2 collective-permute-start.15
  28.9 1.1 %plane_grads.1 = (bf16[256,256]{1,0:T(8,128)(2,1)S(1)}, bf16[256,256]{1,0:T(8,128)(2,1)S(1)}, bf16[256,256]{1,0:T(8,128)(2,1)S(1)}, bf16[256,256]{1,0:T(8,128)(2...) custom-call(bf16[256,256]{1,0:T(8,128)(2,1)S(1)} %get-tuple-element., ...), custom_call_target="tpu_custom_call", output_to_operand_aliasing={{0}: (11, {}), {1}: (12, {}), {2}: (13, {}), {3}: (14, {})} | custom-call | flops 2300000000 | tf_op jit(solution)/shard_map/plane_grads/pallas_call | solution.py:70
  30.0 2.3 %collective-permute-start.10 = (bf16[256,256]{1,0:T(8,128)(2,1)S(1)}, bf16[256,256]{1,0:T(8,128)(2,1)S(1)}, u32[]{:S(2)}, u32[]{:S(2)}) collective-permute-start(bf16[256,256]{1,0:T(8,128)(2,1)S(1)} %get-tuple-element.74), channel_id=1, source_target_pairs={{0,6},{2,4},{4,2},{6,0},{8,14},{10,12},{12,10},{14,8},{16,22},{18,... | collective-permute-start | bytes 393224 | tf_op jit(solution)/shard_map/ppermute | solution.py:24
  32.3 0.5 %collective-permute-start.11 = (bf16[256,256]{1,0:T(8,128)(2,1)S(1)}, bf16[256,256]{1,0:T(8,128)(2,1)S(1)}, u32[]{:S(2)}, u32[]{:S(2)}) collective-permute-start(bf16[256,256]{1,0:T(8,128)(2,1)S(1)} %get-tuple-element.75), channel_id=1, source_target_pairs={{0,2},{2,0},{4,6},{6,4},{8,10},{10,8},{12,14},{14,12},{16,18},{18,... | collective-permute-start | bytes 393224 | tf_op jit(solution)/shard_map/ppermute | solution.py:24
  32.9 0.0 collective-permute-done.13.refs_4_
  32.9 0.7 %collective-permute-start.12 = (bf16[256,256]{1,0:T(8,128)(2,1)S(1)}, bf16[256,256]{1,0:T(8,128)(2,1)S(1)}, u32[]{:S(2)}, u32[]{:S(2)}) collective-permute-start(bf16[256,256]{1,0:T(8,128)(2,1)S(1)} %get-tuple-element.76), channel_id=1, source_target_pairs={{0,4},{2,6},{4,0},{6,2},{8,12},{10,14},{12,8},{14,10},{16,20},{18,... | collective-permute-start | bytes 393224 | tf_op jit(solution)/shard_map/ppermute | solution.py:24
  33.6 0.0 collective-permute-done.14.refs_5_
  33.6 0.8 %collective-permute-done.15.refs_6_ = bf16[256,256]{1,0:T(8,128)(2,1)S(1)} collective-permute-done((bf16[256,256]{1,0:T(8,128)(2,1)S(1)}, bf16[256,256]{1,0:T(8,128)(2,1)S(1)}, u32[]{:S(2)}, u32[]{:S(2)}) %collective-permute-start.15) | collective-permute-done | bytes 131104 | tf_op jit(solution)/shard_map/ppermute | solution.py:24
  34.4 0.3 carry.1
  34.7 1.4 %collective-permute-start.18 = (bf16[256,256]{1,0:T(8,128)(2,1)S(1)}, bf16[256,256]{1,0:T(8,128)(2,1)S(1)}, u32[]{:S(2)}, u32[]{:S(2)}) collective-permute-start(bf16[256,256]{1,0:T(8,128)(2,1)S(1)} %get-tuple-element.89), channel_id=1, source_target_pairs={{0,4},{2,6},{4,0},{6,2},{8,12},{10,14},{12,8},{14,10},{16,20},{18,... | collective-permute-start | bytes 393224 | tf_op jit(solution)/shard_map/ppermute | solution.py:24
  36.1 1.6 %collective-permute-start.19 = (bf16[256,256]{1,0:T(8,128)(2,1)S(1)}, bf16[256,256]{1,0:T(8,128)(2,1)S(1)}, u32[]{:S(2)}, u32[]{:S(2)}) collective-permute-start(bf16[256,256]{1,0:T(8,128)(2,1)S(1)} %get-tuple-element.90), channel_id=1, source_target_pairs={{0,6},{2,4},{4,2},{6,0},{8,14},{10,12},{12,10},{14,8},{16,22},{18,... | collective-permute-start | bytes 393224 | tf_op jit(solution)/shard_map/ppermute | solution.py:24
  37.7 0.0 collective-permute-done.10.refs_0_
  37.7 0.5 %collective-permute-start.20 = (bf16[256,256]{1,0:T(8,128)(2,1)S(1)}, bf16[256,256]{1,0:T(8,128)(2,1)S(1)}, u32[]{:S(2)}, u32[]{:S(2)}) collective-permute-start(bf16[256,256]{1,0:T(8,128)(2,1)S(1)} %get-tuple-element.91), channel_id=1, source_target_pairs={{0,2},{2,0},{4,6},{6,4},{8,10},{10,8},{12,14},{14,12},{16,18},{18,... | collective-permute-start | bytes 393224 | tf_op jit(solution)/shard_map/ppermute | solution.py:24
  38.3 1.3 %collective-permute-done.11.refs_1_ = bf16[256,256]{1,0:T(8,128)(2,1)S(1)} collective-permute-done((bf16[256,256]{1,0:T(8,128)(2,1)S(1)}, bf16[256,256]{1,0:T(8,128)(2,1)S(1)}, u32[]{:S(2)}, u32[]{:S(2)}) %collective-permute-start.11) | collective-permute-done | bytes 131104 | tf_op jit(solution)/shard_map/ppermute | solution.py:24
  39.5 0.5 %collective-permute-done.12.refs_2_ = bf16[256,256]{1,0:T(8,128)(2,1)S(1)} collective-permute-done((bf16[256,256]{1,0:T(8,128)(2,1)S(1)}, bf16[256,256]{1,0:T(8,128)(2,1)S(1)}, u32[]{:S(2)}, u32[]{:S(2)}) %collective-permute-start.12) | collective-permute-done | bytes 131104 | tf_op jit(solution)/shard_map/ppermute | solution.py:24
  40.1 1.3 %project.1 = (bf16[128,1024]{1,0:T(8,128)(2,1)}, bf16[128,1024]{1,0:T(8,128)(2,1)}, bf16[128,1024]{1,0:T(8,128)(2,1)}, f32[128,1024]{1,0:T(8,128)S(1)}, bf16[64,...) custom-call(bf16[256,256]{1,0:T(8,128)(2,1)S(1)} %collective-permute-done.10.refs_0_, ...), custom_call_target="tpu_custom_call" | custom-call | flops 10000000 | tf_op jit(solution)/shard_map/project/pallas_call | solution.py:70
  41.4 0.1 collective-permute-start.16
  41.5 0.5 %collective-permute-start.17 = (bf16[64,1024]{1,0:T(8,128)(2,1)S(1)}, bf16[64,1024]{1,0:T(8,128)(2,1)S(1)}, u32[]{:S(2)}, u32[]{:S(2)}) collective-permute-start(bf16[64,1024]{1,0:T(8,128)(2,1)S(1)} %get-tuple-element.88), channel_id=1, source_target_pairs={{0,1},{1,0},{2,3},{3,2},{4,5},{5,4},{6,7},{7,6},{8,9},{9,8},{10,11... | collective-permute-start | bytes 393224 | tf_op jit(solution)/shard_map/ppermute | solution.py:24
  42.0 0.9 %collective-permute-done.18.refs_3_ = bf16[256,256]{1,0:T(8,128)(2,1)S(1)} collective-permute-done((bf16[256,256]{1,0:T(8,128)(2,1)S(1)}, bf16[256,256]{1,0:T(8,128)(2,1)S(1)}, u32[]{:S(2)}, u32[]{:S(2)}) %collective-permute-start.18) | collective-permute-done | bytes 131104 | tf_op jit(solution)/shard_map/ppermute | solution.py:24
  42.9 0.0 collective-permute-done.19.refs_4_
  42.9 0.1 collective-permute-done.20.refs_5_
  42.9 0.0 collective-permute-done.16.refs_1_
  42.9 0.1 collective-permute-done.17.refs_2_
  43.0 0.9 %join.1 = (bf16[128,1024]{1,0:T(8,128)(2,1)}, bf16[128,1024]{1,0:T(8,128)(2,1)}, bf16[128,1024]{1,0:T(8,128)(2,1)}) custom-call(f32[128,1024]{1,0:T(8,128)S(1)} %get-tuple-element.86.refs_0_, bf16[64,1024]{1,0:T(8,128)(2,1)S(1)} %collective-permute-done.16.refs_1_, ...), custom_call_target="tpu_custom_call", output_to_operand_aliasing={{1}: (6, {}), {2}: (7, {})} | custom-call | flops 1000000000 | tf_op jit(solution)/shard_map/join/pallas_call | solution.py:70
Async XLA Ops:
  0.6 5.9 %copy-start.2 = (bf16[128,1024]{1,0:T(8,128)(2,1)S(1)}, bf16[128,1024]{1,0:T(8,128)(2,1)}, u32[]{:S(2)}) copy-start(bf16[128,1024]{1,0:T(8,128)(2,1)} %refs_1_.2) | copy-start | bytes 786436
  0.6 5.9 %copy-start = (bf16[1024,2048]{1,0:T(8,128)(2,1)S(1)}, bf16[1024,2048]{1,0:T(8,128)(2,1)}, u32[]{:S(2)}) copy-start(bf16[1024,2048]{1,0:T(8,128)(2,1)} %refs_4_.3) | copy-start | bytes 12582916
  0.7 5.9 %copy-start.1 = (bf16[128,1024]{1,0:T(8,128)(2,1)S(1)}, bf16[128,1024]{1,0:T(8,128)(2,1)}, u32[]{:S(2)}) copy-start(bf16[128,1024]{1,0:T(8,128)(2,1)} %refs_0_.2) | copy-start | bytes 786436
  0.7 5.9 %collective-permute-start = (bf16[128,1024]{1,0:T(8,128)(2,1)}, bf16[128,1024]{1,0:T(8,128)(2,1)S(1)}, u32[]{:S(2)}, u32[]{:S(2)}) collective-permute-start(bf16[128,1024]{1,0:T(8,128)(2,1)} %refs_1_.2), channel_id=1, source_target_pairs={{0,1},{1,0},{2,3},{3,2},{4,5},{5,4},{6,7},{7,6},{8,9},{9,8},{10,11... | collective-permute-start | bytes 786440 | tf_op jit(solution)/shard_map/ppermute | solution.py:24
  2.5 9.8 %collective-permute-start.4 = (bf16[256,256]{1,0:T(8,128)(2,1)S(1)}, bf16[256,256]{1,0:T(8,128)(2,1)S(1)}, u32[]{:S(2)}, u32[]{:S(2)}) collective-permute-start(bf16[256,256]{1,0:T(8,128)(2,1)S(1)} %get-tuple-element.55), channel_id=1, source_target_pairs={{0,6},{2,4},{4,2},{6,0},{8,14},{10,12},{12,10},{14,8},{16,22},{18,... | collective-permute-start | bytes 393224 | tf_op jit(solution)/shard_map/ppermute | solution.py:24
  5.9 7.7 %collective-permute-start.5 = (bf16[256,256]{1,0:T(8,128)(2,1)S(1)}, bf16[256,256]{1,0:T(8,128)(2,1)S(1)}, u32[]{:S(2)}, u32[]{:S(2)}) collective-permute-start(bf16[256,256]{1,0:T(8,128)(2,1)S(1)} %get-tuple-element.56), channel_id=1, source_target_pairs={{0,2},{2,0},{4,6},{6,4},{8,10},{10,8},{12,14},{14,12},{16,18},{18,... | collective-permute-start | bytes 393224 | tf_op jit(solution)/shard_map/ppermute | solution.py:24
  6.5 7.2 %collective-permute-start.6 = (bf16[256,256]{1,0:T(8,128)(2,1)S(1)}, bf16[256,256]{1,0:T(8,128)(2,1)S(1)}, u32[]{:S(2)}, u32[]{:S(2)}) collective-permute-start(bf16[256,256]{1,0:T(8,128)(2,1)S(1)} %get-tuple-element.57), channel_id=1, source_target_pairs={{0,4},{2,6},{4,0},{6,2},{8,12},{10,14},{12,8},{14,10},{16,20},{18,... | collective-permute-start | bytes 393224 | tf_op jit(solution)/shard_map/ppermute | solution.py:24
  8.8 9.3 %collective-permute-start.1 = (bf16[256,256]{1,0:T(8,128)(2,1)S(1)}, bf16[256,256]{1,0:T(8,128)(2,1)S(1)}, u32[]{:S(2)}, u32[]{:S(2)}) collective-permute-start(bf16[256,256]{1,0:T(8,128)(2,1)S(1)} %get-tuple-element.52), channel_id=1, source_target_pairs={{0,2},{2,0},{4,6},{6,4},{8,10},{10,8},{12,14},{14,12},{16,18},{18,... | collective-permute-start | bytes 393224 | tf_op jit(solution)/shard_map/ppermute | solution.py:24
  10.7 9.3 %collective-permute-start.2 = (bf16[256,256]{1,0:T(8,128)(2,1)S(1)}, bf16[256,256]{1,0:T(8,128)(2,1)S(1)}, u32[]{:S(2)}, u32[]{:S(2)}) collective-permute-start(bf16[256,256]{1,0:T(8,128)(2,1)S(1)} %get-tuple-element.53), channel_id=1, source_target_pairs={{0,4},{2,6},{4,0},{6,2},{8,12},{10,14},{12,8},{14,10},{16,20},{18,... | collective-permute-start | bytes 393224 | tf_op jit(solution)/shard_map/ppermute | solution.py:24
  12.3 7.8 %collective-permute-start.3 = (bf16[256,256]{1,0:T(8,128)(2,1)S(1)}, bf16[256,256]{1,0:T(8,128)(2,1)S(1)}, u32[]{:S(2)}, u32[]{:S(2)}) collective-permute-start(bf16[256,256]{1,0:T(8,128)(2,1)S(1)} %get-tuple-element.54), channel_id=1, source_target_pairs={{0,6},{2,4},{4,2},{6,0},{8,14},{10,12},{12,10},{14,8},{16,22},{18,... | collective-permute-start | bytes 393224 | tf_op jit(solution)/shard_map/ppermute | solution.py:24
  13.9 6.2 %collective-permute-start.9 = (bf16[256,256]{1,0:T(8,128)(2,1)S(1)}, bf16[256,256]{1,0:T(8,128)(2,1)S(1)}, u32[]{:S(2)}, u32[]{:S(2)}) collective-permute-start(bf16[256,256]{1,0:T(8,128)(2,1)S(1)} %get-tuple-element.61), channel_id=1, source_target_pairs={{0,8},{2,10},{4,12},{6,14},{8,0},{10,2},{12,4},{14,6},{16,24},{18,... | collective-permute-start | bytes 393224 | tf_op jit(solution)/shard_map/ppermute | solution.py:24
  15.5 6.4 %collective-permute-start.7 = (bf16[128,256]{1,0:T(8,128)(2,1)S(1)}, bf16[128,256]{1,0:T(8,128)(2,1)S(1)}, u32[]{:S(2)}, u32[]{:S(2)}) collective-permute-start(bf16[128,256]{1,0:T(8,128)(2,1)S(1)} %get-tuple-element.59), channel_id=1, source_target_pairs={{0,16},{2,18},{4,20},{6,22},{8,24},{10,26},{12,28},{14,30},{16,0},... | collective-permute-start | bytes 196616 | tf_op jit(solution)/shard_map/ppermute | solution.py:24
  18.1 6.1 %collective-permute-start.8 = (bf16[128,256]{1,0:T(8,128)(2,1)S(1)}, bf16[128,256]{1,0:T(8,128)(2,1)S(1)}, u32[]{:S(2)}, u32[]{:S(2)}) collective-permute-start(bf16[128,256]{1,0:T(8,128)(2,1)S(1)} %get-tuple-element.60), channel_id=1, source_target_pairs={{0,24},{2,26},{4,28},{6,30},{8,16},{10,18},{12,20},{14,22},{16,8},... | collective-permute-start | bytes 196616 | tf_op jit(solution)/shard_map/ppermute | solution.py:24
  25.3 7.6 %collective-permute-start.13 = (bf16[128,256]{1,0:T(8,128)(2,1)S(1)}, bf16[128,256]{1,0:T(8,128)(2,1)S(1)}, u32[]{:S(2)}, u32[]{:S(2)}) collective-permute-start(bf16[128,256]{1,0:T(8,128)(2,1)S(1)} %get-tuple-element.82), channel_id=1, source_target_pairs={{0,16},{2,18},{4,20},{6,22},{8,24},{10,26},{12,28},{14,30},{16,0},... | collective-permute-start | bytes 196616 | tf_op jit(solution)/shard_map/ppermute | solution.py:24
  27.2 6.4 %collective-permute-start.14 = (bf16[128,256]{1,0:T(8,128)(2,1)S(1)}, bf16[128,256]{1,0:T(8,128)(2,1)S(1)}, u32[]{:S(2)}, u32[]{:S(2)}) collective-permute-start(bf16[128,256]{1,0:T(8,128)(2,1)S(1)} %get-tuple-element.83), channel_id=1, source_target_pairs={{0,24},{2,26},{4,28},{6,30},{8,16},{10,18},{12,20},{14,22},{16,8},... | collective-permute-start | bytes 196616 | tf_op jit(solution)/shard_map/ppermute | solution.py:24
  28.7 5.7 %collective-permute-start.15 = (bf16[256,256]{1,0:T(8,128)(2,1)S(1)}, bf16[256,256]{1,0:T(8,128)(2,1)S(1)}, u32[]{:S(2)}, u32[]{:S(2)}) collective-permute-start(bf16[256,256]{1,0:T(8,128)(2,1)S(1)} %get-tuple-element.84), channel_id=1, source_target_pairs={{0,8},{2,10},{4,12},{6,14},{8,0},{10,2},{12,4},{14,6},{16,24},{18,... | collective-permute-start | bytes 393224 | tf_op jit(solution)/shard_map/ppermute | solution.py:24
  30.0 7.7 %collective-permute-start.10 = (bf16[256,256]{1,0:T(8,128)(2,1)S(1)}, bf16[256,256]{1,0:T(8,128)(2,1)S(1)}, u32[]{:S(2)}, u32[]{:S(2)}) collective-permute-start(bf16[256,256]{1,0:T(8,128)(2,1)S(1)} %get-tuple-element.74), channel_id=1, source_target_pairs={{0,6},{2,4},{4,2},{6,0},{8,14},{10,12},{12,10},{14,8},{16,22},{18,... | collective-permute-start | bytes 393224 | tf_op jit(solution)/shard_map/ppermute | solution.py:24
  32.3 7.2 %collective-permute-start.11 = (bf16[256,256]{1,0:T(8,128)(2,1)S(1)}, bf16[256,256]{1,0:T(8,128)(2,1)S(1)}, u32[]{:S(2)}, u32[]{:S(2)}) collective-permute-start(bf16[256,256]{1,0:T(8,128)(2,1)S(1)} %get-tuple-element.75), channel_id=1, source_target_pairs={{0,2},{2,0},{4,6},{6,4},{8,10},{10,8},{12,14},{14,12},{16,18},{18,... | collective-permute-start | bytes 393224 | tf_op jit(solution)/shard_map/ppermute | solution.py:24
  32.9 7.2 %collective-permute-start.12 = (bf16[256,256]{1,0:T(8,128)(2,1)S(1)}, bf16[256,256]{1,0:T(8,128)(2,1)S(1)}, u32[]{:S(2)}, u32[]{:S(2)}) collective-permute-start(bf16[256,256]{1,0:T(8,128)(2,1)S(1)} %get-tuple-element.76), channel_id=1, source_target_pairs={{0,4},{2,6},{4,0},{6,2},{8,12},{10,14},{12,8},{14,10},{16,20},{18,... | collective-permute-start | bytes 393224 | tf_op jit(solution)/shard_map/ppermute | solution.py:24
  34.7 8.2 %collective-permute-start.18 = (bf16[256,256]{1,0:T(8,128)(2,1)S(1)}, bf16[256,256]{1,0:T(8,128)(2,1)S(1)}, u32[]{:S(2)}, u32[]{:S(2)}) collective-permute-start(bf16[256,256]{1,0:T(8,128)(2,1)S(1)} %get-tuple-element.89), channel_id=1, source_target_pairs={{0,4},{2,6},{4,0},{6,2},{8,12},{10,14},{12,8},{14,10},{16,20},{18,... | collective-permute-start | bytes 393224 | tf_op jit(solution)/shard_map/ppermute | solution.py:24
  36.1 6.7 %collective-permute-start.19 = (bf16[256,256]{1,0:T(8,128)(2,1)S(1)}, bf16[256,256]{1,0:T(8,128)(2,1)S(1)}, u32[]{:S(2)}, u32[]{:S(2)}) collective-permute-start(bf16[256,256]{1,0:T(8,128)(2,1)S(1)} %get-tuple-element.90), channel_id=1, source_target_pairs={{0,6},{2,4},{4,2},{6,0},{8,14},{10,12},{12,10},{14,8},{16,22},{18,... | collective-permute-start | bytes 393224 | tf_op jit(solution)/shard_map/ppermute | solution.py:24
  37.7 5.2 %collective-permute-start.20 = (bf16[256,256]{1,0:T(8,128)(2,1)S(1)}, bf16[256,256]{1,0:T(8,128)(2,1)S(1)}, u32[]{:S(2)}, u32[]{:S(2)}) collective-permute-start(bf16[256,256]{1,0:T(8,128)(2,1)S(1)} %get-tuple-element.91), channel_id=1, source_target_pairs={{0,2},{2,0},{4,6},{6,4},{8,10},{10,8},{12,14},{14,12},{16,18},{18,... | collective-permute-start | bytes 393224 | tf_op jit(solution)/shard_map/ppermute | solution.py:24
  41.4 1.5 %collective-permute-start.16 = (bf16[64,1024]{1,0:T(8,128)(2,1)S(1)}, bf16[64,1024]{1,0:T(8,128)(2,1)S(1)}, u32[]{:S(2)}, u32[]{:S(2)}) collective-permute-start(bf16[64,1024]{1,0:T(8,128)(2,1)S(1)} %get-tuple-element.87), channel_id=1, source_target_pairs={{0,1},{1,0},{2,3},{3,2},{4,5},{5,4},{6,7},{7,6},{8,9},{9,8},{10,11... | collective-permute-start | bytes 393224 | tf_op jit(solution)/shard_map/ppermute | solution.py:24
  41.5 1.5 %collective-permute-start.17 = (bf16[64,1024]{1,0:T(8,128)(2,1)S(1)}, bf16[64,1024]{1,0:T(8,128)(2,1)S(1)}, u32[]{:S(2)}, u32[]{:S(2)}) collective-permute-start(bf16[64,1024]{1,0:T(8,128)(2,1)S(1)} %get-tuple-element.88), channel_id=1, source_target_pairs={{0,1},{1,0},{2,3},{3,2},{4,5},{5,4},{6,7},{7,6},{8,9},{9,8},{10,11... | collective-permute-start | bytes 393224 | tf_op jit(solution)/shard_map/ppermute | solution.py:24
